TPU v7x, 32 devices: a whole 2x2x4 slice. The times are simulated.
32 devices in a mesh: groups: 2 (over x), bl: 16 (over z, y, core).
Axes of the slice: x: 2, y: 2, z: 4, core: 2. Of those that a mesh axis runs over, the one named last changes fastest.
Arguments:
- visibilities: bfloat16 [4096, 8, 384], P(('groups', 'bl')), parts along dimension 0, may hold values from -6 to 6
- row_owner: int32 [4096, 1], P(('groups', 'bl')), parts along dimension 0, may hold values from 0 to 15; in each aligned block of 128 rows (0 to 127, 128 to 255, ...) at most 16 rows name the same one
- row_slot: int32 [4096], P(('groups', 'bl')), parts along dimension 0, may hold values from 0 to 63
- baseline_station_pairs: int32 [1024, 2], P('bl'), may hold values from 0 to 511
- gains_coarse: float32 [1024, 8, 6], P(('groups', 'bl')), parts along dimension 0, may hold values from -3 to 3
- band_weights: float32 [768, 3], P('groups'), parts along dimension 0, may hold values from 0.2 to 1
- band_offset: int32 [768], P('groups'), parts along dimension 0, may hold values from 0 to 3
Outputs:
- averaged: bfloat16 [2048, 8, 384], P(('groups', 'bl')), parts along dimension 0
There are 2 independent parts, one for each index of `groups`. A program takes and returns all parts, laid end to end along the dimension named above; an argument that names none is the same for every part. Nothing has to cross between parts.
Inputs may be any that keep to these rules, and one draw needn't show every extreme that they name: `row_owner`: among the rows of one device no owner is named by more than 16 rows, a bound that some block reaches.
All inputs are finite; a program needn't handle non-finite values.
Results may differ from a plain program's by a relative error of at most 0.0062.
Values may be sent and summed in bfloat16 or wider, within the bound.
No kernel may reach another device: no remote copies, remote signals or barrier semaphores. Data moves between devices by JAX's collectives and lax.ppermute only.
A program may use at most 64 MiB of HBM per device.

v0:
```python
import math

import jax
import jax.numpy as jnp
from jax import lax
from jax.sharding import PartitionSpec as P


def spline_basis(band_weights, band_offset, coarse_count):
    knots = jnp.arange(coarse_count, dtype=jnp.int32)
    basis = jnp.zeros((coarse_count, band_weights.shape[0]), jnp.float32)
    for step in range(3):
        match = (knots[:, None] == band_offset[None, :] + step).astype(jnp.float32)
        basis = basis + match * band_weights[None, :, step]
    return basis


def interpolate(coarse, basis):
    return jnp.einsum("sjk,kc->sjc", coarse, basis, precision=lax.Precision.HIGHEST).astype(
        jnp.bfloat16
    )


def jones(block_vis, left_gain, right_gain):
    vis = block_vis.astype(jnp.float32)
    lhs = left_gain.astype(jnp.float32)
    rhs = right_gain.astype(jnp.float32)
    mid_re = []
    mid_im = []
    for row_a in range(2):
        for col_b in range(2):
            real_part = 0.0
            imag_part = 0.0
            for inner in range(2):
                lr = lhs[:, 2 * row_a + inner]
                li = lhs[:, 4 + 2 * row_a + inner]
                vr = vis[:, 2 * inner + col_b]
                vi = vis[:, 4 + 2 * inner + col_b]
                real_part = real_part + lr * vr - li * vi
                imag_part = imag_part + lr * vi + li * vr
            mid_re.append(real_part)
            mid_im.append(imag_part)
    out_re = []
    out_im = []
    for row_a in range(2):
        for col_b in range(2):
            real_part = 0.0
            imag_part = 0.0
            for inner in range(2):
                mr = mid_re[2 * row_a + inner]
                mi = mid_im[2 * row_a + inner]
                rr = rhs[:, 2 * col_b + inner]
                ri = rhs[:, 4 + 2 * col_b + inner]
                real_part = real_part + mr * rr + mi * ri
                imag_part = imag_part + mi * rr - mr * ri
            out_re.append(real_part)
            out_im.append(imag_part)
    return jnp.stack(out_re + out_im, axis=1).astype(jnp.bfloat16)


def sandwich(vis, left_idx, right_idx, table):
    count = vis.shape[0]
    width = math.gcd(count, 512)
    blocks = count // width

    def one_block(items):
        block_vis, left_block, right_block = items
        return jones(block_vis, table[left_block], table[right_block])

    shaped = vis.reshape(blocks, width, vis.shape[1], vis.shape[2])
    result = lax.map(
        one_block, (shaped, left_idx.reshape(blocks, width), right_idx.reshape(blocks, width))
    )
    return result.reshape(vis.shape)


def on_device(
    visibilities,
    row_owner,
    row_slot,
    baseline_station_pairs,
    gains_coarse,
    band_weights,
    band_offset,
):
    devices = lax.axis_size("bl")
    row_count = visibilities.shape[0]
    channels = visibilities.shape[2]
    capacity = 2 * row_count // devices
    owned = baseline_station_pairs.shape[0]
    basis = spline_basis(band_weights, band_offset, gains_coarse.shape[2])
    local_table = interpolate(gains_coarse, basis)
    table = lax.all_gather(local_table, "bl", axis=0, tiled=True)
    owners = row_owner[:, 0]
    member = (owners[:, None] == jnp.arange(devices, dtype=jnp.int32)[None, :]).astype(jnp.int32)
    ranking = jnp.sum((jnp.cumsum(member, axis=0) - member) * member, axis=1)
    target = owners * capacity + ranking
    slot_ids = jnp.full((devices * capacity,), -1, jnp.int32).at[target].set(row_slot)
    outgoing = (
        jnp.zeros((devices * capacity, 8, channels), jnp.bfloat16).at[target].set(visibilities)
    )
    received, arrived = (
        lax.all_to_all(outgoing, "bl", split_axis=0, concat_axis=0, tiled=True),
        lax.all_to_all(slot_ids, "bl", split_axis=0, concat_axis=0, tiled=True),
    )
    safe = jnp.clip(arrived, 0, owned - 1)
    fixed = sandwich(
        received, baseline_station_pairs[safe, 0], baseline_station_pairs[safe, 1], table
    )
    matches = arrived[None, :] == jnp.arange(owned, dtype=jnp.int32)[:, None]
    totals = jnp.dot(
        matches.astype(jnp.bfloat16),
        fixed.reshape(devices * capacity, 8 * channels),
        preferred_element_type=jnp.float32,
    )
    tallies = jnp.sum(matches.astype(jnp.float32), axis=1)
    averaged = totals / jnp.maximum(tallies, 1.0)[:, None]
    return averaged.reshape(owned, 8, channels).astype(jnp.bfloat16)


def solution(mesh):
    placed = (
        P(("groups", "bl"), None, None),
        P(("groups", "bl"), None),
        P(("groups", "bl")),
        P("bl", None),
        P(("groups", "bl"), None, None),
        P("groups", None),
        P("groups"),
    )
    return jax.shard_map(
        on_device,
        mesh=mesh,
        in_specs=placed,
        out_specs=P(("groups", "bl"), None, None),
        check_vma=False,
    )
```

profile of v0, /device:TPU:15, one launch (start us, length us, event | category | flops | bytes accessed | tf_op | source)
XLA Modules:
  0.0 120.6 jit_solution(13332186389391559038)
XLA Ops:
  7.3 0.8 slice_reduce_fusion.2
  8.1 1.9 %fusion.1 = bf16[32,8,384]{2,0,1:T(8,128)(2,1)} fusion(f32[32,8,6]{0,1,2:T(8,128)S(1)} %copy-done, f32[384]{0:T(512)S(1)} %get-tuple-element.24, s32[384]{0:T(512)S(1)} %get-tuple-element.41, f32[384]{0:T(512)S(1)} %get-tuple-element.26, s32[384]{0:T(512)S(1)} %get-tuple-element.40, f32[384]{0:T(512)S(1)} %get-tuple-element.17, s32[384]{0:T(512)} %param.13), kind=kOutput, calls=%fused_computation.12 | convolution fusion | flops 7194624 | bytes 211968 | tf_op jit(solution)/shard_map/sjk,kc->sjc/dot_general | solution.py:19
  11.0 0.8 select_reduce_fusion
  12.5 1.1 scatter_custom_fusion
  14.3 6.6 %all-to-all-start = ((s32[16,16,1]{1,2,0:T(1,128)}), s32[16,16,1]{1,2,0:T(1,128)S(1)}, u32[]{:S(2)}, u32[]{:S(2)}) async-start(s32[16,16,1]{1,2,0:T(1,128)} %bitcast.3), calls=%async_computation | async-start | bytes 16384 | tf_op jit(solution)/shard_map/all_to_all | solution.py:104
  20.8 1.3 %broadcast_in_dim.9 = bf16[256,8,384]{2,1,0:T(8,128)(2,1)} broadcast(bf16[]{:T(256)} %constant.30.clone.1), dimensions={} | broadcast | bytes 1572866 | tf_op jit(solution)/shard_map/broadcast_in_dim | solution.py:100
  22.1 15.4 %scatter_fusion = bf16[256,8,384]{2,1,0:T(8,128)(2,1)} fusion(bf16[256,8,384]{2,1,0:T(8,128)(2,1)} %broadcast_in_dim.9, s32[128]{0:T(128)S(1)} %fusion.28, bf16[128,8,384]{2,1,0:T(8,128)(2,1)S(1)} %copy-done.3), kind=kCustom, calls=%fused_computation.5 | custom fusion | bytes 2359808 | tf_op jit(solution)/shard_map/scatter | solution.py:100
  37.5 6.2 %all-to-all-start.1 = ((bf16[256,8,384]{2,1,0:T(8,128)(2,1)}), bf16[256,8,384]{2,1,0:T(8,128)(2,1)}, u32[]{:S(2)}, u32[]{:S(2)}) async-start(bf16[256,8,384]{2,1,0:T(8,128)(2,1)} %scatter_fusion), calls=%async_computation.1 | async-start | bytes 3145728 | tf_op jit(solution)/shard_map/all_to_all | solution.py:103
  45.0 2.4 %gather_fusion.2 = s32[256]{0:T(256)S(1)} fusion(s32[64,2]{0,1:T(2,128)S(1)} %copy-done.1, s32[256]{0:T(256)S(1)} %bitcast.27), kind=kCustom, calls=%fused_computation.2 | custom fusion | bytes 4096 | tf_op jit(solution)/shard_map/gather | solution.py:108
  47.4 2.4 %gather_fusion = s32[256]{0:T(256)S(1)} fusion(s32[64,2]{0,1:T(2,128)S(1)} %copy-done.1, s32[256]{0:T(256)S(1)} %bitcast.26), kind=kCustom, calls=%fused_computation | custom fusion | bytes 4096 | tf_op jit(solution)/shard_map/gather | solution.py:108
  50.0 36.5 %all-to-all-done.1 = bf16[256,8,384]{2,1,0:T(8,128)(2,1)} async-done(((bf16[256,8,384]{2,1,0:T(8,128)(2,1)}), bf16[256,8,384]{2,1,0:T(8,128)(2,1)}, u32[]{:S(2)}, u32[]{:S(2)}) %all-to-all-start.1) | async-done | bytes 1572896 | tf_op jit(solution)/shard_map/all_to_all | solution.py:103
  86.5 1.6 %copy_convert_fusion.1 = f32[256,8,384]{2,0,1:T(8,128)S(1)} fusion(bf16[256,8,384]{2,1,0:T(8,128)(2,1)} %all-to-all-done.1), kind=kLoop, calls=%fused_computation.9 | loop fusion | flops 786432 | bytes 4718592 | tf_op jit(solution)/shard_map/while/body/eval_jaxpr/convert_element_type | solution.py:25
  88.1 5.4 %copy.34 = bf16[512,8,384]{2,1,0:T(8,128)(2,1)} copy(bf16[512,8,384]{2,0,1:T(8,128)(2,1)} %all-gather.2.cloned.1.call-done) | data formatting | bytes 6291456 | tf_op jit(solution)/shard_map/all_gather | solution.py:93
  93.6 3.9 %gather_fusion.3 = bf16[256,8,384]{2,1,0:T(8,128)(2,1)} fusion(bf16[512,8,384]{2,1,0:T(8,128)(2,1)} %copy.34, s32[1024]{0:T(1024)S(1)} %get-tuple-element.42), kind=kCustom, calls=%fused_computation.3 | custom fusion | bytes 3146752 | tf_op jit(solution)/shard_map/while/body/eval_jaxpr/gather | solution.py:68
  97.5 3.9 %gather_fusion.1 = bf16[256,8,384]{2,1,0:T(8,128)(2,1)} fusion(bf16[512,8,384]{2,1,0:T(8,128)(2,1)} %copy.34, s32[1024]{0:T(1024)S(1)} %get-tuple-element.43), kind=kCustom, calls=%fused_computation.1 | custom fusion | bytes 3146752 | tf_op jit(solution)/shard_map/while/body/eval_jaxpr/gather | solution.py:68
  101.4 1.7 %copy_convert_fusion = f32[256,8,384]{2,0,1:T(8,128)S(1)} fusion(bf16[256,8,384]{2,1,0:T(8,128)(2,1)} %gather_fusion.3), kind=kLoop, calls=%fused_computation.8 | loop fusion | flops 786432 | bytes 4718592 | tf_op jit(solution)/shard_map/while/body/eval_jaxpr/convert_element_type | solution.py:27
  103.5 1.1 fusion.2
  104.6 0.8 fusion.3
  105.4 1.1 fusion.4
  107.4 0.8 fusion.6
  108.2 0.8 fusion.7
  109.0 0.8 fusion.8
  109.8 0.8 fusion.9
  110.7 1.7 %copy.39 = bf16[256,8,384]{0,2,1:T(8,128)(2,1)S(1)} copy(bf16[256,8,384]{2,0,1:T(8,128)(2,1)} %fusion.9) | data formatting | bytes 3145728 | tf_op jit(solution)/shard_map/while/body/eval_jaxpr/stack | solution.py:58
  (31 shorter events, 7.1 us)
Async XLA Ops:
  6.5 1.6 %copy-start = (f32[32,8,6]{0,1,2:T(8,128)S(1)}, f32[32,8,6]{0,1,2:T(8,128)}, u32[]{:S(2)}) copy-start(f32[32,8,6]{0,1,2:T(8,128)} %param.11) | copy-start | bytes 18436
  6.5 15.6 %copy-start.3 = (bf16[128,8,384]{2,1,0:T(8,128)(2,1)S(1)}, bf16[128,8,384]{2,1,0:T(8,128)(2,1)}, u32[]{:S(2)}) copy-start(bf16[128,8,384]{2,1,0:T(8,128)(2,1)} %param.7) | copy-start | bytes 2359300
  6.5 81.6 %all-gather.2.cloned.1.call-start = ((), (), s32[]{:S(2)}) async-start(), calls=%async_computation.2 | async-start | bytes 3342336 | tf_op jit(solution)/shard_map/all_gather | solution.py:93
  14.3 23.2 %all-to-all-start = ((s32[16,16,1]{1,2,0:T(1,128)}), s32[16,16,1]{1,2,0:T(1,128)S(1)}, u32[]{:S(2)}, u32[]{:S(2)}) async-start(s32[16,16,1]{1,2,0:T(1,128)} %bitcast.3), calls=%async_computation | async-start | bytes 16384 | tf_op jit(solution)/shard_map/all_to_all | solution.py:104
  37.5 7.5 %copy-start.1 = (s32[64,2]{0,1:T(2,128)S(1)}, s32[64,2]{0,1:T(2,128)}, u32[]{:S(2)}) copy-start(s32[64,2]{0,1:T(2,128)} %param.10) | copy-start | bytes 1540
  37.5 49.0 %all-to-all-start.1 = ((bf16[256,8,384]{2,1,0:T(8,128)(2,1)}), bf16[256,8,384]{2,1,0:T(8,128)(2,1)}, u32[]{:S(2)}, u32[]{:S(2)}) async-start(bf16[256,8,384]{2,1,0:T(8,128)(2,1)} %scatter_fusion), calls=%async_computation.1 | async-start | bytes 3145728 | tf_op jit(solution)/shard_map/all_to_all | solution.py:103
  101.4 1.9 %copy-start.2 = (bf16[256,8,384]{2,1,0:T(8,128)(2,1)S(1)}, bf16[256,8,384]{2,1,0:T(8,128)(2,1)}, u32[]{:S(2)}) copy-start(bf16[256,8,384]{2,1,0:T(8,128)(2,1)} %gather_fusion.1) | copy-start | bytes 4718596
Sparse Core Ops, SparseCore 0:
  10.2 53.0 all-gather.1
where the time goes:
time: 122 us; the launch traced here: 121 us
  local copies, waits for them, and re-layouts  40.7 us (33%)
  waiting for transfers between devices  36.6 us (30%)
  other arithmetic  14.6 us (12%)
  between operations  13.5 us (11%)
  starting transfers between devices  12.7 us (10%)
  matrix products  2.5 us (2%)
    all_to_all x1, waiting for transfers between devices, on_device(): lax.all_to_all(outgoing, 'bl', split_axis=0, concat_axis=0, tiled=True)  36.5 us
    scatter x1, local copies, waits for them, and re-layouts, on_device(): jnp.zeros((devices * capacity, 8, channels), jnp.bfloat16).at[target]  15.4 us
    gather x2, local copies, waits for them, and re-layouts, one_block(): return jones(block_vis, table[left_block], table[right_block])  7.81 us
    all_to_all x1, starting transfers between devices, on_device(): lax.all_to_all(slot_ids, 'bl', split_axis=0, concat_axis=0, tiled=True)  6.55 us
    unnamed x7, other arithmetic  6.34 us
    all_to_all x1, starting transfers between devices, on_device(): lax.all_to_all(outgoing, 'bl', split_axis=0, concat_axis=0, tiled=True)  6.15 us
    all_gather x1, local copies, waits for them, and re-layouts, on_device(): table = lax.all_gather(local_table, 'bl', axis=0, tiled=True)  5.44 us
  transfers between devices with their start and end apart: 3, of which 1 were waited for; matrix products, arithmetic and copies ran while one was open for 23% of the time, Pallas kernels for 0%

commit v1 on v0

v1 whole, which is shorter than its diff:
```python
import functools

import jax
import jax.numpy as jnp
from jax import lax
from jax.experimental import pallas as pl
from jax.experimental.pallas import tpu as pltpu
from jax.sharding import PartitionSpec as P

LANES = 128


def pack_kernel(capacity, owned, owner_s, vis_ref, owner_ref, slot_ref, coarse_ref, send_ref, aux_ref, count_s, turn_ref):
    rows = vis_ref.shape[0]
    devices = send_ref.shape[0] // capacity
    stations = coarse_ref.shape[1]
    half = stations // 2
    terms = coarse_ref.shape[0]
    for d in range(devices):
        count_s[d] = 0

    turn_ref[...] = jnp.zeros_like(turn_ref)
    turn_ref[0:terms, 0:half] = coarse_ref[:, 0:half]
    turn_ref[64 : 64 + terms, 0:half] = coarse_ref[:, half:stations]
    aux_ref[...] = jnp.full(aux_ref.shape, -1.0, jnp.float32)
    aux_ref[0:half, :] = turn_ref[...].T[0:half, :]
    codes = owner_ref[...] * owned + slot_ref[...]
    aux_ref[half : half + 1, 0:rows] = codes.astype(jnp.float32)

    def place(r, carry):
        d = owner_s[r]
        k = count_s[d]
        count_s[d] = k + 1
        send_ref[d * capacity + k] = vis_ref[r]
        return carry

    lax.fori_loop(0, rows, place, 0, unroll=8)


def prep_kernel(
    capacity,
    owned,
    stations,
    me_s,
    pairs_s,
    aux_ref,
    pairs_ref,
    weights_ref,
    offset_ref,
    left_ref,
    right_ref,
    recip_ref,
    slots_ref,
    pick_ref,
):
    devices, aux_rows, width = aux_ref.shape
    half = stations // 2
    channels = weights_ref.shape[1]
    me = me_s[0]
    first = (me * owned).astype(jnp.float32)

    codes = aux_ref[:, half, :] - first
    mine = jnp.logical_and(codes >= 0.0, codes < float(owned))
    mine_f = mine.astype(jnp.float32)
    before = (
        lax.broadcasted_iota(jnp.int32, (width, width), 0)
        < lax.broadcasted_iota(jnp.int32, (width, width), 1)
    ).astype(jnp.float32)
    rank = jnp.dot(mine_f, before, preferred_element_type=jnp.float32)
    lane = lax.broadcasted_iota(jnp.int32, (devices, LANES), 1)
    count = jnp.sum(mine_f, axis=1, keepdims=True)
    listing = jnp.where(lane < capacity, float(owned), 0.0)
    for k in range(capacity):
        here = jnp.logical_and(mine, rank == float(k))
        slot = jnp.sum(jnp.where(here, codes, 0.0), axis=1, keepdims=True)
        slot = jnp.where(count > float(k), slot, float(owned))
        listing = jnp.where(lane == k, slot, listing)
    listing = jnp.where(lane == capacity, count, listing)
    slots_ref[...] = listing.astype(jnp.int32)

    which = lax.broadcasted_iota(jnp.int32, (owned, width), 0).astype(jnp.float32)
    hits = jnp.zeros((owned, width), jnp.float32)
    for d in range(devices):
        hits = hits + (codes[d : d + 1, :] == which).astype(jnp.float32)
    tally = jnp.sum(hits, axis=1, keepdims=True)
    recip_ref[...] = jnp.broadcast_to(1.0 / jnp.maximum(tally, 1.0), recip_ref.shape)

    def pick(b, carry):
        for side in range(2):
            s = pairs_s[side, b]
            d = s // stations
            within = s - d * stations
            row = jnp.where(within >= half, within - half, within)
            pick_ref[pl.ds(side * owned + b, 1), :] = aux_ref[d, pl.ds(row, 1), :]
        return carry

    lax.fori_loop(0, owned, pick, 0, unroll=4)

    knot = lax.broadcasted_iota(jnp.int32, (LANES, channels), 0)
    knot = (knot & 63) >> 3
    basis = jnp.zeros((LANES, channels), jnp.float32)
    for step in range(3):
        basis = basis + jnp.where(
            knot == offset_ref[...] + step, weights_ref[step : step + 1, :], 0.0
        )
    part = lax.broadcasted_iota(jnp.int32, (LANES, channels), 0) & 7
    upper = lax.broadcasted_iota(jnp.int32, (owned, LANES), 1) >= 64
    for side, out in ((0, left_ref), (1, right_ref)):
        within = lax.rem(pairs_ref[:, side : side + 1], stations)
        picked = pick_ref[side * owned : (side + 1) * owned, :]
        picked = jnp.where(upper == (within >= half), picked, 0.0)
        for j in range(8):
            fine = jnp.dot(
                picked,
                jnp.where(part == j, basis, 0.0),
                precision=lax.Precision.HIGHEST,
                preferred_element_type=jnp.float32,
            )
            out[:, j * channels : (j + 1) * channels] = fine.astype(jnp.bfloat16).astype(jnp.float32)


def finish_kernel(capacity, slots_s, recv_ref, left_ref, right_ref, recip_ref, out_ref, acc_ref, res_ref):
    owned, parts, channels = out_ref.shape
    devices = recv_ref.shape[0] // capacity
    chunks = channels // LANES
    step = 4 if capacity % 4 == 0 else 1
    acc_ref[...] = jnp.zeros_like(acc_ref)

    def from_device(d, carry):
        count = slots_s[d, capacity]

        def some(i, inner):
            for u in range(step):
                k = i * step + u
                b = slots_s[d, k]
                row = recv_ref[d * capacity + k].astype(jnp.float32)
                for c in range(chunks):
                    acc_ref[c, b] += row[:, c * LANES : (c + 1) * LANES]
            return inner

        lax.fori_loop(0, (count + (step - 1)) // step, some, 0)
        return carry

    lax.fori_loop(0, devices, from_device, 0)

    flat = acc_ref.reshape(chunks * (owned + 1) * parts, LANES)
    done = res_ref.reshape(chunks * owned * parts, LANES)
    for b0 in range(0, owned, 8):
        for c in range(chunks):
            c0 = c * LANES
            from_row = (c * (owned + 1) + b0) * parts
            to_row = (c * owned + b0) * parts

            def plane(ref, j):
                return ref[b0 : b0 + 8, pl.ds(j * channels + c0, LANES)]

            vis = [flat[pl.ds(from_row + j, 8, stride=parts), :] for j in range(parts)]
            lhs = [plane(left_ref, j) for j in range(parts)]
            rhs = [plane(right_ref, j) for j in range(parts)]
            scale = recip_ref[b0 : b0 + 8, :]
            mid_re, mid_im = [], []
            for row_a in range(2):
                for col_b in range(2):
                    re = im = 0.0
                    for inner in range(2):
                        lr, li = lhs[2 * row_a + inner], lhs[4 + 2 * row_a + inner]
                        vr, vi = vis[2 * inner + col_b], vis[4 + 2 * inner + col_b]
                        re = re + lr * vr - li * vi
                        im = im + lr * vi + li * vr
                    mid_re.append(re * scale)
                    mid_im.append(im * scale)
            for row_a in range(2):
                for col_b in range(2):
                    re = im = 0.0
                    for inner in range(2):
                        mr, mi = mid_re[2 * row_a + inner], mid_im[2 * row_a + inner]
                        rr, ri = rhs[2 * col_b + inner], rhs[4 + 2 * col_b + inner]
                        re = re + mr * rr + mi * ri
                        im = im + mi * rr - mr * ri
                    j = 2 * row_a + col_b
                    done[pl.ds(to_row + j, 8, stride=parts), :] = re
                    done[pl.ds(to_row + 4 + j, 8, stride=parts), :] = im
    for c in range(chunks):
        out_ref[:, :, c * LANES : (c + 1) * LANES] = res_ref[c].astype(out_ref.dtype)


def on_device(
    visibilities,
    row_owner,
    row_slot,
    baseline_station_pairs,
    gains_coarse,
    band_weights,
    band_offset,
):
    devices = lax.axis_size("bl")
    rows, parts, channels = visibilities.shape
    capacity = 2 * rows // devices
    owned = baseline_station_pairs.shape[0]
    stations, _, knots = gains_coarse.shape
    half = stations // 2
    aux_rows = -(-(half + 1) // 8) * 8
    width = -(-rows // LANES) * LANES
    vmem = pl.BlockSpec(memory_space=pltpu.VMEM)
    smem = pl.BlockSpec(memory_space=pltpu.SMEM)
    params = pltpu.CompilerParams(vmem_limit_bytes=32 * 1024 * 1024)
    f32 = jnp.float32

    coarse = gains_coarse.transpose(2, 1, 0).reshape(knots * parts, stations)
    send, aux = pl.pallas_call(
        functools.partial(pack_kernel, capacity, owned),
        out_shape=(
            jax.ShapeDtypeStruct((devices * capacity, parts, channels), jnp.bfloat16),
            jax.ShapeDtypeStruct((aux_rows, width), f32),
        ),
        in_specs=[smem, vmem, vmem, vmem, vmem],
        out_specs=(vmem, vmem),
        scratch_shapes=[pltpu.SMEM((devices,), jnp.int32), pltpu.VMEM((LANES, LANES), f32)],
        compiler_params=params,
        name="pack_rows",
    )(
        row_owner.reshape(rows),
        visibilities,
        row_owner.reshape(1, rows),
        row_slot.reshape(1, rows),
        coarse,
    )
    every = lax.all_gather(aux, "bl", axis=0)
    received = lax.all_to_all(send, "bl", split_axis=0, concat_axis=0, tiled=True)

    me = lax.axis_index("bl").astype(jnp.int32).reshape(1)
    left, right, recip, slots = pl.pallas_call(
        functools.partial(prep_kernel, capacity, owned, stations),
        out_shape=(
            jax.ShapeDtypeStruct((owned, parts * channels), f32),
            jax.ShapeDtypeStruct((owned, parts * channels), f32),
            jax.ShapeDtypeStruct((owned, LANES), f32),
            jax.ShapeDtypeStruct((devices, LANES), jnp.int32),
        ),
        in_specs=[smem, smem, vmem, vmem, vmem, vmem],
        out_specs=(vmem, vmem, vmem, vmem),
        scratch_shapes=[pltpu.VMEM((2 * owned, LANES), f32)],
        compiler_params=params,
        name="gains_and_slots",
    )(
        me,
        baseline_station_pairs.T,
        every,
        baseline_station_pairs,
        band_weights.T,
        band_offset.reshape(1, channels),
    )
    return pl.pallas_call(
        functools.partial(finish_kernel, capacity),
        out_shape=jax.ShapeDtypeStruct((owned, parts, channels), jnp.bfloat16),
        in_specs=[smem, vmem, vmem, vmem, vmem],
        out_specs=vmem,
        scratch_shapes=[
            pltpu.VMEM((channels // LANES, owned + 1, parts, LANES), f32),
            pltpu.VMEM((channels // LANES, owned, parts, LANES), f32),
        ],
        compiler_params=params,
        name="sum_and_apply",
    )(slots, received, left, right, recip)


def solution(mesh):
    placed = (
        P(("groups", "bl"), None, None),
        P(("groups", "bl"), None),
        P(("groups", "bl")),
        P("bl", None),
        P(("groups", "bl"), None, None),
        P("groups", None),
        P("groups"),
    )
    return jax.shard_map(
        on_device,
        mesh=mesh,
        in_specs=placed,
        out_specs=P(("groups", "bl"), None, None),
        check_vma=False,
    )
```

time: 122 us -> 67.1 us (0.55)
  the two profiles are of different devices: /device:TPU:15 before, /device:TPU:17 now
where the time goes in v1:
time: 67.1 us; the launch traced here: 66.8 us
  blocking collectives  47.1 us (70%)
  Pallas kernels  9.71 us (14%)
  starting transfers between devices  6.63 us (10%)
  local copies, waits for them, and re-layouts  3.29 us (5%)
    all_gather x1, blocking collectives, on_device(): every = lax.all_gather(aux, 'bl', axis=0)  47.1 us
    all_to_all x1, starting transfers between devices, on_device(): lax.all_to_all(send, 'bl', split_axis=0, concat_axis=0, tiled=True)  6.63 us
    pallas_call x1, Pallas kernels, on_device(): pl.pallas_call(functools.partial(prep_kernel, capacity, owned, stations),...  3.75 us
    pallas_call x1, Pallas kernels, on_device(): pl.pallas_call(functools.partial(finish_kernel, capacity), out_shape=jax....  3.56 us
    unnamed x15, local copies, waits for them, and re-layouts  3.29 us
    pallas_call x1, Pallas kernels, on_device(): pl.pallas_call(functools.partial(pack_kernel, capacity, owned), out_shape...  2.4 us
  transfers between devices with their start and end apart: 1, of which 0 were waited for; matrix products, arithmetic and copies ran while one was open for 0% of the time, Pallas kernels for 6%

profile of v1, /device:TPU:17, one launch (start us, length us, event | category | flops | bytes accessed | tf_op | source)
XLA Modules:
  0.0 66.8 jit_solution(8451654524512821806)
XLA Ops:
  0.0 0.0 copy-start
  0.0 1.1 %copy-done = bf16[128,8,384]{2,1,0:T(8,128)(2,1)S(1)} copy-done((bf16[128,8,384]{2,1,0:T(8,128)(2,1)S(1)}, bf16[128,8,384]{2,1,0:T(8,128)(2,1)}, u32[]{:S(2)}) %copy-start) | copy-done | bytes 786456
  1.1 0.0 copy-start.1
  1.1 0.7 %copy-done.1 = f32[32,8,6]{0,1,2:T(8,128)S(1)} copy-done((f32[32,8,6]{0,1,2:T(8,128)S(1)}, f32[32,8,6]{0,1,2:T(8,128)}, u32[]{:S(2)}) %copy-start.1) | copy-done | bytes 6168
  1.9 0.0 copy-start.4
  1.9 0.7 copy-done.4
  2.5 0.0 copy-start.5
  2.5 0.7 copy-done.5
  3.2 2.4 %pack_rows.1 = (bf16[256,8,384]{2,1,0:T(8,128)(2,1)}, f32[24,128]{1,0:T(8,128)S(1)}) custom-call(s32[128]{0:T(128)S(1)} %bitcast.14, bf16[128,8,384]{2,1,0:T(8,128)(2,1)S(1)} %copy-done, s32[1,128]{1,0:T(1,128)S(1)} %bitcast.15, s32[1,128]{1,0:T(1,128)S(1)} %bitcast.16, f32[48,32]{1,0:T(8,128)S(1)} %bitcast.11), custom_call_target="tpu_custom_call" | custom-call | tf_op jit(solution)/shard_map/pack_rows/pallas_call | solution.py:210
  5.6 0.0 copy-start.6
  5.6 0.0 copy-start.3
  5.6 0.0 copy-start.2
  5.6 6.6 %all-to-all-start = ((bf16[256,8,384]{2,1,0:T(8,128)(2,1)}), bf16[256,8,384]{2,1,0:T(8,128)(2,1)S(1)}, u32[]{:S(2)}, u32[]{:S(2)}) async-start(bf16[256,8,384]{2,1,0:T(8,128)(2,1)} %get-tuple-element.13), calls=%async_computation | async-start | bytes 3145728 | tf_op jit(solution)/shard_map/all_to_all | solution.py:229
  12.2 0.0 copy-done.6
  12.2 0.0 copy-done.3
  12.2 0.1 copy.8.pairs_ref
  12.3 47.1 %all-gather = f32[384,128]{1,0:T(8,128)S(1)} all-gather(f32[24,128]{1,0:T(8,128)S(1)} %get-tuple-element.11), channel_id=2, replica_groups=mesh['groups'=2,'bl'=16] {'bl'}, dimensions={0}, use_global_device_ids=true | all-gather | bytes 208896 | tf_op jit(solution)/shard_map/all_gather | solution.py:228
  59.4 0.0 copy-done.2
  59.4 3.7 %gains_and_slots.1 = (f32[64,3072]{1,0:T(8,128)S(1)}, f32[64,3072]{1,0:T(8,128)S(1)}, f32[64,128]{1,0:T(8,128)S(1)}, s32[16,128]{1,0:T(8,128)S(1)}) custom-call(s32[1]{0:T(128)} %bitcast.me_s, s32[2,64]{1,0:T(2,128)S(1)} %bitcast.13, f32[16,24,128]{2,1,0:T(8,128)S(1)} %bitcast.10, s32[64,2]{1,0:T(8,128)S(1)} %copy.8.pairs_ref, f32[3,384]{1,0:T(4,128)S(1)} %bitcast.12, ...), custom_call_target="tpu_custom_call" | custom-call | tf_op jit(solution)/shard_map/gains_and_slots/pallas_call | solution.py:232
  63.2 0.0 all-to-all-done.recv_ref
  63.2 3.6 %sum_and_apply.1 = bf16[64,8,384]{2,1,0:T(8,128)(2,1)} custom-call(s32[16,128]{1,0:T(8,128)S(1)} %get-tuple-element.12.slots_s, bf16[256,8,384]{2,1,0:T(8,128)(2,1)S(1)} %all-to-all-done.recv_ref, f32[64,3072]{1,0:T(8,128)S(1)} %get-tuple-element.14.left_ref, f32[64,3072]{1,0:T(8,128)S(1)} %get-tuple-element.15.right_ref, ...), custom_call_target="tpu_custom_call" | custom-call | tf_op jit(solution)/shard_map/sum_and_apply/pallas_call | solution.py:253
  (1 shorter events, 0.0 us)
Async XLA Ops:
  0.0 1.1 %copy-start = (bf16[128,8,384]{2,1,0:T(8,128)(2,1)S(1)}, bf16[128,8,384]{2,1,0:T(8,128)(2,1)}, u32[]{:S(2)}) copy-start(bf16[128,8,384]{2,1,0:T(8,128)(2,1)} %vis_ref.1) | copy-start | bytes 2359300
  1.1 0.7 %copy-start.1 = (f32[32,8,6]{0,1,2:T(8,128)S(1)}, f32[32,8,6]{0,1,2:T(8,128)}, u32[]{:S(2)}) copy-start(f32[32,8,6]{0,1,2:T(8,128)} %param.11) | copy-start | bytes 18436
  1.9 0.7 copy-start.4
  2.5 0.7 copy-start.5
  5.6 6.6 %copy-start.6 = (s32[384]{0:T(512)S(1)}, s32[384]{0:T(512)}, u32[]{:S(2)}) copy-start(s32[384]{0:T(512)} %param.13) | copy-start | bytes 4612
  5.6 6.7 %copy-start.3 = (s32[64,2]{0,1:T(2,128)S(1)}, s32[64,2]{0,1:T(2,128)}, u32[]{:S(2)}) copy-start(s32[64,2]{0,1:T(2,128)} %param.10) | copy-start | bytes 1540
  5.6 53.8 %copy-start.2 = (f32[384,3]{0,1:T(4,128)S(1)}, f32[384,3]{0,1:T(4,128)}, u32[]{:S(2)}) copy-start(f32[384,3]{0,1:T(4,128)} %param.12) | copy-start | bytes 13828
  5.6 57.6 %all-to-all-start = ((bf16[256,8,384]{2,1,0:T(8,128)(2,1)}), bf16[256,8,384]{2,1,0:T(8,128)(2,1)S(1)}, u32[]{:S(2)}, u32[]{:S(2)}) async-start(bf16[256,8,384]{2,1,0:T(8,128)(2,1)} %get-tuple-element.13), calls=%async_computation | async-start | bytes 3145728 | tf_op jit(solution)/shard_map/all_to_all | solution.py:229

commit v2 on v1

v2 whole, which is shorter than its diff:
```python
import functools

import jax
import jax.numpy as jnp
from jax import lax
from jax.experimental import pallas as pl
from jax.experimental.pallas import tpu as pltpu
from jax.sharding import PartitionSpec as P

LANES = 128
SUB = 8
SPARE = 48


def round_up(value, unit):
    return -(-value // unit) * unit


def pack_kernel(
    capacity,
    early,
    owned,
    owner_hbm,
    slot_hbm,
    vis_hbm,
    coarse_hbm,
    first_ref,
    second_ref,
    owner_s,
    slot_s,
    count_s,
    vis_ref,
    coarse_ref,
    turn_ref,
    slots_ref,
    sems,
):
    rows = vis_ref.shape[0]
    devices, meta, _ = slots_ref.shape
    chunks = vis_ref.shape[2] // LANES
    terms, stations = coarse_ref.shape
    half = stations // 2
    moves = [
        pltpu.make_async_copy(src, dst, sems.at[i])
        for i, (src, dst) in enumerate(
            (
                (vis_hbm, vis_ref),
                (coarse_hbm, coarse_ref),
                (owner_hbm, owner_s),
                (slot_hbm, slot_s),
            )
        )
    ]
    for move in moves:
        move.start()
    slots_ref[...] = jnp.full(slots_ref.shape, float(owned), jnp.float32)
    turn_ref[...] = jnp.zeros_like(turn_ref)
    for d in range(devices):
        count_s[d] = 0
    for move in moves[1:]:
        move.wait()

    turn_ref[0:terms, 0:half] = coarse_ref[:, 0:half]
    turn_ref[64 : 64 + terms, 0:half] = coarse_ref[:, half:stations]
    gains = turn_ref[...].T[0:meta, :]
    low = (gains - gains.astype(jnp.bfloat16).astype(jnp.float32)).astype(jnp.bfloat16)
    moves[0].wait()

    def place(r, carry):
        d = owner_s[r]
        k = count_s[d]
        count_s[d] = k + 1
        slots_ref[d, pl.ds(k, 1), :] = jnp.full((1, LANES), slot_s[r].astype(jnp.float32))

        @pl.when(k < early)
        def _():
            for c in range(chunks):
                first_ref[d, chunks * k + c] = vis_ref[r, :, c * LANES : (c + 1) * LANES]

        @pl.when(k >= early)
        def _():
            for c in range(chunks):
                second_ref[d, chunks * (k - early) + c] = vis_ref[r, :, c * LANES : (c + 1) * LANES]

        return carry

    lax.fori_loop(0, rows, place, 0, unroll=4)

    lane = lax.broadcasted_iota(jnp.int32, (meta, LANES), 1)
    spare = jnp.logical_and(lane >= SPARE, lane < 64)
    at = chunks * early
    for d in range(devices):
        high = jnp.where(spare, slots_ref[d], gains).astype(jnp.bfloat16)
        for i in range(meta // SUB):
            first_ref[d, at + i] = high[i * SUB : (i + 1) * SUB, :]
            first_ref[d, at + meta // SUB + i] = low[i * SUB : (i + 1) * SUB, :]


def add_rows(chunks, start, stop, base, d, slots_s, recv_ref, acc_ref):
    def add(k, carry):
        b = slots_s[d, k]
        for c in range(chunks):
            acc_ref[c, b] += recv_ref[d, chunks * (k - base) + c].astype(jnp.float32)
        return carry

    lax.fori_loop(start, stop, add, 0)


def early_kernel(
    capacity,
    early,
    owned,
    stations,
    pairs_s,
    recv_ref,
    pairs_ref,
    weights_ref,
    offset_ref,
    left_ref,
    right_ref,
    recip_ref,
    slots_ref,
    acc_ref,
    table_ref,
    pick_ref,
    slots_s,
    sem,
):
    devices = recv_ref.shape[0]
    half = stations // 2
    channels = weights_ref.shape[1]
    chunks = channels // LANES
    at = chunks * early
    tiles = (recv_ref.shape[1] - at) // 2
    meta = tiles * SUB

    sub = lax.broadcasted_iota(jnp.int32, (meta, LANES), 0)
    lane = lax.broadcasted_iota(jnp.int32, (meta, LANES), 1)
    lane_f = lane.astype(jnp.float32)
    hits = jnp.zeros((meta, LANES), jnp.float32)
    for d in range(devices):
        high = jnp.concatenate([recv_ref[d, at + i] for i in range(tiles)], axis=0).astype(jnp.float32)
        low = jnp.concatenate([recv_ref[d, at + tiles + i] for i in range(tiles)], axis=0).astype(jnp.float32)
        table_ref[d] = high + low
        slot = jnp.broadcast_to(high[:, SPARE : SPARE + 1], (meta, LANES))
        inside = jnp.logical_and(sub < capacity, slot < float(owned))
        hits = hits + jnp.where(jnp.logical_and(inside, slot == lane_f), 1.0, 0.0)
        line = jnp.sum(jnp.where(lane == sub, slot, 0.0), axis=0, keepdims=True)
        count = jnp.sum(inside.astype(jnp.float32), axis=0, keepdims=True)
        line = jnp.where(lane[0:1, :] == capacity, count, line)
        slots_ref[d : d + 1, :] = line.astype(jnp.int32)
    move = pltpu.make_async_copy(slots_ref, slots_s, sem)
    move.start()

    tally = jnp.broadcast_to(jnp.sum(hits, axis=0, keepdims=True), (owned, LANES))
    own = lax.broadcasted_iota(jnp.int32, (owned, LANES), 0) == lax.broadcasted_iota(
        jnp.int32, (owned, LANES), 1
    )
    tally = jnp.sum(jnp.where(own, tally, 0.0), axis=1, keepdims=True)
    recip_ref[...] = jnp.broadcast_to(1.0 / jnp.maximum(tally, 1.0), recip_ref.shape)

    acc_ref[...] = jnp.zeros_like(acc_ref)
    move.wait()

    def from_device(d, carry):
        stop = jnp.minimum(slots_s[d, capacity], early)
        add_rows(chunks, 0, stop, 0, d, slots_s, recv_ref, acc_ref)
        return carry

    lax.fori_loop(0, devices, from_device, 0)

    def pick(b, carry):
        for side in range(2):
            s = pairs_s[side, b]
            d = s // stations
            within = s - d * stations
            row = jnp.where(within >= half, within - half, within)
            pick_ref[pl.ds(side * owned + b, 1), :] = table_ref[d, pl.ds(row, 1), :]
        return carry

    lax.fori_loop(0, owned, pick, 0, unroll=4)

    knot = lax.broadcasted_iota(jnp.int32, (LANES, channels), 0)
    knot = (knot & 63) >> 3
    basis = jnp.zeros((LANES, channels), jnp.float32)
    for step in range(3):
        basis = basis + jnp.where(
            knot == offset_ref[...] + step, weights_ref[step : step + 1, :], 0.0
        )
    part = lax.broadcasted_iota(jnp.int32, (LANES, channels), 0) & 7
    column = lax.broadcasted_iota(jnp.int32, (owned, LANES), 1)
    used = (column & 63) < SPARE
    for side, out in ((0, left_ref), (1, right_ref)):
        within = lax.rem(pairs_ref[:, side : side + 1], stations)
        mine = jnp.logical_and(used, (column >= 64) == (within >= half))
        picked = jnp.where(mine, pick_ref[side * owned : (side + 1) * owned, :], 0.0)
        for j in range(8):
            fine = jnp.dot(
                picked,
                jnp.where(part == j, basis, 0.0),
                precision=lax.Precision.HIGHEST,
                preferred_element_type=jnp.float32,
            )
            out[:, j * channels : (j + 1) * channels] = fine.astype(jnp.bfloat16).astype(jnp.float32)


def finish_kernel(
    capacity, early, slots_s, recv_ref, sums_ref, left_ref, right_ref, recip_ref, out_ref, acc_ref, res_ref
):
    owned, parts, channels = out_ref.shape
    devices = recv_ref.shape[0]
    chunks = channels // LANES
    acc_ref[...] = sums_ref[...]

    def from_device(d, carry):
        add_rows(chunks, early, slots_s[d, capacity], early, d, slots_s, recv_ref, acc_ref)
        return carry

    lax.fori_loop(0, devices, from_device, 0)

    flat = acc_ref.reshape(chunks * owned * parts, LANES)
    done = res_ref.reshape(chunks * owned * parts, LANES)
    for b0 in range(0, owned, SUB):
        for c in range(chunks):
            row = (c * owned + b0) * parts

            def plane(ref, j):
                return ref[b0 : b0 + SUB, pl.ds(j * channels + c * LANES, LANES)]

            vis = [flat[pl.ds(row + j, SUB, stride=parts), :] for j in range(parts)]
            lhs = [plane(left_ref, j) for j in range(parts)]
            rhs = [plane(right_ref, j) for j in range(parts)]
            scale = recip_ref[b0 : b0 + SUB, :]
            mid_re, mid_im = [], []
            for row_a in range(2):
                for col_b in range(2):
                    re = im = 0.0
                    for inner in range(2):
                        lr, li = lhs[2 * row_a + inner], lhs[4 + 2 * row_a + inner]
                        vr, vi = vis[2 * inner + col_b], vis[4 + 2 * inner + col_b]
                        re = re + lr * vr - li * vi
                        im = im + lr * vi + li * vr
                    mid_re.append(re * scale)
                    mid_im.append(im * scale)
            for row_a in range(2):
                for col_b in range(2):
                    re = im = 0.0
                    for inner in range(2):
                        mr, mi = mid_re[2 * row_a + inner], mid_im[2 * row_a + inner]
                        rr, ri = rhs[2 * col_b + inner], rhs[4 + 2 * col_b + inner]
                        re = re + mr * rr + mi * ri
                        im = im + mi * rr - mr * ri
                    j = 2 * row_a + col_b
                    done[pl.ds(row + j, SUB, stride=parts), :] = re
                    done[pl.ds(row + 4 + j, SUB, stride=parts), :] = im
    for c in range(chunks):
        out_ref[:, :, c * LANES : (c + 1) * LANES] = res_ref[c].astype(out_ref.dtype)


def on_device(
    visibilities,
    row_owner,
    row_slot,
    baseline_station_pairs,
    gains_coarse,
    band_weights,
    band_offset,
):
    devices = lax.axis_size("bl")
    rows, parts, channels = visibilities.shape
    capacity = 2 * rows // devices
    early = capacity // 2
    owned = baseline_station_pairs.shape[0]
    stations, _, knots = gains_coarse.shape
    chunks = channels // LANES
    meta = round_up(max(stations // 2, capacity), SUB)
    vmem = pl.BlockSpec(memory_space=pltpu.VMEM)
    smem = pl.BlockSpec(memory_space=pltpu.SMEM)
    hbm = pl.BlockSpec(memory_space=pltpu.HBM)
    params = pltpu.CompilerParams(vmem_limit_bytes=32 * 1024 * 1024)
    f32, bf16, i32 = jnp.float32, jnp.bfloat16, jnp.int32

    coarse = gains_coarse.transpose(2, 1, 0).reshape(knots * parts, stations)
    first, second = pl.pallas_call(
        functools.partial(pack_kernel, capacity, early, owned),
        out_shape=(
            jax.ShapeDtypeStruct((devices, chunks * early + 2 * meta // SUB, parts, LANES), bf16),
            jax.ShapeDtypeStruct((devices, chunks * (capacity - early), parts, LANES), bf16),
        ),
        in_specs=[hbm] * 4,
        out_specs=(vmem, vmem),
        scratch_shapes=[
            pltpu.SMEM((rows,), i32),
            pltpu.SMEM((rows,), i32),
            pltpu.SMEM((devices,), i32),
            pltpu.VMEM((rows, parts, channels), bf16),
            pltpu.VMEM((knots * parts, stations), f32),
            pltpu.VMEM((LANES, LANES), f32),
            pltpu.VMEM((devices, meta, LANES), f32),
            pltpu.SemaphoreType.DMA((4,)),
        ],
        compiler_params=params,
        name="pack_rows",
    )(row_owner.reshape(rows), row_slot, visibilities, coarse)
    first = lax.all_to_all(first, "bl", split_axis=0, concat_axis=0, tiled=True)
    second = lax.all_to_all(second, "bl", split_axis=0, concat_axis=0, tiled=True)

    left, right, recip, slots, sums = pl.pallas_call(
        functools.partial(early_kernel, capacity, early, owned, stations),
        out_shape=(
            jax.ShapeDtypeStruct((owned, parts * channels), f32),
            jax.ShapeDtypeStruct((owned, parts * channels), f32),
            jax.ShapeDtypeStruct((owned, LANES), f32),
            jax.ShapeDtypeStruct((devices, LANES), i32),
            jax.ShapeDtypeStruct((chunks, owned, parts, LANES), f32),
        ),
        in_specs=[smem, vmem, vmem, vmem, vmem],
        out_specs=(vmem,) * 5,
        scratch_shapes=[
            pltpu.VMEM((devices, meta, LANES), f32),
            pltpu.VMEM((2 * owned, LANES), f32),
            pltpu.SMEM((devices, LANES), i32),
            pltpu.SemaphoreType.DMA,
        ],
        compiler_params=params,
        name="gains_and_early_sums",
    )(
        baseline_station_pairs.T,
        first,
        baseline_station_pairs,
        band_weights.T,
        band_offset.reshape(1, channels),
    )
    return pl.pallas_call(
        functools.partial(finish_kernel, capacity, early),
        out_shape=jax.ShapeDtypeStruct((owned, parts, channels), bf16),
        in_specs=[smem, vmem, vmem, vmem, vmem, vmem],
        out_specs=vmem,
        scratch_shapes=[
            pltpu.VMEM((chunks, owned, parts, LANES), f32),
            pltpu.VMEM((chunks, owned, parts, LANES), f32),
        ],
        compiler_params=params,
        name="late_sums_and_gains",
    )(slots, second, sums, left, right, recip)


def solution(mesh):
    placed = (
        P(("groups", "bl"), None, None),
        P(("groups", "bl"), None),
        P(("groups", "bl")),
        P("bl", None),
        P(("groups", "bl"), None, None),
        P("groups", None),
        P("groups"),
    )
    return jax.shard_map(
        on_device,
        mesh=mesh,
        in_specs=placed,
        out_specs=P(("groups", "bl"), None, None),
        check_vma=False,
    )
```

time: 67.1 us -> 64.5 us (0.961)
  the two profiles are of different devices: /device:TPU:17 before, /device:TPU:0 now
where the time goes in v2:
time: 64.5 us; the launch traced here: 64.1 us
  blocking collectives  29.7 us (46%)
  Pallas kernels  13.1 us (20%)
  waiting for transfers between devices  10.7 us (17%)
  local copies, waits for them, and re-layouts  5.93 us (9%)
  starting transfers between devices  4.61 us (7%)
    all_to_all x1, blocking collectives, on_device(): first = lax.all_to_all(first, 'bl', split_axis=0, concat_axis=0, tiled=True)  29.7 us
    all_to_all x1, waiting for transfers between devices, on_device(): lax.all_to_all(second, 'bl', split_axis=0, concat_axis=0, tiled=True)  10.7 us
    unnamed x19, local copies, waits for them, and re-layouts  5.93 us
    pallas_call x1, Pallas kernels, on_device(): pl.pallas_call(functools.partial(early_kernel, capacity, early, owned, st...  5.73 us
    all_to_all x1, starting transfers between devices, on_device(): lax.all_to_all(second, 'bl', split_axis=0, concat_axis=0, tiled=True)  4.61 us
    pallas_call x1, Pallas kernels, on_device(): pl.pallas_call(functools.partial(pack_kernel, capacity, early, owned), ou...  4.22 us
    pallas_call x1, Pallas kernels, on_device(): pl.pallas_call(functools.partial(finish_kernel, capacity, early), out_sha...  3.15 us
  transfers between devices with their start and end apart: 1, of which 1 were waited for; matrix products, arithmetic and copies ran while one was open for 0% of the time, Pallas kernels for 9%

profile of v2, /device:TPU:0, one launch (start us, length us, event | category | flops | bytes accessed | tf_op | source)
XLA Modules:
  0.0 64.1 jit_solution(11513928704006787751)
XLA Ops:
  0.0 0.0 copy-start.6
  0.0 0.0 copy-start.7
  0.0 0.7 %copy-done.6 = s32[128,1]{0,1:T(1,128)S(1)} copy-done((s32[128,1]{0,1:T(1,128)S(1)}, s32[128,1]{0,1:T(1,128)}, u32[]{:S(2)}) %copy-start.6) | copy-done | bytes 536
  0.7 0.0 copy-done.7
  0.7 0.0 copy-start.2
  0.7 1.1 %copy-done.2 = bf16[128,8,384]{2,1,0:T(8,128)(2,1)S(1)} copy-done((bf16[128,8,384]{2,1,0:T(8,128)(2,1)S(1)}, bf16[128,8,384]{2,1,0:T(8,128)(2,1)}, u32[]{:S(2)}) %copy-start.2) | copy-done | bytes 786456
  1.8 0.0 copy-start.3
  1.8 0.7 %copy-done.3 = f32[32,8,6]{0,1,2:T(8,128)S(1)} copy-done((f32[32,8,6]{0,1,2:T(8,128)S(1)}, f32[32,8,6]{0,1,2:T(8,128)}, u32[]{:S(2)}) %copy-start.3) | copy-done | bytes 6168
  2.5 4.2 %pack_rows.1 = (bf16[16,28,8,128]{3,2,1,0:T(8,128)(2,1)S(1)}, bf16[16,24,8,128]{3,2,1,0:T(8,128)(2,1)}) custom-call(s32[128]{0:T(128)S(1)} %bitcast.9, s32[128]{0:T(128)S(1)} %copy-done.7, bf16[128,8,384]{2,1,0:T(8,128)(2,1)S(1)} %copy-done.2, f32[48,32]{1,0:T(8,128)S(1)} %bitcast.6), custom_call_target="tpu_custom_call" | custom-call | tf_op jit(solution)/shard_map/pack_rows/pallas_call | solution.py:284
  6.8 29.7 %all_to_all.10.recv_ref = bf16[16,28,8,128]{3,2,1,0:T(8,128)(2,1)S(1)} all-to-all(bf16[16,28,8,128]{3,2,1,0:T(8,128)(2,1)S(1)} %get-tuple-element.12), channel_id=1, replica_groups=mesh['groups'=2,'bl'=16] {'bl'}, dimensions={0} | all-to-all | bytes 1835008 | tf_op jit(solution)/shard_map/all_to_all | solution.py:305
  36.5 0.0 copy-start.8
  36.5 4.6 %all-to-all-start.1 = ((bf16[16,24,8,128]{3,2,1,0:T(8,128)(2,1)}), bf16[16,24,8,128]{3,2,1,0:T(8,128)(2,1)S(1)}, u32[]{:S(2)}, u32[]{:S(2)}) async-start(bf16[16,24,8,128]{3,2,1,0:T(8,128)(2,1)} %get-tuple-element.14), calls=%async_computation.1 | async-start | bytes 1572864 | tf_op jit(solution)/shard_map/all_to_all | solution.py:306
  41.1 0.0 copy-done.8
  41.1 0.0 copy-start.5
  41.2 0.7 %copy-done.5 = s32[64,2]{0,1:T(2,128)S(1)} copy-done((s32[64,2]{0,1:T(2,128)S(1)}, s32[64,2]{0,1:T(2,128)}, u32[]{:S(2)}) %copy-start.5) | copy-done | bytes 536
  41.8 0.0 copy-start.4
  41.8 0.1 copy.8.pairs_ref
  41.9 0.6 copy-done.4
  42.5 5.7 %gains_and_early_sums.1 = (f32[64,3072]{1,0:T(8,128)S(1)}, f32[64,3072]{1,0:T(8,128)S(1)}, f32[64,128]{1,0:T(8,128)S(1)}, s32[16,128]{1,0:T(8,128)S(1)}, f32[3,64,8,128]{3,2,1,0:T(8,128)S(1)}) custom-call(s32[2,64]{1,0:T(2,128)S(1)} %bitcast.8, bf16[16,28,8,128]{3,2,1,0:T(8,128)(2,1)S(1)} %all_to_all.10.recv_ref, s32[64,2]{1,0:T(8,128)S(1)} %copy.8.pairs_ref, ...), custom_call_target="tpu_custom_call" | custom-call | tf_op jit(solution)/shard_map/gains_and_early_sums/pallas_call | solution.py:308
  48.3 0.0 copy-start
  48.3 0.9 %copy-done = f32[3,64,8,128]{3,2,1,0:T(8,128)} copy-done((f32[3,64,8,128]{3,2,1,0:T(8,128)}, f32[3,64,8,128]{3,2,1,0:T(8,128)S(1)}, u32[]{:S(2)}) %copy-start) | copy-done | bytes 786456
  49.2 10.7 %all-to-all-done.1.recv_ref = bf16[16,24,8,128]{3,2,1,0:T(8,128)(2,1)S(1)} async-done(((bf16[16,24,8,128]{3,2,1,0:T(8,128)(2,1)}), bf16[16,24,8,128]{3,2,1,0:T(8,128)(2,1)S(1)}, u32[]{:S(2)}, u32[]{:S(2)}) %all-to-all-start.1) | async-done | bytes 786464 | tf_op jit(solution)/shard_map/all_to_all | solution.py:306
  59.8 1.1 %copy-done.1 = f32[3,64,8,128]{3,2,1,0:T(8,128)S(1)} copy-done((f32[3,64,8,128]{3,2,1,0:T(8,128)S(1)}, f32[3,64,8,128]{3,2,1,0:T(8,128)}, u32[]{:S(2)}) %copy-start.1) | copy-done | bytes 786456
  61.0 3.1 %late_sums_and_gains.1 = bf16[64,8,384]{2,1,0:T(8,128)(2,1)} custom-call(s32[16,128]{1,0:T(8,128)S(1)} %get-tuple-element.13.slots_s, bf16[16,24,8,128]{3,2,1,0:T(8,128)(2,1)S(1)} %all-to-all-done.1.recv_ref, f32[3,64,8,128]{3,2,1,0:T(8,128)S(1)} %copy-done.1, f32[64,3072]{1,0:T(8,128)S(1)} %get-tuple-element.16.left_ref, ...), custom_call_target="tpu_custom_call" | custom-call | tf_op jit(solution)/shard_map/late_sums_and_gains/pallas_call | solution.py:334
  (2 shorter events, 0.0 us)
Async XLA Ops:
  0.0 0.7 %copy-start.6 = (s32[128,1]{0,1:T(1,128)S(1)}, s32[128,1]{0,1:T(1,128)}, u32[]{:S(2)}) copy-start(s32[128,1]{0,1:T(1,128)} %param.8) | copy-start | bytes 1540
  0.0 0.7 %copy-start.7 = (s32[128]{0:T(128)S(1)}, s32[128]{0:T(128)}, u32[]{:S(2)}) copy-start(s32[128]{0:T(128)} %slot_hbm.1) | copy-start | bytes 1540
  0.7 1.1 %copy-start.2 = (bf16[128,8,384]{2,1,0:T(8,128)(2,1)S(1)}, bf16[128,8,384]{2,1,0:T(8,128)(2,1)}, u32[]{:S(2)}) copy-start(bf16[128,8,384]{2,1,0:T(8,128)(2,1)} %vis_hbm.1) | copy-start | bytes 2359300
  1.8 0.7 %copy-start.3 = (f32[32,8,6]{0,1,2:T(8,128)S(1)}, f32[32,8,6]{0,1,2:T(8,128)}, u32[]{:S(2)}) copy-start(f32[32,8,6]{0,1,2:T(8,128)} %param.11) | copy-start | bytes 18436
  36.5 4.6 %copy-start.8 = (s32[384]{0:T(512)S(1)}, s32[384]{0:T(512)}, u32[]{:S(2)}) copy-start(s32[384]{0:T(512)} %param.13) | copy-start | bytes 4612
  36.5 23.3 %all-to-all-start.1 = ((bf16[16,24,8,128]{3,2,1,0:T(8,128)(2,1)}), bf16[16,24,8,128]{3,2,1,0:T(8,128)(2,1)S(1)}, u32[]{:S(2)}, u32[]{:S(2)}) async-start(bf16[16,24,8,128]{3,2,1,0:T(8,128)(2,1)} %get-tuple-element.14), calls=%async_computation.1 | async-start | bytes 1572864 | tf_op jit(solution)/shard_map/all_to_all | solution.py:306
  41.1 0.7 %copy-start.5 = (s32[64,2]{0,1:T(2,128)S(1)}, s32[64,2]{0,1:T(2,128)}, u32[]{:S(2)}) copy-start(s32[64,2]{0,1:T(2,128)} %param.10) | copy-start | bytes 1540
  41.8 0.7 %copy-start.4 = (f32[384,3]{0,1:T(4,128)S(1)}, f32[384,3]{0,1:T(4,128)}, u32[]{:S(2)}) copy-start(f32[384,3]{0,1:T(4,128)} %param.12) | copy-start | bytes 13828
  48.3 0.9 %copy-start = (f32[3,64,8,128]{3,2,1,0:T(8,128)}, f32[3,64,8,128]{3,2,1,0:T(8,128)S(1)}, u32[]{:S(2)}) copy-start(f32[3,64,8,128]{3,2,1,0:T(8,128)S(1)} %get-tuple-element.15.sums_ref) | copy-start | bytes 2359300
  59.8 1.1 %copy-start.1 = (f32[3,64,8,128]{3,2,1,0:T(8,128)S(1)}, f32[3,64,8,128]{3,2,1,0:T(8,128)}, u32[]{:S(2)}) copy-start(f32[3,64,8,128]{3,2,1,0:T(8,128)} %copy-done) | copy-start | bytes 2359300

commit v3 on v2

v3 whole, which is shorter than its diff:
```python
import functools

import jax
import jax.numpy as jnp
from jax import lax
from jax.experimental import pallas as pl
from jax.experimental.pallas import tpu as pltpu
from jax.sharding import PartitionSpec as P

LANES = 128
SUB = 8
SPARE = 48
NO_ROW = 128
VMEM_BYTES = 60 * 1024 * 1024


def round_up(value, unit):
    return -(-value // unit) * unit


def pack_kernel(
    capacity,
    owned,
    me_s,
    owner_hbm,
    slot_hbm,
    vis_hbm,
    coarse_hbm,
    *rest,
):
    outs, (owner_s, slot_s, count_s, vis_ref, coarse_ref, turn_ref, slots_ref, block_ref, sems) = rest[:-9], rest[-9:]
    rows = vis_ref.shape[0]
    devices, meta, _ = slots_ref.shape
    chunks = vis_ref.shape[2] // LANES
    terms, stations = coarse_ref.shape
    half = stations // 2
    moves = [
        pltpu.make_async_copy(src, dst, sems.at[i])
        for i, (src, dst) in enumerate(
            (
                (vis_hbm, vis_ref),
                (coarse_hbm, coarse_ref),
                (owner_hbm, owner_s),
                (slot_hbm, slot_s),
            )
        )
    ]
    for move in moves:
        move.start()
    slots_ref[...] = jnp.full(slots_ref.shape, float(NO_ROW), jnp.float32)
    turn_ref[...] = jnp.zeros_like(turn_ref)
    for d in range(devices):
        count_s[d] = 0
    for move in moves[1:]:
        move.wait()

    turn_ref[0:terms, 0:half] = coarse_ref[:, 0:half]
    turn_ref[64 : 64 + terms, 0:half] = coarse_ref[:, half:stations]
    gains = turn_ref[...].T[0:meta, :]
    low = (gains - gains.astype(jnp.bfloat16).astype(jnp.float32)).astype(jnp.bfloat16)
    me = me_s[0]
    moves[0].wait()

    def place(r, carry):
        m = owner_s[r] ^ me
        k = count_s[m]
        count_s[m] = k + 1
        slots_ref[m, pl.ds(k, 1), :] = jnp.full((1, LANES), slot_s[r].astype(jnp.float32))
        for c in range(chunks):
            block_ref[m, chunks * k + c] = vis_ref[r, :, c * LANES : (c + 1) * LANES]
        return carry

    lax.fori_loop(0, rows, place, 0, unroll=8)

    lane = lax.broadcasted_iota(jnp.int32, (meta, LANES), 1)
    spare = jnp.logical_and(lane >= SPARE, lane < 64)
    at = chunks * capacity
    sends = []
    for m in range(devices):
        high = jnp.where(spare, slots_ref[m], gains).astype(jnp.bfloat16)
        for i in range(meta // SUB):
            block_ref[m, at + i] = high[i * SUB : (i + 1) * SUB, :]
            block_ref[m, at + meta // SUB + i] = low[i * SUB : (i + 1) * SUB, :]
        if len(outs) > 1:
            sends.append(pltpu.make_async_copy(block_ref.at[m], outs[m], sems.at[4 + m]))
            sends[-1].start()
    if len(outs) == 1:
        sends.append(pltpu.make_async_copy(block_ref, outs[0], sems.at[4]))
        sends[-1].start()
    for send in sends:
        send.wait()


def finish_kernel(capacity, stations, me_s, pairs_s, pairs_ref, weights_ref, offset_ref, *rest):
    (out_ref, recv_ref, table_ref, pick_ref, gains_ref, slots_ref, slots_s, acc_ref, res_ref, sems) = rest[-10:]
    blocks = rest[:-10]
    owned, parts, channels = out_ref.shape
    devices = recv_ref.shape[0]
    half = stations // 2
    chunks = channels // LANES
    at = chunks * capacity
    tiles = (recv_ref.shape[1] - at) // 2
    meta = tiles * SUB
    me = me_s[0]
    if len(blocks) == 1:
        moves = [pltpu.make_async_copy(blocks[0], recv_ref, sems.at[0])]
    else:
        moves = [pltpu.make_async_copy(b, recv_ref.at[i], sems.at[i]) for i, b in enumerate(blocks)]
    for move in moves:
        move.start()
    acc_ref[...] = jnp.zeros_like(acc_ref)
    for move in moves:
        move.wait()

    sub = lax.broadcasted_iota(jnp.int32, (meta, LANES), 0)
    lane = lax.broadcasted_iota(jnp.int32, (meta, LANES), 1)
    lane_f = lane.astype(jnp.float32)
    hits = jnp.zeros((meta, LANES), jnp.float32)
    for d in range(devices):
        high = jnp.concatenate([recv_ref[d, at + i] for i in range(tiles)], axis=0).astype(jnp.float32)
        low = jnp.concatenate([recv_ref[d, at + tiles + i] for i in range(tiles)], axis=0).astype(jnp.float32)
        table_ref[d] = high + low
        slot = jnp.broadcast_to(high[:, SPARE : SPARE + 1], (meta, LANES))
        inside = jnp.logical_and(sub < capacity, slot < float(NO_ROW))
        hits = hits + jnp.where(jnp.logical_and(inside, slot == lane_f), 1.0, 0.0)
        line = jnp.sum(jnp.where(lane == sub, slot, 0.0), axis=0, keepdims=True)
        count = jnp.sum(inside.astype(jnp.float32), axis=0, keepdims=True)
        line = jnp.where(lane[0:1, :] == capacity, count, line)
        slots_ref[d : d + 1, :] = line.astype(jnp.int32)
    move = pltpu.make_async_copy(slots_ref, slots_s, sems.at[0])
    move.start()

    tally = jnp.broadcast_to(jnp.sum(hits, axis=0, keepdims=True), (owned, LANES))
    own = lax.broadcasted_iota(jnp.int32, (owned, LANES), 0) == lax.broadcasted_iota(
        jnp.int32, (owned, LANES), 1
    )
    tally = jnp.sum(jnp.where(own, tally, 0.0), axis=1, keepdims=True)
    recip = jnp.broadcast_to(1.0 / jnp.maximum(tally, 1.0), (owned, LANES))

    def pick(b, carry):
        for side in range(2):
            s = pairs_s[side, b]
            d = s // stations
            within = s - d * stations
            row = jnp.where(within >= half, within - half, within)
            pick_ref[pl.ds(side * owned + b, 1), :] = table_ref[d ^ me, pl.ds(row, 1), :]
        return carry

    lax.fori_loop(0, owned, pick, 0, unroll=4)

    knot = lax.broadcasted_iota(jnp.int32, (LANES, channels), 0)
    knot = (knot & 63) >> 3
    basis = jnp.zeros((LANES, channels), jnp.float32)
    for step in range(3):
        basis = basis + jnp.where(
            knot == offset_ref[...] + step, weights_ref[step : step + 1, :], 0.0
        )
    part = lax.broadcasted_iota(jnp.int32, (LANES, channels), 0) & 7
    column = lax.broadcasted_iota(jnp.int32, (owned, LANES), 1)
    used = (column & 63) < SPARE
    picked = []
    for side in range(2):
        within = lax.rem(pairs_ref[:, side : side + 1], stations)
        mine = jnp.logical_and(used, (column >= 64) == (within >= half))
        picked.append(jnp.where(mine, pick_ref[side * owned : (side + 1) * owned, :], 0.0))
    both = jnp.concatenate(picked, axis=0)
    both_high = both.astype(jnp.bfloat16)
    both_low = (both - both_high.astype(jnp.float32)).astype(jnp.bfloat16)
    both_two = jnp.concatenate([both_high, both_low], axis=1)
    for j in range(8):
        there = jnp.where(part == j, basis, 0.0)
        high = there.astype(jnp.bfloat16)
        low = (there - high.astype(jnp.float32)).astype(jnp.bfloat16)
        fine = jnp.dot(
            both_two, jnp.concatenate([high, high], axis=0), preferred_element_type=jnp.float32
        ) + jnp.dot(both_high, low, preferred_element_type=jnp.float32)
        gains_ref[j] = fine.astype(jnp.bfloat16).astype(jnp.float32)

    move.wait()

    def from_device(d, carry):
        def add(k, inner):
            b = slots_s[d, k]
            for c in range(chunks):
                acc_ref[c, b] += recv_ref[d, chunks * k + c].astype(jnp.float32)
            return inner

        lax.fori_loop(0, slots_s[d, capacity], add, 0)
        return carry

    lax.fori_loop(0, devices, from_device, 0)

    flat = acc_ref.reshape(chunks * owned * parts, LANES)
    done = res_ref.reshape(chunks * owned * parts, LANES)
    for b0 in range(0, owned, SUB):
        scale = recip[b0 : b0 + SUB, :]
        for c in range(chunks):
            row = (c * owned + b0) * parts
            cols = slice(c * LANES, (c + 1) * LANES)
            vis = [flat[pl.ds(row + j, SUB, stride=parts), :] for j in range(parts)]
            lhs = [gains_ref[j, b0 : b0 + SUB, cols] for j in range(parts)]
            rhs = [gains_ref[j, owned + b0 : owned + b0 + SUB, cols] for j in range(parts)]
            mid_re, mid_im = [], []
            for row_a in range(2):
                for col_b in range(2):
                    re = im = 0.0
                    for inner in range(2):
                        lr, li = lhs[2 * row_a + inner], lhs[4 + 2 * row_a + inner]
                        vr, vi = vis[2 * inner + col_b], vis[4 + 2 * inner + col_b]
                        re = re + lr * vr - li * vi
                        im = im + lr * vi + li * vr
                    mid_re.append(re * scale)
                    mid_im.append(im * scale)
            for row_a in range(2):
                for col_b in range(2):
                    re = im = 0.0
                    for inner in range(2):
                        mr, mi = mid_re[2 * row_a + inner], mid_im[2 * row_a + inner]
                        rr, ri = rhs[2 * col_b + inner], rhs[4 + 2 * col_b + inner]
                        re = re + mr * rr + mi * ri
                        im = im + mi * rr - mr * ri
                    j = 2 * row_a + col_b
                    done[pl.ds(row + j, SUB, stride=parts), :] = re
                    done[pl.ds(row + 4 + j, SUB, stride=parts), :] = im
    for c in range(chunks):
        out_ref[:, :, c * LANES : (c + 1) * LANES] = res_ref[c].astype(out_ref.dtype)


def on_device(
    visibilities,
    row_owner,
    row_slot,
    baseline_station_pairs,
    gains_coarse,
    band_weights,
    band_offset,
):
    devices = lax.axis_size("bl")
    rows, parts, channels = visibilities.shape
    capacity = 2 * rows // devices
    owned = baseline_station_pairs.shape[0]
    stations, _, knots = gains_coarse.shape
    chunks = channels // LANES
    meta = round_up(max(stations // 2, capacity), SUB)
    depth = chunks * capacity + 2 * meta // SUB
    pairwise = devices <= 16
    count = devices if pairwise else 1
    vmem = pl.BlockSpec(memory_space=pltpu.VMEM)
    smem = pl.BlockSpec(memory_space=pltpu.SMEM)
    hbm = pl.BlockSpec(memory_space=pltpu.HBM)
    anywhere = pl.BlockSpec(memory_space=pl.ANY)
    params = pltpu.CompilerParams(vmem_limit_bytes=VMEM_BYTES)
    f32, bf16, i32 = jnp.float32, jnp.bfloat16, jnp.int32

    me = lax.axis_index("bl").astype(i32)
    turn = (me if pairwise else jnp.zeros_like(me)).reshape(1)
    coarse = gains_coarse.transpose(2, 1, 0).reshape(knots * parts, stations)
    block = (depth, parts, LANES)
    blocks = pl.pallas_call(
        functools.partial(pack_kernel, capacity, owned),
        out_shape=[jax.ShapeDtypeStruct(block if pairwise else (devices,) + block, bf16)] * count,
        in_specs=[smem] + [hbm] * 4,
        out_specs=[hbm] * count,
        scratch_shapes=[
            pltpu.SMEM((rows,), i32),
            pltpu.SMEM((rows,), i32),
            pltpu.SMEM((devices,), i32),
            pltpu.VMEM((rows, parts, channels), bf16),
            pltpu.VMEM((knots * parts, stations), f32),
            pltpu.VMEM((LANES, LANES), f32),
            pltpu.VMEM((devices, meta, LANES), f32),
            pltpu.VMEM((devices,) + block, bf16),
            pltpu.SemaphoreType.DMA((4 + count,)),
        ],
        compiler_params=params,
        name="pack_rows",
    )(turn, row_owner.reshape(rows), row_slot, visibilities, coarse)
    if pairwise:
        arrived = list(blocks)
        for m in list(range(devices // 2, devices)) + list(range(1, devices // 2)):
            arrived[m] = lax.ppermute(blocks[m], "bl", [(d, d ^ m) for d in range(devices)])
    else:
        arrived = [lax.all_to_all(blocks[0], "bl", split_axis=0, concat_axis=0, tiled=True)]

    return pl.pallas_call(
        functools.partial(finish_kernel, capacity, stations),
        out_shape=jax.ShapeDtypeStruct((owned, parts, channels), bf16),
        in_specs=[smem, smem, vmem, vmem, vmem] + [anywhere] * count,
        out_specs=vmem,
        scratch_shapes=[
            pltpu.VMEM((devices,) + block, bf16),
            pltpu.VMEM((devices, meta, LANES), f32),
            pltpu.VMEM((2 * owned, LANES), f32),
            pltpu.VMEM((parts, 2 * owned, channels), f32),
            pltpu.VMEM((devices, LANES), i32),
            pltpu.SMEM((devices, LANES), i32),
            pltpu.VMEM((chunks, owned, parts, LANES), f32),
            pltpu.VMEM((chunks, owned, parts, LANES), f32),
            pltpu.SemaphoreType.DMA((count,)),
        ],
        compiler_params=pltpu.CompilerParams(vmem_limit_bytes=VMEM_BYTES // 2),
        name="sum_and_apply",
    )(
        turn,
        baseline_station_pairs.T,
        baseline_station_pairs,
        band_weights.T,
        band_offset.reshape(1, channels),
        *arrived,
    )


def solution(mesh):
    placed = (
        P(("groups", "bl"), None, None),
        P(("groups", "bl"), None),
        P(("groups", "bl")),
        P("bl", None),
        P(("groups", "bl"), None, None),
        P("groups", None),
        P("groups"),
    )
    return jax.shard_map(
        on_device,
        mesh=mesh,
        in_specs=placed,
        out_specs=P(("groups", "bl"), None, None),
        check_vma=False,
    )
```

time: 64.5 us -> 61.8 us (0.958)
  the two profiles are of different devices: /device:TPU:0 before, /device:TPU:19 now
where the time goes in v3:
time: 61.8 us; the launch traced here: 60.8 us
  starting transfers between devices  31.3 us (51%)
  waiting for transfers between devices  17.9 us (29%)
  Pallas kernels  10.5 us (17%)
  local copies, waits for them, and re-layouts  1.01 us (2%)
    ppermute x15, starting transfers between devices, on_device(): lax.ppermute(blocks[m], 'bl', [(d, d ^ m) for d in range(devices)])  31.3 us
    ppermute x15, waiting for transfers between devices, on_device(): lax.ppermute(blocks[m], 'bl', [(d, d ^ m) for d in range(devices)])  17.9 us
    pallas_call x1, Pallas kernels, on_device(): pl.pallas_call(functools.partial(finish_kernel, capacity, stations), out_...  7.32 us
    pallas_call x1, Pallas kernels, on_device(): pl.pallas_call(functools.partial(pack_kernel, capacity, owned), out_shape...  3.19 us
  transfers between devices with their start and end apart: 15, of which 6 were waited for; matrix products, arithmetic and copies ran while one was open for 0% of the time, Pallas kernels for 0%

profile of v3, /device:TPU:19, one launch (start us, length us, event | category | flops | bytes accessed | tf_op | source)
XLA Modules:
  0.0 60.8 jit_solution(15166498815269490716)
XLA Ops:
  0.0 3.2 %pack_rows.1 = (bf16[52,8,128]{2,1,0:T(8,128)(2,1)}, bf16[52,8,128]{2,1,0:T(8,128)(2,1)}, bf16[52,8,128]{2,1,0:T(8,128)(2,1)}, bf16[52,8,128]{2,1,0:T(8,128)(2,1...) custom-call(s32[1]{0:T(128)} %bitcast.me_s, ...), custom_call_target="tpu_custom_call" | custom-call | tf_op jit(solution)/shard_map/pack_rows/pallas_call | solution.py:259
  3.2 0.7 %collective-permute-start = (bf16[52,8,128]{2,1,0:T(8,128)(2,1)}, bf16[52,8,128]{2,1,0:T(8,128)(2,1)S(1)}, u32[]{:S(2)}, u32[]{:S(2)}) collective-permute-start(bf16[52,8,128]{2,1,0:T(8,128)(2,1)} %get-tuple-element.22), channel_id=1, source_target_pairs={{0,1},{1,0},{2,3},{3,2},{4,5},{5,4},{6,7},{7,6},{8,9},{9,8},{10,11... | collective-permute-start | bytes 319496 | tf_op jit(solution)/shard_map/ppermute | solution.py:281
  3.9 1.3 %collective-permute-start.1 = (bf16[52,8,128]{2,1,0:T(8,128)(2,1)}, bf16[52,8,128]{2,1,0:T(8,128)(2,1)S(1)}, u32[]{:S(2)}, u32[]{:S(2)}) collective-permute-start(bf16[52,8,128]{2,1,0:T(8,128)(2,1)} %get-tuple-element.23), channel_id=1, source_target_pairs={{0,2},{1,3},{2,0},{3,1},{4,6},{5,7},{6,4},{7,5},{8,10},{9,11},{10,... | collective-permute-start | bytes 319496 | tf_op jit(solution)/shard_map/ppermute | solution.py:281
  5.2 0.5 collective-permute-start.2
  5.6 1.3 %collective-permute-start.3 = (bf16[52,8,128]{2,1,0:T(8,128)(2,1)}, bf16[52,8,128]{2,1,0:T(8,128)(2,1)S(1)}, u32[]{:S(2)}, u32[]{:S(2)}) collective-permute-start(bf16[52,8,128]{2,1,0:T(8,128)(2,1)} %get-tuple-element.25), channel_id=1, source_target_pairs={{0,4},{1,5},{2,6},{3,7},{4,0},{5,1},{6,2},{7,3},{8,12},{9,13},{10,... | collective-permute-start | bytes 319496 | tf_op jit(solution)/shard_map/ppermute | solution.py:281
  6.9 0.5 collective-permute-start.4
  7.4 2.3 %collective-permute-start.5 = (bf16[52,8,128]{2,1,0:T(8,128)(2,1)}, bf16[52,8,128]{2,1,0:T(8,128)(2,1)S(1)}, u32[]{:S(2)}, u32[]{:S(2)}) collective-permute-start(bf16[52,8,128]{2,1,0:T(8,128)(2,1)} %get-tuple-element.27), channel_id=1, source_target_pairs={{0,6},{1,7},{2,4},{3,5},{4,2},{5,3},{6,0},{7,1},{8,14},{9,15},{10,... | collective-permute-start | bytes 319496 | tf_op jit(solution)/shard_map/ppermute | solution.py:281
  9.7 2.4 %collective-permute-start.6 = (bf16[52,8,128]{2,1,0:T(8,128)(2,1)}, bf16[52,8,128]{2,1,0:T(8,128)(2,1)S(1)}, u32[]{:S(2)}, u32[]{:S(2)}) collective-permute-start(bf16[52,8,128]{2,1,0:T(8,128)(2,1)} %get-tuple-element.28), channel_id=1, source_target_pairs={{0,7},{1,6},{2,5},{3,4},{4,3},{5,2},{6,1},{7,0},{8,15},{9,14},{10,... | collective-permute-start | bytes 319496 | tf_op jit(solution)/shard_map/ppermute | solution.py:281
  12.2 1.7 %collective-permute-start.8 = (bf16[52,8,128]{2,1,0:T(8,128)(2,1)}, bf16[52,8,128]{2,1,0:T(8,128)(2,1)S(1)}, u32[]{:S(2)}, u32[]{:S(2)}) collective-permute-start(bf16[52,8,128]{2,1,0:T(8,128)(2,1)} %get-tuple-element.30), channel_id=1, source_target_pairs={{0,9},{1,8},{2,11},{3,10},{4,13},{5,12},{6,15},{7,14},{8,1},{9,0},... | collective-permute-start | bytes 319496 | tf_op jit(solution)/shard_map/ppermute | solution.py:281
  13.9 1.1 %collective-permute-start.9 = (bf16[52,8,128]{2,1,0:T(8,128)(2,1)}, bf16[52,8,128]{2,1,0:T(8,128)(2,1)S(1)}, u32[]{:S(2)}, u32[]{:S(2)}) collective-permute-start(bf16[52,8,128]{2,1,0:T(8,128)(2,1)} %get-tuple-element.31), channel_id=1, source_target_pairs={{0,10},{1,11},{2,8},{3,9},{4,14},{5,15},{6,12},{7,13},{8,2},{9,3},... | collective-permute-start | bytes 319496 | tf_op jit(solution)/shard_map/ppermute | solution.py:281
  15.0 0.8 %collective-permute-done.5.rest_6_ = bf16[52,8,128]{2,1,0:T(8,128)(2,1)S(1)} collective-permute-done((bf16[52,8,128]{2,1,0:T(8,128)(2,1)}, bf16[52,8,128]{2,1,0:T(8,128)(2,1)S(1)}, u32[]{:S(2)}, u32[]{:S(2)}) %collective-permute-start.5) | collective-permute-done | bytes 106528 | tf_op jit(solution)/shard_map/ppermute | solution.py:281
  15.8 5.2 %collective-permute-start.10 = (bf16[52,8,128]{2,1,0:T(8,128)(2,1)}, bf16[52,8,128]{2,1,0:T(8,128)(2,1)S(1)}, u32[]{:S(2)}, u32[]{:S(2)}) collective-permute-start(bf16[52,8,128]{2,1,0:T(8,128)(2,1)} %get-tuple-element.32), channel_id=1, source_target_pairs={{0,11},{1,10},{2,9},{3,8},{4,15},{5,14},{6,13},{7,12},{8,3},{9,2},... | collective-permute-start | bytes 319496 | tf_op jit(solution)/shard_map/ppermute | solution.py:281
  21.0 1.0 %collective-permute-start.11 = (bf16[52,8,128]{2,1,0:T(8,128)(2,1)}, bf16[52,8,128]{2,1,0:T(8,128)(2,1)S(1)}, u32[]{:S(2)}, u32[]{:S(2)}) collective-permute-start(bf16[52,8,128]{2,1,0:T(8,128)(2,1)} %get-tuple-element.33), channel_id=1, source_target_pairs={{0,12},{1,13},{2,14},{3,15},{4,8},{5,9},{6,10},{7,11},{8,4},{9,5},... | collective-permute-start | bytes 319496 | tf_op jit(solution)/shard_map/ppermute | solution.py:281
  21.9 0.2 collective-permute-start.12
  22.1 0.4 collective-permute-done.8.rest_9_
  22.5 10.0 %collective-permute-start.13 = (bf16[52,8,128]{2,1,0:T(8,128)(2,1)}, bf16[52,8,128]{2,1,0:T(8,128)(2,1)S(1)}, u32[]{:S(2)}, u32[]{:S(2)}) collective-permute-start(bf16[52,8,128]{2,1,0:T(8,128)(2,1)} %get-tuple-element.35), channel_id=1, source_target_pairs={{0,14},{1,15},{2,12},{3,13},{4,10},{5,11},{6,8},{7,9},{8,6},{9,7},... | collective-permute-start | bytes 319496 | tf_op jit(solution)/shard_map/ppermute | solution.py:281
  32.5 3.2 %collective-permute-start.14 = (bf16[52,8,128]{2,1,0:T(8,128)(2,1)}, bf16[52,8,128]{2,1,0:T(8,128)(2,1)S(1)}, u32[]{:S(2)}, u32[]{:S(2)}) collective-permute-start(bf16[52,8,128]{2,1,0:T(8,128)(2,1)} %get-tuple-element.36), channel_id=1, source_target_pairs={{0,15},{1,14},{2,13},{3,12},{4,11},{5,10},{6,9},{7,8},{8,7},{9,6},... | collective-permute-start | bytes 319496 | tf_op jit(solution)/shard_map/ppermute | solution.py:281
  35.7 0.1 copy.8.pairs_ref
  35.8 8.9 %collective-permute-done.11.rest_12_ = bf16[52,8,128]{2,1,0:T(8,128)(2,1)S(1)} collective-permute-done((bf16[52,8,128]{2,1,0:T(8,128)(2,1)}, bf16[52,8,128]{2,1,0:T(8,128)(2,1)S(1)}, u32[]{:S(2)}, u32[]{:S(2)}) %collective-permute-start.11) | collective-permute-done | bytes 106528 | tf_op jit(solution)/shard_map/ppermute | solution.py:281
  44.8 2.6 %collective-permute-done.12.rest_13_ = bf16[52,8,128]{2,1,0:T(8,128)(2,1)S(1)} collective-permute-done((bf16[52,8,128]{2,1,0:T(8,128)(2,1)}, bf16[52,8,128]{2,1,0:T(8,128)(2,1)S(1)}, u32[]{:S(2)}, u32[]{:S(2)}) %collective-permute-start.12) | collective-permute-done | bytes 106528 | tf_op jit(solution)/shard_map/ppermute | solution.py:281
  47.4 2.9 %collective-permute-done.13.rest_14_ = bf16[52,8,128]{2,1,0:T(8,128)(2,1)S(1)} collective-permute-done((bf16[52,8,128]{2,1,0:T(8,128)(2,1)}, bf16[52,8,128]{2,1,0:T(8,128)(2,1)S(1)}, u32[]{:S(2)}, u32[]{:S(2)}) %collective-permute-start.13) | collective-permute-done | bytes 106528 | tf_op jit(solution)/shard_map/ppermute | solution.py:281
  50.3 2.3 %collective-permute-done.14.rest_15_ = bf16[52,8,128]{2,1,0:T(8,128)(2,1)S(1)} collective-permute-done((bf16[52,8,128]{2,1,0:T(8,128)(2,1)}, bf16[52,8,128]{2,1,0:T(8,128)(2,1)S(1)}, u32[]{:S(2)}, u32[]{:S(2)}) %collective-permute-start.14) | collective-permute-done | bytes 106528 | tf_op jit(solution)/shard_map/ppermute | solution.py:281
  52.6 0.9 %copy-done = bf16[52,8,128]{2,1,0:T(8,128)(2,1)S(1)} copy-done((bf16[52,8,128]{2,1,0:T(8,128)(2,1)S(1)}, bf16[52,8,128]{2,1,0:T(8,128)(2,1)}, u32[]{:S(2)}) %copy-start) | copy-done | bytes 106520
  53.5 7.3 %sum_and_apply.1 = bf16[64,8,384]{2,1,0:T(8,128)(2,1)} custom-call(s32[1]{0:T(128)} %bitcast.me_s, s32[2,64]{1,0:T(2,128)S(1)} %bitcast.8, s32[64,2]{1,0:T(8,128)S(1)} %copy.8.pairs_ref, f32[3,384]{1,0:T(4,128)S(1)} %bitcast.7, s32[1,384]{1,0:T(1,128)S(1)} %reshape.13.offset_ref, bf16[52,8,128]{2,1,0:T(8,128)(2,1)S(1)} %copy-done, ...), custom_call_target="tpu_custom_call" | custom-call | tf_op jit(solution)/shard_map/sum_and_apply/pallas_call | solution.py:285
  (18 shorter events, 0.1 us)
Async XLA Ops:
  3.2 4.3 %collective-permute-start = (bf16[52,8,128]{2,1,0:T(8,128)(2,1)}, bf16[52,8,128]{2,1,0:T(8,128)(2,1)S(1)}, u32[]{:S(2)}, u32[]{:S(2)}) collective-permute-start(bf16[52,8,128]{2,1,0:T(8,128)(2,1)} %get-tuple-element.22), channel_id=1, source_target_pairs={{0,1},{1,0},{2,3},{3,2},{4,5},{5,4},{6,7},{7,6},{8,9},{9,8},{10,11... | collective-permute-start | bytes 319496 | tf_op jit(solution)/shard_map/ppermute | solution.py:281
  3.9 5.8 %collective-permute-start.1 = (bf16[52,8,128]{2,1,0:T(8,128)(2,1)}, bf16[52,8,128]{2,1,0:T(8,128)(2,1)S(1)}, u32[]{:S(2)}, u32[]{:S(2)}) collective-permute-start(bf16[52,8,128]{2,1,0:T(8,128)(2,1)} %get-tuple-element.23), channel_id=1, source_target_pairs={{0,2},{1,3},{2,0},{3,1},{4,6},{5,7},{6,4},{7,5},{8,10},{9,11},{10,... | collective-permute-start | bytes 319496 | tf_op jit(solution)/shard_map/ppermute | solution.py:281
  5.2 6.9 %collective-permute-start.2 = (bf16[52,8,128]{2,1,0:T(8,128)(2,1)}, bf16[52,8,128]{2,1,0:T(8,128)(2,1)S(1)}, u32[]{:S(2)}, u32[]{:S(2)}) collective-permute-start(bf16[52,8,128]{2,1,0:T(8,128)(2,1)} %get-tuple-element.24), channel_id=1, source_target_pairs={{0,3},{1,2},{2,1},{3,0},{4,7},{5,6},{6,5},{7,4},{8,11},{9,10},{10,... | collective-permute-start | bytes 319496 | tf_op jit(solution)/shard_map/ppermute | solution.py:281
  5.6 6.5 %collective-permute-start.3 = (bf16[52,8,128]{2,1,0:T(8,128)(2,1)}, bf16[52,8,128]{2,1,0:T(8,128)(2,1)S(1)}, u32[]{:S(2)}, u32[]{:S(2)}) collective-permute-start(bf16[52,8,128]{2,1,0:T(8,128)(2,1)} %get-tuple-element.25), channel_id=1, source_target_pairs={{0,4},{1,5},{2,6},{3,7},{4,0},{5,1},{6,2},{7,3},{8,12},{9,13},{10,... | collective-permute-start | bytes 319496 | tf_op jit(solution)/shard_map/ppermute | solution.py:281
  6.9 7.0 %collective-permute-start.4 = (bf16[52,8,128]{2,1,0:T(8,128)(2,1)}, bf16[52,8,128]{2,1,0:T(8,128)(2,1)S(1)}, u32[]{:S(2)}, u32[]{:S(2)}) collective-permute-start(bf16[52,8,128]{2,1,0:T(8,128)(2,1)} %get-tuple-element.26), channel_id=1, source_target_pairs={{0,5},{1,4},{2,7},{3,6},{4,1},{5,0},{6,3},{7,2},{8,13},{9,12},{10,... | collective-permute-start | bytes 319496 | tf_op jit(solution)/shard_map/ppermute | solution.py:281
  7.4 8.3 %collective-permute-start.5 = (bf16[52,8,128]{2,1,0:T(8,128)(2,1)}, bf16[52,8,128]{2,1,0:T(8,128)(2,1)S(1)}, u32[]{:S(2)}, u32[]{:S(2)}) collective-permute-start(bf16[52,8,128]{2,1,0:T(8,128)(2,1)} %get-tuple-element.27), channel_id=1, source_target_pairs={{0,6},{1,7},{2,4},{3,5},{4,2},{5,3},{6,0},{7,1},{8,14},{9,15},{10,... | collective-permute-start | bytes 319496 | tf_op jit(solution)/shard_map/ppermute | solution.py:281
  9.7 11.3 %collective-permute-start.6 = (bf16[52,8,128]{2,1,0:T(8,128)(2,1)}, bf16[52,8,128]{2,1,0:T(8,128)(2,1)S(1)}, u32[]{:S(2)}, u32[]{:S(2)}) collective-permute-start(bf16[52,8,128]{2,1,0:T(8,128)(2,1)} %get-tuple-element.28), channel_id=1, source_target_pairs={{0,7},{1,6},{2,5},{3,4},{4,3},{5,2},{6,1},{7,0},{8,15},{9,14},{10,... | collective-permute-start | bytes 319496 | tf_op jit(solution)/shard_map/ppermute | solution.py:281
  12.1 9.8 %collective-permute-start.7 = (bf16[52,8,128]{2,1,0:T(8,128)(2,1)}, bf16[52,8,128]{2,1,0:T(8,128)(2,1)S(1)}, u32[]{:S(2)}, u32[]{:S(2)}) collective-permute-start(bf16[52,8,128]{2,1,0:T(8,128)(2,1)} %get-tuple-element.29), channel_id=1, source_target_pairs={{0,8},{1,9},{2,10},{3,11},{4,12},{5,13},{6,14},{7,15},{8,0},{9,1},... | collective-permute-start | bytes 319496 | tf_op jit(solution)/shard_map/ppermute | solution.py:281
  12.2 10.3 %collective-permute-start.8 = (bf16[52,8,128]{2,1,0:T(8,128)(2,1)}, bf16[52,8,128]{2,1,0:T(8,128)(2,1)S(1)}, u32[]{:S(2)}, u32[]{:S(2)}) collective-permute-start(bf16[52,8,128]{2,1,0:T(8,128)(2,1)} %get-tuple-element.30), channel_id=1, source_target_pairs={{0,9},{1,8},{2,11},{3,10},{4,13},{5,12},{6,15},{7,14},{8,1},{9,0},... | collective-permute-start | bytes 319496 | tf_op jit(solution)/shard_map/ppermute | solution.py:281
  13.9 18.6 %collective-permute-start.9 = (bf16[52,8,128]{2,1,0:T(8,128)(2,1)}, bf16[52,8,128]{2,1,0:T(8,128)(2,1)S(1)}, u32[]{:S(2)}, u32[]{:S(2)}) collective-permute-start(bf16[52,8,128]{2,1,0:T(8,128)(2,1)} %get-tuple-element.31), channel_id=1, source_target_pairs={{0,10},{1,11},{2,8},{3,9},{4,14},{5,15},{6,12},{7,13},{8,2},{9,3},... | collective-permute-start | bytes 319496 | tf_op jit(solution)/shard_map/ppermute | solution.py:281
  15.8 20.0 %collective-permute-start.10 = (bf16[52,8,128]{2,1,0:T(8,128)(2,1)}, bf16[52,8,128]{2,1,0:T(8,128)(2,1)S(1)}, u32[]{:S(2)}, u32[]{:S(2)}) collective-permute-start(bf16[52,8,128]{2,1,0:T(8,128)(2,1)} %get-tuple-element.32), channel_id=1, source_target_pairs={{0,11},{1,10},{2,9},{3,8},{4,15},{5,14},{6,13},{7,12},{8,3},{9,2},... | collective-permute-start | bytes 319496 | tf_op jit(solution)/shard_map/ppermute | solution.py:281
  21.0 23.8 %collective-permute-start.11 = (bf16[52,8,128]{2,1,0:T(8,128)(2,1)}, bf16[52,8,128]{2,1,0:T(8,128)(2,1)S(1)}, u32[]{:S(2)}, u32[]{:S(2)}) collective-permute-start(bf16[52,8,128]{2,1,0:T(8,128)(2,1)} %get-tuple-element.33), channel_id=1, source_target_pairs={{0,12},{1,13},{2,14},{3,15},{4,8},{5,9},{6,10},{7,11},{8,4},{9,5},... | collective-permute-start | bytes 319496 | tf_op jit(solution)/shard_map/ppermute | solution.py:281
  21.9 13.8 %copy-start.3 = (s32[384]{0:T(512)S(1)}, s32[384]{0:T(512)}, u32[]{:S(2)}) copy-start(s32[384]{0:T(512)} %param.13) | copy-start | bytes 4612
  21.9 25.5 %collective-permute-start.12 = (bf16[52,8,128]{2,1,0:T(8,128)(2,1)}, bf16[52,8,128]{2,1,0:T(8,128)(2,1)S(1)}, u32[]{:S(2)}, u32[]{:S(2)}) collective-permute-start(bf16[52,8,128]{2,1,0:T(8,128)(2,1)} %get-tuple-element.34), channel_id=1, source_target_pairs={{0,13},{1,12},{2,15},{3,14},{4,9},{5,8},{6,11},{7,10},{8,5},{9,4},... | collective-permute-start | bytes 319496 | tf_op jit(solution)/shard_map/ppermute | solution.py:281
  22.5 27.8 %collective-permute-start.13 = (bf16[52,8,128]{2,1,0:T(8,128)(2,1)}, bf16[52,8,128]{2,1,0:T(8,128)(2,1)S(1)}, u32[]{:S(2)}, u32[]{:S(2)}) collective-permute-start(bf16[52,8,128]{2,1,0:T(8,128)(2,1)} %get-tuple-element.35), channel_id=1, source_target_pairs={{0,14},{1,15},{2,12},{3,13},{4,10},{5,11},{6,8},{7,9},{8,6},{9,7},... | collective-permute-start | bytes 319496 | tf_op jit(solution)/shard_map/ppermute | solution.py:281
  32.5 3.2 %copy-start.2 = (s32[64,2]{0,1:T(2,128)S(1)}, s32[64,2]{0,1:T(2,128)}, u32[]{:S(2)}) copy-start(s32[64,2]{0,1:T(2,128)} %param.10) | copy-start | bytes 1540
  32.5 20.0 %collective-permute-start.14 = (bf16[52,8,128]{2,1,0:T(8,128)(2,1)}, bf16[52,8,128]{2,1,0:T(8,128)(2,1)S(1)}, u32[]{:S(2)}, u32[]{:S(2)}) collective-permute-start(bf16[52,8,128]{2,1,0:T(8,128)(2,1)} %get-tuple-element.36), channel_id=1, source_target_pairs={{0,15},{1,14},{2,13},{3,12},{4,11},{5,10},{6,9},{7,8},{8,7},{9,6},... | collective-permute-start | bytes 319496 | tf_op jit(solution)/shard_map/ppermute | solution.py:281
  35.7 16.9 %copy-start.1 = (f32[384,3]{0,1:T(4,128)S(1)}, f32[384,3]{0,1:T(4,128)}, u32[]{:S(2)}) copy-start(f32[384,3]{0,1:T(4,128)} %param.12) | copy-start | bytes 13828
  52.6 0.9 %copy-start = (bf16[52,8,128]{2,1,0:T(8,128)(2,1)S(1)}, bf16[52,8,128]{2,1,0:T(8,128)(2,1)}, u32[]{:S(2)}) copy-start(bf16[52,8,128]{2,1,0:T(8,128)(2,1)} %get-tuple-element.21.rest_0_) | copy-start | bytes 319492

commit v4 on v3

v4 whole, which is shorter than its diff:
```python
import functools

import jax
import jax.numpy as jnp
from jax import lax
from jax.experimental import pallas as pl
from jax.experimental.pallas import tpu as pltpu
from jax.sharding import PartitionSpec as P

LANES = 128
SUB = 8
USED = 48
ALL_VMEM = 60 * 1024 * 1024
SOME_VMEM = 24 * 1024 * 1024


def round_up(value, unit):
    return -(-value // unit) * unit


def start_all(pairs, sems):
    moves = [pltpu.make_async_copy(src, dst, sems.at[i]) for i, (src, dst) in enumerate(pairs)]
    for move in moves:
        move.start()
    return moves


def pack_kernel(
    capacity,
    tiles,
    owner_hbm,
    owner_row_hbm,
    slot_row_hbm,
    vis_hbm,
    coarse_hbm,
    direct_ref,
    meta_ref,
    owner_s,
    count_s,
    owner_ref,
    slot_ref,
    vis_ref,
    coarse_ref,
    turn_ref,
    sems,
):
    rows = vis_ref.shape[0]
    devices = direct_ref.shape[0]
    terms, stations = coarse_ref.shape
    half = stations // 2
    gain_tiles = (meta_ref.shape[0] - 1) // 2
    moves = start_all(
        (
            (vis_hbm.at[:, :, pl.ds(0, tiles * LANES)], vis_ref),
            (coarse_hbm, coarse_ref),
            (owner_hbm, owner_s),
            (owner_row_hbm, owner_ref),
            (slot_row_hbm, slot_ref),
        ),
        sems,
    )
    turn_ref[...] = jnp.zeros_like(turn_ref)
    for d in range(devices):
        count_s[d] = 0
    for move in moves[1:]:
        move.wait()

    turn_ref[0:terms, 0:half] = coarse_ref[:, 0:half]
    turn_ref[64 : 64 + terms, 0:half] = coarse_ref[:, half:stations]
    gains = turn_ref[...].T
    high = gains.astype(jnp.bfloat16)
    low = (gains - high.astype(jnp.float32)).astype(jnp.bfloat16)
    for i in range(gain_tiles):
        meta_ref[i] = high[i * SUB : (i + 1) * SUB, :]
        meta_ref[gain_tiles + i] = low[i * SUB : (i + 1) * SUB, :]
    sub = lax.broadcasted_iota(jnp.int32, (SUB, LANES), 0)
    codes = jnp.where(sub == 0, owner_ref[...], slot_ref[...])
    meta_ref[2 * gain_tiles] = codes.astype(jnp.float32).astype(jnp.bfloat16)
    moves[0].wait()

    def place(r, carry):
        d = owner_s[r]
        k = count_s[d]
        count_s[d] = k + 1
        for c in range(tiles):
            direct_ref[d, tiles * k + c] = vis_ref[r, :, c * LANES : (c + 1) * LANES]
        return carry

    lax.fori_loop(0, rows, place, 0, unroll=8)


def pack_shared_kernel(capacity, tiles, me_s, owner_hbm, vis_hbm, meta_hbm, partner_hbm, *rest):
    outs = rest[:-7]
    owner_s, count_s, vis_ref, meta_ref, partner_ref, block_ref, sems = rest[-7:]
    rows = vis_ref.shape[0]
    shared = vis_ref.shape[2] // LANES
    near = block_ref.shape[0]
    depth = meta_ref.shape[0]
    at = 2 * capacity * shared
    moves = start_all(
        (
            (vis_hbm.at[:, :, pl.ds(tiles * LANES, shared * LANES)], vis_ref),
            (owner_hbm, owner_s),
            (meta_hbm, meta_ref),
            (partner_hbm, partner_ref),
        ),
        sems,
    )
    for x in range(2 * near):
        count_s[x] = 0
    me = me_s[0]
    for move in moves[1:]:
        move.wait()
    for m in range(near):
        for i in range(depth):
            block_ref[m, at + i] = meta_ref[i]
            block_ref[m, at + depth + i] = partner_ref[i]
    moves[0].wait()

    def place(r, carry):
        x = owner_s[r] ^ me
        k = count_s[x]
        count_s[x] = k + 1
        far = jnp.where(x >= near, 1, 0)
        for c in range(shared):
            block_ref[x - far * near, (far * capacity + k) * shared + c] = vis_ref[
                r, :, c * LANES : (c + 1) * LANES
            ]
        return carry

    lax.fori_loop(0, rows, place, 0, unroll=8)
    sends = start_all([(block_ref.at[m], outs[m]) for m in range(near)], sems)
    for send in sends:
        send.wait()


def list_rows(owner, slot, target, capacity):
    senders = owner.shape[0]
    mine = owner == target
    counted = mine.astype(jnp.float32)
    before = lax.broadcasted_iota(jnp.int32, (LANES, LANES), 0) < lax.broadcasted_iota(
        jnp.int32, (LANES, LANES), 1
    )
    rank = jnp.dot(
        counted.astype(jnp.bfloat16),
        before.astype(jnp.float32).astype(jnp.bfloat16),
        preferred_element_type=jnp.float32,
    )
    lane = lax.broadcasted_iota(jnp.int32, (senders, LANES), 1)
    count = jnp.sum(counted, axis=1, keepdims=True)
    listing = jnp.where(lane == capacity, count, 0.0)
    for k in range(capacity):
        here = jnp.logical_and(mine, rank == float(k))
        kth = jnp.sum(jnp.where(here, slot, 0.0), axis=1, keepdims=True)
        listing = jnp.where(lane == k, kth, listing)
    return listing.astype(jnp.int32), mine


def add_rows(acc_ref, first_tile, slots_s, line, capacity, rows_ref, block, tiles):
    def add(k, carry):
        b = slots_s[line, k]
        for c in range(tiles):
            acc_ref[first_tile + c, b] += rows_ref[block, tiles * k + c].astype(jnp.float32)
        return carry

    lax.fori_loop(0, slots_s[line, capacity], add, 0)


def helper_kernel(capacity, shared, me_s, *rest):
    blocks = rest[:-7]
    out_ref, rows_ref, codes_ref, acc_ref, slots_ref, slots_s, sems = rest[-7:]
    near = rows_ref.shape[0]
    depth = (blocks[0].shape[0] - 2 * capacity * shared) // 2
    code_at = 2 * capacity * shared + depth - 1
    part = capacity * shared
    moves = start_all(
        [(blocks[m].at[code_at], codes_ref.at[m]) for m in range(near)]
        + [(blocks[m].at[pl.ds(part, part)], rows_ref.at[m]) for m in range(near)],
        sems,
    )
    for c in range(shared):
        acc_ref[c] = jnp.zeros_like(acc_ref[c])
    for move in moves[:near]:
        move.wait()
    codes = [codes_ref[m].astype(jnp.float32) for m in range(near)]
    owner = jnp.concatenate([c[0:1, :] for c in codes], axis=0)
    slot = jnp.concatenate([c[1:2, :] for c in codes], axis=0)
    target = (me_s[0] ^ near).astype(jnp.float32)
    slots_ref[...], _ = list_rows(owner, slot, target, capacity)
    move = pltpu.make_async_copy(slots_ref, slots_s, sems.at[0])
    move.start()
    for other in moves[near:]:
        other.wait()
    move.wait()
    for m in range(near):
        add_rows(acc_ref, 0, slots_s, m, capacity, rows_ref, m, shared)
    for c in range(shared):
        out_ref[c] = acc_ref[c].astype(out_ref.dtype)


def prepare_kernel(
    capacity, shared, stations, turn_s, me_s, pairs_s, pairs_ref, weights_ref, offset_ref, *rest
):
    inputs = rest[:-12]
    (gains_ref, recip_ref, slots_ref, sums_ref) = rest[-12:-8]
    (metas_ref, table_ref, pick_ref, rows_ref, codes_ref, slots_s, slots_v, sems) = rest[-8:]
    devices, depth, _, _ = metas_ref.shape
    owned = recip_ref.shape[0]
    channels = weights_ref.shape[1]
    half = stations // 2
    gain_tiles = (depth - 1) // 2
    near = len(inputs)
    if near == 1:
        moves = start_all([(inputs[0], metas_ref)], sems)
    else:
        at = 2 * capacity * shared
        moves = start_all(
            [(inputs[m].at[pl.ds(at, depth)], metas_ref.at[m]) for m in range(near)]
            + [(inputs[m].at[pl.ds(at + depth, depth)], metas_ref.at[near + m]) for m in range(near)]
            + [(inputs[m].at[pl.ds(0, capacity * shared)], rows_ref.at[m]) for m in range(near)],
            sems,
        )
    for move in moves:
        move.wait()

    for x in range(devices):
        for i in range(gain_tiles):
            table_ref[x, i * SUB : (i + 1) * SUB, :] = metas_ref[x, i].astype(
                jnp.float32
            ) + metas_ref[x, gain_tiles + i].astype(jnp.float32)
        code = metas_ref[x, 2 * gain_tiles].astype(jnp.float32)
        codes_ref[0, x : x + 1, :] = code[0:1, :]
        codes_ref[1, x : x + 1, :] = code[1:2, :]
    owner, slot = codes_ref[0], codes_ref[1]
    listing, mine = list_rows(owner, slot, me_s[0].astype(jnp.float32), capacity)
    slots_ref[...] = listing
    slots_v[...] = listing
    move = pltpu.make_async_copy(slots_v, slots_s, sems.at[0])
    move.start()

    which = lax.broadcasted_iota(jnp.int32, (owned, LANES), 0).astype(jnp.float32)
    codes_ref[0] = jnp.where(mine, slot, -1.0)
    hits = jnp.zeros((owned, LANES), jnp.float32)
    for x in range(devices):
        hits = hits + (codes_ref[0, x : x + 1, :] == which).astype(jnp.float32)
    tally = jnp.sum(hits, axis=1, keepdims=True)
    recip_ref[...] = jnp.broadcast_to(1.0 / jnp.maximum(tally, 1.0), recip_ref.shape)

    turn = turn_s[0]

    def pick(b, carry):
        for side in range(2):
            s = pairs_s[side, b]
            d = s // stations
            within = s - d * stations
            row = jnp.where(within >= half, within - half, within)
            pick_ref[pl.ds(side * owned + b, 1), :] = table_ref[d ^ turn, pl.ds(row, 1), :]
        return carry

    lax.fori_loop(0, owned, pick, 0, unroll=4)

    knot = (lax.broadcasted_iota(jnp.int32, (LANES, channels), 0) & 63) >> 3
    basis = jnp.zeros((LANES, channels), jnp.float32)
    for step in range(3):
        basis = basis + jnp.where(
            knot == offset_ref[...] + step, weights_ref[step : step + 1, :], 0.0
        )
    part = lax.broadcasted_iota(jnp.int32, (LANES, channels), 0) & 7
    column = lax.broadcasted_iota(jnp.int32, (owned, LANES), 1)
    used = (column & 63) < USED
    picked = []
    for side in range(2):
        within = lax.rem(pairs_ref[:, side : side + 1], stations)
        keep = jnp.logical_and(used, (column >= 64) == (within >= half))
        picked.append(jnp.where(keep, pick_ref[side * owned : (side + 1) * owned, :], 0.0))
    both = jnp.concatenate(picked, axis=0)
    for j in range(8):
        fine = jnp.dot(
            both,
            jnp.where(part == j, basis, 0.0),
            precision=lax.Precision.HIGHEST,
            preferred_element_type=jnp.float32,
        )
        gains_ref[j] = fine.astype(jnp.bfloat16).astype(jnp.float32)

    for c in range(sums_ref.shape[0]):
        sums_ref[c] = jnp.zeros_like(sums_ref[c])
    move.wait()
    if near > 1:
        for m in range(near):
            add_rows(sums_ref, 0, slots_s, m, capacity, rows_ref, m, shared)


def finish_kernel(
    capacity, shared, turn_s, slots_s, direct_ref, sums_ref, gains_ref, recip_ref, *rest
):
    far = rest[:-3]
    out_ref, acc_ref, res_ref = rest[-3:]
    owned, parts, channels = out_ref.shape
    devices = direct_ref.shape[0]
    chunks = channels // LANES
    tiles = chunks - shared
    turn = turn_s[0]
    for c in range(tiles):
        acc_ref[c] = jnp.zeros_like(acc_ref[c])
    for c in range(shared):
        acc_ref[tiles + c] = sums_ref[c] + far[0][c].astype(jnp.float32)

    def from_device(d, carry):
        add_rows(acc_ref, 0, slots_s, d ^ turn, capacity, direct_ref, d, tiles)
        return carry

    lax.fori_loop(0, devices, from_device, 0)

    flat = acc_ref.reshape(chunks * owned * parts, LANES)
    done = res_ref.reshape(chunks * owned * parts, LANES)
    for b0 in range(0, owned, SUB):
        scale = recip_ref[b0 : b0 + SUB, :]
        for c in range(chunks):
            row = (c * owned + b0) * parts
            cols = slice(c * LANES, (c + 1) * LANES)
            vis = [flat[pl.ds(row + j, SUB, stride=parts), :] for j in range(parts)]
            lhs = [gains_ref[j, b0 : b0 + SUB, cols] for j in range(parts)]
            rhs = [gains_ref[j, owned + b0 : owned + b0 + SUB, cols] for j in range(parts)]
            mid_re, mid_im = [], []
            for row_a in range(2):
                for col_b in range(2):
                    re = im = 0.0
                    for inner in range(2):
                        lr, li = lhs[2 * row_a + inner], lhs[4 + 2 * row_a + inner]
                        vr, vi = vis[2 * inner + col_b], vis[4 + 2 * inner + col_b]
                        re = re + lr * vr - li * vi
                        im = im + lr * vi + li * vr
                    mid_re.append(re * scale)
                    mid_im.append(im * scale)
            for row_a in range(2):
                for col_b in range(2):
                    re = im = 0.0
                    for inner in range(2):
                        mr, mi = mid_re[2 * row_a + inner], mid_im[2 * row_a + inner]
                        rr, ri = rhs[2 * col_b + inner], rhs[4 + 2 * col_b + inner]
                        re = re + mr * rr + mi * ri
                        im = im + mi * rr - mr * ri
                    j = 2 * row_a + col_b
                    done[pl.ds(row + j, SUB, stride=parts), :] = re
                    done[pl.ds(row + 4 + j, SUB, stride=parts), :] = im
    for c in range(chunks):
        out_ref[:, :, c * LANES : (c + 1) * LANES] = res_ref[c].astype(out_ref.dtype)


def on_device(
    visibilities,
    row_owner,
    row_slot,
    baseline_station_pairs,
    gains_coarse,
    band_weights,
    band_offset,
):
    devices = lax.axis_size("bl")
    rows, parts, channels = visibilities.shape
    capacity = 2 * rows // devices
    owned = baseline_station_pairs.shape[0]
    stations, _, knots = gains_coarse.shape
    chunks = channels // LANES
    gain_tiles = round_up(stations // 2, SUB) // SUB
    depth = 2 * gain_tiles + 1
    near = devices // 2 if devices <= 16 else 1
    shared = 1 if near > 1 else 0
    tiles = chunks - shared
    f32, bf16, i32 = jnp.float32, jnp.bfloat16, jnp.int32
    vmem = pl.BlockSpec(memory_space=pltpu.VMEM)
    smem = pl.BlockSpec(memory_space=pltpu.SMEM)
    hbm = pl.BlockSpec(memory_space=pltpu.HBM)
    anywhere = pl.BlockSpec(memory_space=pl.ANY)
    most = pltpu.CompilerParams(vmem_limit_bytes=ALL_VMEM)
    some = pltpu.CompilerParams(vmem_limit_bytes=SOME_VMEM)
    shape = jax.ShapeDtypeStruct
    dma = pltpu.SemaphoreType.DMA

    me = lax.axis_index("bl").astype(i32).reshape(1)
    turn = me if shared else jnp.zeros_like(me)
    owner = row_owner.reshape(rows)
    coarse = gains_coarse.transpose(2, 1, 0).reshape(knots * parts, stations)
    direct, meta = pl.pallas_call(
        functools.partial(pack_kernel, capacity, tiles),
        out_shape=(
            shape((devices, tiles * capacity, parts, LANES), bf16),
            shape((depth, SUB, LANES), bf16),
        ),
        in_specs=[hbm] * 5,
        out_specs=(vmem, vmem),
        scratch_shapes=[
            pltpu.SMEM((rows,), i32),
            pltpu.SMEM((devices,), i32),
            pltpu.VMEM((1, rows), i32),
            pltpu.VMEM((1, rows), i32),
            pltpu.VMEM((rows, parts, tiles * LANES), bf16),
            pltpu.VMEM((knots * parts, stations), f32),
            pltpu.VMEM((LANES, LANES), f32),
            dma((5,)),
        ],
        compiler_params=most,
        name="pack_direct",
    )(owner, row_owner.reshape(1, rows), row_slot.reshape(1, rows), visibilities, coarse)

    if shared:
        partner = lax.ppermute(meta, "bl", [(d, d ^ near) for d in range(devices)])
    received = lax.all_to_all(direct, "bl", split_axis=0, concat_axis=0, tiled=True)
    if shared:
        block = (2 * capacity * shared + 2 * depth, parts, LANES)
        blocks = pl.pallas_call(
            functools.partial(pack_shared_kernel, capacity, tiles),
            out_shape=[shape(block, bf16)] * near,
            in_specs=[smem] + [hbm] * 4,
            out_specs=[hbm] * near,
            scratch_shapes=[
                pltpu.SMEM((rows,), i32),
                pltpu.SMEM((devices,), i32),
                pltpu.VMEM((rows, parts, shared * LANES), bf16),
                pltpu.VMEM((depth, SUB, LANES), bf16),
                pltpu.VMEM((depth, SUB, LANES), bf16),
                pltpu.VMEM((near,) + block, bf16),
                dma((near,)),
            ],
            compiler_params=most,
            name="pack_shared",
        )(me, owner, visibilities, meta, partner)
        inputs = [blocks[0]] + [
            lax.ppermute(blocks[m], "bl", [(d, d ^ m) for d in range(devices)])
            for m in range(1, near)
        ]
        helped = pl.pallas_call(
            functools.partial(helper_kernel, capacity, shared),
            out_shape=shape((shared, owned, parts, LANES), bf16),
            in_specs=[smem] + [anywhere] * near,
            out_specs=vmem,
            scratch_shapes=[
                pltpu.VMEM((near, capacity * shared, parts, LANES), bf16),
                pltpu.VMEM((near, SUB, LANES), bf16),
                pltpu.VMEM((shared, owned, parts, LANES), f32),
                pltpu.VMEM((near, LANES), i32),
                pltpu.SMEM((near, LANES), i32),
                dma((2 * near,)),
            ],
            compiler_params=some,
            name="help_partner",
        )(me, *inputs)
        far = [lax.ppermute(helped, "bl", [(d, d ^ near) for d in range(devices)])]
    else:
        inputs = [lax.all_gather(meta, "bl", axis=0)]
        far = []

    gains, recip, slots, sums = pl.pallas_call(
        functools.partial(prepare_kernel, capacity, shared, stations),
        out_shape=(
            shape((parts, 2 * owned, channels), f32),
            shape((owned, LANES), f32),
            shape((devices, LANES), i32),
            shape((max(shared, 1), owned, parts, LANES), f32),
        ),
        in_specs=[smem, smem, smem, vmem, vmem, vmem] + [anywhere] * near,
        out_specs=(vmem,) * 4,
        scratch_shapes=[
            pltpu.VMEM((devices, depth, SUB, LANES), bf16),
            pltpu.VMEM((devices, gain_tiles * SUB, LANES), f32),
            pltpu.VMEM((2 * owned, LANES), f32),
            pltpu.VMEM((near, capacity * max(shared, 1), parts, LANES), bf16),
            pltpu.VMEM((2, devices, LANES), f32),
            pltpu.SMEM((devices, LANES), i32),
            pltpu.VMEM((devices, LANES), i32),
            dma((3 * near,)),
        ],
        compiler_params=some,
        name="gains_and_lists",
    )(
        turn,
        me,
        baseline_station_pairs.T,
        baseline_station_pairs,
        band_weights.T,
        band_offset.reshape(1, channels),
        *inputs,
    )
    return pl.pallas_call(
        functools.partial(finish_kernel, capacity, shared),
        out_shape=shape((owned, parts, channels), bf16),
        in_specs=[smem, smem] + [vmem] * (4 + len(far)),
        out_specs=vmem,
        scratch_shapes=[
            pltpu.VMEM((chunks, owned, parts, LANES), f32),
            pltpu.VMEM((chunks, owned, parts, LANES), f32),
        ],
        compiler_params=some,
        name="sum_and_apply",
    )(turn, slots, received, sums, gains, recip, *far)


def solution(mesh):
    placed = (
        P(("groups", "bl"), None, None),
        P(("groups", "bl"), None),
        P(("groups", "bl")),
        P("bl", None),
        P(("groups", "bl"), None, None),
        P("groups", None),
        P("groups"),
    )
    return jax.shard_map(
        on_device,
        mesh=mesh,
        in_specs=placed,
        out_specs=P(("groups", "bl"), None, None),
        check_vma=False,
    )
```

time: 61.8 us -> 71.4 us (1.16)
  the two profiles are of different devices: /device:TPU:19 before, /device:TPU:0 now
where the time goes in v4:
time: 71.4 us; the launch traced here: 71.7 us
  waiting for transfers between devices  31.8 us (45%)
  Pallas kernels  17.9 us (25%)
  starting transfers between devices  16.8 us (24%)
  local copies, waits for them, and re-layouts  5.14 us (7%)
    ppermute x1, waiting for transfers between devices, on_device(): partner = lax.ppermute(meta, 'bl', [(d, d ^ near) for d in range(devices)])  24.1 us
    all_to_all x1, starting transfers between devices, on_device(): lax.all_to_all(direct, 'bl', split_axis=0, concat_axis=0, tiled=True)  7.53 us
    ppermute x7, waiting for transfers between devices, on_device(): lax.ppermute(blocks[m], 'bl', [(d, d ^ m) for d in range(devices)])  7.19 us
    ppermute x7, starting transfers between devices, on_device(): lax.ppermute(blocks[m], 'bl', [(d, d ^ m) for d in range(devices)])  5.59 us
    unnamed x21, local copies, waits for them, and re-layouts  5.14 us
    pallas_call x1, Pallas kernels, on_device(): pl.pallas_call(functools.partial(prepare_kernel, capacity, shared, statio...  5.14 us
    pallas_call x1, Pallas kernels, on_device(): pl.pallas_call(functools.partial(finish_kernel, capacity, shared), out_sh...  4.57 us
    pallas_call x1, Pallas kernels, on_device(): pl.pallas_call(functools.partial(helper_kernel, capacity, shared), out_sh...  3.02 us
  transfers between devices with their start and end apart: 10, of which 8 were waited for; matrix products, arithmetic and copies ran while one was open for 0% of the time, Pallas kernels for 15%

profile of v4, /device:TPU:0, one launch (start us, length us, event | category | flops | bytes accessed | tf_op | source)
XLA Modules:
  0.0 71.7 jit_solution(14897877684456475275)
XLA Ops:
  0.0 2.7 %pack_direct.1 = (bf16[16,32,8,128]{3,2,1,0:T(8,128)(2,1)}, bf16[5,8,128]{2,1,0:T(8,128)(2,1)}) custom-call(s32[128]{0:T(128)} %bitcast.12, s32[1,128]{1,0:T(1,128)} %bitcast.13, s32[1,128]{1,0:T(1,128)} %bitcast.15, bf16[128,8,384]{2,1,0:T(8,128)(2,1)} %vis_hbm.3, f32[48,32]{1,0:T(8,128)} %bitcast.11), custom_call_target="tpu_custom_call" | custom-call | tf_op jit(solution)/shard_map/pack_direct/pallas_call | solution.py:385
  2.7 7.5 %all-to-all-start = ((bf16[16,32,8,128]{3,2,1,0:T(8,128)(2,1)}), bf16[16,32,8,128]{3,2,1,0:T(8,128)(2,1)S(1)}, u32[]{:S(2)}, u32[]{:S(2)}) async-start(bf16[16,32,8,128]{3,2,1,0:T(8,128)(2,1)} %get-tuple-element.29), calls=%async_computation | async-start | bytes 2097152 | tf_op jit(solution)/shard_map/all_to_all | solution.py:409
  10.3 2.9 %collective-permute-start = (bf16[5,8,128]{2,1,0:T(8,128)(2,1)S(1)}, bf16[5,8,128]{2,1,0:T(8,128)(2,1)S(1)}, u32[]{:S(2)}, u32[]{:S(2)}) collective-permute-start(bf16[5,8,128]{2,1,0:T(8,128)(2,1)S(1)} %copy-done.7), channel_id=1, source_target_pairs={{0,8},{1,9},{2,10},{3,11},{4,12},{5,13},{6,14},{7,15},{8,0},{9,1},... | collective-permute-start | bytes 30728 | tf_op jit(solution)/shard_map/ppermute | solution.py:408
  13.2 24.1 %collective-permute-done.partner_hbm = bf16[5,8,128]{2,1,0:T(8,128)(2,1)S(1)} collective-permute-done((bf16[5,8,128]{2,1,0:T(8,128)(2,1)S(1)}, bf16[5,8,128]{2,1,0:T(8,128)(2,1)S(1)}, u32[]{:S(2)}, u32[]{:S(2)}) %collective-permute-start) | collective-permute-done | bytes 10272 | tf_op jit(solution)/shard_map/ppermute | solution.py:408
  37.3 0.6 copy-done.8
  37.9 2.5 %pack_shared.1 = (bf16[42,8,128]{2,1,0:T(8,128)(2,1)}, bf16[42,8,128]{2,1,0:T(8,128)(2,1)}, bf16[42,8,128]{2,1,0:T(8,128)(2,1)}, bf16[42,8,128]{2,1,0:T(8,128)(2...) custom-call(s32[1]{0:T(128)} %bitcast.me_s.turn_s, ...), custom_call_target="tpu_custom_call" | custom-call | tf_op jit(solution)/shard_map/pack_shared/pallas_call | solution.py:412
  40.4 1.5 %collective-permute-start.2 = (bf16[42,8,128]{2,1,0:T(8,128)(2,1)}, bf16[42,8,128]{2,1,0:T(8,128)(2,1)S(1)}, u32[]{:S(2)}, u32[]{:S(2)}) collective-permute-start(bf16[42,8,128]{2,1,0:T(8,128)(2,1)} %get-tuple-element.22), channel_id=1, source_target_pairs={{0,2},{1,3},{2,0},{3,1},{4,6},{5,7},{6,4},{7,5},{8,10},{9,11},{10,... | collective-permute-start | bytes 258056 | tf_op jit(solution)/shard_map/ppermute | solution.py:430
  42.3 1.7 %collective-permute-start.5 = (bf16[42,8,128]{2,1,0:T(8,128)(2,1)}, bf16[42,8,128]{2,1,0:T(8,128)(2,1)S(1)}, u32[]{:S(2)}, u32[]{:S(2)}) collective-permute-start(bf16[42,8,128]{2,1,0:T(8,128)(2,1)} %get-tuple-element.25), channel_id=1, source_target_pairs={{0,5},{1,4},{2,7},{3,6},{4,1},{5,0},{6,3},{7,2},{8,13},{9,12},{10,... | collective-permute-start | bytes 258056 | tf_op jit(solution)/shard_map/ppermute | solution.py:430
  44.0 1.3 %collective-permute-start.6 = (bf16[42,8,128]{2,1,0:T(8,128)(2,1)}, bf16[42,8,128]{2,1,0:T(8,128)(2,1)S(1)}, u32[]{:S(2)}, u32[]{:S(2)}) collective-permute-start(bf16[42,8,128]{2,1,0:T(8,128)(2,1)} %get-tuple-element.26), channel_id=1, source_target_pairs={{0,6},{1,7},{2,4},{3,5},{4,2},{5,3},{6,0},{7,1},{8,14},{9,15},{10,... | collective-permute-start | bytes 258056 | tf_op jit(solution)/shard_map/ppermute | solution.py:430
  45.2 0.7 %collective-permute-done.2.rest_2_ = bf16[42,8,128]{2,1,0:T(8,128)(2,1)S(1)} collective-permute-done((bf16[42,8,128]{2,1,0:T(8,128)(2,1)}, bf16[42,8,128]{2,1,0:T(8,128)(2,1)S(1)}, u32[]{:S(2)}, u32[]{:S(2)}) %collective-permute-start.2) | collective-permute-done | bytes 86048 | tf_op jit(solution)/shard_map/ppermute | solution.py:430
  46.0 0.7 collective-permute-start.7
  47.0 0.9 %collective-permute-done.4.rest_4_ = bf16[42,8,128]{2,1,0:T(8,128)(2,1)S(1)} collective-permute-done((bf16[42,8,128]{2,1,0:T(8,128)(2,1)}, bf16[42,8,128]{2,1,0:T(8,128)(2,1)S(1)}, u32[]{:S(2)}, u32[]{:S(2)}) %collective-permute-start.4) | collective-permute-done | bytes 86048 | tf_op jit(solution)/shard_map/ppermute | solution.py:430
  47.9 0.7 collective-permute-done.5.rest_5_
  48.5 3.9 %collective-permute-done.6.rest_6_ = bf16[42,8,128]{2,1,0:T(8,128)(2,1)S(1)} collective-permute-done((bf16[42,8,128]{2,1,0:T(8,128)(2,1)}, bf16[42,8,128]{2,1,0:T(8,128)(2,1)S(1)}, u32[]{:S(2)}, u32[]{:S(2)}) %collective-permute-start.6) | collective-permute-done | bytes 86048 | tf_op jit(solution)/shard_map/ppermute | solution.py:430
  52.5 0.7 collective-permute-done.7.rest_7_
  53.1 0.9 %copy-done = bf16[42,8,128]{2,1,0:T(8,128)(2,1)S(1)} copy-done((bf16[42,8,128]{2,1,0:T(8,128)(2,1)S(1)}, bf16[42,8,128]{2,1,0:T(8,128)(2,1)}, u32[]{:S(2)}) %copy-start) | copy-done | bytes 86040
  54.0 3.0 %help_partner.1 = bf16[1,64,8,128]{3,2,1,0:T(8,128)(2,1)} custom-call(s32[1]{0:T(128)} %bitcast.me_s.turn_s, bf16[42,8,128]{2,1,0:T(8,128)(2,1)S(1)} %copy-done, bf16[42,8,128]{2,1,0:T(8,128)(2,1)S(1)} %collective-permute-done.1.rest_1_, bf16[42,8,128]{2,1,0:T(8,128)(2,1)S(1)} %collective-permute-done.2.rest_2_, ...), custom_call_target="tpu_custom_call" | custom-call | tf_op jit(solution)/shard_map/help_partner/pallas_call | solution.py:433
  57.0 0.8 %collective-permute-start.8 = (bf16[1,64,8,128]{3,2,1,0:T(8,128)(2,1)}, bf16[1,64,8,128]{3,2,1,0:T(8,128)(2,1)}, u32[]{:S(2)}, u32[]{:S(2)}) collective-permute-start(bf16[1,64,8,128]{3,2,1,0:T(8,128)(2,1)} %help_partner.1), channel_id=1, source_target_pairs={{0,8},{1,9},{2,10},{3,11},{4,12},{5,13},{6,14},{7,15},{8,0},{9,1},... | collective-permute-start | bytes 393224 | tf_op jit(solution)/shard_map/ppermute | solution.py:449
  57.9 0.9 %copy-done.1 = bf16[42,8,128]{2,1,0:T(8,128)(2,1)S(1)} copy-done((bf16[42,8,128]{2,1,0:T(8,128)(2,1)S(1)}, bf16[42,8,128]{2,1,0:T(8,128)(2,1)}, u32[]{:S(2)}) %copy-start.1) | copy-done | bytes 86040
  58.8 0.7 copy-done.4
  59.5 0.7 copy-done.6
  60.2 5.1 %gains_and_lists.1 = (f32[8,128,384]{2,1,0:T(8,128)S(1)}, f32[64,128]{1,0:T(8,128)S(1)}, s32[16,128]{1,0:T(8,128)S(1)}, f32[1,64,8,128]{3,2,1,0:T(8,128)S(1)}) custom-call(s32[1]{0:T(128)} %bitcast.me_s.turn_s, s32[1]{0:T(128)} %bitcast.me_s.turn_s, s32[2,64]{1,0:T(2,128)S(1)} %bitcast.10, s32[64,2]{1,0:T(8,128)S(1)} %copy.8.pairs_ref, ...), custom_call_target="tpu_custom_call" | custom-call | tf_op jit(solution)/shard_map/gains_and_lists/pallas_call | solution.py:454
  66.5 0.7 copy-done.3
  67.2 4.6 %sum_and_apply.1 = bf16[64,8,384]{2,1,0:T(8,128)(2,1)} custom-call(s32[1]{0:T(128)} %bitcast.me_s.turn_s, s32[16,128]{1,0:T(8,128)S(1)} %copy-done.3, bf16[16,32,8,128]{3,2,1,0:T(8,128)(2,1)S(1)} %all-to-all-done.direct_ref, f32[1,64,8,128]{3,2,1,0:T(8,128)S(1)} %get-tuple-element.30.sums_ref, f32[8,128,384]{2,1,0:T(8,128)S(1)} %get-tuple-element.31.gains_ref, ...), custom_call_target="tpu_custom_call" | custom-call | tf_op jit(solution)/shard_map/sum_and_apply/pallas_call | solution.py:485
  (23 shorter events, 1.9 us)
Async XLA Ops:
  2.7 7.6 %copy-start.7 = (bf16[5,8,128]{2,1,0:T(8,128)(2,1)S(1)}, bf16[5,8,128]{2,1,0:T(8,128)(2,1)}, u32[]{:S(2)}) copy-start(bf16[5,8,128]{2,1,0:T(8,128)(2,1)} %get-tuple-element.19.meta_hbm) | copy-start | bytes 30724
  2.7 55.1 %copy-start.9 = (s32[384]{0:T(512)S(1)}, s32[384]{0:T(512)}, u32[]{:S(2)}) copy-start(s32[384]{0:T(512)} %param.13) | copy-start | bytes 4612
  2.7 55.1 %copy-start.5 = (s32[64,2]{0,1:T(2,128)S(1)}, s32[64,2]{0,1:T(2,128)}, u32[]{:S(2)}) copy-start(s32[64,2]{0,1:T(2,128)} %param.10) | copy-start | bytes 1540
  2.7 63.7 %all-to-all-start = ((bf16[16,32,8,128]{3,2,1,0:T(8,128)(2,1)}), bf16[16,32,8,128]{3,2,1,0:T(8,128)(2,1)S(1)}, u32[]{:S(2)}, u32[]{:S(2)}) async-start(bf16[16,32,8,128]{3,2,1,0:T(8,128)(2,1)} %get-tuple-element.29), calls=%async_computation | async-start | bytes 2097152 | tf_op jit(solution)/shard_map/all_to_all | solution.py:409
  10.3 27.0 %collective-permute-start = (bf16[5,8,128]{2,1,0:T(8,128)(2,1)S(1)}, bf16[5,8,128]{2,1,0:T(8,128)(2,1)S(1)}, u32[]{:S(2)}, u32[]{:S(2)}) collective-permute-start(bf16[5,8,128]{2,1,0:T(8,128)(2,1)S(1)} %copy-done.7), channel_id=1, source_target_pairs={{0,8},{1,9},{2,10},{3,11},{4,12},{5,13},{6,14},{7,15},{8,0},{9,1},... | collective-permute-start | bytes 30728 | tf_op jit(solution)/shard_map/ppermute | solution.py:408
  37.3 0.6 copy-start.8
  40.3 3.6 %collective-permute-start.1 = (bf16[42,8,128]{2,1,0:T(8,128)(2,1)}, bf16[42,8,128]{2,1,0:T(8,128)(2,1)S(1)}, u32[]{:S(2)}, u32[]{:S(2)}) collective-permute-start(bf16[42,8,128]{2,1,0:T(8,128)(2,1)} %get-tuple-element.21), channel_id=1, source_target_pairs={{0,1},{1,0},{2,3},{3,2},{4,5},{5,4},{6,7},{7,6},{8,9},{9,8},{10,11... | collective-permute-start | bytes 258056 | tf_op jit(solution)/shard_map/ppermute | solution.py:430
  40.4 5.6 %collective-permute-start.2 = (bf16[42,8,128]{2,1,0:T(8,128)(2,1)}, bf16[42,8,128]{2,1,0:T(8,128)(2,1)S(1)}, u32[]{:S(2)}, u32[]{:S(2)}) collective-permute-start(bf16[42,8,128]{2,1,0:T(8,128)(2,1)} %get-tuple-element.22), channel_id=1, source_target_pairs={{0,2},{1,3},{2,0},{3,1},{4,6},{5,7},{6,4},{7,5},{8,10},{9,11},{10,... | collective-permute-start | bytes 258056 | tf_op jit(solution)/shard_map/ppermute | solution.py:430
  42.0 5.0 %collective-permute-start.3 = (bf16[42,8,128]{2,1,0:T(8,128)(2,1)}, bf16[42,8,128]{2,1,0:T(8,128)(2,1)S(1)}, u32[]{:S(2)}, u32[]{:S(2)}) collective-permute-start(bf16[42,8,128]{2,1,0:T(8,128)(2,1)} %get-tuple-element.23), channel_id=1, source_target_pairs={{0,3},{1,2},{2,1},{3,0},{4,7},{5,6},{6,5},{7,4},{8,11},{9,10},{10,... | collective-permute-start | bytes 258056 | tf_op jit(solution)/shard_map/ppermute | solution.py:430
  42.3 5.6 %collective-permute-start.4 = (bf16[42,8,128]{2,1,0:T(8,128)(2,1)}, bf16[42,8,128]{2,1,0:T(8,128)(2,1)S(1)}, u32[]{:S(2)}, u32[]{:S(2)}) collective-permute-start(bf16[42,8,128]{2,1,0:T(8,128)(2,1)} %get-tuple-element.24), channel_id=1, source_target_pairs={{0,4},{1,5},{2,6},{3,7},{4,0},{5,1},{6,2},{7,3},{8,12},{9,13},{10,... | collective-permute-start | bytes 258056 | tf_op jit(solution)/shard_map/ppermute | solution.py:430
  42.3 6.2 %collective-permute-start.5 = (bf16[42,8,128]{2,1,0:T(8,128)(2,1)}, bf16[42,8,128]{2,1,0:T(8,128)(2,1)S(1)}, u32[]{:S(2)}, u32[]{:S(2)}) collective-permute-start(bf16[42,8,128]{2,1,0:T(8,128)(2,1)} %get-tuple-element.25), channel_id=1, source_target_pairs={{0,5},{1,4},{2,7},{3,6},{4,1},{5,0},{6,3},{7,2},{8,13},{9,12},{10,... | collective-permute-start | bytes 258056 | tf_op jit(solution)/shard_map/ppermute | solution.py:430
  44.0 8.5 %collective-permute-start.6 = (bf16[42,8,128]{2,1,0:T(8,128)(2,1)}, bf16[42,8,128]{2,1,0:T(8,128)(2,1)S(1)}, u32[]{:S(2)}, u32[]{:S(2)}) collective-permute-start(bf16[42,8,128]{2,1,0:T(8,128)(2,1)} %get-tuple-element.26), channel_id=1, source_target_pairs={{0,6},{1,7},{2,4},{3,5},{4,2},{5,3},{6,0},{7,1},{8,14},{9,15},{10,... | collective-permute-start | bytes 258056 | tf_op jit(solution)/shard_map/ppermute | solution.py:430
  46.0 7.1 %collective-permute-start.7 = (bf16[42,8,128]{2,1,0:T(8,128)(2,1)}, bf16[42,8,128]{2,1,0:T(8,128)(2,1)S(1)}, u32[]{:S(2)}, u32[]{:S(2)}) collective-permute-start(bf16[42,8,128]{2,1,0:T(8,128)(2,1)} %get-tuple-element.27), channel_id=1, source_target_pairs={{0,7},{1,6},{2,5},{3,4},{4,3},{5,2},{6,1},{7,0},{8,15},{9,14},{10,... | collective-permute-start | bytes 258056 | tf_op jit(solution)/shard_map/ppermute | solution.py:430
  53.1 0.9 %copy-start = (bf16[42,8,128]{2,1,0:T(8,128)(2,1)S(1)}, bf16[42,8,128]{2,1,0:T(8,128)(2,1)}, u32[]{:S(2)}) copy-start(bf16[42,8,128]{2,1,0:T(8,128)(2,1)} %get-tuple-element.20.rest_0_) | copy-start | bytes 258052
  57.0 9.4 %collective-permute-start.8 = (bf16[1,64,8,128]{3,2,1,0:T(8,128)(2,1)}, bf16[1,64,8,128]{3,2,1,0:T(8,128)(2,1)}, u32[]{:S(2)}, u32[]{:S(2)}) collective-permute-start(bf16[1,64,8,128]{3,2,1,0:T(8,128)(2,1)} %help_partner.1), channel_id=1, source_target_pairs={{0,8},{1,9},{2,10},{3,11},{4,12},{5,13},{6,14},{7,15},{8,0},{9,1},... | collective-permute-start | bytes 393224 | tf_op jit(solution)/shard_map/ppermute | solution.py:449
  57.9 0.9 %copy-start.1 = (bf16[42,8,128]{2,1,0:T(8,128)(2,1)S(1)}, bf16[42,8,128]{2,1,0:T(8,128)(2,1)}, u32[]{:S(2)}) copy-start(bf16[42,8,128]{2,1,0:T(8,128)(2,1)} %get-tuple-element.20.rest_0_) | copy-start | bytes 258052
  58.8 0.7 copy-start.4
  59.5 0.7 copy-start.6
  65.3 0.6 copy-start.2
  66.5 0.7 copy-start.3

commit v5 on v4

v5 whole, which is shorter than its diff:
```python
import functools

import jax
import jax.numpy as jnp
from jax import lax
from jax.experimental import pallas as pl
from jax.experimental.pallas import tpu as pltpu
from jax.sharding import PartitionSpec as P

LANES = 128
SUB = 8
USED = 48
ALL_VMEM = 60 * 1024 * 1024
SOME_VMEM = 24 * 1024 * 1024


def round_up(value, unit):
    return -(-value // unit) * unit


def start_all(pairs, sems):
    moves = [pltpu.make_async_copy(src, dst, sems.at[i]) for i, (src, dst) in enumerate(pairs)]
    for move in moves:
        move.start()
    return moves


def pack_kernel(
    capacity,
    near,
    me_s,
    owner_hbm,
    owner_row_hbm,
    slot_row_hbm,
    vis_hbm,
    coarse_hbm,
    meta_hbm,
    *rest,
):
    outs = rest[:-10]
    (
        owner_s,
        count_s,
        owner_ref,
        slot_ref,
        vis_ref,
        coarse_ref,
        turn_ref,
        meta_ref,
        block_ref,
        sems,
    ) = rest[-10:]
    rows = vis_ref.shape[0]
    chunks = vis_ref.shape[2] // LANES
    devices = block_ref.shape[0]
    terms, stations = coarse_ref.shape
    half = stations // 2
    gain_tiles = (meta_ref.shape[0] - 1) // 2
    moves = start_all(
        (
            (vis_hbm, vis_ref),
            (coarse_hbm, coarse_ref),
            (owner_hbm, owner_s),
            (owner_row_hbm, owner_ref),
            (slot_row_hbm, slot_ref),
        ),
        sems,
    )
    turn_ref[...] = jnp.zeros_like(turn_ref)
    for d in range(devices):
        count_s[d] = 0
    me = me_s[0]
    for move in moves[1:]:
        move.wait()

    turn_ref[0:terms, 0:half] = coarse_ref[:, 0:half]
    turn_ref[64 : 64 + terms, 0:half] = coarse_ref[:, half:stations]
    gains = turn_ref[...].T
    high = gains.astype(jnp.bfloat16)
    low = (gains - high.astype(jnp.float32)).astype(jnp.bfloat16)
    for i in range(gain_tiles):
        meta_ref[i] = high[i * SUB : (i + 1) * SUB, :]
        meta_ref[gain_tiles + i] = low[i * SUB : (i + 1) * SUB, :]
    sub = lax.broadcasted_iota(jnp.int32, (SUB, LANES), 0)
    codes = jnp.where(sub == 0, owner_ref[...], slot_ref[...])
    meta_ref[2 * gain_tiles] = codes.astype(jnp.float32).astype(jnp.bfloat16)
    sends = start_all([(meta_ref, meta_hbm)], sems.at[pl.ds(1, 1)])
    moves[0].wait()

    def place(r, carry):
        x = owner_s[r] ^ me
        k = count_s[x]
        count_s[x] = k + 1
        for c in range(chunks):
            block_ref[x, chunks * k + c] = vis_ref[r, :, c * LANES : (c + 1) * LANES]
        return carry

    lax.fori_loop(0, rows, place, 0, unroll=8)
    if near > 1:
        pairs = [(block_ref.at[near + i], outs[i]) for i in range(near)]
    else:
        pairs = [(block_ref, outs[0])]
    sends += start_all(pairs, sems.at[pl.ds(2, len(pairs))])
    for send in sends:
        send.wait()


def pack_near_kernel(
    capacity,
    me_s,
    owner_hbm,
    vis_hbm,
    meta_hbm,
    partner_hbm,
    out_ref,
    owner_s,
    count_s,
    vis_ref,
    meta_ref,
    partner_ref,
    sems,
):
    rows = vis_ref.shape[0]
    chunks = vis_ref.shape[2] // LANES
    near = out_ref.shape[0]
    depth = meta_ref.shape[0]
    at = capacity * chunks
    moves = start_all(
        (
            (vis_hbm, vis_ref),
            (owner_hbm, owner_s),
            (meta_hbm, meta_ref),
            (partner_hbm, partner_ref),
        ),
        sems,
    )
    for d in range(near):
        count_s[d] = 0
    half = me_s[0] & near
    for move in moves[1:]:
        move.wait()
    for d in range(near):
        for i in range(depth):
            out_ref[d, at + i] = meta_ref[i]
            out_ref[d, at + depth + i] = partner_ref[i]
    moves[0].wait()

    def place(r, carry):
        x = owner_s[r] ^ half

        @pl.when(x < near)
        def _():
            k = count_s[x]
            count_s[x] = k + 1
            for c in range(chunks):
                out_ref[x, chunks * k + c] = vis_ref[r, :, c * LANES : (c + 1) * LANES]

        return carry

    lax.fori_loop(0, rows, place, 0, unroll=4)


def list_rows(owner, slot, target, capacity):
    senders = owner.shape[0]
    mine = owner == target
    counted = mine.astype(jnp.float32)
    before = lax.broadcasted_iota(jnp.int32, (LANES, LANES), 0) < lax.broadcasted_iota(
        jnp.int32, (LANES, LANES), 1
    )
    rank = jnp.dot(
        counted.astype(jnp.bfloat16),
        before.astype(jnp.float32).astype(jnp.bfloat16),
        preferred_element_type=jnp.float32,
    )
    lane = lax.broadcasted_iota(jnp.int32, (senders, LANES), 1)
    count = jnp.sum(counted, axis=1, keepdims=True)
    listing = jnp.where(lane == capacity, count, 0.0)
    for k in range(capacity):
        here = jnp.logical_and(mine, rank == float(k))
        kth = jnp.sum(jnp.where(here, slot, 0.0), axis=1, keepdims=True)
        listing = jnp.where(lane == k, kth, listing)
    return listing.astype(jnp.int32), mine


def add_rows(acc_ref, slots_s, line, capacity, rows_ref):
    chunks = acc_ref.shape[0]

    def add(k, carry):
        b = slots_s[line, k]
        for c in range(chunks):
            acc_ref[c, b] += rows_ref[chunks * k + c].astype(jnp.float32)
        return carry

    lax.fori_loop(0, slots_s[line, capacity], add, 0)


def prepare_kernel(
    capacity,
    near,
    stations,
    turn_s,
    me_s,
    pairs_s,
    arrived_hbm,
    pairs_ref,
    weights_ref,
    offset_ref,
    gains_ref,
    recip_ref,
    slots_ref,
    sums_ref,
    metas_ref,
    table_ref,
    pick_ref,
    rows_ref,
    codes_ref,
    slots_s,
    slots_v,
    sems,
):
    devices, depth, _, _ = metas_ref.shape
    owned = recip_ref.shape[0]
    channels = weights_ref.shape[1]
    half = stations // 2
    gain_tiles = (depth - 1) // 2
    chunks = channels // LANES
    if near == 1:
        moves = start_all([(arrived_hbm, metas_ref)], sems)
    else:
        at = capacity * chunks
        moves = start_all(
            (
                (arrived_hbm.at[:, pl.ds(at, depth)], metas_ref.at[pl.ds(0, near)]),
                (arrived_hbm.at[:, pl.ds(at + depth, depth)], metas_ref.at[pl.ds(near, near)]),
                (arrived_hbm.at[:, pl.ds(0, at)], rows_ref),
            ),
            sems,
        )
    for move in moves:
        move.wait()

    for x in range(devices):
        for i in range(gain_tiles):
            table_ref[x, i * SUB : (i + 1) * SUB, :] = metas_ref[x, i].astype(
                jnp.float32
            ) + metas_ref[x, gain_tiles + i].astype(jnp.float32)
        code = metas_ref[x, 2 * gain_tiles].astype(jnp.float32)
        codes_ref[0, x : x + 1, :] = code[0:1, :]
        codes_ref[1, x : x + 1, :] = code[1:2, :]
    owner, slot = codes_ref[0], codes_ref[1]
    listing, mine = list_rows(owner, slot, me_s[0].astype(jnp.float32), capacity)
    slots_ref[...] = listing
    slots_v[...] = listing
    move = pltpu.make_async_copy(slots_v, slots_s, sems.at[0])
    move.start()

    which = lax.broadcasted_iota(jnp.int32, (owned, LANES), 0).astype(jnp.float32)
    codes_ref[0] = jnp.where(mine, slot, -1.0)
    hits = jnp.zeros((owned, LANES), jnp.float32)
    for x in range(devices):
        hits = hits + (codes_ref[0, x : x + 1, :] == which).astype(jnp.float32)
    tally = jnp.sum(hits, axis=1, keepdims=True)
    recip_ref[...] = jnp.broadcast_to(1.0 / jnp.maximum(tally, 1.0), recip_ref.shape)

    turn = turn_s[0]

    def pick(b, carry):
        for side in range(2):
            s = pairs_s[side, b]
            d = s // stations
            within = s - d * stations
            row = jnp.where(within >= half, within - half, within)
            pick_ref[pl.ds(side * owned + b, 1), :] = table_ref[d ^ turn, pl.ds(row, 1), :]
        return carry

    lax.fori_loop(0, owned, pick, 0, unroll=4)

    knot = (lax.broadcasted_iota(jnp.int32, (LANES, channels), 0) & 63) >> 3
    basis = jnp.zeros((LANES, channels), jnp.float32)
    for step in range(3):
        basis = basis + jnp.where(
            knot == offset_ref[...] + step, weights_ref[step : step + 1, :], 0.0
        )
    part = lax.broadcasted_iota(jnp.int32, (LANES, channels), 0) & 7
    column = lax.broadcasted_iota(jnp.int32, (owned, LANES), 1)
    used = (column & 63) < USED
    picked = []
    for side in range(2):
        within = lax.rem(pairs_ref[:, side : side + 1], stations)
        keep = jnp.logical_and(used, (column >= 64) == (within >= half))
        picked.append(jnp.where(keep, pick_ref[side * owned : (side + 1) * owned, :], 0.0))
    both = jnp.concatenate(picked, axis=0)
    for j in range(8):
        fine = jnp.dot(
            both,
            jnp.where(part == j, basis, 0.0),
            precision=lax.Precision.HIGHEST,
            preferred_element_type=jnp.float32,
        )
        gains_ref[j] = fine.astype(jnp.bfloat16).astype(jnp.float32)

    for c in range(sums_ref.shape[0]):
        sums_ref[c] = jnp.zeros_like(sums_ref[c])
    move.wait()
    if near > 1:
        for m in range(near):
            add_rows(sums_ref, slots_s, m, capacity, rows_ref.at[m])


def finish_kernel(capacity, turn_s, me_s, slots_s, sums_ref, gains_ref, recip_ref, *rest):
    far = rest[:-3]
    out_ref, acc_ref, res_ref = rest[-3:]
    owned, parts, channels = out_ref.shape
    chunks = channels // LANES
    acc_ref[...] = sums_ref[...]
    if len(far) > 1:
        for i in range(len(far)):
            line = me_s[0] ^ turn_s[0] ^ (len(far) + i)
            add_rows(acc_ref, slots_s, line, capacity, far[i])
    else:

        def from_device(d, carry):
            add_rows(acc_ref, slots_s, d, capacity, far[0].at[d])
            return carry

        lax.fori_loop(0, far[0].shape[0], from_device, 0)

    flat = acc_ref.reshape(chunks * owned * parts, LANES)
    done = res_ref.reshape(chunks * owned * parts, LANES)
    for b0 in range(0, owned, SUB):
        scale = recip_ref[b0 : b0 + SUB, :]
        for c in range(chunks):
            row = (c * owned + b0) * parts
            cols = slice(c * LANES, (c + 1) * LANES)
            vis = [flat[pl.ds(row + j, SUB, stride=parts), :] for j in range(parts)]
            lhs = [gains_ref[j, b0 : b0 + SUB, cols] for j in range(parts)]
            rhs = [gains_ref[j, owned + b0 : owned + b0 + SUB, cols] for j in range(parts)]
            mid_re, mid_im = [], []
            for row_a in range(2):
                for col_b in range(2):
                    re = im = 0.0
                    for inner in range(2):
                        lr, li = lhs[2 * row_a + inner], lhs[4 + 2 * row_a + inner]
                        vr, vi = vis[2 * inner + col_b], vis[4 + 2 * inner + col_b]
                        re = re + lr * vr - li * vi
                        im = im + lr * vi + li * vr
                    mid_re.append(re * scale)
                    mid_im.append(im * scale)
            for row_a in range(2):
                for col_b in range(2):
                    re = im = 0.0
                    for inner in range(2):
                        mr, mi = mid_re[2 * row_a + inner], mid_im[2 * row_a + inner]
                        rr, ri = rhs[2 * col_b + inner], rhs[4 + 2 * col_b + inner]
                        re = re + mr * rr + mi * ri
                        im = im + mi * rr - mr * ri
                    j = 2 * row_a + col_b
                    done[pl.ds(row + j, SUB, stride=parts), :] = re
                    done[pl.ds(row + 4 + j, SUB, stride=parts), :] = im
    for c in range(chunks):
        out_ref[:, :, c * LANES : (c + 1) * LANES] = res_ref[c].astype(out_ref.dtype)


def on_device(
    visibilities,
    row_owner,
    row_slot,
    baseline_station_pairs,
    gains_coarse,
    band_weights,
    band_offset,
):
    devices = lax.axis_size("bl")
    rows, parts, channels = visibilities.shape
    capacity = 2 * rows // devices
    owned = baseline_station_pairs.shape[0]
    stations, _, knots = gains_coarse.shape
    chunks = channels // LANES
    gain_tiles = round_up(stations // 2, SUB) // SUB
    depth = 2 * gain_tiles + 1
    near = devices // 2 if devices <= 16 else 1
    halves = near > 1
    f32, bf16, i32 = jnp.float32, jnp.bfloat16, jnp.int32
    vmem = pl.BlockSpec(memory_space=pltpu.VMEM)
    smem = pl.BlockSpec(memory_space=pltpu.SMEM)
    hbm = pl.BlockSpec(memory_space=pltpu.HBM)
    anywhere = pl.BlockSpec(memory_space=pl.ANY)
    most = pltpu.CompilerParams(vmem_limit_bytes=ALL_VMEM)
    some = pltpu.CompilerParams(vmem_limit_bytes=SOME_VMEM)
    shape = jax.ShapeDtypeStruct
    dma = pltpu.SemaphoreType.DMA

    me = lax.axis_index("bl").astype(i32).reshape(1)
    turn = me & near if halves else jnp.zeros_like(me)
    owner = row_owner.reshape(rows)
    coarse = gains_coarse.transpose(2, 1, 0).reshape(knots * parts, stations)
    block = (chunks * capacity, parts, LANES)
    meta, *sent = pl.pallas_call(
        functools.partial(pack_kernel, capacity, near),
        out_shape=[shape((depth, SUB, LANES), bf16)]
        + [shape(block if halves else (devices,) + block, bf16)] * near,
        in_specs=[smem] + [hbm] * 5,
        out_specs=[hbm] * (1 + near),
        scratch_shapes=[
            pltpu.SMEM((rows,), i32),
            pltpu.SMEM((devices,), i32),
            pltpu.VMEM((1, rows), i32),
            pltpu.VMEM((1, rows), i32),
            pltpu.VMEM((rows, parts, channels), bf16),
            pltpu.VMEM((knots * parts, stations), f32),
            pltpu.VMEM((LANES, LANES), f32),
            pltpu.VMEM((depth, SUB, LANES), bf16),
            pltpu.VMEM((devices,) + block, bf16),
            dma((5 + near,)),
        ],
        compiler_params=most,
        name="pack_rows",
    )(
        me if halves else turn,
        owner,
        row_owner.reshape(1, rows),
        row_slot.reshape(1, rows),
        visibilities,
        coarse,
    )

    if halves:
        partner = lax.ppermute(meta, "bl", [(d, d ^ near) for d in range(devices)])
        far = [
            lax.ppermute(sent[i], "bl", [(d, d ^ (near + i)) for d in range(devices)])
            for i in range(near)
        ]
        packed = pl.pallas_call(
            functools.partial(pack_near_kernel, capacity),
            out_shape=shape((near, chunks * capacity + 2 * depth, parts, LANES), bf16),
            in_specs=[smem] + [hbm] * 4,
            out_specs=vmem,
            scratch_shapes=[
                pltpu.SMEM((rows,), i32),
                pltpu.SMEM((near,), i32),
                pltpu.VMEM((rows, parts, channels), bf16),
                pltpu.VMEM((depth, SUB, LANES), bf16),
                pltpu.VMEM((depth, SUB, LANES), bf16),
                dma((4,)),
            ],
            compiler_params=most,
            name="pack_near",
        )(me, owner, visibilities, meta, partner)
        groups = [list(range(0, near)), list(range(near, devices))]
        arrived = lax.all_to_all(
            packed, "bl", split_axis=0, concat_axis=0, axis_index_groups=groups, tiled=True
        )
    else:
        far = [lax.all_to_all(sent[0], "bl", split_axis=0, concat_axis=0, tiled=True)]
        arrived = lax.all_gather(meta, "bl", axis=0)

    gains, recip, slots, sums = pl.pallas_call(
        functools.partial(prepare_kernel, capacity, near, stations),
        out_shape=(
            shape((parts, 2 * owned, channels), f32),
            shape((owned, LANES), f32),
            shape((devices, LANES), i32),
            shape((chunks, owned, parts, LANES), f32),
        ),
        in_specs=[smem, smem, smem, anywhere, vmem, vmem, vmem],
        out_specs=(vmem,) * 4,
        scratch_shapes=[
            pltpu.VMEM((devices, depth, SUB, LANES), bf16),
            pltpu.VMEM((devices, gain_tiles * SUB, LANES), f32),
            pltpu.VMEM((2 * owned, LANES), f32),
            pltpu.VMEM((near,) + block, bf16),
            pltpu.VMEM((2, devices, LANES), f32),
            pltpu.SMEM((devices, LANES), i32),
            pltpu.VMEM((devices, LANES), i32),
            dma((3,)),
        ],
        compiler_params=some,
        name="gains_and_near",
    )(
        turn,
        me,
        baseline_station_pairs.T,
        arrived,
        baseline_station_pairs,
        band_weights.T,
        band_offset.reshape(1, channels),
    )
    return pl.pallas_call(
        functools.partial(finish_kernel, capacity),
        out_shape=shape((owned, parts, channels), bf16),
        in_specs=[smem, smem, smem] + [vmem] * (3 + len(far)),
        out_specs=vmem,
        scratch_shapes=[
            pltpu.VMEM((chunks, owned, parts, LANES), f32),
            pltpu.VMEM((chunks, owned, parts, LANES), f32),
        ],
        compiler_params=some,
        name="sum_and_apply",
    )(turn, me, slots, sums, gains, recip, *far)


def solution(mesh):
    placed = (
        P(("groups", "bl"), None, None),
        P(("groups", "bl"), None),
        P(("groups", "bl")),
        P("bl", None),
        P(("groups", "bl"), None, None),
        P("groups", None),
        P("groups"),
    )
    return jax.shard_map(
        on_device,
        mesh=mesh,
        in_specs=placed,
        out_specs=P(("groups", "bl"), None, None),
        check_vma=False,
    )
```

time: 71.4 us -> 58 us (0.81)
  the two profiles are of different devices: /device:TPU:0 before, /device:TPU:19 now
where the time goes in v5:
time: 58 us; the launch traced here: 57.4 us
  waiting for transfers between devices  21.9 us (38%)
  starting transfers between devices  21.1 us (36%)
  Pallas kernels  13.5 us (23%)
  local copies, waits for them, and re-layouts  0.75 us (1%)
    ppermute x8, waiting for transfers between devices, on_device(): lax.ppermute(sent[i], 'bl', [(d, d ^ near + i) for d in range(devices)])  18.3 us
    ppermute x8, starting transfers between devices, on_device(): lax.ppermute(sent[i], 'bl', [(d, d ^ near + i) for d in range(devices)])  15.3 us
    all_to_all x1, starting transfers between devices, on_device(): lax.all_to_all(packed, 'bl', split_axis=0, concat_axis=0, axis_index_grou...  5.63 us
    pallas_call x1, Pallas kernels, on_device(): pl.pallas_call(functools.partial(prepare_kernel, capacity, near, stations...  4.38 us
    ppermute x1, waiting for transfers between devices, on_device(): partner = lax.ppermute(meta, 'bl', [(d, d ^ near) for d in range(devices)])  3.58 us
    pallas_call x1, Pallas kernels, on_device(): pl.pallas_call(functools.partial(pack_near_kernel, capacity), out_shape=s...  3.53 us
    pallas_call x1, Pallas kernels, on_device(): pl.pallas_call(functools.partial(finish_kernel, capacity), out_shape=shap...  2.89 us
    pallas_call x1, Pallas kernels, on_device(): pl.pallas_call(functools.partial(pack_kernel, capacity, near), out_shape=...  2.71 us
  transfers between devices with their start and end apart: 10, of which 6 were waited for; matrix products, arithmetic and copies ran while one was open for 0% of the time, Pallas kernels for 8%

profile of v5, /device:TPU:19, one launch (start us, length us, event | category | flops | bytes accessed | tf_op | source)
XLA Modules:
  0.0 57.4 jit_solution(8500210748864216575)
XLA Ops:
  0.0 2.7 %pack_rows.1 = (bf16[5,8,128]{2,1,0:T(8,128)(2,1)}, bf16[48,8,128]{2,1,0:T(8,128)(2,1)}, bf16[48,8,128]{2,1,0:T(8,128)(2,1)}, bf16[48,8,128]{2,1,0:T(8,128)(2,1)...) custom-call(s32[1]{0:T(128)} %bitcast.me_s, ...), custom_call_target="tpu_custom_call" | custom-call | tf_op jit(solution)/shard_map/pack_rows/pallas_call | solution.py:398
  2.7 0.0 copy-start.11
  2.8 0.0 copy-start.3
  2.8 0.1 collective-permute-start
  3.0 3.6 %collective-permute-done.partner_hbm = bf16[5,8,128]{2,1,0:T(8,128)(2,1)S(1)} collective-permute-done((bf16[5,8,128]{2,1,0:T(8,128)(2,1)}, bf16[5,8,128]{2,1,0:T(8,128)(2,1)S(1)}, u32[]{:S(2)}, u32[]{:S(2)}) %collective-permute-start) | collective-permute-done | bytes 10272 | tf_op jit(solution)/shard_map/ppermute | solution.py:428
  6.5 0.6 %copy-done.2 = bf16[5,8,128]{2,1,0:T(8,128)(2,1)} copy-done((bf16[5,8,128]{2,1,0:T(8,128)(2,1)}, bf16[5,8,128]{2,1,0:T(8,128)(2,1)S(1)}, u32[]{:S(2)}) %copy-start.2) | copy-done | bytes 10264
  7.1 3.5 %pack_near.1 = bf16[8,58,8,128]{3,2,1,0:T(8,128)(2,1)} custom-call(s32[1]{0:T(128)} %bitcast.me_s, s32[128]{0:T(128)} %bitcast.14, bf16[128,8,384]{2,1,0:T(8,128)(2,1)} %vis_hbm.3, bf16[5,8,128]{2,1,0:T(8,128)(2,1)} %get-tuple-element.18.meta_hbm, bf16[5,8,128]{2,1,0:T(8,128)(2,1)} %copy-done.2), custom_call_target="tpu_custom_call" | custom-call | tf_op jit(solution)/shard_map/pack_near/pallas_call | solution.py:433
  10.7 5.6 %all-to-all-start = ((bf16[8,58,8,128]{3,2,1,0:T(8,128)(2,1)}), bf16[8,58,8,128]{3,2,1,0:T(8,128)(2,1)S(1)}, u32[]{:S(2)}, u32[]{:S(2)}) async-start(bf16[8,58,8,128]{3,2,1,0:T(8,128)(2,1)} %pack_near.1), calls=%async_computation | async-start | bytes 1900544 | tf_op jit(solution)/shard_map/all_to_all | solution.py:450
  16.3 0.1 collective-permute-start.1
  16.4 2.5 %collective-permute-start.2 = (bf16[48,8,128]{2,1,0:T(8,128)(2,1)S(1)}, bf16[48,8,128]{2,1,0:T(8,128)(2,1)S(1)}, u32[]{:S(2)}, u32[]{:S(2)}) collective-permute-start(bf16[48,8,128]{2,1,0:T(8,128)(2,1)S(1)} %copy-done.10), channel_id=1, source_target_pairs={{0,9},{1,8},{2,11},{3,10},{4,13},{5,12},{6,15},{7,14},{8,1},{9,0},... | collective-permute-start | bytes 294920 | tf_op jit(solution)/shard_map/ppermute | solution.py:430
  18.9 1.5 %collective-permute-start.3 = (bf16[48,8,128]{2,1,0:T(8,128)(2,1)S(1)}, bf16[48,8,128]{2,1,0:T(8,128)(2,1)S(1)}, u32[]{:S(2)}, u32[]{:S(2)}) collective-permute-start(bf16[48,8,128]{2,1,0:T(8,128)(2,1)S(1)} %copy-done.9), channel_id=1, source_target_pairs={{0,10},{1,11},{2,8},{3,9},{4,14},{5,15},{6,12},{7,13},{8,2},{9,3},... | collective-permute-start | bytes 294920 | tf_op jit(solution)/shard_map/ppermute | solution.py:430
  20.4 2.1 %collective-permute-start.4 = (bf16[48,8,128]{2,1,0:T(8,128)(2,1)S(1)}, bf16[48,8,128]{2,1,0:T(8,128)(2,1)S(1)}, u32[]{:S(2)}, u32[]{:S(2)}) collective-permute-start(bf16[48,8,128]{2,1,0:T(8,128)(2,1)S(1)} %copy-done.8), channel_id=1, source_target_pairs={{0,11},{1,10},{2,9},{3,8},{4,15},{5,14},{6,13},{7,12},{8,3},{9,2},... | collective-permute-start | bytes 294920 | tf_op jit(solution)/shard_map/ppermute | solution.py:430
  22.5 0.6 collective-permute-start.5
  23.1 6.9 %collective-permute-done.1.rest_0_ = bf16[48,8,128]{2,1,0:T(8,128)(2,1)S(1)} collective-permute-done((bf16[48,8,128]{2,1,0:T(8,128)(2,1)S(1)}, bf16[48,8,128]{2,1,0:T(8,128)(2,1)S(1)}, u32[]{:S(2)}, u32[]{:S(2)}) %collective-permute-start.1) | collective-permute-done | bytes 98336 | tf_op jit(solution)/shard_map/ppermute | solution.py:430
  30.0 3.4 %collective-permute-start.6 = (bf16[48,8,128]{2,1,0:T(8,128)(2,1)S(1)}, bf16[48,8,128]{2,1,0:T(8,128)(2,1)S(1)}, u32[]{:S(2)}, u32[]{:S(2)}) collective-permute-start(bf16[48,8,128]{2,1,0:T(8,128)(2,1)S(1)} %copy-done.6), channel_id=1, source_target_pairs={{0,13},{1,12},{2,15},{3,14},{4,9},{5,8},{6,11},{7,10},{8,5},{9,4},... | collective-permute-start | bytes 294920 | tf_op jit(solution)/shard_map/ppermute | solution.py:430
  33.4 2.7 %collective-permute-start.7 = (bf16[48,8,128]{2,1,0:T(8,128)(2,1)S(1)}, bf16[48,8,128]{2,1,0:T(8,128)(2,1)S(1)}, u32[]{:S(2)}, u32[]{:S(2)}) collective-permute-start(bf16[48,8,128]{2,1,0:T(8,128)(2,1)S(1)} %copy-done.5), channel_id=1, source_target_pairs={{0,14},{1,15},{2,12},{3,13},{4,10},{5,11},{6,8},{7,9},{8,6},{9,7},... | collective-permute-start | bytes 294920 | tf_op jit(solution)/shard_map/ppermute | solution.py:430
  36.1 2.5 %collective-permute-start.8 = (bf16[48,8,128]{2,1,0:T(8,128)(2,1)S(1)}, bf16[48,8,128]{2,1,0:T(8,128)(2,1)S(1)}, u32[]{:S(2)}, u32[]{:S(2)}) collective-permute-start(bf16[48,8,128]{2,1,0:T(8,128)(2,1)S(1)} %copy-done.4), channel_id=1, source_target_pairs={{0,15},{1,14},{2,13},{3,12},{4,11},{5,10},{6,9},{7,8},{8,7},{9,6},... | collective-permute-start | bytes 294920 | tf_op jit(solution)/shard_map/ppermute | solution.py:430
  38.6 0.1 copy.8.pairs_ref
  38.7 4.4 %gains_and_near.1 = (f32[8,128,384]{2,1,0:T(8,128)S(1)}, f32[64,128]{1,0:T(8,128)S(1)}, s32[16,128]{1,0:T(8,128)S(1)}, f32[3,64,8,128]{3,2,1,0:T(8,128)S(1)}) custom-call(s32[1]{0:T(128)S(6)} %and.4.turn_s, s32[1]{0:T(128)} %bitcast.me_s, s32[2,64]{1,0:T(2,128)S(1)} %bitcast.10, bf16[8,58,8,128]{3,2,1,0:T(8,128)(2,1)S(1)} %all-to-all-done.arrived_hbm, ...), custom_call_target="tpu_custom_call" | custom-call | tf_op jit(solution)/shard_map/gains_and_near/pallas_call | solution.py:457
  43.1 4.1 %collective-permute-done.5.rest_4_ = bf16[48,8,128]{2,1,0:T(8,128)(2,1)S(1)} collective-permute-done((bf16[48,8,128]{2,1,0:T(8,128)(2,1)S(1)}, bf16[48,8,128]{2,1,0:T(8,128)(2,1)S(1)}, u32[]{:S(2)}, u32[]{:S(2)}) %collective-permute-start.5) | collective-permute-done | bytes 98336 | tf_op jit(solution)/shard_map/ppermute | solution.py:430
  47.2 2.6 %collective-permute-done.6.rest_5_ = bf16[48,8,128]{2,1,0:T(8,128)(2,1)S(1)} collective-permute-done((bf16[48,8,128]{2,1,0:T(8,128)(2,1)S(1)}, bf16[48,8,128]{2,1,0:T(8,128)(2,1)S(1)}, u32[]{:S(2)}, u32[]{:S(2)}) %collective-permute-start.6) | collective-permute-done | bytes 98336 | tf_op jit(solution)/shard_map/ppermute | solution.py:430
  49.8 2.1 %collective-permute-done.7.rest_6_ = bf16[48,8,128]{2,1,0:T(8,128)(2,1)S(1)} collective-permute-done((bf16[48,8,128]{2,1,0:T(8,128)(2,1)S(1)}, bf16[48,8,128]{2,1,0:T(8,128)(2,1)S(1)}, u32[]{:S(2)}, u32[]{:S(2)}) %collective-permute-start.7) | collective-permute-done | bytes 98336 | tf_op jit(solution)/shard_map/ppermute | solution.py:430
  51.9 2.6 %collective-permute-done.8.rest_7_ = bf16[48,8,128]{2,1,0:T(8,128)(2,1)S(1)} collective-permute-done((bf16[48,8,128]{2,1,0:T(8,128)(2,1)S(1)}, bf16[48,8,128]{2,1,0:T(8,128)(2,1)S(1)}, u32[]{:S(2)}, u32[]{:S(2)}) %collective-permute-start.8) | collective-permute-done | bytes 98336 | tf_op jit(solution)/shard_map/ppermute | solution.py:430
  54.5 2.9 %sum_and_apply.1 = bf16[64,8,384]{2,1,0:T(8,128)(2,1)} custom-call(s32[1]{0:T(128)S(6)} %and.4.turn_s, s32[1]{0:T(128)} %bitcast.me_s, s32[16,128]{1,0:T(8,128)S(1)} %get-tuple-element.19.slots_s, f32[3,64,8,128]{3,2,1,0:T(8,128)S(1)} %get-tuple-element.20.sums_ref, f32[8,128,384]{2,1,0:T(8,128)S(1)} %get-tuple-element.21.gains_ref, ...), custom_call_target="tpu_custom_call" | custom-call | tf_op jit(solution)/shard_map/sum_and_apply/pallas_call | solution.py:488
  (26 shorter events, 0.1 us)
Async XLA Ops:
  2.7 13.6 %copy-start.11 = (bf16[48,8,128]{2,1,0:T(8,128)(2,1)S(1)}, bf16[48,8,128]{2,1,0:T(8,128)(2,1)}, u32[]{:S(2)}) copy-start(bf16[48,8,128]{2,1,0:T(8,128)(2,1)} %get-tuple-element.23) | copy-start | bytes 294916
  2.7 13.6 %copy-start.10 = (bf16[48,8,128]{2,1,0:T(8,128)(2,1)S(1)}, bf16[48,8,128]{2,1,0:T(8,128)(2,1)}, u32[]{:S(2)}) copy-start(bf16[48,8,128]{2,1,0:T(8,128)(2,1)} %get-tuple-element.24) | copy-start | bytes 294916
  2.7 16.2 %copy-start.9 = (bf16[48,8,128]{2,1,0:T(8,128)(2,1)S(1)}, bf16[48,8,128]{2,1,0:T(8,128)(2,1)}, u32[]{:S(2)}) copy-start(bf16[48,8,128]{2,1,0:T(8,128)(2,1)} %get-tuple-element.25) | copy-start | bytes 294916
  2.8 17.6 %copy-start.8 = (bf16[48,8,128]{2,1,0:T(8,128)(2,1)S(1)}, bf16[48,8,128]{2,1,0:T(8,128)(2,1)}, u32[]{:S(2)}) copy-start(bf16[48,8,128]{2,1,0:T(8,128)(2,1)} %get-tuple-element.26) | copy-start | bytes 294916
  2.8 19.7 %copy-start.7 = (bf16[48,8,128]{2,1,0:T(8,128)(2,1)S(1)}, bf16[48,8,128]{2,1,0:T(8,128)(2,1)}, u32[]{:S(2)}) copy-start(bf16[48,8,128]{2,1,0:T(8,128)(2,1)} %get-tuple-element.27) | copy-start | bytes 294916
  2.8 27.2 %copy-start.6 = (bf16[48,8,128]{2,1,0:T(8,128)(2,1)S(1)}, bf16[48,8,128]{2,1,0:T(8,128)(2,1)}, u32[]{:S(2)}) copy-start(bf16[48,8,128]{2,1,0:T(8,128)(2,1)} %get-tuple-element.28) | copy-start | bytes 294916
  2.8 30.6 %copy-start.5 = (bf16[48,8,128]{2,1,0:T(8,128)(2,1)S(1)}, bf16[48,8,128]{2,1,0:T(8,128)(2,1)}, u32[]{:S(2)}) copy-start(bf16[48,8,128]{2,1,0:T(8,128)(2,1)} %get-tuple-element.29) | copy-start | bytes 294916
  2.8 33.3 %copy-start.4 = (bf16[48,8,128]{2,1,0:T(8,128)(2,1)S(1)}, bf16[48,8,128]{2,1,0:T(8,128)(2,1)}, u32[]{:S(2)}) copy-start(bf16[48,8,128]{2,1,0:T(8,128)(2,1)} %get-tuple-element.30) | copy-start | bytes 294916
  2.8 35.8 %copy-start.3 = (s32[384]{0:T(512)S(1)}, s32[384]{0:T(512)}, u32[]{:S(2)}) copy-start(s32[384]{0:T(512)} %param.13) | copy-start | bytes 4612
  2.8 35.8 %copy-start.1 = (s32[64,2]{0,1:T(2,128)S(1)}, s32[64,2]{0,1:T(2,128)}, u32[]{:S(2)}) copy-start(s32[64,2]{0,1:T(2,128)} %param.10) | copy-start | bytes 1540
  2.8 35.9 %copy-start = (f32[384,3]{0,1:T(4,128)S(1)}, f32[384,3]{0,1:T(4,128)}, u32[]{:S(2)}) copy-start(f32[384,3]{0,1:T(4,128)} %param.12) | copy-start | bytes 13828
  2.8 3.7 %collective-permute-start = (bf16[5,8,128]{2,1,0:T(8,128)(2,1)}, bf16[5,8,128]{2,1,0:T(8,128)(2,1)S(1)}, u32[]{:S(2)}, u32[]{:S(2)}) collective-permute-start(bf16[5,8,128]{2,1,0:T(8,128)(2,1)} %get-tuple-element.18.meta_hbm), channel_id=1, source_target_pairs={{0,8},{1,9},{2,10},{3,11},{4,12},{5,13},{6,14},{7,15},{8,0},{9,1},... | collective-permute-start | bytes 30728 | tf_op jit(solution)/shard_map/ppermute | solution.py:428
  6.5 0.6 %copy-start.2 = (bf16[5,8,128]{2,1,0:T(8,128)(2,1)}, bf16[5,8,128]{2,1,0:T(8,128)(2,1)S(1)}, u32[]{:S(2)}) copy-start(bf16[5,8,128]{2,1,0:T(8,128)(2,1)S(1)} %collective-permute-done.partner_hbm) | copy-start | bytes 30724
  10.7 28.0 %all-to-all-start = ((bf16[8,58,8,128]{3,2,1,0:T(8,128)(2,1)}), bf16[8,58,8,128]{3,2,1,0:T(8,128)(2,1)S(1)}, u32[]{:S(2)}, u32[]{:S(2)}) async-start(bf16[8,58,8,128]{3,2,1,0:T(8,128)(2,1)} %pack_near.1), calls=%async_computation | async-start | bytes 1900544 | tf_op jit(solution)/shard_map/all_to_all | solution.py:450
  16.3 13.7 %collective-permute-start.1 = (bf16[48,8,128]{2,1,0:T(8,128)(2,1)S(1)}, bf16[48,8,128]{2,1,0:T(8,128)(2,1)S(1)}, u32[]{:S(2)}, u32[]{:S(2)}) collective-permute-start(bf16[48,8,128]{2,1,0:T(8,128)(2,1)S(1)} %copy-done.11), channel_id=1, source_target_pairs={{0,8},{1,9},{2,10},{3,11},{4,12},{5,13},{6,14},{7,15},{8,0},{9,1},... | collective-permute-start | bytes 294920 | tf_op jit(solution)/shard_map/ppermute | solution.py:430
  16.4 17.0 %collective-permute-start.2 = (bf16[48,8,128]{2,1,0:T(8,128)(2,1)S(1)}, bf16[48,8,128]{2,1,0:T(8,128)(2,1)S(1)}, u32[]{:S(2)}, u32[]{:S(2)}) collective-permute-start(bf16[48,8,128]{2,1,0:T(8,128)(2,1)S(1)} %copy-done.10), channel_id=1, source_target_pairs={{0,9},{1,8},{2,11},{3,10},{4,13},{5,12},{6,15},{7,14},{8,1},{9,0},... | collective-permute-start | bytes 294920 | tf_op jit(solution)/shard_map/ppermute | solution.py:430
  18.9 17.2 %collective-permute-start.3 = (bf16[48,8,128]{2,1,0:T(8,128)(2,1)S(1)}, bf16[48,8,128]{2,1,0:T(8,128)(2,1)S(1)}, u32[]{:S(2)}, u32[]{:S(2)}) collective-permute-start(bf16[48,8,128]{2,1,0:T(8,128)(2,1)S(1)} %copy-done.9), channel_id=1, source_target_pairs={{0,10},{1,11},{2,8},{3,9},{4,14},{5,15},{6,12},{7,13},{8,2},{9,3},... | collective-permute-start | bytes 294920 | tf_op jit(solution)/shard_map/ppermute | solution.py:430
  20.4 22.7 %collective-permute-start.4 = (bf16[48,8,128]{2,1,0:T(8,128)(2,1)S(1)}, bf16[48,8,128]{2,1,0:T(8,128)(2,1)S(1)}, u32[]{:S(2)}, u32[]{:S(2)}) collective-permute-start(bf16[48,8,128]{2,1,0:T(8,128)(2,1)S(1)} %copy-done.8), channel_id=1, source_target_pairs={{0,11},{1,10},{2,9},{3,8},{4,15},{5,14},{6,13},{7,12},{8,3},{9,2},... | collective-permute-start | bytes 294920 | tf_op jit(solution)/shard_map/ppermute | solution.py:430
  22.5 24.6 %collective-permute-start.5 = (bf16[48,8,128]{2,1,0:T(8,128)(2,1)S(1)}, bf16[48,8,128]{2,1,0:T(8,128)(2,1)S(1)}, u32[]{:S(2)}, u32[]{:S(2)}) collective-permute-start(bf16[48,8,128]{2,1,0:T(8,128)(2,1)S(1)} %copy-done.7), channel_id=1, source_target_pairs={{0,12},{1,13},{2,14},{3,15},{4,8},{5,9},{6,10},{7,11},{8,4},{9,5},... | collective-permute-start | bytes 294920 | tf_op jit(solution)/shard_map/ppermute | solution.py:430
  30.0 19.7 %collective-permute-start.6 = (bf16[48,8,128]{2,1,0:T(8,128)(2,1)S(1)}, bf16[48,8,128]{2,1,0:T(8,128)(2,1)S(1)}, u32[]{:S(2)}, u32[]{:S(2)}) collective-permute-start(bf16[48,8,128]{2,1,0:T(8,128)(2,1)S(1)} %copy-done.6), channel_id=1, source_target_pairs={{0,13},{1,12},{2,15},{3,14},{4,9},{5,8},{6,11},{7,10},{8,5},{9,4},... | collective-permute-start | bytes 294920 | tf_op jit(solution)/shard_map/ppermute | solution.py:430
  33.4 18.5 %collective-permute-start.7 = (bf16[48,8,128]{2,1,0:T(8,128)(2,1)S(1)}, bf16[48,8,128]{2,1,0:T(8,128)(2,1)S(1)}, u32[]{:S(2)}, u32[]{:S(2)}) collective-permute-start(bf16[48,8,128]{2,1,0:T(8,128)(2,1)S(1)} %copy-done.5), channel_id=1, source_target_pairs={{0,14},{1,15},{2,12},{3,13},{4,10},{5,11},{6,8},{7,9},{8,6},{9,7},... | collective-permute-start | bytes 294920 | tf_op jit(solution)/shard_map/ppermute | solution.py:430
  36.1 18.3 %collective-permute-start.8 = (bf16[48,8,128]{2,1,0:T(8,128)(2,1)S(1)}, bf16[48,8,128]{2,1,0:T(8,128)(2,1)S(1)}, u32[]{:S(2)}, u32[]{:S(2)}) collective-permute-start(bf16[48,8,128]{2,1,0:T(8,128)(2,1)S(1)} %copy-done.4), channel_id=1, source_target_pairs={{0,15},{1,14},{2,13},{3,12},{4,11},{5,10},{6,9},{7,8},{8,7},{9,6},... | collective-permute-start | bytes 294920 | tf_op jit(solution)/shard_map/ppermute | solution.py:430

commit v6 on v5

--- a/solution.py
+++ b/solution.py
@@ -34,7 +34,6 @@
     slot_row_hbm,
     vis_hbm,
     coarse_hbm,
-    meta_hbm,
     *rest,
 ):
     outs = rest[:-10]
@@ -55,7 +54,8 @@
     devices = block_ref.shape[0]
     terms, stations = coarse_ref.shape
     half = stations // 2
-    gain_tiles = (meta_ref.shape[0] - 1) // 2
+    depth = meta_ref.shape[0]
+    gain_tiles = (depth - 1) // 2
     moves = start_all(
         (
             (vis_hbm, vis_ref),
@@ -84,11 +84,20 @@
     sub = lax.broadcasted_iota(jnp.int32, (SUB, LANES), 0)
     codes = jnp.where(sub == 0, owner_ref[...], slot_ref[...])
     meta_ref[2 * gain_tiles] = codes.astype(jnp.float32).astype(jnp.bfloat16)
-    sends = start_all([(meta_ref, meta_hbm)], sems.at[pl.ds(1, 1)])
+    at = chunks * capacity
+    if near > 1:
+        pairs = [(meta_ref, outs[0].at[pl.ds(at, depth)])]
+        pairs += [(meta_ref, outs[near].at[d, pl.ds(at, depth)]) for d in range(near)]
+    else:
+        pairs = [(meta_ref, outs[1])]
+    sends = start_all(pairs, sems.at[pl.ds(1, len(pairs))])
     moves[0].wait()
 
     def place(r, carry):
-        x = owner_s[r] ^ me
+        d = owner_s[r]
+        x = d ^ me
+        if near > 1:
+            x = jnp.where(x < near, d & (near - 1), x)
         k = count_s[x]
         count_s[x] = k + 1
         for c in range(chunks):
@@ -96,68 +105,28 @@
         return carry
 
     lax.fori_loop(0, rows, place, 0, unroll=8)
+    start = 1 + len(pairs)
     if near > 1:
-        pairs = [(block_ref.at[near + i], outs[i]) for i in range(near)]
+        pairs = [(block_ref.at[near + i], outs[i].at[pl.ds(0, at)]) for i in range(near)]
+        pairs += [(block_ref.at[pl.ds(0, near)], outs[near].at[:, pl.ds(0, at)])]
     else:
         pairs = [(block_ref, outs[0])]
-    sends += start_all(pairs, sems.at[pl.ds(2, len(pairs))])
+    sends += start_all(pairs, sems.at[pl.ds(start, len(pairs))])
     for send in sends:
         send.wait()
 
 
-def pack_near_kernel(
-    capacity,
-    me_s,
-    owner_hbm,
-    vis_hbm,
-    meta_hbm,
-    partner_hbm,
-    out_ref,
-    owner_s,
-    count_s,
-    vis_ref,
-    meta_ref,
-    partner_ref,
-    sems,
-):
-    rows = vis_ref.shape[0]
-    chunks = vis_ref.shape[2] // LANES
-    near = out_ref.shape[0]
-    depth = meta_ref.shape[0]
-    at = capacity * chunks
+def add_partner_kernel(at, depth, first_hbm, _, out_hbm, sems):
+    near = out_hbm.shape[0]
     moves = start_all(
-        (
-            (vis_hbm, vis_ref),
-            (owner_hbm, owner_s),
-            (meta_hbm, meta_ref),
-            (partner_hbm, partner_ref),
-        ),
+        [
+            (first_hbm.at[pl.ds(at, depth)], out_hbm.at[d, pl.ds(at + depth, depth)])
+            for d in range(near)
+        ],
         sems,
     )
-    for d in range(near):
-        count_s[d] = 0
-    half = me_s[0] & near
-    for move in moves[1:]:
+    for move in moves:
         move.wait()
-    for d in range(near):
-        for i in range(depth):
-            out_ref[d, at + i] = meta_ref[i]
-            out_ref[d, at + depth + i] = partner_ref[i]
-    moves[0].wait()
-
-    def place(r, carry):
-        x = owner_s[r] ^ half
-
-        @pl.when(x < near)
-        def _():
-            k = count_s[x]
-            count_s[x] = k + 1
-            for c in range(chunks):
-                out_ref[x, chunks * k + c] = vis_ref[r, :, c * LANES : (c + 1) * LANES]
-
-        return carry
-
-    lax.fori_loop(0, rows, place, 0, unroll=4)
 
 
 def list_rows(owner, slot, target, capacity):
@@ -395,12 +364,18 @@
     owner = row_owner.reshape(rows)
     coarse = gains_coarse.transpose(2, 1, 0).reshape(knots * parts, stations)
     block = (chunks * capacity, parts, LANES)
-    meta, *sent = pl.pallas_call(
+    rows_at = chunks * capacity
+    if halves:
+        outs = [shape((rows_at + depth, parts, LANES), bf16)]
+        outs += [shape(block, bf16)] * (near - 1)
+        outs += [shape((near, rows_at + 2 * depth, parts, LANES), bf16)]
+    else:
+        outs = [shape((devices,) + block, bf16), shape((depth, SUB, LANES), bf16)]
+    *sent, last = pl.pallas_call(
         functools.partial(pack_kernel, capacity, near),
-        out_shape=[shape((depth, SUB, LANES), bf16)]
-        + [shape(block if halves else (devices,) + block, bf16)] * near,
+        out_shape=outs,
         in_specs=[smem] + [hbm] * 5,
-        out_specs=[hbm] * (1 + near),
+        out_specs=[hbm] * len(outs),
         scratch_shapes=[
             pltpu.SMEM((rows,), i32),
             pltpu.SMEM((devices,), i32),
@@ -411,7 +386,7 @@
             pltpu.VMEM((LANES, LANES), f32),
             pltpu.VMEM((depth, SUB, LANES), bf16),
             pltpu.VMEM((devices,) + block, bf16),
-            dma((5 + near,)),
+            dma((5 + 2 * near + 2,)),
         ],
         compiler_params=most,
         name="pack_rows",
@@ -425,34 +400,27 @@
     )
 
     if halves:
-        partner = lax.ppermute(meta, "bl", [(d, d ^ near) for d in range(devices)])
         far = [
             lax.ppermute(sent[i], "bl", [(d, d ^ (near + i)) for d in range(devices)])
             for i in range(near)
         ]
         packed = pl.pallas_call(
-            functools.partial(pack_near_kernel, capacity),
-            out_shape=shape((near, chunks * capacity + 2 * depth, parts, LANES), bf16),
-            in_specs=[smem] + [hbm] * 4,
-            out_specs=vmem,
-            scratch_shapes=[
-                pltpu.SMEM((rows,), i32),
-                pltpu.SMEM((near,), i32),
-                pltpu.VMEM((rows, parts, channels), bf16),
-                pltpu.VMEM((depth, SUB, LANES), bf16),
-                pltpu.VMEM((depth, SUB, LANES), bf16),
-                dma((4,)),
-            ],
-            compiler_params=most,
-            name="pack_near",
-        )(me, owner, visibilities, meta, partner)
+            functools.partial(add_partner_kernel, rows_at, depth),
+            out_shape=shape(last.shape, last.dtype),
+            in_specs=[anywhere, hbm],
+            out_specs=hbm,
+            scratch_shapes=[dma((near,))],
+            input_output_aliases={1: 0},
+            compiler_params=some,
+            name="add_partner",
+        )(far[0], last)
         groups = [list(range(0, near)), list(range(near, devices))]
         arrived = lax.all_to_all(
             packed, "bl", split_axis=0, concat_axis=0, axis_index_groups=groups, tiled=True
         )
     else:
         far = [lax.all_to_all(sent[0], "bl", split_axis=0, concat_axis=0, tiled=True)]
-        arrived = lax.all_gather(meta, "bl", axis=0)
+        arrived = lax.all_gather(last, "bl", axis=0)
 
     gains, recip, slots, sums = pl.pallas_call(
         functools.partial(prepare_kernel, capacity, near, stations),

time: 58 us -> 55.6 us (0.959)
  the two profiles are of different devices: /device:TPU:19 before, /device:TPU:17 now
where the time goes in v6:
time: 55.6 us; the launch traced here: 54.9 us
  waiting for transfers between devices  22.2 us (40%)
  starting transfers between devices  20.6 us (37%)
  Pallas kernels  9.63 us (17%)
  local copies, waits for them, and re-layouts  2.28 us (4%)
    ppermute x8, waiting for transfers between devices, on_device(): lax.ppermute(sent[i], 'bl', [(d, d ^ near + i) for d in range(devices)])  22.2 us
    ppermute x8, starting transfers between devices, on_device(): lax.ppermute(sent[i], 'bl', [(d, d ^ near + i) for d in range(devices)])  13.1 us
    all_to_all x1, starting transfers between devices, on_device(): lax.all_to_all(packed, 'bl', split_axis=0, concat_axis=0, axis_index_grou...  7.56 us
    pallas_call x1, Pallas kernels, on_device(): pl.pallas_call(functools.partial(prepare_kernel, capacity, near, stations...  3.89 us
    pallas_call x1, Pallas kernels, on_device(): pl.pallas_call(functools.partial(pack_kernel, capacity, near), out_shape=...  3.15 us
    pallas_call x1, Pallas kernels, on_device(): pl.pallas_call(functools.partial(finish_kernel, capacity), out_shape=shap...  2.41 us
    unnamed x25, local copies, waits for them, and re-layouts  2.28 us
  transfers between devices with their start and end apart: 9, of which 6 were waited for; matrix products, arithmetic and copies ran while one was open for 0% of the time, Pallas kernels for 7%

profile of v6, /device:TPU:17, one launch (start us, length us, event | category | flops | bytes accessed | tf_op | source)
XLA Modules:
  0.0 54.9 jit_solution(5687133199607821582)
XLA Ops:
  0.0 3.2 %pack_rows.1 = (bf16[53,8,128]{2,1,0:T(8,128)(2,1)}, bf16[48,8,128]{2,1,0:T(8,128)(2,1)}, bf16[48,8,128]{2,1,0:T(8,128)(2,1)}, bf16[48,8,128]{2,1,0:T(8,128)(2,1...) custom-call(s32[1]{0:T(128)} %bitcast.me_s, ...), custom_call_target="tpu_custom_call" | custom-call | tf_op jit(solution)/shard_map/pack_rows/pallas_call | solution.py:374
  3.2 0.1 collective-permute-start
  3.2 5.0 %collective-permute-done.first_hbm.rest_0_ = bf16[53,8,128]{2,1,0:T(8,128)(2,1)S(1)} collective-permute-done((bf16[53,8,128]{2,1,0:T(8,128)(2,1)}, bf16[53,8,128]{2,1,0:T(8,128)(2,1)S(1)}, u32[]{:S(2)}, u32[]{:S(2)}) %collective-permute-start) | collective-permute-done | bytes 108576 | tf_op jit(solution)/shard_map/ppermute | solution.py:404
  8.2 1.2 %copy-done = bf16[8,58,8,128]{3,2,1,0:T(8,128)(2,1)S(1)} copy-done((bf16[8,58,8,128]{3,2,1,0:T(8,128)(2,1)S(1)}, bf16[8,58,8,128]{3,2,1,0:T(8,128)(2,1)}, u32[]{:S(2)}) %copy-start) | copy-done | bytes 950296
  9.5 0.0 copy-start.4
  9.5 0.0 copy-start.3
  9.5 0.0 copy-start.2
  9.5 0.2 add_partner.1
  9.7 0.9 %copy-done.1 = bf16[8,58,8,128]{3,2,1,0:T(8,128)(2,1)} copy-done((bf16[8,58,8,128]{3,2,1,0:T(8,128)(2,1)}, bf16[8,58,8,128]{3,2,1,0:T(8,128)(2,1)S(1)}, u32[]{:S(2)}) %copy-start.1) | copy-done | bytes 950296
  10.6 7.6 %all-to-all-start = ((bf16[8,58,8,128]{3,2,1,0:T(8,128)(2,1)}), bf16[8,58,8,128]{3,2,1,0:T(8,128)(2,1)S(1)}, u32[]{:S(2)}, u32[]{:S(2)}) async-start(bf16[8,58,8,128]{3,2,1,0:T(8,128)(2,1)} %copy-done.1), calls=%async_computation | async-start | bytes 1900544 | tf_op jit(solution)/shard_map/all_to_all | solution.py:418
  18.2 3.7 %collective-permute-start.2 = (bf16[48,8,128]{2,1,0:T(8,128)(2,1)S(1)}, bf16[48,8,128]{2,1,0:T(8,128)(2,1)S(1)}, u32[]{:S(2)}, u32[]{:S(2)}) collective-permute-start(bf16[48,8,128]{2,1,0:T(8,128)(2,1)S(1)} %copy-done.10), channel_id=1, source_target_pairs={{0,10},{1,11},{2,8},{3,9},{4,14},{5,15},{6,12},{7,13},{8,2},{9,3},... | collective-permute-start | bytes 294920 | tf_op jit(solution)/shard_map/ppermute | solution.py:404
  21.9 0.1 collective-permute-start.3
  22.0 2.6 %collective-permute-start.4 = (bf16[48,8,128]{2,1,0:T(8,128)(2,1)S(1)}, bf16[48,8,128]{2,1,0:T(8,128)(2,1)S(1)}, u32[]{:S(2)}, u32[]{:S(2)}) collective-permute-start(bf16[48,8,128]{2,1,0:T(8,128)(2,1)S(1)} %copy-done.8), channel_id=1, source_target_pairs={{0,12},{1,13},{2,14},{3,15},{4,8},{5,9},{6,10},{7,11},{8,4},{9,5},... | collective-permute-start | bytes 294920 | tf_op jit(solution)/shard_map/ppermute | solution.py:404
  24.6 0.0 collective-permute-start.5
  24.7 7.1 %collective-permute-done.1.rest_1_ = bf16[48,8,128]{2,1,0:T(8,128)(2,1)S(1)} collective-permute-done((bf16[48,8,128]{2,1,0:T(8,128)(2,1)S(1)}, bf16[48,8,128]{2,1,0:T(8,128)(2,1)S(1)}, u32[]{:S(2)}, u32[]{:S(2)}) %collective-permute-start.1) | collective-permute-done | bytes 98336 | tf_op jit(solution)/shard_map/ppermute | solution.py:404
  31.8 3.8 %collective-permute-start.6 = (bf16[48,8,128]{2,1,0:T(8,128)(2,1)S(1)}, bf16[48,8,128]{2,1,0:T(8,128)(2,1)S(1)}, u32[]{:S(2)}, u32[]{:S(2)}) collective-permute-start(bf16[48,8,128]{2,1,0:T(8,128)(2,1)S(1)} %copy-done.6), channel_id=1, source_target_pairs={{0,14},{1,15},{2,12},{3,13},{4,10},{5,11},{6,8},{7,9},{8,6},{9,7},... | collective-permute-start | bytes 294920 | tf_op jit(solution)/shard_map/ppermute | solution.py:404
  35.6 2.8 %collective-permute-start.7 = (bf16[48,8,128]{2,1,0:T(8,128)(2,1)S(1)}, bf16[48,8,128]{2,1,0:T(8,128)(2,1)S(1)}, u32[]{:S(2)}, u32[]{:S(2)}) collective-permute-start(bf16[48,8,128]{2,1,0:T(8,128)(2,1)S(1)} %copy-done.5), channel_id=1, source_target_pairs={{0,15},{1,14},{2,13},{3,12},{4,11},{5,10},{6,9},{7,8},{8,7},{9,6},... | collective-permute-start | bytes 294920 | tf_op jit(solution)/shard_map/ppermute | solution.py:404
  38.4 0.1 copy.9.pairs_ref
  38.5 3.9 %gains_and_near.1 = (f32[8,128,384]{2,1,0:T(8,128)S(1)}, f32[64,128]{1,0:T(8,128)S(1)}, s32[16,128]{1,0:T(8,128)S(1)}, f32[3,64,8,128]{3,2,1,0:T(8,128)S(1)}) custom-call(s32[1]{0:T(128)S(6)} %and.4.turn_s, s32[1]{0:T(128)} %bitcast.me_s, s32[2,64]{1,0:T(2,128)S(1)} %bitcast.10, bf16[8,58,8,128]{3,2,1,0:T(8,128)(2,1)S(1)} %all-to-all-done.arrived_hbm, ...), custom_call_target="tpu_custom_call" | custom-call | tf_op jit(solution)/shard_map/gains_and_near/pallas_call | solution.py:425
  42.4 2.8 %collective-permute-done.4.rest_4_ = bf16[48,8,128]{2,1,0:T(8,128)(2,1)S(1)} collective-permute-done((bf16[48,8,128]{2,1,0:T(8,128)(2,1)S(1)}, bf16[48,8,128]{2,1,0:T(8,128)(2,1)S(1)}, u32[]{:S(2)}, u32[]{:S(2)}) %collective-permute-start.4) | collective-permute-done | bytes 98336 | tf_op jit(solution)/shard_map/ppermute | solution.py:404
  45.2 2.5 %collective-permute-done.5.rest_5_ = bf16[48,8,128]{2,1,0:T(8,128)(2,1)S(1)} collective-permute-done((bf16[48,8,128]{2,1,0:T(8,128)(2,1)S(1)}, bf16[48,8,128]{2,1,0:T(8,128)(2,1)S(1)}, u32[]{:S(2)}, u32[]{:S(2)}) %collective-permute-start.5) | collective-permute-done | bytes 98336 | tf_op jit(solution)/shard_map/ppermute | solution.py:404
  47.7 2.6 %collective-permute-done.6.rest_6_ = bf16[48,8,128]{2,1,0:T(8,128)(2,1)S(1)} collective-permute-done((bf16[48,8,128]{2,1,0:T(8,128)(2,1)S(1)}, bf16[48,8,128]{2,1,0:T(8,128)(2,1)S(1)}, u32[]{:S(2)}, u32[]{:S(2)}) %collective-permute-start.6) | collective-permute-done | bytes 98336 | tf_op jit(solution)/shard_map/ppermute | solution.py:404
  50.3 2.1 %collective-permute-done.7.rest_7_ = bf16[48,8,128]{2,1,0:T(8,128)(2,1)S(1)} collective-permute-done((bf16[48,8,128]{2,1,0:T(8,128)(2,1)S(1)}, bf16[48,8,128]{2,1,0:T(8,128)(2,1)S(1)}, u32[]{:S(2)}, u32[]{:S(2)}) %collective-permute-start.7) | collective-permute-done | bytes 98336 | tf_op jit(solution)/shard_map/ppermute | solution.py:404
  52.4 2.4 %sum_and_apply.1 = bf16[64,8,384]{2,1,0:T(8,128)(2,1)} custom-call(s32[1]{0:T(128)S(6)} %and.4.turn_s, s32[1]{0:T(128)} %bitcast.me_s, s32[16,128]{1,0:T(8,128)S(1)} %get-tuple-element.20.slots_s, f32[3,64,8,128]{3,2,1,0:T(8,128)S(1)} %get-tuple-element.21.sums_ref, f32[8,128,384]{2,1,0:T(8,128)S(1)} %get-tuple-element.22.gains_ref, ...), custom_call_target="tpu_custom_call" | custom-call | tf_op jit(solution)/shard_map/sum_and_apply/pallas_call | solution.py:456
  (24 shorter events, 0.1 us)
Async XLA Ops:
  3.2 5.1 %collective-permute-start = (bf16[53,8,128]{2,1,0:T(8,128)(2,1)}, bf16[53,8,128]{2,1,0:T(8,128)(2,1)S(1)}, u32[]{:S(2)}, u32[]{:S(2)}) collective-permute-start(bf16[53,8,128]{2,1,0:T(8,128)(2,1)} %get-tuple-element.18), channel_id=1, source_target_pairs={{0,8},{1,9},{2,10},{3,11},{4,12},{5,13},{6,14},{7,15},{8,0},{9,1},... | collective-permute-start | bytes 325640 | tf_op jit(solution)/shard_map/ppermute | solution.py:404
  8.2 1.2 %copy-start = (bf16[8,58,8,128]{3,2,1,0:T(8,128)(2,1)S(1)}, bf16[8,58,8,128]{3,2,1,0:T(8,128)(2,1)}, u32[]{:S(2)}) copy-start(bf16[8,58,8,128]{3,2,1,0:T(8,128)(2,1)} %get-tuple-element.19._) | copy-start | bytes 2850820
  9.4 8.8 %copy-start.11 = (bf16[48,8,128]{2,1,0:T(8,128)(2,1)S(1)}, bf16[48,8,128]{2,1,0:T(8,128)(2,1)}, u32[]{:S(2)}) copy-start(bf16[48,8,128]{2,1,0:T(8,128)(2,1)} %get-tuple-element.24) | copy-start | bytes 294916
  9.4 8.8 %copy-start.10 = (bf16[48,8,128]{2,1,0:T(8,128)(2,1)S(1)}, bf16[48,8,128]{2,1,0:T(8,128)(2,1)}, u32[]{:S(2)}) copy-start(bf16[48,8,128]{2,1,0:T(8,128)(2,1)} %get-tuple-element.25) | copy-start | bytes 294916
  9.4 12.5 %copy-start.9 = (bf16[48,8,128]{2,1,0:T(8,128)(2,1)S(1)}, bf16[48,8,128]{2,1,0:T(8,128)(2,1)}, u32[]{:S(2)}) copy-start(bf16[48,8,128]{2,1,0:T(8,128)(2,1)} %get-tuple-element.26) | copy-start | bytes 294916
  9.4 12.6 %copy-start.8 = (bf16[48,8,128]{2,1,0:T(8,128)(2,1)S(1)}, bf16[48,8,128]{2,1,0:T(8,128)(2,1)}, u32[]{:S(2)}) copy-start(bf16[48,8,128]{2,1,0:T(8,128)(2,1)} %get-tuple-element.27) | copy-start | bytes 294916
  9.4 15.2 %copy-start.7 = (bf16[48,8,128]{2,1,0:T(8,128)(2,1)S(1)}, bf16[48,8,128]{2,1,0:T(8,128)(2,1)}, u32[]{:S(2)}) copy-start(bf16[48,8,128]{2,1,0:T(8,128)(2,1)} %get-tuple-element.28) | copy-start | bytes 294916
  9.4 22.4 %copy-start.6 = (bf16[48,8,128]{2,1,0:T(8,128)(2,1)S(1)}, bf16[48,8,128]{2,1,0:T(8,128)(2,1)}, u32[]{:S(2)}) copy-start(bf16[48,8,128]{2,1,0:T(8,128)(2,1)} %get-tuple-element.29) | copy-start | bytes 294916
  9.4 26.1 %copy-start.5 = (bf16[48,8,128]{2,1,0:T(8,128)(2,1)S(1)}, bf16[48,8,128]{2,1,0:T(8,128)(2,1)}, u32[]{:S(2)}) copy-start(bf16[48,8,128]{2,1,0:T(8,128)(2,1)} %get-tuple-element.30) | copy-start | bytes 294916
  9.5 28.9 %copy-start.4 = (s32[384]{0:T(512)S(1)}, s32[384]{0:T(512)}, u32[]{:S(2)}) copy-start(s32[384]{0:T(512)} %param.13) | copy-start | bytes 4612
  9.5 28.9 %copy-start.3 = (s32[64,2]{0,1:T(2,128)S(1)}, s32[64,2]{0,1:T(2,128)}, u32[]{:S(2)}) copy-start(s32[64,2]{0,1:T(2,128)} %param.10) | copy-start | bytes 1540
  9.5 29.0 %copy-start.2 = (f32[384,3]{0,1:T(4,128)S(1)}, f32[384,3]{0,1:T(4,128)}, u32[]{:S(2)}) copy-start(f32[384,3]{0,1:T(4,128)} %param.12) | copy-start | bytes 13828
  9.7 1.0 %copy-start.1 = (bf16[8,58,8,128]{3,2,1,0:T(8,128)(2,1)}, bf16[8,58,8,128]{3,2,1,0:T(8,128)(2,1)S(1)}, u32[]{:S(2)}) copy-start(bf16[8,58,8,128]{3,2,1,0:T(8,128)(2,1)S(1)} %add_partner.1) | copy-start | bytes 2850820
  10.6 27.8 %all-to-all-start = ((bf16[8,58,8,128]{3,2,1,0:T(8,128)(2,1)}), bf16[8,58,8,128]{3,2,1,0:T(8,128)(2,1)S(1)}, u32[]{:S(2)}, u32[]{:S(2)}) async-start(bf16[8,58,8,128]{3,2,1,0:T(8,128)(2,1)} %copy-done.1), calls=%async_computation | async-start | bytes 1900544 | tf_op jit(solution)/shard_map/all_to_all | solution.py:418
  18.2 13.6 %collective-permute-start.1 = (bf16[48,8,128]{2,1,0:T(8,128)(2,1)S(1)}, bf16[48,8,128]{2,1,0:T(8,128)(2,1)S(1)}, u32[]{:S(2)}, u32[]{:S(2)}) collective-permute-start(bf16[48,8,128]{2,1,0:T(8,128)(2,1)S(1)} %copy-done.11), channel_id=1, source_target_pairs={{0,9},{1,8},{2,11},{3,10},{4,13},{5,12},{6,15},{7,14},{8,1},{9,0},... | collective-permute-start | bytes 294920 | tf_op jit(solution)/shard_map/ppermute | solution.py:404
  18.2 17.4 %collective-permute-start.2 = (bf16[48,8,128]{2,1,0:T(8,128)(2,1)S(1)}, bf16[48,8,128]{2,1,0:T(8,128)(2,1)S(1)}, u32[]{:S(2)}, u32[]{:S(2)}) collective-permute-start(bf16[48,8,128]{2,1,0:T(8,128)(2,1)S(1)} %copy-done.10), channel_id=1, source_target_pairs={{0,10},{1,11},{2,8},{3,9},{4,14},{5,15},{6,12},{7,13},{8,2},{9,3},... | collective-permute-start | bytes 294920 | tf_op jit(solution)/shard_map/ppermute | solution.py:404
  21.9 20.5 %collective-permute-start.3 = (bf16[48,8,128]{2,1,0:T(8,128)(2,1)S(1)}, bf16[48,8,128]{2,1,0:T(8,128)(2,1)S(1)}, u32[]{:S(2)}, u32[]{:S(2)}) collective-permute-start(bf16[48,8,128]{2,1,0:T(8,128)(2,1)S(1)} %copy-done.9), channel_id=1, source_target_pairs={{0,11},{1,10},{2,9},{3,8},{4,15},{5,14},{6,13},{7,12},{8,3},{9,2},... | collective-permute-start | bytes 294920 | tf_op jit(solution)/shard_map/ppermute | solution.py:404
  22.0 23.2 %collective-permute-start.4 = (bf16[48,8,128]{2,1,0:T(8,128)(2,1)S(1)}, bf16[48,8,128]{2,1,0:T(8,128)(2,1)S(1)}, u32[]{:S(2)}, u32[]{:S(2)}) collective-permute-start(bf16[48,8,128]{2,1,0:T(8,128)(2,1)S(1)} %copy-done.8), channel_id=1, source_target_pairs={{0,12},{1,13},{2,14},{3,15},{4,8},{5,9},{6,10},{7,11},{8,4},{9,5},... | collective-permute-start | bytes 294920 | tf_op jit(solution)/shard_map/ppermute | solution.py:404
  24.6 23.0 %collective-permute-start.5 = (bf16[48,8,128]{2,1,0:T(8,128)(2,1)S(1)}, bf16[48,8,128]{2,1,0:T(8,128)(2,1)S(1)}, u32[]{:S(2)}, u32[]{:S(2)}) collective-permute-start(bf16[48,8,128]{2,1,0:T(8,128)(2,1)S(1)} %copy-done.7), channel_id=1, source_target_pairs={{0,13},{1,12},{2,15},{3,14},{4,9},{5,8},{6,11},{7,10},{8,5},{9,4},... | collective-permute-start | bytes 294920 | tf_op jit(solution)/shard_map/ppermute | solution.py:404
  31.8 18.5 %collective-permute-start.6 = (bf16[48,8,128]{2,1,0:T(8,128)(2,1)S(1)}, bf16[48,8,128]{2,1,0:T(8,128)(2,1)S(1)}, u32[]{:S(2)}, u32[]{:S(2)}) collective-permute-start(bf16[48,8,128]{2,1,0:T(8,128)(2,1)S(1)} %copy-done.6), channel_id=1, source_target_pairs={{0,14},{1,15},{2,12},{3,13},{4,10},{5,11},{6,8},{7,9},{8,6},{9,7},... | collective-permute-start | bytes 294920 | tf_op jit(solution)/shard_map/ppermute | solution.py:404
  35.6 16.9 %collective-permute-start.7 = (bf16[48,8,128]{2,1,0:T(8,128)(2,1)S(1)}, bf16[48,8,128]{2,1,0:T(8,128)(2,1)S(1)}, u32[]{:S(2)}, u32[]{:S(2)}) collective-permute-start(bf16[48,8,128]{2,1,0:T(8,128)(2,1)S(1)} %copy-done.5), channel_id=1, source_target_pairs={{0,15},{1,14},{2,13},{3,12},{4,11},{5,10},{6,9},{7,8},{8,7},{9,6},... | collective-permute-start | bytes 294920 | tf_op jit(solution)/shard_map/ppermute | solution.py:404

commit v7 on v6

--- a/solution.py
+++ b/solution.py
@@ -86,18 +86,14 @@
     meta_ref[2 * gain_tiles] = codes.astype(jnp.float32).astype(jnp.bfloat16)
     at = chunks * capacity
     if near > 1:
-        pairs = [(meta_ref, outs[0].at[pl.ds(at, depth)])]
-        pairs += [(meta_ref, outs[near].at[d, pl.ds(at, depth)]) for d in range(near)]
+        pairs = [(meta_ref, outs[x].at[pl.ds(at, depth)]) for x in range(near + 1)]
     else:
         pairs = [(meta_ref, outs[1])]
     sends = start_all(pairs, sems.at[pl.ds(1, len(pairs))])
     moves[0].wait()
 
     def place(r, carry):
-        d = owner_s[r]
-        x = d ^ me
-        if near > 1:
-            x = jnp.where(x < near, d & (near - 1), x)
+        x = owner_s[r] ^ me
         k = count_s[x]
         count_s[x] = k + 1
         for c in range(chunks):
@@ -107,8 +103,7 @@
     lax.fori_loop(0, rows, place, 0, unroll=8)
     start = 1 + len(pairs)
     if near > 1:
-        pairs = [(block_ref.at[near + i], outs[i].at[pl.ds(0, at)]) for i in range(near)]
-        pairs += [(block_ref.at[pl.ds(0, near)], outs[near].at[:, pl.ds(0, at)])]
+        pairs = [(block_ref.at[x], outs[x].at[pl.ds(0, at)]) for x in range(devices)]
     else:
         pairs = [(block_ref, outs[0])]
     sends += start_all(pairs, sems.at[pl.ds(start, len(pairs))])
@@ -116,14 +111,11 @@
         send.wait()
 
 
-def add_partner_kernel(at, depth, first_hbm, _, out_hbm, sems):
-    near = out_hbm.shape[0]
+def add_partner_kernel(at, depth, first_hbm, *rest):
+    sems = rest[-1]
+    outs = rest[len(rest) // 2 : -1]
     moves = start_all(
-        [
-            (first_hbm.at[pl.ds(at, depth)], out_hbm.at[d, pl.ds(at + depth, depth)])
-            for d in range(near)
-        ],
-        sems,
+        [(first_hbm.at[pl.ds(at, depth)], out.at[pl.ds(at + depth, depth)]) for out in outs], sems
     )
     for move in moves:
         move.wait()
@@ -167,45 +159,36 @@
     capacity,
     near,
     stations,
+    order,
     turn_s,
     me_s,
     pairs_s,
-    arrived_hbm,
     pairs_ref,
     weights_ref,
     offset_ref,
-    gains_ref,
-    recip_ref,
-    slots_ref,
-    sums_ref,
-    metas_ref,
-    table_ref,
-    pick_ref,
-    rows_ref,
-    codes_ref,
-    slots_s,
-    slots_v,
-    sems,
+    *rest,
 ):
+    arrived = dict(zip(order, rest[:-12]))
+    gains_ref, recip_ref, slots_ref, sums_ref = rest[-12:-8]
+    metas_ref, table_ref, pick_ref, rows_ref, codes_ref, slots_s, slots_v, sems = rest[-8:]
     devices, depth, _, _ = metas_ref.shape
     owned = recip_ref.shape[0]
     channels = weights_ref.shape[1]
     half = stations // 2
     gain_tiles = (depth - 1) // 2
     chunks = channels // LANES
+    at = capacity * chunks
     if near == 1:
-        moves = start_all([(arrived_hbm, metas_ref)], sems)
-    else:
-        at = capacity * chunks
-        moves = start_all(
-            (
-                (arrived_hbm.at[:, pl.ds(at, depth)], metas_ref.at[pl.ds(0, near)]),
-                (arrived_hbm.at[:, pl.ds(at + depth, depth)], metas_ref.at[pl.ds(near, near)]),
-                (arrived_hbm.at[:, pl.ds(0, at)], rows_ref),
-            ),
-            sems,
-        )
-    for move in moves:
+        pairs = [(arrived[0], metas_ref)]
+    else:
+        pairs = [(arrived[x].at[pl.ds(at, depth)], metas_ref.at[x]) for x in range(near)]
+        pairs += [
+            (arrived[x].at[pl.ds(at + depth, depth)], metas_ref.at[near + x]) for x in range(near)
+        ]
+        pairs += [(arrived[x].at[pl.ds(0, at)], rows_ref.at[i]) for i, x in enumerate(order)]
+    moves = start_all(pairs, sems)
+    early = min(len(moves), 2 * near)
+    for move in moves[:early]:
         move.wait()
 
     for x in range(devices):
@@ -270,22 +253,23 @@
 
     for c in range(sums_ref.shape[0]):
         sums_ref[c] = jnp.zeros_like(sums_ref[c])
+    for other in moves[early:]:
+        other.wait()
     move.wait()
     if near > 1:
-        for m in range(near):
-            add_rows(sums_ref, slots_s, m, capacity, rows_ref.at[m])
-
-
-def finish_kernel(capacity, turn_s, me_s, slots_s, sums_ref, gains_ref, recip_ref, *rest):
+        for i, x in enumerate(order):
+            add_rows(sums_ref, slots_s, x, capacity, rows_ref.at[i])
+
+
+def finish_kernel(capacity, order, slots_s, sums_ref, gains_ref, recip_ref, *rest):
     far = rest[:-3]
     out_ref, acc_ref, res_ref = rest[-3:]
     owned, parts, channels = out_ref.shape
     chunks = channels // LANES
     acc_ref[...] = sums_ref[...]
     if len(far) > 1:
-        for i in range(len(far)):
-            line = me_s[0] ^ turn_s[0] ^ (len(far) + i)
-            add_rows(acc_ref, slots_s, line, capacity, far[i])
+        for x, rows_ref in zip(order, far):
+            add_rows(acc_ref, slots_s, x, capacity, rows_ref)
     else:
 
         def from_device(d, carry):
@@ -360,18 +344,18 @@
     dma = pltpu.SemaphoreType.DMA
 
     me = lax.axis_index("bl").astype(i32).reshape(1)
-    turn = me & near if halves else jnp.zeros_like(me)
+    turn = me if halves else jnp.zeros_like(me)
     owner = row_owner.reshape(rows)
     coarse = gains_coarse.transpose(2, 1, 0).reshape(knots * parts, stations)
     block = (chunks * capacity, parts, LANES)
     rows_at = chunks * capacity
     if halves:
-        outs = [shape((rows_at + depth, parts, LANES), bf16)]
+        outs = [shape((rows_at + 2 * depth, parts, LANES), bf16)] * near
+        outs += [shape((rows_at + depth, parts, LANES), bf16)]
         outs += [shape(block, bf16)] * (near - 1)
-        outs += [shape((near, rows_at + 2 * depth, parts, LANES), bf16)]
     else:
         outs = [shape((devices,) + block, bf16), shape((depth, SUB, LANES), bf16)]
-    *sent, last = pl.pallas_call(
+    sent = pl.pallas_call(
         functools.partial(pack_kernel, capacity, near),
         out_shape=outs,
         in_specs=[smem] + [hbm] * 5,
@@ -386,12 +370,12 @@
             pltpu.VMEM((LANES, LANES), f32),
             pltpu.VMEM((depth, SUB, LANES), bf16),
             pltpu.VMEM((devices,) + block, bf16),
-            dma((5 + 2 * near + 2,)),
+            dma((5 + near + devices,)),
         ],
         compiler_params=most,
         name="pack_rows",
     )(
-        me if halves else turn,
+        turn,
         owner,
         row_owner.reshape(1, rows),
         row_slot.reshape(1, rows),
@@ -399,64 +383,73 @@
         coarse,
     )
 
+    def swap(array, x):
+        return lax.ppermute(array, "bl", [(d, d ^ x) for d in range(devices)])
+
     if halves:
-        far = [
-            lax.ppermute(sent[i], "bl", [(d, d ^ (near + i)) for d in range(devices)])
-            for i in range(near)
-        ]
+        arrived = {near: swap(sent[near], near)}
         packed = pl.pallas_call(
             functools.partial(add_partner_kernel, rows_at, depth),
-            out_shape=shape(last.shape, last.dtype),
-            in_specs=[anywhere, hbm],
-            out_specs=hbm,
+            out_shape=[shape(a.shape, a.dtype) for a in sent[:near]],
+            in_specs=[hbm] * (1 + near),
+            out_specs=[hbm] * near,
             scratch_shapes=[dma((near,))],
-            input_output_aliases={1: 0},
-            compiler_params=some,
+            input_output_aliases={1 + x: x for x in range(near)},
+            compiler_params=most,
             name="add_partner",
-        )(far[0], last)
-        groups = [list(range(0, near)), list(range(near, devices))]
-        arrived = lax.all_to_all(
-            packed, "bl", split_axis=0, concat_axis=0, axis_index_groups=groups, tiled=True
-        )
-    else:
-        far = [lax.all_to_all(sent[0], "bl", split_axis=0, concat_axis=0, tiled=True)]
-        arrived = lax.all_gather(last, "bl", axis=0)
+        )(arrived[near], *sent[:near])
+        arrived[0] = packed[0]
+        for x in range(1, near):
+            arrived[x] = swap(packed[x], x)
+            arrived[near + x] = swap(sent[near + x], near + x)
+        spread = list(range(near + 4, devices - 2)) + [None] * near
+        order = list(range(near, near + 4))
+        for x in range(1, near):
+            order += [x] + ([spread.pop(0)] if x % 2 else [])
+        order = [0] + [x for x in order if x is not None]
+        late = [x for x in range(devices) if x not in order]
+    else:
+        arrived = {
+            0: lax.all_gather(sent[1], "bl", axis=0),
+            1: lax.all_to_all(sent[0], "bl", split_axis=0, concat_axis=0, tiled=True),
+        }
+        order, late = [0], [1]
 
     gains, recip, slots, sums = pl.pallas_call(
-        functools.partial(prepare_kernel, capacity, near, stations),
+        functools.partial(prepare_kernel, capacity, near, stations, order),
         out_shape=(
             shape((parts, 2 * owned, channels), f32),
             shape((owned, LANES), f32),
             shape((devices, LANES), i32),
             shape((chunks, owned, parts, LANES), f32),
         ),
-        in_specs=[smem, smem, smem, anywhere, vmem, vmem, vmem],
+        in_specs=[smem, smem, smem, vmem, vmem, vmem] + [anywhere] * len(order),
         out_specs=(vmem,) * 4,
         scratch_shapes=[
             pltpu.VMEM((devices, depth, SUB, LANES), bf16),
             pltpu.VMEM((devices, gain_tiles * SUB, LANES), f32),
             pltpu.VMEM((2 * owned, LANES), f32),
-            pltpu.VMEM((near,) + block, bf16),
+            pltpu.VMEM((len(order),) + block, bf16),
             pltpu.VMEM((2, devices, LANES), f32),
             pltpu.SMEM((devices, LANES), i32),
             pltpu.VMEM((devices, LANES), i32),
-            dma((3,)),
+            dma((2 * near + len(order),)),
         ],
         compiler_params=some,
-        name="gains_and_near",
+        name="gains_and_sums",
     )(
         turn,
         me,
         baseline_station_pairs.T,
-        arrived,
         baseline_station_pairs,
         band_weights.T,
         band_offset.reshape(1, channels),
+        *[arrived[x] for x in order],
     )
     return pl.pallas_call(
-        functools.partial(finish_kernel, capacity),
+        functools.partial(finish_kernel, capacity, late),
         out_shape=shape((owned, parts, channels), bf16),
-        in_specs=[smem, smem, smem] + [vmem] * (3 + len(far)),
+        in_specs=[smem] + [vmem] * (3 + len(late)),
         out_specs=vmem,
         scratch_shapes=[
             pltpu.VMEM((chunks, owned, parts, LANES), f32),
@@ -464,7 +457,7 @@
         ],
         compiler_params=some,
         name="sum_and_apply",
-    )(turn, me, slots, sums, gains, recip, *far)
+    )(slots, sums, gains, recip, *[arrived[x] for x in late])
 
 
 def solution(mesh):

time: 55.6 us -> 58.4 us (1.050)
  the two profiles are of different devices: /device:TPU:17 before, /device:TPU:12 now
where the time goes in v7:
time: 58.4 us; the launch traced here: 57.4 us
  waiting for transfers between devices  20.2 us (35%)
  starting transfers between devices  18.3 us (31%)
  Pallas kernels  16.2 us (28%)
  local copies, waits for them, and re-layouts  2.55 us (4%)
    ppermute x15, waiting for transfers between devices, swap(): return lax.ppermute(array, 'bl', [(d, d ^ x) for d in range(devices)])  20.2 us
    ppermute x15, starting transfers between devices, swap(): return lax.ppermute(array, 'bl', [(d, d ^ x) for d in range(devices)])  18.3 us
    pallas_call x1, Pallas kernels, on_device(): pl.pallas_call(functools.partial(prepare_kernel, capacity, near, stations...  7.24 us
    pallas_call x1, Pallas kernels, on_device(): pl.pallas_call(functools.partial(add_partner_kernel, rows_at, depth), out...  3.65 us
    pallas_call x1, Pallas kernels, on_device(): pl.pallas_call(functools.partial(pack_kernel, capacity, near), out_shape=...  3.17 us
    unnamed x13, local copies, waits for them, and re-layouts  2.55 us
    pallas_call x1, Pallas kernels, on_device(): pl.pallas_call(functools.partial(finish_kernel, capacity, late), out_shap...  2.19 us
  transfers between devices with their start and end apart: 15, of which 6 were waited for; matrix products, arithmetic and copies ran while one was open for 0% of the time, Pallas kernels for 19%

profile of v7, /device:TPU:12, one launch (start us, length us, event | category | flops | bytes accessed | tf_op | source)
XLA Modules:
  0.0 57.4 jit_solution(13267038012234261230)
XLA Ops:
  0.0 3.2 %pack_rows.1 = (bf16[58,8,128]{2,1,0:T(8,128)(2,1)}, bf16[58,8,128]{2,1,0:T(8,128)(2,1)}, bf16[58,8,128]{2,1,0:T(8,128)(2,1)}, bf16[58,8,128]{2,1,0:T(8,128)(2,1...) custom-call(s32[1]{0:T(128)} %bitcast.me_s.turn_s, ...), custom_call_target="tpu_custom_call" | custom-call | tf_op jit(solution)/shard_map/pack_rows/pallas_call | solution.py:358
  3.2 2.7 %collective-permute-start = (bf16[53,8,128]{2,1,0:T(8,128)(2,1)}, bf16[53,8,128]{2,1,0:T(8,128)(2,1)S(1)}, u32[]{:S(2)}, u32[]{:S(2)}) collective-permute-start(bf16[53,8,128]{2,1,0:T(8,128)(2,1)} %get-tuple-element.33), channel_id=1, source_target_pairs={{0,8},{1,9},{2,10},{3,11},{4,12},{5,13},{6,14},{7,15},{8,0},{9,1},... | collective-permute-start | bytes 325640 | tf_op jit(solution)/shard_map/ppermute | solution.py:387
  5.8 2.0 %collective-permute-start.2 = (bf16[48,8,128]{2,1,0:T(8,128)(2,1)}, bf16[48,8,128]{2,1,0:T(8,128)(2,1)S(1)}, u32[]{:S(2)}, u32[]{:S(2)}) collective-permute-start(bf16[48,8,128]{2,1,0:T(8,128)(2,1)} %get-tuple-element.44), channel_id=1, source_target_pairs={{0,10},{1,11},{2,8},{3,9},{4,14},{5,15},{6,12},{7,13},{8,2},{9,3},... | collective-permute-start | bytes 294920 | tf_op jit(solution)/shard_map/ppermute | solution.py:387
  7.9 1.6 %collective-permute-start.3 = (bf16[48,8,128]{2,1,0:T(8,128)(2,1)}, bf16[48,8,128]{2,1,0:T(8,128)(2,1)S(1)}, u32[]{:S(2)}, u32[]{:S(2)}) collective-permute-start(bf16[48,8,128]{2,1,0:T(8,128)(2,1)} %get-tuple-element.45), channel_id=1, source_target_pairs={{0,11},{1,10},{2,9},{3,8},{4,15},{5,14},{6,13},{7,12},{8,3},{9,2},... | collective-permute-start | bytes 294920 | tf_op jit(solution)/shard_map/ppermute | solution.py:387
  9.4 1.6 %collective-permute-start.5 = (bf16[48,8,128]{2,1,0:T(8,128)(2,1)}, bf16[48,8,128]{2,1,0:T(8,128)(2,1)S(1)}, u32[]{:S(2)}, u32[]{:S(2)}) collective-permute-start(bf16[48,8,128]{2,1,0:T(8,128)(2,1)} %get-tuple-element.47), channel_id=1, source_target_pairs={{0,12},{1,13},{2,14},{3,15},{4,8},{5,9},{6,10},{7,11},{8,4},{9,5},... | collective-permute-start | bytes 294920 | tf_op jit(solution)/shard_map/ppermute | solution.py:387
  11.0 8.1 %collective-permute-done.first_hbm.rest_1_ = bf16[53,8,128]{2,1,0:T(8,128)(2,1)S(1)} collective-permute-done((bf16[53,8,128]{2,1,0:T(8,128)(2,1)}, bf16[53,8,128]{2,1,0:T(8,128)(2,1)S(1)}, u32[]{:S(2)}, u32[]{:S(2)}) %collective-permute-start) | collective-permute-done | bytes 108576 | tf_op jit(solution)/shard_map/ppermute | solution.py:387
  19.2 0.6 %copy-done.1 = bf16[53,8,128]{2,1,0:T(8,128)(2,1)} copy-done((bf16[53,8,128]{2,1,0:T(8,128)(2,1)}, bf16[53,8,128]{2,1,0:T(8,128)(2,1)S(1)}, u32[]{:S(2)}) %copy-start.1) | copy-done | bytes 108568
  19.8 3.7 %add_partner.1 = (bf16[58,8,128]{2,1,0:T(8,128)(2,1)}, bf16[58,8,128]{2,1,0:T(8,128)(2,1)}, bf16[58,8,128]{2,1,0:T(8,128)(2,1)}, bf16[58,8,128]{2,1,0:T(8,128)(2...) custom-call(bf16[53,8,128]{2,1,0:T(8,128)(2,1)} %copy-done.1, ...), custom_call_target="tpu_custom_call", output_to_operand_aliasing={{0}: (1, {}), {1}: (2, {}), {2}: (3, {}), {3}: (4, {}), {4}... | custom-call | tf_op jit(solution)/shard_map/add_partner/pallas_call | solution.py:391
  23.6 0.6 collective-permute-start.6
  24.2 1.3 %collective-permute-done.3.rest_4_ = bf16[48,8,128]{2,1,0:T(8,128)(2,1)S(1)} collective-permute-done((bf16[48,8,128]{2,1,0:T(8,128)(2,1)}, bf16[48,8,128]{2,1,0:T(8,128)(2,1)S(1)}, u32[]{:S(2)}, u32[]{:S(2)}) %collective-permute-start.3) | collective-permute-done | bytes 98336 | tf_op jit(solution)/shard_map/ppermute | solution.py:387
  25.8 1.7 %collective-permute-done.5.rest_6_ = bf16[48,8,128]{2,1,0:T(8,128)(2,1)S(1)} collective-permute-done((bf16[48,8,128]{2,1,0:T(8,128)(2,1)}, bf16[48,8,128]{2,1,0:T(8,128)(2,1)S(1)}, u32[]{:S(2)}, u32[]{:S(2)}) %collective-permute-start.5) | collective-permute-done | bytes 98336 | tf_op jit(solution)/shard_map/ppermute | solution.py:387
  27.6 2.5 %collective-permute-start.9 = (bf16[58,8,128]{2,1,0:T(8,128)(2,1)}, bf16[58,8,128]{2,1,0:T(8,128)(2,1)S(1)}, u32[]{:S(2)}, u32[]{:S(2)}) collective-permute-start(bf16[58,8,128]{2,1,0:T(8,128)(2,1)} %get-tuple-element.51), channel_id=1, source_target_pairs={{0,4},{1,5},{2,6},{3,7},{4,0},{5,1},{6,2},{7,3},{8,12},{9,13},{10,... | collective-permute-start | bytes 356360 | tf_op jit(solution)/shard_map/ppermute | solution.py:387
  30.1 1.5 %collective-permute-done.8.rest_9_ = bf16[48,8,128]{2,1,0:T(8,128)(2,1)S(1)} collective-permute-done((bf16[48,8,128]{2,1,0:T(8,128)(2,1)}, bf16[48,8,128]{2,1,0:T(8,128)(2,1)S(1)}, u32[]{:S(2)}, u32[]{:S(2)}) %collective-permute-start.8) | collective-permute-done | bytes 98336 | tf_op jit(solution)/shard_map/ppermute | solution.py:387
  31.6 1.0 %collective-permute-start.10 = (bf16[58,8,128]{2,1,0:T(8,128)(2,1)}, bf16[58,8,128]{2,1,0:T(8,128)(2,1)S(1)}, u32[]{:S(2)}, u32[]{:S(2)}) collective-permute-start(bf16[58,8,128]{2,1,0:T(8,128)(2,1)} %get-tuple-element.52), channel_id=1, source_target_pairs={{0,5},{1,4},{2,7},{3,6},{4,1},{5,0},{6,3},{7,2},{8,13},{9,12},{10,... | collective-permute-start | bytes 356360 | tf_op jit(solution)/shard_map/ppermute | solution.py:387
  32.6 1.6 %collective-permute-start.11 = (bf16[58,8,128]{2,1,0:T(8,128)(2,1)}, bf16[58,8,128]{2,1,0:T(8,128)(2,1)S(1)}, u32[]{:S(2)}, u32[]{:S(2)}) collective-permute-start(bf16[58,8,128]{2,1,0:T(8,128)(2,1)} %get-tuple-element.53), channel_id=1, source_target_pairs={{0,6},{1,7},{2,4},{3,5},{4,2},{5,3},{6,0},{7,1},{8,14},{9,15},{10,... | collective-permute-start | bytes 356360 | tf_op jit(solution)/shard_map/ppermute | solution.py:387
  34.2 0.9 %collective-permute-start.12 = (bf16[58,8,128]{2,1,0:T(8,128)(2,1)}, bf16[58,8,128]{2,1,0:T(8,128)(2,1)S(1)}, u32[]{:S(2)}, u32[]{:S(2)}) collective-permute-start(bf16[58,8,128]{2,1,0:T(8,128)(2,1)} %get-tuple-element.54), channel_id=1, source_target_pairs={{0,7},{1,6},{2,5},{3,4},{4,3},{5,2},{6,1},{7,0},{8,15},{9,14},{10,... | collective-permute-start | bytes 356360 | tf_op jit(solution)/shard_map/ppermute | solution.py:387
  35.1 3.1 %collective-permute-start.13 = (bf16[48,8,128]{2,1,0:T(8,128)(2,1)}, bf16[48,8,128]{2,1,0:T(8,128)(2,1)S(1)}, u32[]{:S(2)}, u32[]{:S(2)}) collective-permute-start(bf16[48,8,128]{2,1,0:T(8,128)(2,1)} %get-tuple-element.59), channel_id=1, source_target_pairs={{0,14},{1,15},{2,12},{3,13},{4,10},{5,11},{6,8},{7,9},{8,6},{9,7},... | collective-permute-start | bytes 294920 | tf_op jit(solution)/shard_map/ppermute | solution.py:387
  38.2 0.4 collective-permute-start.14
  38.7 3.6 %collective-permute-done.11.rest_12_ = bf16[58,8,128]{2,1,0:T(8,128)(2,1)S(1)} collective-permute-done((bf16[58,8,128]{2,1,0:T(8,128)(2,1)}, bf16[58,8,128]{2,1,0:T(8,128)(2,1)S(1)}, u32[]{:S(2)}, u32[]{:S(2)}) %collective-permute-start.11) | collective-permute-done | bytes 118816 | tf_op jit(solution)/shard_map/ppermute | solution.py:387
  42.2 3.9 %collective-permute-done.12.rest_13_ = bf16[58,8,128]{2,1,0:T(8,128)(2,1)S(1)} collective-permute-done((bf16[58,8,128]{2,1,0:T(8,128)(2,1)}, bf16[58,8,128]{2,1,0:T(8,128)(2,1)S(1)}, u32[]{:S(2)}, u32[]{:S(2)}) %collective-permute-start.12) | collective-permute-done | bytes 118816 | tf_op jit(solution)/shard_map/ppermute | solution.py:387
  46.1 0.9 %copy-done = bf16[58,8,128]{2,1,0:T(8,128)(2,1)S(1)} copy-done((bf16[58,8,128]{2,1,0:T(8,128)(2,1)S(1)}, bf16[58,8,128]{2,1,0:T(8,128)(2,1)}, u32[]{:S(2)}) %copy-start) | copy-done | bytes 118808
  47.0 0.9 %copy-done.2 = bf16[53,8,128]{2,1,0:T(8,128)(2,1)S(1)} copy-done((bf16[53,8,128]{2,1,0:T(8,128)(2,1)S(1)}, bf16[53,8,128]{2,1,0:T(8,128)(2,1)}, u32[]{:S(2)}) %copy-start.2) | copy-done | bytes 108568
  47.9 7.2 %gains_and_sums.1 = (f32[8,128,384]{2,1,0:T(8,128)S(1)}, f32[64,128]{1,0:T(8,128)S(1)}, s32[16,128]{1,0:T(8,128)S(1)}, f32[3,64,8,128]{3,2,1,0:T(8,128)S(1)}) custom-call(s32[1]{0:T(128)} %bitcast.me_s.turn_s, s32[1]{0:T(128)} %bitcast.me_s.turn_s, s32[2,64]{1,0:T(2,128)S(1)} %bitcast.10, s32[64,2]{1,0:T(8,128)S(1)} %copy.16.pairs_ref, ...), custom_call_target="tpu_custom_call" | custom-call | tf_op jit(solution)/shard_map/gains_and_sums/pallas_call | solution.py:418
  55.2 2.2 %sum_and_apply.1 = bf16[64,8,384]{2,1,0:T(8,128)(2,1)} custom-call(s32[16,128]{1,0:T(8,128)S(1)} %get-tuple-element.55.slots_s, f32[3,64,8,128]{3,2,1,0:T(8,128)S(1)} %get-tuple-element.56.sums_ref, f32[8,128,384]{2,1,0:T(8,128)S(1)} %get-tuple-element.57.gains_ref, f32[64,128]{1,0:T(8,128)S(1)} %get-tuple-element.58.recip_ref, ...), custom_call_target="tpu_custom_call" | custom-call | tf_op jit(solution)/shard_map/sum_and_apply/pallas_call | solution.py:449
  (24 shorter events, 0.6 us)
Async XLA Ops:
  0.0 38.6 %copy-start.5 = (s32[384]{0:T(512)S(1)}, s32[384]{0:T(512)}, u32[]{:S(2)}) copy-start(s32[384]{0:T(512)} %param.13) | copy-start | bytes 4612
  0.0 38.6 %copy-start.4 = (s32[64,2]{0,1:T(2,128)S(1)}, s32[64,2]{0,1:T(2,128)}, u32[]{:S(2)}) copy-start(s32[64,2]{0,1:T(2,128)} %param.10) | copy-start | bytes 1540
  0.0 46.1 %copy-start.3 = (f32[384,3]{0,1:T(4,128)S(1)}, f32[384,3]{0,1:T(4,128)}, u32[]{:S(2)}) copy-start(f32[384,3]{0,1:T(4,128)} %param.12) | copy-start | bytes 13828
  3.2 16.0 %collective-permute-start = (bf16[53,8,128]{2,1,0:T(8,128)(2,1)}, bf16[53,8,128]{2,1,0:T(8,128)(2,1)S(1)}, u32[]{:S(2)}, u32[]{:S(2)}) collective-permute-start(bf16[53,8,128]{2,1,0:T(8,128)(2,1)} %get-tuple-element.33), channel_id=1, source_target_pairs={{0,8},{1,9},{2,10},{3,11},{4,12},{5,13},{6,14},{7,15},{8,0},{9,1},... | collective-permute-start | bytes 325640 | tf_op jit(solution)/shard_map/ppermute | solution.py:387
  5.8 17.7 %collective-permute-start.1 = (bf16[48,8,128]{2,1,0:T(8,128)(2,1)}, bf16[48,8,128]{2,1,0:T(8,128)(2,1)S(1)}, u32[]{:S(2)}, u32[]{:S(2)}) collective-permute-start(bf16[48,8,128]{2,1,0:T(8,128)(2,1)} %get-tuple-element.43), channel_id=1, source_target_pairs={{0,9},{1,8},{2,11},{3,10},{4,13},{5,12},{6,15},{7,14},{8,1},{9,0},... | collective-permute-start | bytes 294920 | tf_op jit(solution)/shard_map/ppermute | solution.py:387
  5.8 18.3 %collective-permute-start.2 = (bf16[48,8,128]{2,1,0:T(8,128)(2,1)}, bf16[48,8,128]{2,1,0:T(8,128)(2,1)S(1)}, u32[]{:S(2)}, u32[]{:S(2)}) collective-permute-start(bf16[48,8,128]{2,1,0:T(8,128)(2,1)} %get-tuple-element.44), channel_id=1, source_target_pairs={{0,10},{1,11},{2,8},{3,9},{4,14},{5,15},{6,12},{7,13},{8,2},{9,3},... | collective-permute-start | bytes 294920 | tf_op jit(solution)/shard_map/ppermute | solution.py:387
  7.9 17.6 %collective-permute-start.3 = (bf16[48,8,128]{2,1,0:T(8,128)(2,1)}, bf16[48,8,128]{2,1,0:T(8,128)(2,1)S(1)}, u32[]{:S(2)}, u32[]{:S(2)}) collective-permute-start(bf16[48,8,128]{2,1,0:T(8,128)(2,1)} %get-tuple-element.45), channel_id=1, source_target_pairs={{0,11},{1,10},{2,9},{3,8},{4,15},{5,14},{6,13},{7,12},{8,3},{9,2},... | collective-permute-start | bytes 294920 | tf_op jit(solution)/shard_map/ppermute | solution.py:387
  9.4 18.1 %collective-permute-start.5 = (bf16[48,8,128]{2,1,0:T(8,128)(2,1)}, bf16[48,8,128]{2,1,0:T(8,128)(2,1)S(1)}, u32[]{:S(2)}, u32[]{:S(2)}) collective-permute-start(bf16[48,8,128]{2,1,0:T(8,128)(2,1)} %get-tuple-element.47), channel_id=1, source_target_pairs={{0,12},{1,13},{2,14},{3,15},{4,8},{5,9},{6,10},{7,11},{8,4},{9,5},... | collective-permute-start | bytes 294920 | tf_op jit(solution)/shard_map/ppermute | solution.py:387
  19.2 0.6 %copy-start.1 = (bf16[53,8,128]{2,1,0:T(8,128)(2,1)}, bf16[53,8,128]{2,1,0:T(8,128)(2,1)S(1)}, u32[]{:S(2)}) copy-start(bf16[53,8,128]{2,1,0:T(8,128)(2,1)S(1)} %collective-permute-done.first_hbm.rest_1_) | copy-start | bytes 325636
  23.5 9.1 %collective-permute-start.4 = (bf16[58,8,128]{2,1,0:T(8,128)(2,1)}, bf16[58,8,128]{2,1,0:T(8,128)(2,1)S(1)}, u32[]{:S(2)}, u32[]{:S(2)}) collective-permute-start(bf16[58,8,128]{2,1,0:T(8,128)(2,1)} %get-tuple-element.46), channel_id=1, source_target_pairs={{0,1},{1,0},{2,3},{3,2},{4,5},{5,4},{6,7},{7,6},{8,9},{9,8},{10,11... | collective-permute-start | bytes 356360 | tf_op jit(solution)/shard_map/ppermute | solution.py:387
  23.6 10.7 %collective-permute-start.6 = (bf16[58,8,128]{2,1,0:T(8,128)(2,1)}, bf16[58,8,128]{2,1,0:T(8,128)(2,1)S(1)}, u32[]{:S(2)}, u32[]{:S(2)}) collective-permute-start(bf16[58,8,128]{2,1,0:T(8,128)(2,1)} %get-tuple-element.48), channel_id=1, source_target_pairs={{0,2},{1,3},{2,0},{3,1},{4,6},{5,7},{6,4},{7,5},{8,10},{9,11},{10,... | collective-permute-start | bytes 356360 | tf_op jit(solution)/shard_map/ppermute | solution.py:387
  24.1 7.5 %collective-permute-start.8 = (bf16[48,8,128]{2,1,0:T(8,128)(2,1)}, bf16[48,8,128]{2,1,0:T(8,128)(2,1)S(1)}, u32[]{:S(2)}, u32[]{:S(2)}) collective-permute-start(bf16[48,8,128]{2,1,0:T(8,128)(2,1)} %get-tuple-element.50), channel_id=1, source_target_pairs={{0,13},{1,12},{2,15},{3,14},{4,9},{5,8},{6,11},{7,10},{8,5},{9,4},... | collective-permute-start | bytes 294920 | tf_op jit(solution)/shard_map/ppermute | solution.py:387
  25.5 9.6 %collective-permute-start.7 = (bf16[58,8,128]{2,1,0:T(8,128)(2,1)}, bf16[58,8,128]{2,1,0:T(8,128)(2,1)S(1)}, u32[]{:S(2)}, u32[]{:S(2)}) collective-permute-start(bf16[58,8,128]{2,1,0:T(8,128)(2,1)} %get-tuple-element.49), channel_id=1, source_target_pairs={{0,3},{1,2},{2,1},{3,0},{4,7},{5,6},{6,5},{7,4},{8,11},{9,10},{10,... | collective-permute-start | bytes 356360 | tf_op jit(solution)/shard_map/ppermute | solution.py:387
  27.6 10.6 %collective-permute-start.9 = (bf16[58,8,128]{2,1,0:T(8,128)(2,1)}, bf16[58,8,128]{2,1,0:T(8,128)(2,1)S(1)}, u32[]{:S(2)}, u32[]{:S(2)}) collective-permute-start(bf16[58,8,128]{2,1,0:T(8,128)(2,1)} %get-tuple-element.51), channel_id=1, source_target_pairs={{0,4},{1,5},{2,6},{3,7},{4,0},{5,1},{6,2},{7,3},{8,12},{9,13},{10,... | collective-permute-start | bytes 356360 | tf_op jit(solution)/shard_map/ppermute | solution.py:387
  31.6 7.0 %collective-permute-start.10 = (bf16[58,8,128]{2,1,0:T(8,128)(2,1)}, bf16[58,8,128]{2,1,0:T(8,128)(2,1)S(1)}, u32[]{:S(2)}, u32[]{:S(2)}) collective-permute-start(bf16[58,8,128]{2,1,0:T(8,128)(2,1)} %get-tuple-element.52), channel_id=1, source_target_pairs={{0,5},{1,4},{2,7},{3,6},{4,1},{5,0},{6,3},{7,2},{8,13},{9,12},{10,... | collective-permute-start | bytes 356360 | tf_op jit(solution)/shard_map/ppermute | solution.py:387
  32.6 9.6 %collective-permute-start.11 = (bf16[58,8,128]{2,1,0:T(8,128)(2,1)}, bf16[58,8,128]{2,1,0:T(8,128)(2,1)S(1)}, u32[]{:S(2)}, u32[]{:S(2)}) collective-permute-start(bf16[58,8,128]{2,1,0:T(8,128)(2,1)} %get-tuple-element.53), channel_id=1, source_target_pairs={{0,6},{1,7},{2,4},{3,5},{4,2},{5,3},{6,0},{7,1},{8,14},{9,15},{10,... | collective-permute-start | bytes 356360 | tf_op jit(solution)/shard_map/ppermute | solution.py:387
  34.2 11.9 %collective-permute-start.12 = (bf16[58,8,128]{2,1,0:T(8,128)(2,1)}, bf16[58,8,128]{2,1,0:T(8,128)(2,1)S(1)}, u32[]{:S(2)}, u32[]{:S(2)}) collective-permute-start(bf16[58,8,128]{2,1,0:T(8,128)(2,1)} %get-tuple-element.54), channel_id=1, source_target_pairs={{0,7},{1,6},{2,5},{3,4},{4,3},{5,2},{6,1},{7,0},{8,15},{9,14},{10,... | collective-permute-start | bytes 356360 | tf_op jit(solution)/shard_map/ppermute | solution.py:387
  35.1 20.1 %collective-permute-start.13 = (bf16[48,8,128]{2,1,0:T(8,128)(2,1)}, bf16[48,8,128]{2,1,0:T(8,128)(2,1)S(1)}, u32[]{:S(2)}, u32[]{:S(2)}) collective-permute-start(bf16[48,8,128]{2,1,0:T(8,128)(2,1)} %get-tuple-element.59), channel_id=1, source_target_pairs={{0,14},{1,15},{2,12},{3,13},{4,10},{5,11},{6,8},{7,9},{8,6},{9,7},... | collective-permute-start | bytes 294920 | tf_op jit(solution)/shard_map/ppermute | solution.py:387
  38.2 17.0 %collective-permute-start.14 = (bf16[48,8,128]{2,1,0:T(8,128)(2,1)}, bf16[48,8,128]{2,1,0:T(8,128)(2,1)S(1)}, u32[]{:S(2)}, u32[]{:S(2)}) collective-permute-start(bf16[48,8,128]{2,1,0:T(8,128)(2,1)} %get-tuple-element.60), channel_id=1, source_target_pairs={{0,15},{1,14},{2,13},{3,12},{4,11},{5,10},{6,9},{7,8},{8,7},{9,6},... | collective-permute-start | bytes 294920 | tf_op jit(solution)/shard_map/ppermute | solution.py:387
  46.1 0.9 %copy-start = (bf16[58,8,128]{2,1,0:T(8,128)(2,1)S(1)}, bf16[58,8,128]{2,1,0:T(8,128)(2,1)}, u32[]{:S(2)}) copy-start(bf16[58,8,128]{2,1,0:T(8,128)(2,1)} %get-tuple-element.42.rest_0_) | copy-start | bytes 356356
  47.0 0.9 %copy-start.2 = (bf16[53,8,128]{2,1,0:T(8,128)(2,1)S(1)}, bf16[53,8,128]{2,1,0:T(8,128)(2,1)}, u32[]{:S(2)}) copy-start(bf16[53,8,128]{2,1,0:T(8,128)(2,1)} %copy-done.1) | copy-start | bytes 325636

commit v8 on v7

--- a/solution.py
+++ b/solution.py
@@ -16,6 +16,10 @@
 
 def round_up(value, unit):
     return -(-value // unit) * unit
+
+
+def with_gains(near):
+    return list(range(near)) + list(range(near, 2 * near, 2))
 
 
 def start_all(pairs, sems):
@@ -86,7 +90,7 @@
     meta_ref[2 * gain_tiles] = codes.astype(jnp.float32).astype(jnp.bfloat16)
     at = chunks * capacity
     if near > 1:
-        pairs = [(meta_ref, outs[x].at[pl.ds(at, depth)]) for x in range(near + 1)]
+        pairs = [(meta_ref, outs[x].at[pl.ds(at, depth)]) for x in with_gains(near)]
     else:
         pairs = [(meta_ref, outs[1])]
     sends = start_all(pairs, sems.at[pl.ds(1, len(pairs))])
@@ -111,11 +115,14 @@
         send.wait()
 
 
-def add_partner_kernel(at, depth, first_hbm, *rest):
-    sems = rest[-1]
-    outs = rest[len(rest) // 2 : -1]
+def collect_kernel(at, depth, *rest):
+    blocks, (out_ref, sems) = rest[:-2], rest[-2:]
     moves = start_all(
-        [(first_hbm.at[pl.ds(at, depth)], out.at[pl.ds(at + depth, depth)]) for out in outs], sems
+        [
+            (block.at[pl.ds(at, depth)], out_ref.at[pl.ds(i * depth, depth)])
+            for i, block in enumerate(blocks)
+        ],
+        sems,
     )
     for move in moves:
         move.wait()
@@ -168,7 +175,7 @@
     offset_ref,
     *rest,
 ):
-    arrived = dict(zip(order, rest[:-12]))
+    arrived, passed = dict(zip(order, rest)), rest[len(order)]
     gains_ref, recip_ref, slots_ref, sums_ref = rest[-12:-8]
     metas_ref, table_ref, pick_ref, rows_ref, codes_ref, slots_s, slots_v, sems = rest[-8:]
     devices, depth, _, _ = metas_ref.shape
@@ -181,9 +188,10 @@
     if near == 1:
         pairs = [(arrived[0], metas_ref)]
     else:
-        pairs = [(arrived[x].at[pl.ds(at, depth)], metas_ref.at[x]) for x in range(near)]
+        pairs = [(arrived[x].at[pl.ds(at, depth)], metas_ref.at[x]) for x in with_gains(near)]
         pairs += [
-            (arrived[x].at[pl.ds(at + depth, depth)], metas_ref.at[near + x]) for x in range(near)
+            (passed.at[pl.ds(i * depth, depth)], metas_ref.at[near + 1 + 2 * i])
+            for i in range(near // 2)
         ]
         pairs += [(arrived[x].at[pl.ds(0, at)], rows_ref.at[i]) for i, x in enumerate(order)]
     moves = start_all(pairs, sems)
@@ -350,9 +358,10 @@
     block = (chunks * capacity, parts, LANES)
     rows_at = chunks * capacity
     if halves:
-        outs = [shape((rows_at + 2 * depth, parts, LANES), bf16)] * near
-        outs += [shape((rows_at + depth, parts, LANES), bf16)]
-        outs += [shape(block, bf16)] * (near - 1)
+        outs = [
+            shape((rows_at + (depth if x in with_gains(near) else 0), parts, LANES), bf16)
+            for x in range(devices)
+        ]
     else:
         outs = [shape((devices,) + block, bf16), shape((depth, SUB, LANES), bf16)]
     sent = pl.pallas_call(
@@ -370,7 +379,7 @@
             pltpu.VMEM((LANES, LANES), f32),
             pltpu.VMEM((depth, SUB, LANES), bf16),
             pltpu.VMEM((devices,) + block, bf16),
-            dma((5 + near + devices,)),
+            dma((5 + 2 * devices,)),
         ],
         compiler_params=most,
         name="pack_rows",
@@ -387,33 +396,32 @@
         return lax.ppermute(array, "bl", [(d, d ^ x) for d in range(devices)])
 
     if halves:
-        arrived = {near: swap(sent[near], near)}
-        packed = pl.pallas_call(
-            functools.partial(add_partner_kernel, rows_at, depth),
-            out_shape=[shape(a.shape, a.dtype) for a in sent[:near]],
-            in_specs=[hbm] * (1 + near),
-            out_specs=[hbm] * near,
-            scratch_shapes=[dma((near,))],
-            input_output_aliases={1 + x: x for x in range(near)},
-            compiler_params=most,
-            name="add_partner",
-        )(arrived[near], *sent[:near])
-        arrived[0] = packed[0]
-        for x in range(1, near):
-            arrived[x] = swap(packed[x], x)
-            arrived[near + x] = swap(sent[near + x], near + x)
-        spread = list(range(near + 4, devices - 2)) + [None] * near
-        order = list(range(near, near + 4))
-        for x in range(1, near):
-            order += [x] + ([spread.pop(0)] if x % 2 else [])
-        order = [0] + [x for x in order if x is not None]
-        late = [x for x in range(devices) if x not in order]
+        arrived = {0: sent[0]}
+        for x in range(1, devices):
+            arrived[x] = swap(sent[x], x)
+        even = list(range(near, devices, 2))
+        collected = pl.pallas_call(
+            functools.partial(collect_kernel, rows_at, depth),
+            out_shape=shape((len(even) * depth, parts, LANES), bf16),
+            in_specs=[anywhere] * len(even),
+            out_specs=vmem,
+            scratch_shapes=[dma((len(even),))],
+            compiler_params=some,
+            name="collect_gains",
+        )(*[arrived[x] for x in even])
+        passed = swap(collected, 1)
+        order = [0]
+        cross = even + [x + 1 for x in even]
+        for i, x in enumerate(cross[: near // 2 + 1]):
+            order += [x] + ([i] if 0 < i < near // 2 else [])
+        order += [x for x in range(1, near) if x not in order]
+        late = [x for x in cross if x not in order]
     else:
         arrived = {
             0: lax.all_gather(sent[1], "bl", axis=0),
             1: lax.all_to_all(sent[0], "bl", split_axis=0, concat_axis=0, tiled=True),
         }
-        order, late = [0], [1]
+        order, late, passed = [0], [1], arrived[0]
 
     gains, recip, slots, sums = pl.pallas_call(
         functools.partial(prepare_kernel, capacity, near, stations, order),
@@ -423,7 +431,7 @@
             shape((devices, LANES), i32),
             shape((chunks, owned, parts, LANES), f32),
         ),
-        in_specs=[smem, smem, smem, vmem, vmem, vmem] + [anywhere] * len(order),
+        in_specs=[smem, smem, smem, vmem, vmem, vmem, hbm] + [anywhere] * len(order),
         out_specs=(vmem,) * 4,
         scratch_shapes=[
             pltpu.VMEM((devices, depth, SUB, LANES), bf16),
@@ -445,6 +453,7 @@
         band_weights.T,
         band_offset.reshape(1, channels),
         *[arrived[x] for x in order],
+        passed,
     )
     return pl.pallas_call(
         functools.partial(finish_kernel, capacity, late),

time: 58.4 us -> 53.9 us (0.923)
  the two profiles are of different devices: /device:TPU:12 before, /device:TPU:0 now
where the time goes in v8:
time: 53.9 us; the launch traced here: 53 us
  starting transfers between devices  36.3 us (67%)
  Pallas kernels  11.7 us (22%)
  local copies, waits for them, and re-layouts  3.72 us (7%)
  waiting for transfers between devices  1.2 us (2%)
    ppermute x16, starting transfers between devices, swap(): return lax.ppermute(array, 'bl', [(d, d ^ x) for d in range(devices)])  36.3 us
    pallas_call x1, Pallas kernels, on_device(): pl.pallas_call(functools.partial(prepare_kernel, capacity, near, stations...  6.38 us
    pallas_call x1, Pallas kernels, on_device(): pl.pallas_call(functools.partial(pack_kernel, capacity, near), out_shape=...  3.22 us
    unnamed x7, local copies, waits for them, and re-layouts  3.03 us
    pallas_call x1, Pallas kernels, on_device(): pl.pallas_call(functools.partial(finish_kernel, capacity, late), out_shap...  2.06 us
    ppermute x16, waiting for transfers between devices, swap(): return lax.ppermute(array, 'bl', [(d, d ^ x) for d in range(devices)])  1.2 us
  transfers between devices with their start and end apart: 16, of which 3 were waited for; matrix products, arithmetic and copies ran while one was open for 3% of the time, Pallas kernels for 12%

profile of v8, /device:TPU:0, one launch (start us, length us, event | category | flops | bytes accessed | tf_op | source)
XLA Modules:
  0.0 53.0 jit_solution(8621182083469440943)
XLA Ops:
  0.0 3.2 %pack_rows.1 = (bf16[53,8,128]{2,1,0:T(8,128)(2,1)}, bf16[53,8,128]{2,1,0:T(8,128)(2,1)}, bf16[53,8,128]{2,1,0:T(8,128)(2,1)}, bf16[53,8,128]{2,1,0:T(8,128)(2,1...) custom-call(s32[1]{0:T(128)} %bitcast.me_s.turn_s, ...), custom_call_target="tpu_custom_call" | custom-call | tf_op jit(solution)/shard_map/pack_rows/pallas_call | solution.py:367
  3.2 3.5 %collective-permute-start.7 = (bf16[48,8,128]{2,1,0:T(8,128)(2,1)}, bf16[48,8,128]{2,1,0:T(8,128)(2,1)S(1)}, u32[]{:S(2)}, u32[]{:S(2)}) collective-permute-start(bf16[48,8,128]{2,1,0:T(8,128)(2,1)} %get-tuple-element.33), channel_id=1, source_target_pairs={{0,9},{1,8},{2,11},{3,10},{4,13},{5,12},{6,15},{7,14},{8,1},{9,0},... | collective-permute-start | bytes 294920 | tf_op jit(solution)/shard_map/ppermute | solution.py:396
  6.8 0.6 %collective-permute-start = (bf16[53,8,128]{2,1,0:T(8,128)(2,1)}, bf16[53,8,128]{2,1,0:T(8,128)(2,1)S(1)}, u32[]{:S(2)}, u32[]{:S(2)}) collective-permute-start(bf16[53,8,128]{2,1,0:T(8,128)(2,1)} %get-tuple-element.26), channel_id=1, source_target_pairs={{0,8},{1,9},{2,10},{3,11},{4,12},{5,13},{6,14},{7,15},{8,0},{9,1},... | collective-permute-start | bytes 325640 | tf_op jit(solution)/shard_map/ppermute | solution.py:396
  7.4 3.2 %collective-permute-start.1 = (bf16[53,8,128]{2,1,0:T(8,128)(2,1)}, bf16[53,8,128]{2,1,0:T(8,128)(2,1)S(1)}, u32[]{:S(2)}, u32[]{:S(2)}) collective-permute-start(bf16[53,8,128]{2,1,0:T(8,128)(2,1)} %get-tuple-element.27), channel_id=1, source_target_pairs={{0,10},{1,11},{2,8},{3,9},{4,14},{5,15},{6,12},{7,13},{8,2},{9,3},... | collective-permute-start | bytes 325640 | tf_op jit(solution)/shard_map/ppermute | solution.py:396
  10.6 0.1 collective-permute-start.2
  10.8 1.5 %collective-permute-start.3 = (bf16[53,8,128]{2,1,0:T(8,128)(2,1)}, bf16[53,8,128]{2,1,0:T(8,128)(2,1)S(1)}, u32[]{:S(2)}, u32[]{:S(2)}) collective-permute-start(bf16[53,8,128]{2,1,0:T(8,128)(2,1)} %get-tuple-element.29), channel_id=1, source_target_pairs={{0,12},{1,13},{2,14},{3,15},{4,8},{5,9},{6,10},{7,11},{8,4},{9,5},... | collective-permute-start | bytes 325640 | tf_op jit(solution)/shard_map/ppermute | solution.py:396
  12.3 9.0 %collective-permute-start.4 = (bf16[53,8,128]{2,1,0:T(8,128)(2,1)}, bf16[53,8,128]{2,1,0:T(8,128)(2,1)S(1)}, u32[]{:S(2)}, u32[]{:S(2)}) collective-permute-start(bf16[53,8,128]{2,1,0:T(8,128)(2,1)} %get-tuple-element.30), channel_id=1, source_target_pairs={{0,2},{1,3},{2,0},{3,1},{4,6},{5,7},{6,4},{7,5},{8,10},{9,11},{10,... | collective-permute-start | bytes 325640 | tf_op jit(solution)/shard_map/ppermute | solution.py:396
  21.3 0.8 %collective-permute-done.rest_0_.rest_1_ = bf16[53,8,128]{2,1,0:T(8,128)(2,1)S(1)} collective-permute-done((bf16[53,8,128]{2,1,0:T(8,128)(2,1)}, bf16[53,8,128]{2,1,0:T(8,128)(2,1)S(1)}, u32[]{:S(2)}, u32[]{:S(2)}) %collective-permute-start) | collective-permute-done | bytes 108576 | tf_op jit(solution)/shard_map/ppermute | solution.py:396
  22.1 4.7 %collective-permute-start.5 = (bf16[53,8,128]{2,1,0:T(8,128)(2,1)}, bf16[53,8,128]{2,1,0:T(8,128)(2,1)S(1)}, u32[]{:S(2)}, u32[]{:S(2)}) collective-permute-start(bf16[53,8,128]{2,1,0:T(8,128)(2,1)} %get-tuple-element.31), channel_id=1, source_target_pairs={{0,14},{1,15},{2,12},{3,13},{4,10},{5,11},{6,8},{7,9},{8,6},{9,7},... | collective-permute-start | bytes 325640 | tf_op jit(solution)/shard_map/ppermute | solution.py:396
  26.9 1.9 %collective-permute-start.9 = (bf16[53,8,128]{2,1,0:T(8,128)(2,1)}, bf16[53,8,128]{2,1,0:T(8,128)(2,1)S(1)}, u32[]{:S(2)}, u32[]{:S(2)}) collective-permute-start(bf16[53,8,128]{2,1,0:T(8,128)(2,1)} %get-tuple-element.35), channel_id=1, source_target_pairs={{0,5},{1,4},{2,7},{3,6},{4,1},{5,0},{6,3},{7,2},{8,13},{9,12},{10,... | collective-permute-start | bytes 325640 | tf_op jit(solution)/shard_map/ppermute | solution.py:396
  28.8 2.3 %collective-permute-start.10 = (bf16[53,8,128]{2,1,0:T(8,128)(2,1)}, bf16[53,8,128]{2,1,0:T(8,128)(2,1)S(1)}, u32[]{:S(2)}, u32[]{:S(2)}) collective-permute-start(bf16[53,8,128]{2,1,0:T(8,128)(2,1)} %get-tuple-element.36), channel_id=1, source_target_pairs={{0,6},{1,7},{2,4},{3,5},{4,2},{5,3},{6,0},{7,1},{8,14},{9,15},{10,... | collective-permute-start | bytes 325640 | tf_op jit(solution)/shard_map/ppermute | solution.py:396
  31.1 2.0 %collective-permute-start.11 = (bf16[53,8,128]{2,1,0:T(8,128)(2,1)}, bf16[53,8,128]{2,1,0:T(8,128)(2,1)S(1)}, u32[]{:S(2)}, u32[]{:S(2)}) collective-permute-start(bf16[53,8,128]{2,1,0:T(8,128)(2,1)} %get-tuple-element.37), channel_id=1, source_target_pairs={{0,7},{1,6},{2,5},{3,4},{4,3},{5,2},{6,1},{7,0},{8,15},{9,14},{10,... | collective-permute-start | bytes 325640 | tf_op jit(solution)/shard_map/ppermute | solution.py:396
  33.1 2.5 %collective-permute-start.13 = (bf16[48,8,128]{2,1,0:T(8,128)(2,1)}, bf16[48,8,128]{2,1,0:T(8,128)(2,1)S(1)}, u32[]{:S(2)}, u32[]{:S(2)}) collective-permute-start(bf16[48,8,128]{2,1,0:T(8,128)(2,1)} %get-tuple-element.42), channel_id=1, source_target_pairs={{0,11},{1,10},{2,9},{3,8},{4,15},{5,14},{6,13},{7,12},{8,3},{9,2},... | collective-permute-start | bytes 294920 | tf_op jit(solution)/shard_map/ppermute | solution.py:396
  35.6 0.9 %collective-permute-start.14 = (bf16[48,8,128]{2,1,0:T(8,128)(2,1)}, bf16[48,8,128]{2,1,0:T(8,128)(2,1)S(1)}, u32[]{:S(2)}, u32[]{:S(2)}) collective-permute-start(bf16[48,8,128]{2,1,0:T(8,128)(2,1)} %get-tuple-element.43), channel_id=1, source_target_pairs={{0,13},{1,12},{2,15},{3,14},{4,9},{5,8},{6,11},{7,10},{8,5},{9,4},... | collective-permute-start | bytes 294920 | tf_op jit(solution)/shard_map/ppermute | solution.py:396
  36.5 3.9 %collective-permute-start.15 = (bf16[48,8,128]{2,1,0:T(8,128)(2,1)}, bf16[48,8,128]{2,1,0:T(8,128)(2,1)S(1)}, u32[]{:S(2)}, u32[]{:S(2)}) collective-permute-start(bf16[48,8,128]{2,1,0:T(8,128)(2,1)} %get-tuple-element.44), channel_id=1, source_target_pairs={{0,15},{1,14},{2,13},{3,12},{4,11},{5,10},{6,9},{7,8},{8,7},{9,6},... | collective-permute-start | bytes 294920 | tf_op jit(solution)/shard_map/ppermute | solution.py:396
  40.4 0.1 collective-permute-done.10.rest_11_
  40.6 0.7 %reshape.19.offset_ref = s32[1,384]{1,0:T(1,128)S(1)} reshape(s32[384]{0:T(512)} %param.13) | data formatting | bytes 3072 | tf_op jit(solution)/shard_map/reshape | solution.py:454
  41.3 0.8 %copy.8.pairs_ref = s32[64,2]{1,0:T(8,128)S(1)} copy(s32[64,2]{0,1:T(2,128)} %param.10) | data formatting | bytes 1024 | tf_op args[3]
  42.0 0.3 collective-permute-done.11.rest_12_
  42.3 0.9 %copy-done = bf16[53,8,128]{2,1,0:T(8,128)(2,1)S(1)} copy-done((bf16[53,8,128]{2,1,0:T(8,128)(2,1)S(1)}, bf16[53,8,128]{2,1,0:T(8,128)(2,1)}, u32[]{:S(2)}) %copy-start) | copy-done | bytes 108568
  43.2 0.7 %copy-done.1 = f32[384,3]{0,1:T(4,128)S(1)} copy-done((f32[384,3]{0,1:T(4,128)S(1)}, f32[384,3]{0,1:T(4,128)}, u32[]{:S(2)}) %copy-start.1) | copy-done | bytes 4632
  43.9 0.7 %copy-done.2 = s32[64,2]{0,1:T(2,128)S(1)} copy-done((s32[64,2]{0,1:T(2,128)S(1)}, s32[64,2]{0,1:T(2,128)}, u32[]{:S(2)}) %copy-start.2) | copy-done | bytes 536
  44.6 6.4 %gains_and_sums.1 = (f32[8,128,384]{2,1,0:T(8,128)S(1)}, f32[64,128]{1,0:T(8,128)S(1)}, s32[16,128]{1,0:T(8,128)S(1)}, f32[3,64,8,128]{3,2,1,0:T(8,128)S(1)}) custom-call(s32[1]{0:T(128)} %bitcast.me_s.turn_s, s32[1]{0:T(128)} %bitcast.me_s.turn_s, s32[2,64]{1,0:T(2,128)S(1)} %bitcast.10, s32[64,2]{1,0:T(8,128)S(1)} %copy.8.pairs_ref, f32[3,384]{1,0:T(4,128)S(1)} %bitcast.9, ...), custom_call_target="tpu_custom_call" | custom-call | tf_op jit(solution)/shard_map/gains_and_sums/pallas_call | solution.py:426
  51.0 2.1 %sum_and_apply.1 = bf16[64,8,384]{2,1,0:T(8,128)(2,1)} custom-call(s32[16,128]{1,0:T(8,128)S(1)} %get-tuple-element.38.slots_s, f32[3,64,8,128]{3,2,1,0:T(8,128)S(1)} %get-tuple-element.39.sums_ref, f32[8,128,384]{2,1,0:T(8,128)S(1)} %get-tuple-element.40.gains_ref, f32[64,128]{1,0:T(8,128)S(1)} %get-tuple-element.41.recip_ref, ...), custom_call_target="tpu_custom_call" | custom-call | tf_op jit(solution)/shard_map/sum_and_apply/pallas_call | solution.py:458
  (20 shorter events, 0.2 us)
Async XLA Ops:
  3.2 9.1 %collective-permute-start.7 = (bf16[48,8,128]{2,1,0:T(8,128)(2,1)}, bf16[48,8,128]{2,1,0:T(8,128)(2,1)S(1)}, u32[]{:S(2)}, u32[]{:S(2)}) collective-permute-start(bf16[48,8,128]{2,1,0:T(8,128)(2,1)} %get-tuple-element.33), channel_id=1, source_target_pairs={{0,9},{1,8},{2,11},{3,10},{4,13},{5,12},{6,15},{7,14},{8,1},{9,0},... | collective-permute-start | bytes 294920 | tf_op jit(solution)/shard_map/ppermute | solution.py:396
  6.8 15.3 %collective-permute-start = (bf16[53,8,128]{2,1,0:T(8,128)(2,1)}, bf16[53,8,128]{2,1,0:T(8,128)(2,1)S(1)}, u32[]{:S(2)}, u32[]{:S(2)}) collective-permute-start(bf16[53,8,128]{2,1,0:T(8,128)(2,1)} %get-tuple-element.26), channel_id=1, source_target_pairs={{0,8},{1,9},{2,10},{3,11},{4,12},{5,13},{6,14},{7,15},{8,0},{9,1},... | collective-permute-start | bytes 325640 | tf_op jit(solution)/shard_map/ppermute | solution.py:396
  7.4 19.4 %collective-permute-start.1 = (bf16[53,8,128]{2,1,0:T(8,128)(2,1)}, bf16[53,8,128]{2,1,0:T(8,128)(2,1)S(1)}, u32[]{:S(2)}, u32[]{:S(2)}) collective-permute-start(bf16[53,8,128]{2,1,0:T(8,128)(2,1)} %get-tuple-element.27), channel_id=1, source_target_pairs={{0,10},{1,11},{2,8},{3,9},{4,14},{5,15},{6,12},{7,13},{8,2},{9,3},... | collective-permute-start | bytes 325640 | tf_op jit(solution)/shard_map/ppermute | solution.py:396
  10.6 16.2 %collective-permute-start.2 = (bf16[53,8,128]{2,1,0:T(8,128)(2,1)}, bf16[53,8,128]{2,1,0:T(8,128)(2,1)S(1)}, u32[]{:S(2)}, u32[]{:S(2)}) collective-permute-start(bf16[53,8,128]{2,1,0:T(8,128)(2,1)} %get-tuple-element.28), channel_id=1, source_target_pairs={{0,1},{1,0},{2,3},{3,2},{4,5},{5,4},{6,7},{7,6},{8,9},{9,8},{10,11... | collective-permute-start | bytes 325640 | tf_op jit(solution)/shard_map/ppermute | solution.py:396
  10.8 16.1 %collective-permute-start.3 = (bf16[53,8,128]{2,1,0:T(8,128)(2,1)}, bf16[53,8,128]{2,1,0:T(8,128)(2,1)S(1)}, u32[]{:S(2)}, u32[]{:S(2)}) collective-permute-start(bf16[53,8,128]{2,1,0:T(8,128)(2,1)} %get-tuple-element.29), channel_id=1, source_target_pairs={{0,12},{1,13},{2,14},{3,15},{4,8},{5,9},{6,10},{7,11},{8,4},{9,5},... | collective-permute-start | bytes 325640 | tf_op jit(solution)/shard_map/ppermute | solution.py:396
  12.3 16.5 %collective-permute-start.4 = (bf16[53,8,128]{2,1,0:T(8,128)(2,1)}, bf16[53,8,128]{2,1,0:T(8,128)(2,1)S(1)}, u32[]{:S(2)}, u32[]{:S(2)}) collective-permute-start(bf16[53,8,128]{2,1,0:T(8,128)(2,1)} %get-tuple-element.30), channel_id=1, source_target_pairs={{0,2},{1,3},{2,0},{3,1},{4,6},{5,7},{6,4},{7,5},{8,10},{9,11},{10,... | collective-permute-start | bytes 325640 | tf_op jit(solution)/shard_map/ppermute | solution.py:396
  22.1 9.0 %collective-permute-start.5 = (bf16[53,8,128]{2,1,0:T(8,128)(2,1)}, bf16[53,8,128]{2,1,0:T(8,128)(2,1)S(1)}, u32[]{:S(2)}, u32[]{:S(2)}) collective-permute-start(bf16[53,8,128]{2,1,0:T(8,128)(2,1)} %get-tuple-element.31), channel_id=1, source_target_pairs={{0,14},{1,15},{2,12},{3,13},{4,10},{5,11},{6,8},{7,9},{8,6},{9,7},... | collective-permute-start | bytes 325640 | tf_op jit(solution)/shard_map/ppermute | solution.py:396
  26.8 6.3 %collective-permute-start.6 = (bf16[53,8,128]{2,1,0:T(8,128)(2,1)}, bf16[53,8,128]{2,1,0:T(8,128)(2,1)S(1)}, u32[]{:S(2)}, u32[]{:S(2)}) collective-permute-start(bf16[53,8,128]{2,1,0:T(8,128)(2,1)} %get-tuple-element.32), channel_id=1, source_target_pairs={{0,3},{1,2},{2,1},{3,0},{4,7},{5,6},{6,5},{7,4},{8,11},{9,10},{10,... | collective-permute-start | bytes 325640 | tf_op jit(solution)/shard_map/ppermute | solution.py:396
  26.8 8.8 %collective-permute-start.8 = (bf16[53,8,128]{2,1,0:T(8,128)(2,1)}, bf16[53,8,128]{2,1,0:T(8,128)(2,1)S(1)}, u32[]{:S(2)}, u32[]{:S(2)}) collective-permute-start(bf16[53,8,128]{2,1,0:T(8,128)(2,1)} %get-tuple-element.34), channel_id=1, source_target_pairs={{0,4},{1,5},{2,6},{3,7},{4,0},{5,1},{6,2},{7,3},{8,12},{9,13},{10,... | collective-permute-start | bytes 325640 | tf_op jit(solution)/shard_map/ppermute | solution.py:396
  26.9 9.6 %collective-permute-start.9 = (bf16[53,8,128]{2,1,0:T(8,128)(2,1)}, bf16[53,8,128]{2,1,0:T(8,128)(2,1)S(1)}, u32[]{:S(2)}, u32[]{:S(2)}) collective-permute-start(bf16[53,8,128]{2,1,0:T(8,128)(2,1)} %get-tuple-element.35), channel_id=1, source_target_pairs={{0,5},{1,4},{2,7},{3,6},{4,1},{5,0},{6,3},{7,2},{8,13},{9,12},{10,... | collective-permute-start | bytes 325640 | tf_op jit(solution)/shard_map/ppermute | solution.py:396
  28.8 11.8 %collective-permute-start.10 = (bf16[53,8,128]{2,1,0:T(8,128)(2,1)}, bf16[53,8,128]{2,1,0:T(8,128)(2,1)S(1)}, u32[]{:S(2)}, u32[]{:S(2)}) collective-permute-start(bf16[53,8,128]{2,1,0:T(8,128)(2,1)} %get-tuple-element.36), channel_id=1, source_target_pairs={{0,6},{1,7},{2,4},{3,5},{4,2},{5,3},{6,0},{7,1},{8,14},{9,15},{10,... | collective-permute-start | bytes 325640 | tf_op jit(solution)/shard_map/ppermute | solution.py:396
  31.1 11.2 %collective-permute-start.11 = (bf16[53,8,128]{2,1,0:T(8,128)(2,1)}, bf16[53,8,128]{2,1,0:T(8,128)(2,1)S(1)}, u32[]{:S(2)}, u32[]{:S(2)}) collective-permute-start(bf16[53,8,128]{2,1,0:T(8,128)(2,1)} %get-tuple-element.37), channel_id=1, source_target_pairs={{0,7},{1,6},{2,5},{3,4},{4,3},{5,2},{6,1},{7,0},{8,15},{9,14},{10,... | collective-permute-start | bytes 325640 | tf_op jit(solution)/shard_map/ppermute | solution.py:396
  33.1 17.8 %collective-permute-start.13 = (bf16[48,8,128]{2,1,0:T(8,128)(2,1)}, bf16[48,8,128]{2,1,0:T(8,128)(2,1)S(1)}, u32[]{:S(2)}, u32[]{:S(2)}) collective-permute-start(bf16[48,8,128]{2,1,0:T(8,128)(2,1)} %get-tuple-element.42), channel_id=1, source_target_pairs={{0,11},{1,10},{2,9},{3,8},{4,15},{5,14},{6,13},{7,12},{8,3},{9,2},... | collective-permute-start | bytes 294920 | tf_op jit(solution)/shard_map/ppermute | solution.py:396
  35.6 15.4 %collective-permute-start.14 = (bf16[48,8,128]{2,1,0:T(8,128)(2,1)}, bf16[48,8,128]{2,1,0:T(8,128)(2,1)S(1)}, u32[]{:S(2)}, u32[]{:S(2)}) collective-permute-start(bf16[48,8,128]{2,1,0:T(8,128)(2,1)} %get-tuple-element.43), channel_id=1, source_target_pairs={{0,13},{1,12},{2,15},{3,14},{4,9},{5,8},{6,11},{7,10},{8,5},{9,4},... | collective-permute-start | bytes 294920 | tf_op jit(solution)/shard_map/ppermute | solution.py:396
  36.5 14.5 %collective-permute-start.15 = (bf16[48,8,128]{2,1,0:T(8,128)(2,1)}, bf16[48,8,128]{2,1,0:T(8,128)(2,1)S(1)}, u32[]{:S(2)}, u32[]{:S(2)}) collective-permute-start(bf16[48,8,128]{2,1,0:T(8,128)(2,1)} %get-tuple-element.44), channel_id=1, source_target_pairs={{0,15},{1,14},{2,13},{3,12},{4,11},{5,10},{6,9},{7,8},{8,7},{9,6},... | collective-permute-start | bytes 294920 | tf_op jit(solution)/shard_map/ppermute | solution.py:396
  40.6 1.7 %collective-permute-start.12 = (bf16[20,8,128]{2,1,0:T(8,128)(2,1)S(1)}, bf16[20,8,128]{2,1,0:T(8,128)(2,1)S(1)}, u32[]{:S(2)}, u32[]{:S(2)}) collective-permute-start(bf16[20,8,128]{2,1,0:T(8,128)(2,1)S(1)} %collect_gains.1), channel_id=1, source_target_pairs={{0,1},{1,0},{2,3},{3,2},{4,5},{5,4},{6,7},{7,6},{8,9},{9,8},{10,11... | collective-permute-start | bytes 122888 | tf_op jit(solution)/shard_map/ppermute | solution.py:396
  42.3 0.9 %copy-start = (bf16[53,8,128]{2,1,0:T(8,128)(2,1)S(1)}, bf16[53,8,128]{2,1,0:T(8,128)(2,1)}, u32[]{:S(2)}) copy-start(bf16[53,8,128]{2,1,0:T(8,128)(2,1)} %get-tuple-element.25.rest_0_) | copy-start | bytes 325636
  43.2 0.7 %copy-start.1 = (f32[384,3]{0,1:T(4,128)S(1)}, f32[384,3]{0,1:T(4,128)}, u32[]{:S(2)}) copy-start(f32[384,3]{0,1:T(4,128)} %param.12) | copy-start | bytes 13828
  43.9 0.7 %copy-start.2 = (s32[64,2]{0,1:T(2,128)S(1)}, s32[64,2]{0,1:T(2,128)}, u32[]{:S(2)}) copy-start(s32[64,2]{0,1:T(2,128)} %param.10) | copy-start | bytes 1540

commit v9 on v8

--- a/solution.py
+++ b/solution.py
@@ -115,15 +115,36 @@
         send.wait()
 
 
-def collect_kernel(at, depth, *rest):
-    blocks, (out_ref, sems) = rest[:-2], rest[-2:]
+def interpolation(weights, offset, high_ref, low_ref):
+    channels = weights.shape[1]
+    index = lax.broadcasted_iota(jnp.int32, (LANES, channels), 0)
+    knot = (index & 63) >> 3
+    basis = jnp.zeros((LANES, channels), jnp.float32)
+    for step in range(3):
+        basis = basis + jnp.where(knot == offset + step, weights[step : step + 1, :], 0.0)
+    high = basis.astype(jnp.bfloat16).astype(jnp.float32)
+    low = basis - high
+    part = index & 7
+    for j in range(8):
+        high_ref[j] = jnp.where(part == j, high, 0.0).astype(jnp.bfloat16)
+        low_ref[j] = jnp.where(part == j, low, 0.0).astype(jnp.bfloat16)
+
+
+def collect_kernel(
+    at, depth, pairs_ref, weights_ref, offset_ref, own_ref, *rest
+):
+    blocks = rest[:-6]
+    out_ref, own_out_ref, pairs_out_ref, high_ref, low_ref, sems = rest[-6:]
     moves = start_all(
         [
             (block.at[pl.ds(at, depth)], out_ref.at[pl.ds(i * depth, depth)])
             for i, block in enumerate(blocks)
-        ],
+        ]
+        + [(own_ref, own_out_ref)],
         sems,
     )
+    pairs_out_ref[...] = pairs_ref[...]
+    interpolation(weights_ref[...], offset_ref[...], high_ref, low_ref)
     for move in moves:
         move.wait()
 
@@ -170,9 +191,8 @@
     turn_s,
     me_s,
     pairs_s,
-    pairs_ref,
-    weights_ref,
-    offset_ref,
+    high_ref,
+    low_ref,
     *rest,
 ):
     arrived, passed = dict(zip(order, rest)), rest[len(order)]
@@ -180,7 +200,7 @@
     metas_ref, table_ref, pick_ref, rows_ref, codes_ref, slots_s, slots_v, sems = rest[-8:]
     devices, depth, _, _ = metas_ref.shape
     owned = recip_ref.shape[0]
-    channels = weights_ref.shape[1]
+    channels = high_ref.shape[2]
     half = stations // 2
     gain_tiles = (depth - 1) // 2
     chunks = channels // LANES
@@ -223,40 +243,31 @@
     recip_ref[...] = jnp.broadcast_to(1.0 / jnp.maximum(tally, 1.0), recip_ref.shape)
 
     turn = turn_s[0]
+    column = lax.broadcasted_iota(jnp.int32, (1, LANES), 1)
+    used = (column & 63) < USED
+    upper = (column >> 6).astype(jnp.int32)
 
     def pick(b, carry):
         for side in range(2):
             s = pairs_s[side, b]
             d = s // stations
             within = s - d * stations
-            row = jnp.where(within >= half, within - half, within)
-            pick_ref[pl.ds(side * owned + b, 1), :] = table_ref[d ^ turn, pl.ds(row, 1), :]
+            second = jnp.where(within >= half, 1, 0)
+            row = table_ref[d ^ turn, pl.ds(within - second * half, 1), :]
+            keep = jnp.logical_and(used, upper == second)
+            pick_ref[pl.ds(side * owned + b, 1), :] = jnp.where(keep, row, 0.0)
         return carry
 
     lax.fori_loop(0, owned, pick, 0, unroll=4)
-
-    knot = (lax.broadcasted_iota(jnp.int32, (LANES, channels), 0) & 63) >> 3
-    basis = jnp.zeros((LANES, channels), jnp.float32)
-    for step in range(3):
-        basis = basis + jnp.where(
-            knot == offset_ref[...] + step, weights_ref[step : step + 1, :], 0.0
-        )
-    part = lax.broadcasted_iota(jnp.int32, (LANES, channels), 0) & 7
-    column = lax.broadcasted_iota(jnp.int32, (owned, LANES), 1)
-    used = (column & 63) < USED
-    picked = []
-    for side in range(2):
-        within = lax.rem(pairs_ref[:, side : side + 1], stations)
-        keep = jnp.logical_and(used, (column >= 64) == (within >= half))
-        picked.append(jnp.where(keep, pick_ref[side * owned : (side + 1) * owned, :], 0.0))
-    both = jnp.concatenate(picked, axis=0)
+    both = pick_ref[...]
+    both_high = both.astype(jnp.bfloat16)
+    both_low = (both - both_high.astype(jnp.float32)).astype(jnp.bfloat16)
+    both_two = jnp.concatenate([both_high, both_low], axis=1)
     for j in range(8):
+        high = high_ref[j]
         fine = jnp.dot(
-            both,
-            jnp.where(part == j, basis, 0.0),
-            precision=lax.Precision.HIGHEST,
-            preferred_element_type=jnp.float32,
-        )
+            both_two, jnp.concatenate([high, high], axis=0), preferred_element_type=jnp.float32
+        ) + jnp.dot(both_high, low_ref[j], preferred_element_type=jnp.float32)
         gains_ref[j] = fine.astype(jnp.bfloat16).astype(jnp.float32)
 
     for c in range(sums_ref.shape[0]):
@@ -358,8 +369,9 @@
     block = (chunks * capacity, parts, LANES)
     rows_at = chunks * capacity
     if halves:
+        wide = with_gains(near) + [near + 1, near + 3]
         outs = [
-            shape((rows_at + (depth if x in with_gains(near) else 0), parts, LANES), bf16)
+            shape((rows_at + (depth if x in wide else 0), parts, LANES), bf16)
             for x in range(devices)
         ]
     else:
@@ -392,6 +404,10 @@
         coarse,
     )
 
+    pairs = baseline_station_pairs.T
+    weights = band_weights.T
+    offset = band_offset.reshape(1, channels)
+
     def swap(array, x):
         return lax.ppermute(array, "bl", [(d, d ^ x) for d in range(devices)])
 
@@ -400,28 +416,43 @@
         for x in range(1, devices):
             arrived[x] = swap(sent[x], x)
         even = list(range(near, devices, 2))
-        collected = pl.pallas_call(
+        collected, own, pairs, high, low = pl.pallas_call(
             functools.partial(collect_kernel, rows_at, depth),
-            out_shape=shape((len(even) * depth, parts, LANES), bf16),
-            in_specs=[anywhere] * len(even),
-            out_specs=vmem,
-            scratch_shapes=[dma((len(even),))],
+            out_shape=[
+                shape((len(even) * depth, parts, LANES), bf16),
+                shape(sent[0].shape, bf16),
+                shape((2, owned), i32),
+            ]
+            + [shape((parts, LANES, channels), bf16)] * 2,
+            in_specs=[vmem] * 3 + [anywhere] * (1 + len(even)),
+            out_specs=[vmem] * 5,
+            scratch_shapes=[dma((1 + len(even),))],
             compiler_params=some,
             name="collect_gains",
-        )(*[arrived[x] for x in even])
+        )(pairs, weights, offset, sent[0], *[arrived[x] for x in even])
+        arrived[0] = own
         passed = swap(collected, 1)
-        order = [0]
         cross = even + [x + 1 for x in even]
-        for i, x in enumerate(cross[: near // 2 + 1]):
-            order += [x] + ([i] if 0 < i < near // 2 else [])
-        order += [x for x in range(1, near) if x not in order]
-        late = [x for x in cross if x not in order]
+        late = cross[near // 2 + 2 :]
+        close = list(range(1, near))
+        order = [0, cross[0]]
+        for x in cross[1 : near // 2 + 2]:
+            order += [x, close.pop(0)]
+        order += close
     else:
         arrived = {
             0: lax.all_gather(sent[1], "bl", axis=0),
             1: lax.all_to_all(sent[0], "bl", split_axis=0, concat_axis=0, tiled=True),
         }
         order, late, passed = [0], [1], arrived[0]
+        high, low = pl.pallas_call(
+            lambda w, o, h, l: interpolation(w[...], o[...], h, l),
+            out_shape=[shape((parts, LANES, channels), bf16)] * 2,
+            in_specs=[vmem] * 2,
+            out_specs=[vmem] * 2,
+            compiler_params=some,
+            name="interpolation",
+        )(weights, offset)
 
     gains, recip, slots, sums = pl.pallas_call(
         functools.partial(prepare_kernel, capacity, near, stations, order),
@@ -431,7 +462,7 @@
             shape((devices, LANES), i32),
             shape((chunks, owned, parts, LANES), f32),
         ),
-        in_specs=[smem, smem, smem, vmem, vmem, vmem, hbm] + [anywhere] * len(order),
+        in_specs=[smem, smem, smem, vmem, vmem] + [anywhere] * (1 + len(order)),
         out_specs=(vmem,) * 4,
         scratch_shapes=[
             pltpu.VMEM((devices, depth, SUB, LANES), bf16),
@@ -448,10 +479,9 @@
     )(
         turn,
         me,
-        baseline_station_pairs.T,
-        baseline_station_pairs,
-        band_weights.T,
-        band_offset.reshape(1, channels),
+        pairs,
+        high,
+        low,
         *[arrived[x] for x in order],
         passed,
     )

time: 53.9 us -> 55 us (1.020)
  waiting for transfers between devices: 1.2 us -> 15 us
  starting transfers between devices: 36.3 us -> 24.3 us
  local copies, waits for them, and re-layouts: 3.72 us -> 2.95 us
    ppermute x16, waiting for transfers between devices: 1.2 us -> 15 us  [swap(): return lax.ppermute(array, 'bl', [(d, d ^ x) for d in range(devices)])]
    ppermute x16, starting transfers between devices: 36.3 us -> 24.3 us  [swap(): return lax.ppermute(array, 'bl', [(d, d ^ x) for d in range(devices)])]
    unnamed x7 -> x6, local copies, waits for them, and re-layouts: 3.03 us -> 2.27 us
  transfers between devices with their start and end apart: 16 -> 16, of which waited for: 3 -> 5; matrix products, arithmetic and copies ran while one was open for 3% -> 1% of each run, Pallas kernels for 12% -> 12%
where the time goes in v9:
time: 55 us; the launch traced here: 54.1 us
  starting transfers between devices  24.3 us (44%)
  waiting for transfers between devices  15 us (27%)
  Pallas kernels  11.7 us (21%)
  local copies, waits for them, and re-layouts  2.95 us (5%)
    ppermute x16, starting transfers between devices, swap(): return lax.ppermute(array, 'bl', [(d, d ^ x) for d in range(devices)])  24.3 us
    ppermute x16, waiting for transfers between devices, swap(): return lax.ppermute(array, 'bl', [(d, d ^ x) for d in range(devices)])  15 us
    pallas_call x1, Pallas kernels, on_device(): pl.pallas_call(functools.partial(prepare_kernel, capacity, near, stations...  5.87 us
    pallas_call x1, Pallas kernels, on_device(): pl.pallas_call(functools.partial(pack_kernel, capacity, near), out_shape=...  3.22 us
    unnamed x6, local copies, waits for them, and re-layouts  2.27 us
    pallas_call x1, Pallas kernels, on_device(): pl.pallas_call(functools.partial(finish_kernel, capacity, late), out_shap...  2.09 us
  transfers between devices with their start and end apart: 16, of which 5 were waited for; matrix products, arithmetic and copies ran while one was open for 1% of the time, Pallas kernels for 12%

profile of v9, /device:TPU:0, one launch (start us, length us, event | category | flops | bytes accessed | tf_op | source)
XLA Modules:
  0.0 54.1 jit_solution(5483060046847332475)
XLA Ops:
  0.0 3.2 %pack_rows.1 = (bf16[53,8,128]{2,1,0:T(8,128)(2,1)}, bf16[53,8,128]{2,1,0:T(8,128)(2,1)}, bf16[53,8,128]{2,1,0:T(8,128)(2,1)}, bf16[53,8,128]{2,1,0:T(8,128)(2,1...) custom-call(s32[1]{0:T(128)} %bitcast.me_s.turn_s, ...), custom_call_target="tpu_custom_call" | custom-call | tf_op jit(solution)/shard_map/pack_rows/pallas_call | solution.py:379
  3.2 4.1 %collective-permute-start = (bf16[53,8,128]{2,1,0:T(8,128)(2,1)}, bf16[53,8,128]{2,1,0:T(8,128)(2,1)S(1)}, u32[]{:S(2)}, u32[]{:S(2)}) collective-permute-start(bf16[53,8,128]{2,1,0:T(8,128)(2,1)} %get-tuple-element.31), channel_id=1, source_target_pairs={{0,8},{1,9},{2,10},{3,11},{4,12},{5,13},{6,14},{7,15},{8,0},{9,1},... | collective-permute-start | bytes 325640 | tf_op jit(solution)/shard_map/ppermute | solution.py:412
  7.3 1.3 %collective-permute-start.1 = (bf16[53,8,128]{2,1,0:T(8,128)(2,1)}, bf16[53,8,128]{2,1,0:T(8,128)(2,1)S(1)}, u32[]{:S(2)}, u32[]{:S(2)}) collective-permute-start(bf16[53,8,128]{2,1,0:T(8,128)(2,1)} %get-tuple-element.32), channel_id=1, source_target_pairs={{0,10},{1,11},{2,8},{3,9},{4,14},{5,15},{6,12},{7,13},{8,2},{9,3},... | collective-permute-start | bytes 325640 | tf_op jit(solution)/shard_map/ppermute | solution.py:412
  8.6 3.6 %collective-permute-start.2 = (bf16[53,8,128]{2,1,0:T(8,128)(2,1)}, bf16[53,8,128]{2,1,0:T(8,128)(2,1)S(1)}, u32[]{:S(2)}, u32[]{:S(2)}) collective-permute-start(bf16[53,8,128]{2,1,0:T(8,128)(2,1)} %get-tuple-element.33), channel_id=1, source_target_pairs={{0,12},{1,13},{2,14},{3,15},{4,8},{5,9},{6,10},{7,11},{8,4},{9,5},... | collective-permute-start | bytes 325640 | tf_op jit(solution)/shard_map/ppermute | solution.py:412
  12.2 8.5 %collective-permute-done.rest_0_.rest_1_ = bf16[53,8,128]{2,1,0:T(8,128)(2,1)S(1)} collective-permute-done((bf16[53,8,128]{2,1,0:T(8,128)(2,1)}, bf16[53,8,128]{2,1,0:T(8,128)(2,1)S(1)}, u32[]{:S(2)}, u32[]{:S(2)}) %collective-permute-start) | collective-permute-done | bytes 108576 | tf_op jit(solution)/shard_map/ppermute | solution.py:412
  20.7 1.9 %collective-permute-start.5 = (bf16[53,8,128]{2,1,0:T(8,128)(2,1)}, bf16[53,8,128]{2,1,0:T(8,128)(2,1)S(1)}, u32[]{:S(2)}, u32[]{:S(2)}) collective-permute-start(bf16[53,8,128]{2,1,0:T(8,128)(2,1)} %get-tuple-element.40), channel_id=1, source_target_pairs={{0,2},{1,3},{2,0},{3,1},{4,6},{5,7},{6,4},{7,5},{8,10},{9,11},{10,... | collective-permute-start | bytes 325640 | tf_op jit(solution)/shard_map/ppermute | solution.py:412
  22.6 1.7 %collective-permute-done.1.rest_1_.rest_2_ = bf16[53,8,128]{2,1,0:T(8,128)(2,1)S(1)} collective-permute-done((bf16[53,8,128]{2,1,0:T(8,128)(2,1)}, bf16[53,8,128]{2,1,0:T(8,128)(2,1)S(1)}, u32[]{:S(2)}, u32[]{:S(2)}) %collective-permute-start.1) | collective-permute-done | bytes 108576 | tf_op jit(solution)/shard_map/ppermute | solution.py:412
  24.3 2.4 %collective-permute-start.7 = (bf16[53,8,128]{2,1,0:T(8,128)(2,1)}, bf16[53,8,128]{2,1,0:T(8,128)(2,1)S(1)}, u32[]{:S(2)}, u32[]{:S(2)}) collective-permute-start(bf16[53,8,128]{2,1,0:T(8,128)(2,1)} %get-tuple-element.42), channel_id=1, source_target_pairs={{0,9},{1,8},{2,11},{3,10},{4,13},{5,12},{6,15},{7,14},{8,1},{9,0},... | collective-permute-start | bytes 325640 | tf_op jit(solution)/shard_map/ppermute | solution.py:412
  26.8 1.7 %collective-permute-start.8 = (bf16[53,8,128]{2,1,0:T(8,128)(2,1)}, bf16[53,8,128]{2,1,0:T(8,128)(2,1)S(1)}, u32[]{:S(2)}, u32[]{:S(2)}) collective-permute-start(bf16[53,8,128]{2,1,0:T(8,128)(2,1)} %get-tuple-element.43), channel_id=1, source_target_pairs={{0,4},{1,5},{2,6},{3,7},{4,0},{5,1},{6,2},{7,3},{8,12},{9,13},{10,... | collective-permute-start | bytes 325640 | tf_op jit(solution)/shard_map/ppermute | solution.py:412
  28.5 1.5 %collective-permute-start.9 = (bf16[53,8,128]{2,1,0:T(8,128)(2,1)}, bf16[53,8,128]{2,1,0:T(8,128)(2,1)S(1)}, u32[]{:S(2)}, u32[]{:S(2)}) collective-permute-start(bf16[53,8,128]{2,1,0:T(8,128)(2,1)} %get-tuple-element.44), channel_id=1, source_target_pairs={{0,11},{1,10},{2,9},{3,8},{4,15},{5,14},{6,13},{7,12},{8,3},{9,2},... | collective-permute-start | bytes 325640 | tf_op jit(solution)/shard_map/ppermute | solution.py:412
  30.1 2.2 %collective-permute-start.10 = (bf16[53,8,128]{2,1,0:T(8,128)(2,1)}, bf16[53,8,128]{2,1,0:T(8,128)(2,1)S(1)}, u32[]{:S(2)}, u32[]{:S(2)}) collective-permute-start(bf16[53,8,128]{2,1,0:T(8,128)(2,1)} %get-tuple-element.45), channel_id=1, source_target_pairs={{0,5},{1,4},{2,7},{3,6},{4,1},{5,0},{6,3},{7,2},{8,13},{9,12},{10,... | collective-permute-start | bytes 325640 | tf_op jit(solution)/shard_map/ppermute | solution.py:412
  32.2 0.9 %collective-permute-start.11 = (bf16[53,8,128]{2,1,0:T(8,128)(2,1)}, bf16[53,8,128]{2,1,0:T(8,128)(2,1)S(1)}, u32[]{:S(2)}, u32[]{:S(2)}) collective-permute-start(bf16[53,8,128]{2,1,0:T(8,128)(2,1)} %get-tuple-element.46), channel_id=1, source_target_pairs={{0,6},{1,7},{2,4},{3,5},{4,2},{5,3},{6,0},{7,1},{8,14},{9,15},{10,... | collective-permute-start | bytes 325640 | tf_op jit(solution)/shard_map/ppermute | solution.py:412
  33.2 1.0 %collective-permute-start.12 = (bf16[53,8,128]{2,1,0:T(8,128)(2,1)}, bf16[53,8,128]{2,1,0:T(8,128)(2,1)S(1)}, u32[]{:S(2)}, u32[]{:S(2)}) collective-permute-start(bf16[53,8,128]{2,1,0:T(8,128)(2,1)} %get-tuple-element.47), channel_id=1, source_target_pairs={{0,7},{1,6},{2,5},{3,4},{4,3},{5,2},{6,1},{7,0},{8,15},{9,14},{10,... | collective-permute-start | bytes 325640 | tf_op jit(solution)/shard_map/ppermute | solution.py:412
  34.2 2.2 %collective-permute-done.8.rest_9_ = bf16[53,8,128]{2,1,0:T(8,128)(2,1)S(1)} collective-permute-done((bf16[53,8,128]{2,1,0:T(8,128)(2,1)}, bf16[53,8,128]{2,1,0:T(8,128)(2,1)S(1)}, u32[]{:S(2)}, u32[]{:S(2)}) %collective-permute-start.8) | collective-permute-done | bytes 108576 | tf_op jit(solution)/shard_map/ppermute | solution.py:412
  36.4 1.7 %collective-permute-done.9.rest_10_ = bf16[53,8,128]{2,1,0:T(8,128)(2,1)S(1)} collective-permute-done((bf16[53,8,128]{2,1,0:T(8,128)(2,1)}, bf16[53,8,128]{2,1,0:T(8,128)(2,1)S(1)}, u32[]{:S(2)}, u32[]{:S(2)}) %collective-permute-start.9) | collective-permute-done | bytes 108576 | tf_op jit(solution)/shard_map/ppermute | solution.py:412
  38.1 3.0 %collective-permute-start.15 = (bf16[48,8,128]{2,1,0:T(8,128)(2,1)}, bf16[48,8,128]{2,1,0:T(8,128)(2,1)S(1)}, u32[]{:S(2)}, u32[]{:S(2)}) collective-permute-start(bf16[48,8,128]{2,1,0:T(8,128)(2,1)} %get-tuple-element.54), channel_id=1, source_target_pairs={{0,15},{1,14},{2,13},{3,12},{4,11},{5,10},{6,9},{7,8},{8,7},{9,6},... | collective-permute-start | bytes 294920 | tf_op jit(solution)/shard_map/ppermute | solution.py:412
  41.1 0.7 %reshape.19.offset_ref = s32[1,384]{1,0:T(1,128)S(1)} reshape(s32[384]{0:T(512)} %param.13) | data formatting | bytes 3072 | tf_op jit(solution)/shard_map/reshape | solution.py:409
  41.8 0.9 %copy-done = bf16[53,8,128]{2,1,0:T(8,128)(2,1)S(1)} copy-done((bf16[53,8,128]{2,1,0:T(8,128)(2,1)S(1)}, bf16[53,8,128]{2,1,0:T(8,128)(2,1)}, u32[]{:S(2)}) %copy-start) | copy-done | bytes 108568
  42.7 0.7 %copy-done.1 = f32[384,3]{0,1:T(4,128)S(1)} copy-done((f32[384,3]{0,1:T(4,128)S(1)}, f32[384,3]{0,1:T(4,128)}, u32[]{:S(2)}) %copy-start.1) | copy-done | bytes 4632
  43.3 0.7 %copy-done.2 = s32[64,2]{0,1:T(2,128)S(1)} copy-done((s32[64,2]{0,1:T(2,128)S(1)}, s32[64,2]{0,1:T(2,128)}, u32[]{:S(2)}) %copy-start.2) | copy-done | bytes 536
  44.5 0.7 %collective-permute-start.13 = (bf16[20,8,128]{2,1,0:T(8,128)(2,1)S(1)}, bf16[20,8,128]{2,1,0:T(8,128)(2,1)S(1)}, u32[]{:S(2)}, u32[]{:S(2)}) collective-permute-start(bf16[20,8,128]{2,1,0:T(8,128)(2,1)S(1)} %get-tuple-element.48), channel_id=1, source_target_pairs={{0,1},{1,0},{2,3},{3,2},{4,5},{5,4},{6,7},{7,6},{8,9},{9,8},{10,11... | collective-permute-start | bytes 122888 | tf_op jit(solution)/shard_map/ppermute | solution.py:412
  45.2 0.9 %collective-permute-done.13.rest_14_ = bf16[20,8,128]{2,1,0:T(8,128)(2,1)S(1)} collective-permute-done((bf16[20,8,128]{2,1,0:T(8,128)(2,1)S(1)}, bf16[20,8,128]{2,1,0:T(8,128)(2,1)S(1)}, u32[]{:S(2)}, u32[]{:S(2)}) %collective-permute-start.13) | collective-permute-done | bytes 40992 | tf_op jit(solution)/shard_map/ppermute | solution.py:412
  46.1 5.9 %gains_and_sums.1 = (f32[8,128,384]{2,1,0:T(8,128)S(1)}, f32[64,128]{1,0:T(8,128)S(1)}, s32[16,128]{1,0:T(8,128)S(1)}, f32[3,64,8,128]{3,2,1,0:T(8,128)S(1)}) custom-call(s32[1]{0:T(128)} %bitcast.me_s.turn_s, s32[1]{0:T(128)} %bitcast.me_s.turn_s, s32[2,64]{1,0:T(2,128)S(1)} %get-tuple-element.35.pairs_s, ...), custom_call_target="tpu_custom_call" | custom-call | tf_op jit(solution)/shard_map/gains_and_sums/pallas_call | solution.py:457
  52.0 2.1 %sum_and_apply.1 = bf16[64,8,384]{2,1,0:T(8,128)(2,1)} custom-call(s32[16,128]{1,0:T(8,128)S(1)} %get-tuple-element.49.slots_s, f32[3,64,8,128]{3,2,1,0:T(8,128)S(1)} %get-tuple-element.50.sums_ref, f32[8,128,384]{2,1,0:T(8,128)S(1)} %get-tuple-element.51.gains_ref, f32[64,128]{1,0:T(8,128)S(1)} %get-tuple-element.52.recip_ref, ...), custom_call_target="tpu_custom_call" | custom-call | tf_op jit(solution)/shard_map/sum_and_apply/pallas_call | solution.py:488
  (19 shorter events, 0.5 us)
Async XLA Ops:
  3.2 17.5 %collective-permute-start = (bf16[53,8,128]{2,1,0:T(8,128)(2,1)}, bf16[53,8,128]{2,1,0:T(8,128)(2,1)S(1)}, u32[]{:S(2)}, u32[]{:S(2)}) collective-permute-start(bf16[53,8,128]{2,1,0:T(8,128)(2,1)} %get-tuple-element.31), channel_id=1, source_target_pairs={{0,8},{1,9},{2,10},{3,11},{4,12},{5,13},{6,14},{7,15},{8,0},{9,1},... | collective-permute-start | bytes 325640 | tf_op jit(solution)/shard_map/ppermute | solution.py:412
  7.3 17.0 %collective-permute-start.1 = (bf16[53,8,128]{2,1,0:T(8,128)(2,1)}, bf16[53,8,128]{2,1,0:T(8,128)(2,1)S(1)}, u32[]{:S(2)}, u32[]{:S(2)}) collective-permute-start(bf16[53,8,128]{2,1,0:T(8,128)(2,1)} %get-tuple-element.32), channel_id=1, source_target_pairs={{0,10},{1,11},{2,8},{3,9},{4,14},{5,15},{6,12},{7,13},{8,2},{9,3},... | collective-permute-start | bytes 325640 | tf_op jit(solution)/shard_map/ppermute | solution.py:412
  8.6 15.7 %collective-permute-start.2 = (bf16[53,8,128]{2,1,0:T(8,128)(2,1)}, bf16[53,8,128]{2,1,0:T(8,128)(2,1)S(1)}, u32[]{:S(2)}, u32[]{:S(2)}) collective-permute-start(bf16[53,8,128]{2,1,0:T(8,128)(2,1)} %get-tuple-element.33), channel_id=1, source_target_pairs={{0,12},{1,13},{2,14},{3,15},{4,8},{5,9},{6,10},{7,11},{8,4},{9,5},... | collective-permute-start | bytes 325640 | tf_op jit(solution)/shard_map/ppermute | solution.py:412
  12.2 14.6 %collective-permute-start.3 = (bf16[53,8,128]{2,1,0:T(8,128)(2,1)}, bf16[53,8,128]{2,1,0:T(8,128)(2,1)S(1)}, u32[]{:S(2)}, u32[]{:S(2)}) collective-permute-start(bf16[53,8,128]{2,1,0:T(8,128)(2,1)} %get-tuple-element.34), channel_id=1, source_target_pairs={{0,14},{1,15},{2,12},{3,13},{4,10},{5,11},{6,8},{7,9},{8,6},{9,7},... | collective-permute-start | bytes 325640 | tf_op jit(solution)/shard_map/ppermute | solution.py:412
  12.2 16.3 %collective-permute-start.4 = (bf16[53,8,128]{2,1,0:T(8,128)(2,1)}, bf16[53,8,128]{2,1,0:T(8,128)(2,1)S(1)}, u32[]{:S(2)}, u32[]{:S(2)}) collective-permute-start(bf16[53,8,128]{2,1,0:T(8,128)(2,1)} %get-tuple-element.39), channel_id=1, source_target_pairs={{0,1},{1,0},{2,3},{3,2},{4,5},{5,4},{6,7},{7,6},{8,9},{9,8},{10,11... | collective-permute-start | bytes 325640 | tf_op jit(solution)/shard_map/ppermute | solution.py:412
  20.7 9.4 %collective-permute-start.5 = (bf16[53,8,128]{2,1,0:T(8,128)(2,1)}, bf16[53,8,128]{2,1,0:T(8,128)(2,1)S(1)}, u32[]{:S(2)}, u32[]{:S(2)}) collective-permute-start(bf16[53,8,128]{2,1,0:T(8,128)(2,1)} %get-tuple-element.40), channel_id=1, source_target_pairs={{0,2},{1,3},{2,0},{3,1},{4,6},{5,7},{6,4},{7,5},{8,10},{9,11},{10,... | collective-permute-start | bytes 325640 | tf_op jit(solution)/shard_map/ppermute | solution.py:412
  24.3 7.9 %collective-permute-start.6 = (bf16[53,8,128]{2,1,0:T(8,128)(2,1)}, bf16[53,8,128]{2,1,0:T(8,128)(2,1)S(1)}, u32[]{:S(2)}, u32[]{:S(2)}) collective-permute-start(bf16[53,8,128]{2,1,0:T(8,128)(2,1)} %get-tuple-element.41), channel_id=1, source_target_pairs={{0,3},{1,2},{2,1},{3,0},{4,7},{5,6},{6,5},{7,4},{8,11},{9,10},{10,... | collective-permute-start | bytes 325640 | tf_op jit(solution)/shard_map/ppermute | solution.py:412
  24.3 8.9 %collective-permute-start.7 = (bf16[53,8,128]{2,1,0:T(8,128)(2,1)}, bf16[53,8,128]{2,1,0:T(8,128)(2,1)S(1)}, u32[]{:S(2)}, u32[]{:S(2)}) collective-permute-start(bf16[53,8,128]{2,1,0:T(8,128)(2,1)} %get-tuple-element.42), channel_id=1, source_target_pairs={{0,9},{1,8},{2,11},{3,10},{4,13},{5,12},{6,15},{7,14},{8,1},{9,0},... | collective-permute-start | bytes 325640 | tf_op jit(solution)/shard_map/ppermute | solution.py:412
  26.8 9.6 %collective-permute-start.8 = (bf16[53,8,128]{2,1,0:T(8,128)(2,1)}, bf16[53,8,128]{2,1,0:T(8,128)(2,1)S(1)}, u32[]{:S(2)}, u32[]{:S(2)}) collective-permute-start(bf16[53,8,128]{2,1,0:T(8,128)(2,1)} %get-tuple-element.43), channel_id=1, source_target_pairs={{0,4},{1,5},{2,6},{3,7},{4,0},{5,1},{6,2},{7,3},{8,12},{9,13},{10,... | collective-permute-start | bytes 325640 | tf_op jit(solution)/shard_map/ppermute | solution.py:412
  28.5 9.6 %collective-permute-start.9 = (bf16[53,8,128]{2,1,0:T(8,128)(2,1)}, bf16[53,8,128]{2,1,0:T(8,128)(2,1)S(1)}, u32[]{:S(2)}, u32[]{:S(2)}) collective-permute-start(bf16[53,8,128]{2,1,0:T(8,128)(2,1)} %get-tuple-element.44), channel_id=1, source_target_pairs={{0,11},{1,10},{2,9},{3,8},{4,15},{5,14},{6,13},{7,12},{8,3},{9,2},... | collective-permute-start | bytes 325640 | tf_op jit(solution)/shard_map/ppermute | solution.py:412
  30.1 14.5 %collective-permute-start.10 = (bf16[53,8,128]{2,1,0:T(8,128)(2,1)}, bf16[53,8,128]{2,1,0:T(8,128)(2,1)S(1)}, u32[]{:S(2)}, u32[]{:S(2)}) collective-permute-start(bf16[53,8,128]{2,1,0:T(8,128)(2,1)} %get-tuple-element.45), channel_id=1, source_target_pairs={{0,5},{1,4},{2,7},{3,6},{4,1},{5,0},{6,3},{7,2},{8,13},{9,12},{10,... | collective-permute-start | bytes 325640 | tf_op jit(solution)/shard_map/ppermute | solution.py:412
  32.2 13.0 %collective-permute-start.11 = (bf16[53,8,128]{2,1,0:T(8,128)(2,1)}, bf16[53,8,128]{2,1,0:T(8,128)(2,1)S(1)}, u32[]{:S(2)}, u32[]{:S(2)}) collective-permute-start(bf16[53,8,128]{2,1,0:T(8,128)(2,1)} %get-tuple-element.46), channel_id=1, source_target_pairs={{0,6},{1,7},{2,4},{3,5},{4,2},{5,3},{6,0},{7,1},{8,14},{9,15},{10,... | collective-permute-start | bytes 325640 | tf_op jit(solution)/shard_map/ppermute | solution.py:412
  33.2 12.0 %collective-permute-start.12 = (bf16[53,8,128]{2,1,0:T(8,128)(2,1)}, bf16[53,8,128]{2,1,0:T(8,128)(2,1)S(1)}, u32[]{:S(2)}, u32[]{:S(2)}) collective-permute-start(bf16[53,8,128]{2,1,0:T(8,128)(2,1)} %get-tuple-element.47), channel_id=1, source_target_pairs={{0,7},{1,6},{2,5},{3,4},{4,3},{5,2},{6,1},{7,0},{8,15},{9,14},{10,... | collective-permute-start | bytes 325640 | tf_op jit(solution)/shard_map/ppermute | solution.py:412
  36.4 15.6 %collective-permute-start.14 = (bf16[48,8,128]{2,1,0:T(8,128)(2,1)}, bf16[48,8,128]{2,1,0:T(8,128)(2,1)S(1)}, u32[]{:S(2)}, u32[]{:S(2)}) collective-permute-start(bf16[48,8,128]{2,1,0:T(8,128)(2,1)} %get-tuple-element.53), channel_id=1, source_target_pairs={{0,13},{1,12},{2,15},{3,14},{4,9},{5,8},{6,11},{7,10},{8,5},{9,4},... | collective-permute-start | bytes 294920 | tf_op jit(solution)/shard_map/ppermute | solution.py:412
  38.1 13.9 %collective-permute-start.15 = (bf16[48,8,128]{2,1,0:T(8,128)(2,1)}, bf16[48,8,128]{2,1,0:T(8,128)(2,1)S(1)}, u32[]{:S(2)}, u32[]{:S(2)}) collective-permute-start(bf16[48,8,128]{2,1,0:T(8,128)(2,1)} %get-tuple-element.54), channel_id=1, source_target_pairs={{0,15},{1,14},{2,13},{3,12},{4,11},{5,10},{6,9},{7,8},{8,7},{9,6},... | collective-permute-start | bytes 294920 | tf_op jit(solution)/shard_map/ppermute | solution.py:412
  41.8 0.9 %copy-start = (bf16[53,8,128]{2,1,0:T(8,128)(2,1)S(1)}, bf16[53,8,128]{2,1,0:T(8,128)(2,1)}, u32[]{:S(2)}) copy-start(bf16[53,8,128]{2,1,0:T(8,128)(2,1)} %get-tuple-element.30.own_ref) | copy-start | bytes 325636
  42.7 0.7 %copy-start.1 = (f32[384,3]{0,1:T(4,128)S(1)}, f32[384,3]{0,1:T(4,128)}, u32[]{:S(2)}) copy-start(f32[384,3]{0,1:T(4,128)} %param.12) | copy-start | bytes 13828
  43.3 0.7 %copy-start.2 = (s32[64,2]{0,1:T(2,128)S(1)}, s32[64,2]{0,1:T(2,128)}, u32[]{:S(2)}) copy-start(s32[64,2]{0,1:T(2,128)} %param.10) | copy-start | bytes 1540
  44.5 1.5 %collective-permute-start.13 = (bf16[20,8,128]{2,1,0:T(8,128)(2,1)S(1)}, bf16[20,8,128]{2,1,0:T(8,128)(2,1)S(1)}, u32[]{:S(2)}, u32[]{:S(2)}) collective-permute-start(bf16[20,8,128]{2,1,0:T(8,128)(2,1)S(1)} %get-tuple-element.48), channel_id=1, source_target_pairs={{0,1},{1,0},{2,3},{3,2},{4,5},{5,4},{6,7},{7,6},{8,9},{9,8},{10,11... | collective-permute-start | bytes 122888 | tf_op jit(solution)/shard_map/ppermute | solution.py:412

commit v10 on v9

--- a/solution.py
+++ b/solution.py
@@ -117,6 +117,7 @@
 
 def interpolation(weights, offset, high_ref, low_ref):
     channels = weights.shape[1]
+    offset = jnp.concatenate([offset[c : c + 1, :] for c in range(offset.shape[0])], axis=1)
     index = lax.broadcasted_iota(jnp.int32, (LANES, channels), 0)
     knot = (index & 63) >> 3
     basis = jnp.zeros((LANES, channels), jnp.float32)
@@ -133,14 +134,14 @@
 def collect_kernel(
     at, depth, pairs_ref, weights_ref, offset_ref, own_ref, *rest
 ):
-    blocks = rest[:-6]
-    out_ref, own_out_ref, pairs_out_ref, high_ref, low_ref, sems = rest[-6:]
+    blocks, hold_ref = rest[:-8], rest[-8]
+    out_ref, own_out_ref, hold_out_ref, pairs_out_ref, high_ref, low_ref, sems = rest[-7:]
     moves = start_all(
         [
             (block.at[pl.ds(at, depth)], out_ref.at[pl.ds(i * depth, depth)])
             for i, block in enumerate(blocks)
         ]
-        + [(own_ref, own_out_ref)],
+        + [(own_ref, own_out_ref), (hold_ref, hold_out_ref)],
         sems,
     )
     pairs_out_ref[...] = pairs_ref[...]
@@ -195,43 +196,38 @@
     low_ref,
     *rest,
 ):
-    arrived, passed = dict(zip(order, rest)), rest[len(order)]
-    gains_ref, recip_ref, slots_ref, sums_ref = rest[-12:-8]
-    metas_ref, table_ref, pick_ref, rows_ref, codes_ref, slots_s, slots_v, sems = rest[-8:]
-    devices, depth, _, _ = metas_ref.shape
+    arrived, passed = dict(zip(order, rest)), rest[order.index(None)]
+    gains_ref, recip_ref, slots_ref, sums_ref = rest[-10:-6]
+    table_ref, pick_ref, codes_ref, slots_s, slots_v, sem = rest[-6:]
+    devices = codes_ref.shape[1]
+    depth = 2 * (table_ref.shape[1] // SUB) + 1
     owned = recip_ref.shape[0]
     channels = high_ref.shape[2]
     half = stations // 2
     gain_tiles = (depth - 1) // 2
     chunks = channels // LANES
     at = capacity * chunks
-    if near == 1:
-        pairs = [(arrived[0], metas_ref)]
-    else:
-        pairs = [(arrived[x].at[pl.ds(at, depth)], metas_ref.at[x]) for x in with_gains(near)]
-        pairs += [
-            (passed.at[pl.ds(i * depth, depth)], metas_ref.at[near + 1 + 2 * i])
-            for i in range(near // 2)
-        ]
-        pairs += [(arrived[x].at[pl.ds(0, at)], rows_ref.at[i]) for i, x in enumerate(order)]
-    moves = start_all(pairs, sems)
-    early = min(len(moves), 2 * near)
-    for move in moves[:early]:
-        move.wait()
+
+    def meta(x, i):
+        if near == 1:
+            return arrived[0][x, i]
+        if x in with_gains(near):
+            return arrived[x][at + i]
+        return passed[(x - near) // 2 * depth + i]
 
     for x in range(devices):
         for i in range(gain_tiles):
-            table_ref[x, i * SUB : (i + 1) * SUB, :] = metas_ref[x, i].astype(
-                jnp.float32
-            ) + metas_ref[x, gain_tiles + i].astype(jnp.float32)
-        code = metas_ref[x, 2 * gain_tiles].astype(jnp.float32)
+            table_ref[x, i * SUB : (i + 1) * SUB, :] = meta(x, i).astype(jnp.float32) + meta(
+                x, gain_tiles + i
+            ).astype(jnp.float32)
+        code = meta(x, 2 * gain_tiles).astype(jnp.float32)
         codes_ref[0, x : x + 1, :] = code[0:1, :]
         codes_ref[1, x : x + 1, :] = code[1:2, :]
     owner, slot = codes_ref[0], codes_ref[1]
     listing, mine = list_rows(owner, slot, me_s[0].astype(jnp.float32), capacity)
     slots_ref[...] = listing
     slots_v[...] = listing
-    move = pltpu.make_async_copy(slots_v, slots_s, sems.at[0])
+    move = pltpu.make_async_copy(slots_v, slots_s, sem)
     move.start()
 
     which = lax.broadcasted_iota(jnp.int32, (owned, LANES), 0).astype(jnp.float32)
@@ -272,12 +268,11 @@
 
     for c in range(sums_ref.shape[0]):
         sums_ref[c] = jnp.zeros_like(sums_ref[c])
-    for other in moves[early:]:
-        other.wait()
     move.wait()
     if near > 1:
-        for i, x in enumerate(order):
-            add_rows(sums_ref, slots_s, x, capacity, rows_ref.at[i])
+        for x in order:
+            if x is not None:
+                add_rows(sums_ref, slots_s, x, capacity, arrived[x])
 
 
 def finish_kernel(capacity, order, slots_s, sums_ref, gains_ref, recip_ref, *rest):
@@ -406,45 +401,44 @@
 
     pairs = baseline_station_pairs.T
     weights = band_weights.T
-    offset = band_offset.reshape(1, channels)
+    offset = band_offset.reshape(chunks, LANES)
 
     def swap(array, x):
         return lax.ppermute(array, "bl", [(d, d ^ x) for d in range(devices)])
 
     if halves:
-        arrived = {0: sent[0]}
-        for x in range(1, devices):
-            arrived[x] = swap(sent[x], x)
         even = list(range(near, devices, 2))
-        collected, own, pairs, high, low = pl.pallas_call(
+        hold = near // 2 + 1
+        arrived = {x: swap(sent[x], x) for x in range(1, devices) if x != hold}
+        collected, own, held, pairs, high, low = pl.pallas_call(
             functools.partial(collect_kernel, rows_at, depth),
             out_shape=[
                 shape((len(even) * depth, parts, LANES), bf16),
                 shape(sent[0].shape, bf16),
+                shape(sent[hold].shape, bf16),
                 shape((2, owned), i32),
             ]
             + [shape((parts, LANES, channels), bf16)] * 2,
-            in_specs=[vmem] * 3 + [anywhere] * (1 + len(even)),
-            out_specs=[vmem] * 5,
-            scratch_shapes=[dma((1 + len(even),))],
+            in_specs=[vmem] * 3 + [anywhere] * (2 + len(even)),
+            out_specs=[vmem] * 6,
+            scratch_shapes=[dma((2 + len(even),))],
             compiler_params=some,
             name="collect_gains",
-        )(pairs, weights, offset, sent[0], *[arrived[x] for x in even])
+        )(pairs, weights, offset, sent[0], *[arrived[x] for x in even], sent[hold])
+        arrived[hold] = swap(held, hold)
         arrived[0] = own
         passed = swap(collected, 1)
         cross = even + [x + 1 for x in even]
-        late = cross[near // 2 + 2 :]
         close = list(range(1, near))
-        order = [0, cross[0]]
-        for x in cross[1 : near // 2 + 2]:
-            order += [x, close.pop(0)]
-        order += close
+        then = near // 2 + 2
+        order = [0] + cross[:2] + close[:1] + cross[2:then] + close[1:] + [None]
+        late = cross[then:]
     else:
         arrived = {
             0: lax.all_gather(sent[1], "bl", axis=0),
             1: lax.all_to_all(sent[0], "bl", split_axis=0, concat_axis=0, tiled=True),
         }
-        order, late, passed = [0], [1], arrived[0]
+        order, late, passed = [0, None], [1], arrived[0]
         high, low = pl.pallas_call(
             lambda w, o, h, l: interpolation(w[...], o[...], h, l),
             out_shape=[shape((parts, LANES, channels), bf16)] * 2,
@@ -462,17 +456,15 @@
             shape((devices, LANES), i32),
             shape((chunks, owned, parts, LANES), f32),
         ),
-        in_specs=[smem, smem, smem, vmem, vmem] + [anywhere] * (1 + len(order)),
+        in_specs=[smem, smem, smem] + [vmem] * (2 + len(order)),
         out_specs=(vmem,) * 4,
         scratch_shapes=[
-            pltpu.VMEM((devices, depth, SUB, LANES), bf16),
             pltpu.VMEM((devices, gain_tiles * SUB, LANES), f32),
             pltpu.VMEM((2 * owned, LANES), f32),
-            pltpu.VMEM((len(order),) + block, bf16),
             pltpu.VMEM((2, devices, LANES), f32),
             pltpu.SMEM((devices, LANES), i32),
             pltpu.VMEM((devices, LANES), i32),
-            dma((2 * near + len(order),)),
+            dma,
         ],
         compiler_params=some,
         name="gains_and_sums",
@@ -482,8 +474,7 @@
         pairs,
         high,
         low,
-        *[arrived[x] for x in order],
-        passed,
+        *[passed if x is None else arrived[x] for x in order],
     )
     return pl.pallas_call(
         functools.partial(finish_kernel, capacity, late),

time: 55 us -> 57.9 us (1.053); the launches traced: 54.1 us -> 57.6 us
  waiting for transfers between devices: 15 us -> 17.7 us
  starting transfers between devices: 24.3 us -> 26.7 us
  Pallas kernels: 11.7 us -> 9.37 us
  local copies, waits for them, and re-layouts: 2.95 us -> 3.84 us
    ppermute x16, waiting for transfers between devices: 15 us -> 17.7 us  [swap(): return lax.ppermute(array, 'bl', [(d, d ^ x) for d in range(devices)])]
    pallas_call x1, Pallas kernels: 5.87 us -> 3.44 us  [on_device(): pl.pallas_call(functools.partial(prepare_kernel, capacity, near, stations...]
    ppermute x16, starting transfers between devices: 24.3 us -> 26.7 us  [swap(): return lax.ppermute(array, 'bl', [(d, d ^ x) for d in range(devices)])]
    unnamed x6 -> x10, local copies, waits for them, and re-layouts: 2.27 us -> 3.84 us
    reshape x1 -> x0, local copies, waits for them, and re-layouts: 0.68 us -> none  [on_device(): offset = band_offset.reshape(1, channels)]
  transfers between devices with their start and end apart: 16 -> 16, of which waited for: 5 -> 6; matrix products, arithmetic and copies ran while one was open for 1% -> 0% of each run, Pallas kernels for 12% -> 7%
where the time goes in v10:
time: 57.9 us; the launch traced here: 57.6 us
  starting transfers between devices  26.7 us (46%)
  waiting for transfers between devices  17.7 us (31%)
  Pallas kernels  9.37 us (16%)
  local copies, waits for them, and re-layouts  3.84 us (7%)
    ppermute x16, starting transfers between devices, swap(): return lax.ppermute(array, 'bl', [(d, d ^ x) for d in range(devices)])  26.7 us
    ppermute x16, waiting for transfers between devices, swap(): return lax.ppermute(array, 'bl', [(d, d ^ x) for d in range(devices)])  17.7 us
    unnamed x10, local copies, waits for them, and re-layouts  3.84 us
    pallas_call x1, Pallas kernels, on_device(): pl.pallas_call(functools.partial(prepare_kernel, capacity, near, stations...  3.44 us
    pallas_call x1, Pallas kernels, on_device(): pl.pallas_call(functools.partial(pack_kernel, capacity, near), out_shape=...  3.23 us
    pallas_call x1, Pallas kernels, on_device(): pl.pallas_call(functools.partial(finish_kernel, capacity, late), out_shap...  2.05 us
  transfers between devices with their start and end apart: 16, of which 6 were waited for; matrix products, arithmetic and copies ran while one was open for 0% of the time, Pallas kernels for 7%

profile of v10, /device:TPU:0, one launch (start us, length us, event | category | flops | bytes accessed | tf_op | source)
XLA Modules:
  0.0 57.6 jit_solution(17586763465423663787)
XLA Ops:
  0.0 3.2 %pack_rows.1 = (bf16[53,8,128]{2,1,0:T(8,128)(2,1)}, bf16[53,8,128]{2,1,0:T(8,128)(2,1)}, bf16[53,8,128]{2,1,0:T(8,128)(2,1)}, bf16[53,8,128]{2,1,0:T(8,128)(2,1...) custom-call(s32[1]{0:T(128)} %bitcast.me_s.turn_s, ...), custom_call_target="tpu_custom_call" | custom-call | tf_op jit(solution)/shard_map/pack_rows/pallas_call | solution.py:374
  3.2 4.1 %collective-permute-start = (bf16[53,8,128]{2,1,0:T(8,128)(2,1)}, bf16[53,8,128]{2,1,0:T(8,128)(2,1)S(1)}, u32[]{:S(2)}, u32[]{:S(2)}) collective-permute-start(bf16[53,8,128]{2,1,0:T(8,128)(2,1)} %get-tuple-element.32), channel_id=1, source_target_pairs={{0,8},{1,9},{2,10},{3,11},{4,12},{5,13},{6,14},{7,15},{8,0},{9,1},... | collective-permute-start | bytes 325640 | tf_op jit(solution)/shard_map/ppermute | solution.py:407
  7.3 1.3 %collective-permute-start.1 = (bf16[53,8,128]{2,1,0:T(8,128)(2,1)}, bf16[53,8,128]{2,1,0:T(8,128)(2,1)S(1)}, u32[]{:S(2)}, u32[]{:S(2)}) collective-permute-start(bf16[53,8,128]{2,1,0:T(8,128)(2,1)} %get-tuple-element.33), channel_id=1, source_target_pairs={{0,10},{1,11},{2,8},{3,9},{4,14},{5,15},{6,12},{7,13},{8,2},{9,3},... | collective-permute-start | bytes 325640 | tf_op jit(solution)/shard_map/ppermute | solution.py:407
  8.6 3.6 %collective-permute-start.2 = (bf16[53,8,128]{2,1,0:T(8,128)(2,1)}, bf16[53,8,128]{2,1,0:T(8,128)(2,1)S(1)}, u32[]{:S(2)}, u32[]{:S(2)}) collective-permute-start(bf16[53,8,128]{2,1,0:T(8,128)(2,1)} %get-tuple-element.34), channel_id=1, source_target_pairs={{0,12},{1,13},{2,14},{3,15},{4,8},{5,9},{6,10},{7,11},{8,4},{9,5},... | collective-permute-start | bytes 325640 | tf_op jit(solution)/shard_map/ppermute | solution.py:407
  12.2 8.5 %collective-permute-done.rest_0_.rest_1_ = bf16[53,8,128]{2,1,0:T(8,128)(2,1)S(1)} collective-permute-done((bf16[53,8,128]{2,1,0:T(8,128)(2,1)}, bf16[53,8,128]{2,1,0:T(8,128)(2,1)S(1)}, u32[]{:S(2)}, u32[]{:S(2)}) %collective-permute-start) | collective-permute-done | bytes 108576 | tf_op jit(solution)/shard_map/ppermute | solution.py:407
  20.7 3.6 %collective-permute-done.1.rest_1_.rest_2_ = bf16[53,8,128]{2,1,0:T(8,128)(2,1)S(1)} collective-permute-done((bf16[53,8,128]{2,1,0:T(8,128)(2,1)}, bf16[53,8,128]{2,1,0:T(8,128)(2,1)S(1)}, u32[]{:S(2)}, u32[]{:S(2)}) %collective-permute-start.1) | collective-permute-done | bytes 108576 | tf_op jit(solution)/shard_map/ppermute | solution.py:407
  24.8 0.6 %collective-permute-start.8 = (bf16[53,8,128]{2,1,0:T(8,128)(2,1)}, bf16[53,8,128]{2,1,0:T(8,128)(2,1)S(1)}, u32[]{:S(2)}, u32[]{:S(2)}) collective-permute-start(bf16[53,8,128]{2,1,0:T(8,128)(2,1)} %get-tuple-element.45), channel_id=1, source_target_pairs={{0,3},{1,2},{2,1},{3,0},{4,7},{5,6},{6,5},{7,4},{8,11},{9,10},{10,... | collective-permute-start | bytes 325640 | tf_op jit(solution)/shard_map/ppermute | solution.py:407
  25.5 8.8 %collective-permute-start.9 = (bf16[53,8,128]{2,1,0:T(8,128)(2,1)}, bf16[53,8,128]{2,1,0:T(8,128)(2,1)S(1)}, u32[]{:S(2)}, u32[]{:S(2)}) collective-permute-start(bf16[53,8,128]{2,1,0:T(8,128)(2,1)} %get-tuple-element.46), channel_id=1, source_target_pairs={{0,4},{1,5},{2,6},{3,7},{4,0},{5,1},{6,2},{7,3},{8,12},{9,13},{10,... | collective-permute-start | bytes 325640 | tf_op jit(solution)/shard_map/ppermute | solution.py:407
  34.2 1.5 %collective-permute-start.11 = (bf16[53,8,128]{2,1,0:T(8,128)(2,1)}, bf16[53,8,128]{2,1,0:T(8,128)(2,1)S(1)}, u32[]{:S(2)}, u32[]{:S(2)}) collective-permute-start(bf16[53,8,128]{2,1,0:T(8,128)(2,1)} %get-tuple-element.48), channel_id=1, source_target_pairs={{0,6},{1,7},{2,4},{3,5},{4,2},{5,3},{6,0},{7,1},{8,14},{9,15},{10,... | collective-permute-start | bytes 325640 | tf_op jit(solution)/shard_map/ppermute | solution.py:407
  35.7 0.9 %copy-done = bf16[53,8,128]{2,1,0:T(8,128)(2,1)S(1)} copy-done((bf16[53,8,128]{2,1,0:T(8,128)(2,1)S(1)}, bf16[53,8,128]{2,1,0:T(8,128)(2,1)}, u32[]{:S(2)}) %copy-start) | copy-done | bytes 108568
  36.6 0.9 %copy-done.1 = bf16[53,8,128]{2,1,0:T(8,128)(2,1)S(1)} copy-done((bf16[53,8,128]{2,1,0:T(8,128)(2,1)S(1)}, bf16[53,8,128]{2,1,0:T(8,128)(2,1)}, u32[]{:S(2)}) %copy-start.1) | copy-done | bytes 108568
  37.5 0.7 %copy-done.2 = f32[384,3]{0,1:T(4,128)S(1)} copy-done((f32[384,3]{0,1:T(4,128)S(1)}, f32[384,3]{0,1:T(4,128)}, u32[]{:S(2)}) %copy-start.2) | copy-done | bytes 4632
  38.2 0.7 %copy-done.3 = s32[384]{0:T(512)S(1)} copy-done((s32[384]{0:T(512)S(1)}, s32[384]{0:T(512)}, u32[]{:S(2)}) %copy-start.3) | copy-done | bytes 1560
  38.9 0.7 %copy-done.4 = s32[64,2]{0,1:T(2,128)S(1)} copy-done((s32[64,2]{0,1:T(2,128)S(1)}, s32[64,2]{0,1:T(2,128)}, u32[]{:S(2)}) %copy-start.4) | copy-done | bytes 536
  39.5 0.6 %collect_gains.1 = (bf16[20,8,128]{2,1,0:T(8,128)(2,1)S(1)}, bf16[53,8,128]{2,1,0:T(8,128)(2,1)S(1)}, bf16[53,8,128]{2,1,0:T(8,128)(2,1)S(1)}, s32[2,64]{1,0:T(2...) custom-call(s32[2,64]{1,0:T(2,128)S(1)} %bitcast.12, f32[3,384]{1,0:T(4,128)S(1)} %bitcast.10, ...), custom_call_target="tpu_custom_call" | custom-call | tf_op jit(solution)/shard_map/collect_gains/pallas_call | solution.py:413
  40.2 1.4 %collective-permute-start.12 = (bf16[53,8,128]{2,1,0:T(8,128)(2,1)}, bf16[53,8,128]{2,1,0:T(8,128)(2,1)S(1)}, u32[]{:S(2)}, u32[]{:S(2)}) collective-permute-start(bf16[53,8,128]{2,1,0:T(8,128)(2,1)} %get-tuple-element.49), channel_id=1, source_target_pairs={{0,7},{1,6},{2,5},{3,4},{4,3},{5,2},{6,1},{7,0},{8,15},{9,14},{10,... | collective-permute-start | bytes 325640 | tf_op jit(solution)/shard_map/ppermute | solution.py:407
  41.6 0.5 collective-permute-start.10
  42.1 2.5 %collective-permute-start.14 = (bf16[48,8,128]{2,1,0:T(8,128)(2,1)}, bf16[48,8,128]{2,1,0:T(8,128)(2,1)S(1)}, u32[]{:S(2)}, u32[]{:S(2)}) collective-permute-start(bf16[48,8,128]{2,1,0:T(8,128)(2,1)} %get-tuple-element.55), channel_id=1, source_target_pairs={{0,13},{1,12},{2,15},{3,14},{4,9},{5,8},{6,11},{7,10},{8,5},{9,4},... | collective-permute-start | bytes 294920 | tf_op jit(solution)/shard_map/ppermute | solution.py:407
  44.6 1.9 %collective-permute-start.15 = (bf16[48,8,128]{2,1,0:T(8,128)(2,1)}, bf16[48,8,128]{2,1,0:T(8,128)(2,1)S(1)}, u32[]{:S(2)}, u32[]{:S(2)}) collective-permute-start(bf16[48,8,128]{2,1,0:T(8,128)(2,1)} %get-tuple-element.56), channel_id=1, source_target_pairs={{0,15},{1,14},{2,13},{3,12},{4,11},{5,10},{6,9},{7,8},{8,7},{9,6},... | collective-permute-start | bytes 294920 | tf_op jit(solution)/shard_map/ppermute | solution.py:407
  46.6 1.1 %collective-permute-done.13.rest_14_ = bf16[20,8,128]{2,1,0:T(8,128)(2,1)S(1)} collective-permute-done((bf16[20,8,128]{2,1,0:T(8,128)(2,1)S(1)}, bf16[20,8,128]{2,1,0:T(8,128)(2,1)S(1)}, u32[]{:S(2)}, u32[]{:S(2)}) %collective-permute-start.13) | collective-permute-done | bytes 40992 | tf_op jit(solution)/shard_map/ppermute | solution.py:407
  47.8 3.4 %gains_and_sums.1 = (f32[8,128,384]{2,1,0:T(8,128)S(1)}, f32[64,128]{1,0:T(8,128)S(1)}, s32[16,128]{1,0:T(8,128)S(1)}, f32[3,64,8,128]{3,2,1,0:T(8,128)S(1)}) custom-call(s32[1]{0:T(128)} %bitcast.me_s.turn_s, s32[1]{0:T(128)} %bitcast.me_s.turn_s, s32[2,64]{1,0:T(2,128)S(1)} %get-tuple-element.37.pairs_s, ...), custom_call_target="tpu_custom_call" | custom-call | tf_op jit(solution)/shard_map/gains_and_sums/pallas_call | solution.py:451
  51.2 1.6 %collective-permute-done.14.rest_0_ = bf16[48,8,128]{2,1,0:T(8,128)(2,1)S(1)} collective-permute-done((bf16[48,8,128]{2,1,0:T(8,128)(2,1)}, bf16[48,8,128]{2,1,0:T(8,128)(2,1)S(1)}, u32[]{:S(2)}, u32[]{:S(2)}) %collective-permute-start.14) | collective-permute-done | bytes 98336 | tf_op jit(solution)/shard_map/ppermute | solution.py:407
  52.8 2.8 %collective-permute-done.15.rest_1_ = bf16[48,8,128]{2,1,0:T(8,128)(2,1)S(1)} collective-permute-done((bf16[48,8,128]{2,1,0:T(8,128)(2,1)}, bf16[48,8,128]{2,1,0:T(8,128)(2,1)S(1)}, u32[]{:S(2)}, u32[]{:S(2)}) %collective-permute-start.15) | collective-permute-done | bytes 98336 | tf_op jit(solution)/shard_map/ppermute | solution.py:407
  55.6 2.1 %sum_and_apply.1 = bf16[64,8,384]{2,1,0:T(8,128)(2,1)} custom-call(s32[16,128]{1,0:T(8,128)S(1)} %get-tuple-element.51.slots_s, f32[3,64,8,128]{3,2,1,0:T(8,128)S(1)} %get-tuple-element.52.sums_ref, f32[8,128,384]{2,1,0:T(8,128)S(1)} %get-tuple-element.53.gains_ref, f32[64,128]{1,0:T(8,128)S(1)} %get-tuple-element.54.recip_ref, ...), custom_call_target="tpu_custom_call" | custom-call | tf_op jit(solution)/shard_map/sum_and_apply/pallas_call | solution.py:479
  (22 shorter events, 0.6 us)
Async XLA Ops:
  3.2 17.5 %collective-permute-start = (bf16[53,8,128]{2,1,0:T(8,128)(2,1)}, bf16[53,8,128]{2,1,0:T(8,128)(2,1)S(1)}, u32[]{:S(2)}, u32[]{:S(2)}) collective-permute-start(bf16[53,8,128]{2,1,0:T(8,128)(2,1)} %get-tuple-element.32), channel_id=1, source_target_pairs={{0,8},{1,9},{2,10},{3,11},{4,12},{5,13},{6,14},{7,15},{8,0},{9,1},... | collective-permute-start | bytes 325640 | tf_op jit(solution)/shard_map/ppermute | solution.py:407
  7.3 17.0 %collective-permute-start.1 = (bf16[53,8,128]{2,1,0:T(8,128)(2,1)}, bf16[53,8,128]{2,1,0:T(8,128)(2,1)S(1)}, u32[]{:S(2)}, u32[]{:S(2)}) collective-permute-start(bf16[53,8,128]{2,1,0:T(8,128)(2,1)} %get-tuple-element.33), channel_id=1, source_target_pairs={{0,10},{1,11},{2,8},{3,9},{4,14},{5,15},{6,12},{7,13},{8,2},{9,3},... | collective-permute-start | bytes 325640 | tf_op jit(solution)/shard_map/ppermute | solution.py:407
  8.6 16.0 %collective-permute-start.2 = (bf16[53,8,128]{2,1,0:T(8,128)(2,1)}, bf16[53,8,128]{2,1,0:T(8,128)(2,1)S(1)}, u32[]{:S(2)}, u32[]{:S(2)}) collective-permute-start(bf16[53,8,128]{2,1,0:T(8,128)(2,1)} %get-tuple-element.34), channel_id=1, source_target_pairs={{0,12},{1,13},{2,14},{3,15},{4,8},{5,9},{6,10},{7,11},{8,4},{9,5},... | collective-permute-start | bytes 325640 | tf_op jit(solution)/shard_map/ppermute | solution.py:407
  12.2 12.6 %collective-permute-start.3 = (bf16[53,8,128]{2,1,0:T(8,128)(2,1)}, bf16[53,8,128]{2,1,0:T(8,128)(2,1)S(1)}, u32[]{:S(2)}, u32[]{:S(2)}) collective-permute-start(bf16[53,8,128]{2,1,0:T(8,128)(2,1)} %get-tuple-element.35), channel_id=1, source_target_pairs={{0,14},{1,15},{2,12},{3,13},{4,10},{5,11},{6,8},{7,9},{8,6},{9,7},... | collective-permute-start | bytes 325640 | tf_op jit(solution)/shard_map/ppermute | solution.py:407
  12.2 13.2 %collective-permute-start.4 = (bf16[53,8,128]{2,1,0:T(8,128)(2,1)}, bf16[53,8,128]{2,1,0:T(8,128)(2,1)S(1)}, u32[]{:S(2)}, u32[]{:S(2)}) collective-permute-start(bf16[53,8,128]{2,1,0:T(8,128)(2,1)} %get-tuple-element.41), channel_id=1, source_target_pairs={{0,1},{1,0},{2,3},{3,2},{4,5},{5,4},{6,7},{7,6},{8,9},{9,8},{10,11... | collective-permute-start | bytes 325640 | tf_op jit(solution)/shard_map/ppermute | solution.py:407
  20.7 13.5 %collective-permute-start.5 = (bf16[53,8,128]{2,1,0:T(8,128)(2,1)}, bf16[53,8,128]{2,1,0:T(8,128)(2,1)S(1)}, u32[]{:S(2)}, u32[]{:S(2)}) collective-permute-start(bf16[53,8,128]{2,1,0:T(8,128)(2,1)} %get-tuple-element.42), channel_id=1, source_target_pairs={{0,9},{1,8},{2,11},{3,10},{4,13},{5,12},{6,15},{7,14},{8,1},{9,0},... | collective-permute-start | bytes 325640 | tf_op jit(solution)/shard_map/ppermute | solution.py:407
  24.3 15.9 %collective-permute-start.6 = (bf16[53,8,128]{2,1,0:T(8,128)(2,1)}, bf16[53,8,128]{2,1,0:T(8,128)(2,1)S(1)}, u32[]{:S(2)}, u32[]{:S(2)}) collective-permute-start(bf16[53,8,128]{2,1,0:T(8,128)(2,1)} %get-tuple-element.43), channel_id=1, source_target_pairs={{0,11},{1,10},{2,9},{3,8},{4,15},{5,14},{6,13},{7,12},{8,3},{9,2},... | collective-permute-start | bytes 325640 | tf_op jit(solution)/shard_map/ppermute | solution.py:407
  24.6 16.9 %collective-permute-start.7 = (bf16[53,8,128]{2,1,0:T(8,128)(2,1)}, bf16[53,8,128]{2,1,0:T(8,128)(2,1)S(1)}, u32[]{:S(2)}, u32[]{:S(2)}) collective-permute-start(bf16[53,8,128]{2,1,0:T(8,128)(2,1)} %get-tuple-element.44), channel_id=1, source_target_pairs={{0,2},{1,3},{2,0},{3,1},{4,6},{5,7},{6,4},{7,5},{8,10},{9,11},{10,... | collective-permute-start | bytes 325640 | tf_op jit(solution)/shard_map/ppermute | solution.py:407
  24.8 17.3 %collective-permute-start.8 = (bf16[53,8,128]{2,1,0:T(8,128)(2,1)}, bf16[53,8,128]{2,1,0:T(8,128)(2,1)S(1)}, u32[]{:S(2)}, u32[]{:S(2)}) collective-permute-start(bf16[53,8,128]{2,1,0:T(8,128)(2,1)} %get-tuple-element.45), channel_id=1, source_target_pairs={{0,3},{1,2},{2,1},{3,0},{4,7},{5,6},{6,5},{7,4},{8,11},{9,10},{10,... | collective-permute-start | bytes 325640 | tf_op jit(solution)/shard_map/ppermute | solution.py:407
  25.5 19.2 %collective-permute-start.9 = (bf16[53,8,128]{2,1,0:T(8,128)(2,1)}, bf16[53,8,128]{2,1,0:T(8,128)(2,1)S(1)}, u32[]{:S(2)}, u32[]{:S(2)}) collective-permute-start(bf16[53,8,128]{2,1,0:T(8,128)(2,1)} %get-tuple-element.46), channel_id=1, source_target_pairs={{0,4},{1,5},{2,6},{3,7},{4,0},{5,1},{6,2},{7,3},{8,12},{9,13},{10,... | collective-permute-start | bytes 325640 | tf_op jit(solution)/shard_map/ppermute | solution.py:407
  34.2 12.3 %collective-permute-start.11 = (bf16[53,8,128]{2,1,0:T(8,128)(2,1)}, bf16[53,8,128]{2,1,0:T(8,128)(2,1)S(1)}, u32[]{:S(2)}, u32[]{:S(2)}) collective-permute-start(bf16[53,8,128]{2,1,0:T(8,128)(2,1)} %get-tuple-element.48), channel_id=1, source_target_pairs={{0,6},{1,7},{2,4},{3,5},{4,2},{5,3},{6,0},{7,1},{8,14},{9,15},{10,... | collective-permute-start | bytes 325640 | tf_op jit(solution)/shard_map/ppermute | solution.py:407
  35.7 0.9 %copy-start = (bf16[53,8,128]{2,1,0:T(8,128)(2,1)S(1)}, bf16[53,8,128]{2,1,0:T(8,128)(2,1)}, u32[]{:S(2)}) copy-start(bf16[53,8,128]{2,1,0:T(8,128)(2,1)} %get-tuple-element.31.own_ref) | copy-start | bytes 325636
  36.6 0.9 %copy-start.1 = (bf16[53,8,128]{2,1,0:T(8,128)(2,1)S(1)}, bf16[53,8,128]{2,1,0:T(8,128)(2,1)}, u32[]{:S(2)}) copy-start(bf16[53,8,128]{2,1,0:T(8,128)(2,1)} %get-tuple-element.36.rest_4_) | copy-start | bytes 325636
  37.5 0.7 %copy-start.2 = (f32[384,3]{0,1:T(4,128)S(1)}, f32[384,3]{0,1:T(4,128)}, u32[]{:S(2)}) copy-start(f32[384,3]{0,1:T(4,128)} %param.12) | copy-start | bytes 13828
  38.2 0.7 %copy-start.3 = (s32[384]{0:T(512)S(1)}, s32[384]{0:T(512)}, u32[]{:S(2)}) copy-start(s32[384]{0:T(512)} %param.13) | copy-start | bytes 4612
  38.9 0.7 %copy-start.4 = (s32[64,2]{0,1:T(2,128)S(1)}, s32[64,2]{0,1:T(2,128)}, u32[]{:S(2)}) copy-start(s32[64,2]{0,1:T(2,128)} %param.10) | copy-start | bytes 1540
  40.2 6.4 %collective-permute-start.12 = (bf16[53,8,128]{2,1,0:T(8,128)(2,1)}, bf16[53,8,128]{2,1,0:T(8,128)(2,1)S(1)}, u32[]{:S(2)}, u32[]{:S(2)}) collective-permute-start(bf16[53,8,128]{2,1,0:T(8,128)(2,1)} %get-tuple-element.49), channel_id=1, source_target_pairs={{0,7},{1,6},{2,5},{3,4},{4,3},{5,2},{6,1},{7,0},{8,15},{9,14},{10,... | collective-permute-start | bytes 325640 | tf_op jit(solution)/shard_map/ppermute | solution.py:407
  41.6 6.2 %collective-permute-start.10 = (bf16[53,8,128]{2,1,0:T(8,128)(2,1)S(1)}, bf16[53,8,128]{2,1,0:T(8,128)(2,1)S(1)}, u32[]{:S(2)}, u32[]{:S(2)}) collective-permute-start(bf16[53,8,128]{2,1,0:T(8,128)(2,1)S(1)} %get-tuple-element.47), channel_id=1, source_target_pairs={{0,5},{1,4},{2,7},{3,6},{4,1},{5,0},{6,3},{7,2},{8,13},{9,12},{10,... | collective-permute-start | bytes 325640 | tf_op jit(solution)/shard_map/ppermute | solution.py:407
  42.1 10.7 %collective-permute-start.14 = (bf16[48,8,128]{2,1,0:T(8,128)(2,1)}, bf16[48,8,128]{2,1,0:T(8,128)(2,1)S(1)}, u32[]{:S(2)}, u32[]{:S(2)}) collective-permute-start(bf16[48,8,128]{2,1,0:T(8,128)(2,1)} %get-tuple-element.55), channel_id=1, source_target_pairs={{0,13},{1,12},{2,15},{3,14},{4,9},{5,8},{6,11},{7,10},{8,5},{9,4},... | collective-permute-start | bytes 294920 | tf_op jit(solution)/shard_map/ppermute | solution.py:407
  44.6 10.9 %collective-permute-start.15 = (bf16[48,8,128]{2,1,0:T(8,128)(2,1)}, bf16[48,8,128]{2,1,0:T(8,128)(2,1)S(1)}, u32[]{:S(2)}, u32[]{:S(2)}) collective-permute-start(bf16[48,8,128]{2,1,0:T(8,128)(2,1)} %get-tuple-element.56), channel_id=1, source_target_pairs={{0,15},{1,14},{2,13},{3,12},{4,11},{5,10},{6,9},{7,8},{8,7},{9,6},... | collective-permute-start | bytes 294920 | tf_op jit(solution)/shard_map/ppermute | solution.py:407
  46.5 1.2 %collective-permute-start.13 = (bf16[20,8,128]{2,1,0:T(8,128)(2,1)S(1)}, bf16[20,8,128]{2,1,0:T(8,128)(2,1)S(1)}, u32[]{:S(2)}, u32[]{:S(2)}) collective-permute-start(bf16[20,8,128]{2,1,0:T(8,128)(2,1)S(1)} %get-tuple-element.50), channel_id=1, source_target_pairs={{0,1},{1,0},{2,3},{3,2},{4,5},{5,4},{6,7},{7,6},{8,9},{9,8},{10,11... | collective-permute-start | bytes 122888 | tf_op jit(solution)/shard_map/ppermute | solution.py:407

commit v11 on v10

--- a/solution.py
+++ b/solution.py
@@ -18,8 +18,14 @@
     return -(-value // unit) * unit
 
 
-def with_gains(near):
-    return list(range(near)) + list(range(near, 2 * near, 2))
+def schedule(near):
+    cross = list(range(near, 2 * near, 2)) + list(range(near + 1, 2 * near, 2))
+    close = list(range(1, near))
+    order = [0] + cross[:2] + close[:3] + cross[2:4] + close[3:4]
+    for x in cross[4:-2]:
+        order += [x] + close[4:5]
+        close = close[:4] + close[5:]
+    return order + close[4:], cross[-2:]
 
 
 def start_all(pairs, sems):
@@ -90,7 +96,7 @@
     meta_ref[2 * gain_tiles] = codes.astype(jnp.float32).astype(jnp.bfloat16)
     at = chunks * capacity
     if near > 1:
-        pairs = [(meta_ref, outs[x].at[pl.ds(at, depth)]) for x in with_gains(near)]
+        pairs = [(meta_ref, outs[x].at[pl.ds(at, depth)]) for x in schedule(near)[0]]
     else:
         pairs = [(meta_ref, outs[1])]
     sends = start_all(pairs, sems.at[pl.ds(1, len(pairs))])
@@ -131,18 +137,10 @@
         low_ref[j] = jnp.where(part == j, low, 0.0).astype(jnp.bfloat16)
 
 
-def collect_kernel(
-    at, depth, pairs_ref, weights_ref, offset_ref, own_ref, *rest
-):
-    blocks, hold_ref = rest[:-8], rest[-8]
-    out_ref, own_out_ref, hold_out_ref, pairs_out_ref, high_ref, low_ref, sems = rest[-7:]
+def ready_kernel(at, pairs_ref, weights_ref, offset_ref, own_ref, _, *rest):
+    meta_ref, own_out_ref, pairs_out_ref, high_ref, low_ref, sems = rest
     moves = start_all(
-        [
-            (block.at[pl.ds(at, depth)], out_ref.at[pl.ds(i * depth, depth)])
-            for i, block in enumerate(blocks)
-        ]
-        + [(own_ref, own_out_ref), (hold_ref, hold_out_ref)],
-        sems,
+        [(own_ref.at[pl.ds(at, meta_ref.shape[0])], meta_ref), (own_ref, own_out_ref)], sems
     )
     pairs_out_ref[...] = pairs_ref[...]
     interpolation(weights_ref[...], offset_ref[...], high_ref, low_ref)
@@ -189,6 +187,7 @@
     near,
     stations,
     order,
+    late,
     turn_s,
     me_s,
     pairs_s,
@@ -196,7 +195,7 @@
     low_ref,
     *rest,
 ):
-    arrived, passed = dict(zip(order, rest)), rest[order.index(None)]
+    arrived, passed = dict(zip(order, rest)), dict(zip(late, rest[len(order) :]))
     gains_ref, recip_ref, slots_ref, sums_ref = rest[-10:-6]
     table_ref, pick_ref, codes_ref, slots_s, slots_v, sem = rest[-6:]
     devices = codes_ref.shape[1]
@@ -211,9 +210,7 @@
     def meta(x, i):
         if near == 1:
             return arrived[0][x, i]
-        if x in with_gains(near):
-            return arrived[x][at + i]
-        return passed[(x - near) // 2 * depth + i]
+        return passed[x][i] if x in late else arrived[x][at + i]
 
     for x in range(devices):
         for i in range(gain_tiles):
@@ -271,8 +268,7 @@
     move.wait()
     if near > 1:
         for x in order:
-            if x is not None:
-                add_rows(sums_ref, slots_s, x, capacity, arrived[x])
+            add_rows(sums_ref, slots_s, x, capacity, arrived[x])
 
 
 def finish_kernel(capacity, order, slots_s, sums_ref, gains_ref, recip_ref, *rest):
@@ -364,9 +360,9 @@
     block = (chunks * capacity, parts, LANES)
     rows_at = chunks * capacity
     if halves:
-        wide = with_gains(near) + [near + 1, near + 3]
+        order, late = schedule(near)
         outs = [
-            shape((rows_at + (depth if x in wide else 0), parts, LANES), bf16)
+            shape((rows_at + (0 if x in late else depth), parts, LANES), bf16)
             for x in range(devices)
         ]
     else:
@@ -407,38 +403,28 @@
         return lax.ppermute(array, "bl", [(d, d ^ x) for d in range(devices)])
 
     if halves:
-        even = list(range(near, devices, 2))
-        hold = near // 2 + 1
-        arrived = {x: swap(sent[x], x) for x in range(1, devices) if x != hold}
-        collected, own, held, pairs, high, low = pl.pallas_call(
-            functools.partial(collect_kernel, rows_at, depth),
+        arrived = {x: swap(sent[x], x) for x in range(1, devices)}
+        meta, arrived[0], pairs, high, low = pl.pallas_call(
+            functools.partial(ready_kernel, rows_at),
             out_shape=[
-                shape((len(even) * depth, parts, LANES), bf16),
+                shape((depth, parts, LANES), bf16),
                 shape(sent[0].shape, bf16),
-                shape(sent[hold].shape, bf16),
                 shape((2, owned), i32),
             ]
             + [shape((parts, LANES, channels), bf16)] * 2,
-            in_specs=[vmem] * 3 + [anywhere] * (2 + len(even)),
-            out_specs=[vmem] * 6,
-            scratch_shapes=[dma((2 + len(even),))],
+            in_specs=[vmem] * 3 + [anywhere] * 2,
+            out_specs=[vmem] * 5,
+            scratch_shapes=[dma((2,))],
             compiler_params=some,
-            name="collect_gains",
-        )(pairs, weights, offset, sent[0], *[arrived[x] for x in even], sent[hold])
-        arrived[hold] = swap(held, hold)
-        arrived[0] = own
-        passed = swap(collected, 1)
-        cross = even + [x + 1 for x in even]
-        close = list(range(1, near))
-        then = near // 2 + 2
-        order = [0] + cross[:2] + close[:1] + cross[2:then] + close[1:] + [None]
-        late = cross[then:]
+            name="interpolation",
+        )(pairs, weights, offset, sent[0], arrived[near])
+        passed = [swap(meta, x) for x in late]
     else:
         arrived = {
             0: lax.all_gather(sent[1], "bl", axis=0),
             1: lax.all_to_all(sent[0], "bl", split_axis=0, concat_axis=0, tiled=True),
         }
-        order, late, passed = [0, None], [1], arrived[0]
+        order, late, passed = [0], [1], []
         high, low = pl.pallas_call(
             lambda w, o, h, l: interpolation(w[...], o[...], h, l),
             out_shape=[shape((parts, LANES, channels), bf16)] * 2,
@@ -449,14 +435,14 @@
         )(weights, offset)
 
     gains, recip, slots, sums = pl.pallas_call(
-        functools.partial(prepare_kernel, capacity, near, stations, order),
+        functools.partial(prepare_kernel, capacity, near, stations, order, late),
         out_shape=(
             shape((parts, 2 * owned, channels), f32),
             shape((owned, LANES), f32),
             shape((devices, LANES), i32),
             shape((chunks, owned, parts, LANES), f32),
         ),
-        in_specs=[smem, smem, smem] + [vmem] * (2 + len(order)),
+        in_specs=[smem, smem, smem] + [vmem] * (2 + len(order) + len(passed)),
         out_specs=(vmem,) * 4,
         scratch_shapes=[
             pltpu.VMEM((devices, gain_tiles * SUB, LANES), f32),
@@ -474,7 +460,8 @@
         pairs,
         high,
         low,
-        *[passed if x is None else arrived[x] for x in order],
+        *[arrived[x] for x in order],
+        *passed,
     )
     return pl.pallas_call(
         functools.partial(finish_kernel, capacity, late),

time: 57.9 us -> 54.6 us (0.943)
  waiting for transfers between devices: 17.7 us -> 12.7 us
  starting transfers between devices: 26.7 us -> 28.2 us
  local copies, waits for them, and re-layouts: 3.84 us -> 2.95 us
  Pallas kernels: 9.37 us -> 10.2 us
    ppermute x16 -> x17, waiting for transfers between devices: 17.7 us -> 12.7 us  [swap(): return lax.ppermute(array, 'bl', [(d, d ^ x) for d in range(devices)])]
    ppermute x16 -> x17, starting transfers between devices: 26.7 us -> 28.2 us  [swap(): return lax.ppermute(array, 'bl', [(d, d ^ x) for d in range(devices)])]
    unnamed x10 -> x8, local copies, waits for them, and re-layouts: 3.84 us -> 2.95 us
    pallas_call x1, Pallas kernels: 3.44 us -> 4.3 us  [on_device(): pl.pallas_call(functools.partial(prepare_kernel, capacity, near, stations...]
  transfers between devices with their start and end apart: 16 -> 17, of which waited for: 6 -> 6; matrix products, arithmetic and copies ran while one was open for 0% -> 0% of each run, Pallas kernels for 7% -> 9%
where the time goes in v11:
time: 54.6 us; the launch traced here: 54.1 us
  starting transfers between devices  28.2 us (52%)
  waiting for transfers between devices  12.7 us (23%)
  Pallas kernels  10.2 us (19%)
  local copies, waits for them, and re-layouts  2.95 us (5%)
    ppermute x17, starting transfers between devices, swap(): return lax.ppermute(array, 'bl', [(d, d ^ x) for d in range(devices)])  28.2 us
    ppermute x17, waiting for transfers between devices, swap(): return lax.ppermute(array, 'bl', [(d, d ^ x) for d in range(devices)])  12.7 us
    pallas_call x1, Pallas kernels, on_device(): pl.pallas_call(functools.partial(prepare_kernel, capacity, near, stations...  4.3 us
    pallas_call x1, Pallas kernels, on_device(): pl.pallas_call(functools.partial(pack_kernel, capacity, near), out_shape=...  3.23 us
    unnamed x8, local copies, waits for them, and re-layouts  2.95 us
    pallas_call x1, Pallas kernels, on_device(): pl.pallas_call(functools.partial(finish_kernel, capacity, late), out_shap...  2.21 us
  transfers between devices with their start and end apart: 17, of which 6 were waited for; matrix products, arithmetic and copies ran while one was open for 0% of the time, Pallas kernels for 9%

profile of v11, /device:TPU:0, one launch (start us, length us, event | category | flops | bytes accessed | tf_op | source)
XLA Modules:
  0.0 54.1 jit_solution(10681137366451558592)
XLA Ops:
  0.0 3.2 %pack_rows.1 = (bf16[53,8,128]{2,1,0:T(8,128)(2,1)}, bf16[53,8,128]{2,1,0:T(8,128)(2,1)}, bf16[53,8,128]{2,1,0:T(8,128)(2,1)}, bf16[53,8,128]{2,1,0:T(8,128)(2,1...) custom-call(s32[1]{0:T(128)} %bitcast.me_s.turn_s, ...), custom_call_target="tpu_custom_call" | custom-call | tf_op jit(solution)/shard_map/pack_rows/pallas_call | solution.py:370
  3.2 4.1 %collective-permute-start = (bf16[53,8,128]{2,1,0:T(8,128)(2,1)}, bf16[53,8,128]{2,1,0:T(8,128)(2,1)S(1)}, u32[]{:S(2)}, u32[]{:S(2)}) collective-permute-start(bf16[53,8,128]{2,1,0:T(8,128)(2,1)} %get-tuple-element.31), channel_id=1, source_target_pairs={{0,8},{1,9},{2,10},{3,11},{4,12},{5,13},{6,14},{7,15},{8,0},{9,1},... | collective-permute-start | bytes 325640 | tf_op jit(solution)/shard_map/ppermute | solution.py:403
  7.3 1.3 %collective-permute-start.1 = (bf16[53,8,128]{2,1,0:T(8,128)(2,1)}, bf16[53,8,128]{2,1,0:T(8,128)(2,1)S(1)}, u32[]{:S(2)}, u32[]{:S(2)}) collective-permute-start(bf16[53,8,128]{2,1,0:T(8,128)(2,1)} %get-tuple-element.36), channel_id=1, source_target_pairs={{0,10},{1,11},{2,8},{3,9},{4,14},{5,15},{6,12},{7,13},{8,2},{9,3},... | collective-permute-start | bytes 325640 | tf_op jit(solution)/shard_map/ppermute | solution.py:403
  8.9 1.6 %collective-permute-start.4 = (bf16[53,8,128]{2,1,0:T(8,128)(2,1)}, bf16[53,8,128]{2,1,0:T(8,128)(2,1)S(1)}, u32[]{:S(2)}, u32[]{:S(2)}) collective-permute-start(bf16[53,8,128]{2,1,0:T(8,128)(2,1)} %get-tuple-element.39), channel_id=1, source_target_pairs={{0,3},{1,2},{2,1},{3,0},{4,7},{5,6},{6,5},{7,4},{8,11},{9,10},{10,... | collective-permute-start | bytes 325640 | tf_op jit(solution)/shard_map/ppermute | solution.py:403
  10.5 5.5 %collective-permute-done._.rest_1_ = bf16[53,8,128]{2,1,0:T(8,128)(2,1)S(1)} collective-permute-done((bf16[53,8,128]{2,1,0:T(8,128)(2,1)}, bf16[53,8,128]{2,1,0:T(8,128)(2,1)S(1)}, u32[]{:S(2)}, u32[]{:S(2)}) %collective-permute-start) | collective-permute-done | bytes 108576 | tf_op jit(solution)/shard_map/ppermute | solution.py:403
  16.0 2.8 %collective-permute-start.5 = (bf16[53,8,128]{2,1,0:T(8,128)(2,1)}, bf16[53,8,128]{2,1,0:T(8,128)(2,1)S(1)}, u32[]{:S(2)}, u32[]{:S(2)}) collective-permute-start(bf16[53,8,128]{2,1,0:T(8,128)(2,1)} %get-tuple-element.40), channel_id=1, source_target_pairs={{0,12},{1,13},{2,14},{3,15},{4,8},{5,9},{6,10},{7,11},{8,4},{9,5},... | collective-permute-start | bytes 325640 | tf_op jit(solution)/shard_map/ppermute | solution.py:403
  18.9 3.2 %collective-permute-start.6 = (bf16[53,8,128]{2,1,0:T(8,128)(2,1)}, bf16[53,8,128]{2,1,0:T(8,128)(2,1)S(1)}, u32[]{:S(2)}, u32[]{:S(2)}) collective-permute-start(bf16[53,8,128]{2,1,0:T(8,128)(2,1)} %get-tuple-element.41), channel_id=1, source_target_pairs={{0,14},{1,15},{2,12},{3,13},{4,10},{5,11},{6,8},{7,9},{8,6},{9,7},... | collective-permute-start | bytes 325640 | tf_op jit(solution)/shard_map/ppermute | solution.py:403
  22.1 0.8 %collective-permute-start.8 = (bf16[53,8,128]{2,1,0:T(8,128)(2,1)}, bf16[53,8,128]{2,1,0:T(8,128)(2,1)S(1)}, u32[]{:S(2)}, u32[]{:S(2)}) collective-permute-start(bf16[53,8,128]{2,1,0:T(8,128)(2,1)} %get-tuple-element.43), channel_id=1, source_target_pairs={{0,9},{1,8},{2,11},{3,10},{4,13},{5,12},{6,15},{7,14},{8,1},{9,0},... | collective-permute-start | bytes 325640 | tf_op jit(solution)/shard_map/ppermute | solution.py:403
  22.9 1.1 %collective-permute-start.9 = (bf16[53,8,128]{2,1,0:T(8,128)(2,1)}, bf16[53,8,128]{2,1,0:T(8,128)(2,1)S(1)}, u32[]{:S(2)}, u32[]{:S(2)}) collective-permute-start(bf16[53,8,128]{2,1,0:T(8,128)(2,1)} %get-tuple-element.44), channel_id=1, source_target_pairs={{0,5},{1,4},{2,7},{3,6},{4,1},{5,0},{6,3},{7,2},{8,13},{9,12},{10,... | collective-permute-start | bytes 325640 | tf_op jit(solution)/shard_map/ppermute | solution.py:403
  24.0 2.7 %collective-permute-start.10 = (bf16[53,8,128]{2,1,0:T(8,128)(2,1)}, bf16[53,8,128]{2,1,0:T(8,128)(2,1)S(1)}, u32[]{:S(2)}, u32[]{:S(2)}) collective-permute-start(bf16[53,8,128]{2,1,0:T(8,128)(2,1)} %get-tuple-element.45), channel_id=1, source_target_pairs={{0,11},{1,10},{2,9},{3,8},{4,15},{5,14},{6,13},{7,12},{8,3},{9,2},... | collective-permute-start | bytes 325640 | tf_op jit(solution)/shard_map/ppermute | solution.py:403
  26.7 1.0 %collective-permute-done.6.rest_7_ = bf16[53,8,128]{2,1,0:T(8,128)(2,1)S(1)} collective-permute-done((bf16[53,8,128]{2,1,0:T(8,128)(2,1)}, bf16[53,8,128]{2,1,0:T(8,128)(2,1)S(1)}, u32[]{:S(2)}, u32[]{:S(2)}) %collective-permute-start.6) | collective-permute-done | bytes 108576 | tf_op jit(solution)/shard_map/ppermute | solution.py:403
  27.7 1.5 %collective-permute-start.11 = (bf16[53,8,128]{2,1,0:T(8,128)(2,1)}, bf16[53,8,128]{2,1,0:T(8,128)(2,1)S(1)}, u32[]{:S(2)}, u32[]{:S(2)}) collective-permute-start(bf16[53,8,128]{2,1,0:T(8,128)(2,1)} %get-tuple-element.46), channel_id=1, source_target_pairs={{0,6},{1,7},{2,4},{3,5},{4,2},{5,3},{6,0},{7,1},{8,14},{9,15},{10,... | collective-permute-start | bytes 325640 | tf_op jit(solution)/shard_map/ppermute | solution.py:403
  29.2 1.3 %collective-permute-done.7.rest_8_ = bf16[53,8,128]{2,1,0:T(8,128)(2,1)S(1)} collective-permute-done((bf16[53,8,128]{2,1,0:T(8,128)(2,1)}, bf16[53,8,128]{2,1,0:T(8,128)(2,1)S(1)}, u32[]{:S(2)}, u32[]{:S(2)}) %collective-permute-start.7) | collective-permute-done | bytes 108576 | tf_op jit(solution)/shard_map/ppermute | solution.py:403
  30.5 1.6 %collective-permute-done.8.rest_9_ = bf16[53,8,128]{2,1,0:T(8,128)(2,1)S(1)} collective-permute-done((bf16[53,8,128]{2,1,0:T(8,128)(2,1)}, bf16[53,8,128]{2,1,0:T(8,128)(2,1)S(1)}, u32[]{:S(2)}, u32[]{:S(2)}) %collective-permute-start.8) | collective-permute-done | bytes 108576 | tf_op jit(solution)/shard_map/ppermute | solution.py:403
  32.1 2.6 %collective-permute-start.15 = (bf16[48,8,128]{2,1,0:T(8,128)(2,1)}, bf16[48,8,128]{2,1,0:T(8,128)(2,1)S(1)}, u32[]{:S(2)}, u32[]{:S(2)}) collective-permute-start(bf16[48,8,128]{2,1,0:T(8,128)(2,1)} %get-tuple-element.53), channel_id=1, source_target_pairs={{0,13},{1,12},{2,15},{3,14},{4,9},{5,8},{6,11},{7,10},{8,5},{9,4},... | collective-permute-start | bytes 294920 | tf_op jit(solution)/shard_map/ppermute | solution.py:403
  34.8 2.3 %collective-permute-start.16 = (bf16[48,8,128]{2,1,0:T(8,128)(2,1)}, bf16[48,8,128]{2,1,0:T(8,128)(2,1)S(1)}, u32[]{:S(2)}, u32[]{:S(2)}) collective-permute-start(bf16[48,8,128]{2,1,0:T(8,128)(2,1)} %get-tuple-element.54), channel_id=1, source_target_pairs={{0,15},{1,14},{2,13},{3,12},{4,11},{5,10},{6,9},{7,8},{8,7},{9,6},... | collective-permute-start | bytes 294920 | tf_op jit(solution)/shard_map/ppermute | solution.py:403
  37.1 0.9 %copy-done = bf16[53,8,128]{2,1,0:T(8,128)(2,1)S(1)} copy-done((bf16[53,8,128]{2,1,0:T(8,128)(2,1)S(1)}, bf16[53,8,128]{2,1,0:T(8,128)(2,1)}, u32[]{:S(2)}) %copy-start) | copy-done | bytes 108568
  38.0 0.7 %copy-done.1 = f32[384,3]{0,1:T(4,128)S(1)} copy-done((f32[384,3]{0,1:T(4,128)S(1)}, f32[384,3]{0,1:T(4,128)}, u32[]{:S(2)}) %copy-start.1) | copy-done | bytes 4632
  40.5 2.2 %collective-permute-start.14 = (bf16[5,8,128]{2,1,0:T(8,128)(2,1)S(1)}, bf16[5,8,128]{2,1,0:T(8,128)(2,1)S(1)}, u32[]{:S(2)}, u32[]{:S(2)}) collective-permute-start(bf16[5,8,128]{2,1,0:T(8,128)(2,1)S(1)} %get-tuple-element.48), channel_id=1, source_target_pairs={{0,15},{1,14},{2,13},{3,12},{4,11},{5,10},{6,9},{7,8},{8,7},{9,6},... | collective-permute-start | bytes 30728 | tf_op jit(solution)/shard_map/ppermute | solution.py:403
  42.7 1.7 %collective-permute-start.13 = (bf16[5,8,128]{2,1,0:T(8,128)(2,1)S(1)}, bf16[5,8,128]{2,1,0:T(8,128)(2,1)S(1)}, u32[]{:S(2)}, u32[]{:S(2)}) collective-permute-start(bf16[5,8,128]{2,1,0:T(8,128)(2,1)S(1)} %get-tuple-element.48), channel_id=1, source_target_pairs={{0,13},{1,12},{2,15},{3,14},{4,9},{5,8},{6,11},{7,10},{8,5},{9,4},... | collective-permute-start | bytes 30728 | tf_op jit(solution)/shard_map/ppermute | solution.py:403
  44.4 2.0 %collective-permute-done.14.rest_15_ = bf16[5,8,128]{2,1,0:T(8,128)(2,1)S(1)} collective-permute-done((bf16[5,8,128]{2,1,0:T(8,128)(2,1)S(1)}, bf16[5,8,128]{2,1,0:T(8,128)(2,1)S(1)}, u32[]{:S(2)}, u32[]{:S(2)}) %collective-permute-start.14) | collective-permute-done | bytes 10272 | tf_op jit(solution)/shard_map/ppermute | solution.py:403
  46.3 1.2 %collective-permute-done.13.rest_14_ = bf16[5,8,128]{2,1,0:T(8,128)(2,1)S(1)} collective-permute-done((bf16[5,8,128]{2,1,0:T(8,128)(2,1)S(1)}, bf16[5,8,128]{2,1,0:T(8,128)(2,1)S(1)}, u32[]{:S(2)}, u32[]{:S(2)}) %collective-permute-start.13) | collective-permute-done | bytes 10272 | tf_op jit(solution)/shard_map/ppermute | solution.py:403
  47.6 4.3 %gains_and_sums.1 = (f32[8,128,384]{2,1,0:T(8,128)S(1)}, f32[64,128]{1,0:T(8,128)S(1)}, s32[16,128]{1,0:T(8,128)S(1)}, f32[3,64,8,128]{3,2,1,0:T(8,128)S(1)}) custom-call(s32[1]{0:T(128)} %bitcast.me_s.turn_s, s32[1]{0:T(128)} %bitcast.me_s.turn_s, s32[2,64]{1,0:T(2,128)S(1)} %get-tuple-element.32.pairs_s, ...), custom_call_target="tpu_custom_call" | custom-call | tf_op jit(solution)/shard_map/gains_and_sums/pallas_call | solution.py:437
  51.9 2.2 %sum_and_apply.1 = bf16[64,8,384]{2,1,0:T(8,128)(2,1)} custom-call(s32[16,128]{1,0:T(8,128)S(1)} %get-tuple-element.49.slots_s, f32[3,64,8,128]{3,2,1,0:T(8,128)S(1)} %get-tuple-element.50.sums_ref, f32[8,128,384]{2,1,0:T(8,128)S(1)} %get-tuple-element.51.gains_ref, f32[64,128]{1,0:T(8,128)S(1)} %get-tuple-element.52.recip_ref, ...), custom_call_target="tpu_custom_call" | custom-call | tf_op jit(solution)/shard_map/sum_and_apply/pallas_call | solution.py:466
  (22 shorter events, 2.1 us)
Async XLA Ops:
  3.2 12.8 %collective-permute-start = (bf16[53,8,128]{2,1,0:T(8,128)(2,1)}, bf16[53,8,128]{2,1,0:T(8,128)(2,1)S(1)}, u32[]{:S(2)}, u32[]{:S(2)}) collective-permute-start(bf16[53,8,128]{2,1,0:T(8,128)(2,1)} %get-tuple-element.31), channel_id=1, source_target_pairs={{0,8},{1,9},{2,10},{3,11},{4,12},{5,13},{6,14},{7,15},{8,0},{9,1},... | collective-permute-start | bytes 325640 | tf_op jit(solution)/shard_map/ppermute | solution.py:403
  7.3 11.5 %collective-permute-start.1 = (bf16[53,8,128]{2,1,0:T(8,128)(2,1)}, bf16[53,8,128]{2,1,0:T(8,128)(2,1)S(1)}, u32[]{:S(2)}, u32[]{:S(2)}) collective-permute-start(bf16[53,8,128]{2,1,0:T(8,128)(2,1)} %get-tuple-element.36), channel_id=1, source_target_pairs={{0,10},{1,11},{2,8},{3,9},{4,14},{5,15},{6,12},{7,13},{8,2},{9,3},... | collective-permute-start | bytes 325640 | tf_op jit(solution)/shard_map/ppermute | solution.py:403
  8.6 13.5 %collective-permute-start.2 = (bf16[53,8,128]{2,1,0:T(8,128)(2,1)}, bf16[53,8,128]{2,1,0:T(8,128)(2,1)S(1)}, u32[]{:S(2)}, u32[]{:S(2)}) collective-permute-start(bf16[53,8,128]{2,1,0:T(8,128)(2,1)} %get-tuple-element.37), channel_id=1, source_target_pairs={{0,1},{1,0},{2,3},{3,2},{4,5},{5,4},{6,7},{7,6},{8,9},{9,8},{10,11... | collective-permute-start | bytes 325640 | tf_op jit(solution)/shard_map/ppermute | solution.py:403
  8.6 13.5 %collective-permute-start.3 = (bf16[53,8,128]{2,1,0:T(8,128)(2,1)}, bf16[53,8,128]{2,1,0:T(8,128)(2,1)S(1)}, u32[]{:S(2)}, u32[]{:S(2)}) collective-permute-start(bf16[53,8,128]{2,1,0:T(8,128)(2,1)} %get-tuple-element.38), channel_id=1, source_target_pairs={{0,2},{1,3},{2,0},{3,1},{4,6},{5,7},{6,4},{7,5},{8,10},{9,11},{10,... | collective-permute-start | bytes 325640 | tf_op jit(solution)/shard_map/ppermute | solution.py:403
  8.9 14.0 %collective-permute-start.4 = (bf16[53,8,128]{2,1,0:T(8,128)(2,1)}, bf16[53,8,128]{2,1,0:T(8,128)(2,1)S(1)}, u32[]{:S(2)}, u32[]{:S(2)}) collective-permute-start(bf16[53,8,128]{2,1,0:T(8,128)(2,1)} %get-tuple-element.39), channel_id=1, source_target_pairs={{0,3},{1,2},{2,1},{3,0},{4,7},{5,6},{6,5},{7,4},{8,11},{9,10},{10,... | collective-permute-start | bytes 325640 | tf_op jit(solution)/shard_map/ppermute | solution.py:403
  16.0 8.0 %collective-permute-start.5 = (bf16[53,8,128]{2,1,0:T(8,128)(2,1)}, bf16[53,8,128]{2,1,0:T(8,128)(2,1)S(1)}, u32[]{:S(2)}, u32[]{:S(2)}) collective-permute-start(bf16[53,8,128]{2,1,0:T(8,128)(2,1)} %get-tuple-element.40), channel_id=1, source_target_pairs={{0,12},{1,13},{2,14},{3,15},{4,8},{5,9},{6,10},{7,11},{8,4},{9,5},... | collective-permute-start | bytes 325640 | tf_op jit(solution)/shard_map/ppermute | solution.py:403
  18.9 8.9 %collective-permute-start.6 = (bf16[53,8,128]{2,1,0:T(8,128)(2,1)}, bf16[53,8,128]{2,1,0:T(8,128)(2,1)S(1)}, u32[]{:S(2)}, u32[]{:S(2)}) collective-permute-start(bf16[53,8,128]{2,1,0:T(8,128)(2,1)} %get-tuple-element.41), channel_id=1, source_target_pairs={{0,14},{1,15},{2,12},{3,13},{4,10},{5,11},{6,8},{7,9},{8,6},{9,7},... | collective-permute-start | bytes 325640 | tf_op jit(solution)/shard_map/ppermute | solution.py:403
  22.1 8.4 %collective-permute-start.7 = (bf16[53,8,128]{2,1,0:T(8,128)(2,1)}, bf16[53,8,128]{2,1,0:T(8,128)(2,1)S(1)}, u32[]{:S(2)}, u32[]{:S(2)}) collective-permute-start(bf16[53,8,128]{2,1,0:T(8,128)(2,1)} %get-tuple-element.42), channel_id=1, source_target_pairs={{0,4},{1,5},{2,6},{3,7},{4,0},{5,1},{6,2},{7,3},{8,12},{9,13},{10,... | collective-permute-start | bytes 325640 | tf_op jit(solution)/shard_map/ppermute | solution.py:403
  22.1 10.0 %collective-permute-start.8 = (bf16[53,8,128]{2,1,0:T(8,128)(2,1)}, bf16[53,8,128]{2,1,0:T(8,128)(2,1)S(1)}, u32[]{:S(2)}, u32[]{:S(2)}) collective-permute-start(bf16[53,8,128]{2,1,0:T(8,128)(2,1)} %get-tuple-element.43), channel_id=1, source_target_pairs={{0,9},{1,8},{2,11},{3,10},{4,13},{5,12},{6,15},{7,14},{8,1},{9,0},... | collective-permute-start | bytes 325640 | tf_op jit(solution)/shard_map/ppermute | solution.py:403
  22.9 11.9 %collective-permute-start.9 = (bf16[53,8,128]{2,1,0:T(8,128)(2,1)}, bf16[53,8,128]{2,1,0:T(8,128)(2,1)S(1)}, u32[]{:S(2)}, u32[]{:S(2)}) collective-permute-start(bf16[53,8,128]{2,1,0:T(8,128)(2,1)} %get-tuple-element.44), channel_id=1, source_target_pairs={{0,5},{1,4},{2,7},{3,6},{4,1},{5,0},{6,3},{7,2},{8,13},{9,12},{10,... | collective-permute-start | bytes 325640 | tf_op jit(solution)/shard_map/ppermute | solution.py:403
  24.0 16.5 %collective-permute-start.10 = (bf16[53,8,128]{2,1,0:T(8,128)(2,1)}, bf16[53,8,128]{2,1,0:T(8,128)(2,1)S(1)}, u32[]{:S(2)}, u32[]{:S(2)}) collective-permute-start(bf16[53,8,128]{2,1,0:T(8,128)(2,1)} %get-tuple-element.45), channel_id=1, source_target_pairs={{0,11},{1,10},{2,9},{3,8},{4,15},{5,14},{6,13},{7,12},{8,3},{9,2},... | collective-permute-start | bytes 325640 | tf_op jit(solution)/shard_map/ppermute | solution.py:403
  27.7 15.0 %collective-permute-start.11 = (bf16[53,8,128]{2,1,0:T(8,128)(2,1)}, bf16[53,8,128]{2,1,0:T(8,128)(2,1)S(1)}, u32[]{:S(2)}, u32[]{:S(2)}) collective-permute-start(bf16[53,8,128]{2,1,0:T(8,128)(2,1)} %get-tuple-element.46), channel_id=1, source_target_pairs={{0,6},{1,7},{2,4},{3,5},{4,2},{5,3},{6,0},{7,1},{8,14},{9,15},{10,... | collective-permute-start | bytes 325640 | tf_op jit(solution)/shard_map/ppermute | solution.py:403
  30.5 13.8 %collective-permute-start.12 = (bf16[53,8,128]{2,1,0:T(8,128)(2,1)}, bf16[53,8,128]{2,1,0:T(8,128)(2,1)S(1)}, u32[]{:S(2)}, u32[]{:S(2)}) collective-permute-start(bf16[53,8,128]{2,1,0:T(8,128)(2,1)} %get-tuple-element.47), channel_id=1, source_target_pairs={{0,7},{1,6},{2,5},{3,4},{4,3},{5,2},{6,1},{7,0},{8,15},{9,14},{10,... | collective-permute-start | bytes 325640 | tf_op jit(solution)/shard_map/ppermute | solution.py:403
  32.1 19.8 %collective-permute-start.15 = (bf16[48,8,128]{2,1,0:T(8,128)(2,1)}, bf16[48,8,128]{2,1,0:T(8,128)(2,1)S(1)}, u32[]{:S(2)}, u32[]{:S(2)}) collective-permute-start(bf16[48,8,128]{2,1,0:T(8,128)(2,1)} %get-tuple-element.53), channel_id=1, source_target_pairs={{0,13},{1,12},{2,15},{3,14},{4,9},{5,8},{6,11},{7,10},{8,5},{9,4},... | collective-permute-start | bytes 294920 | tf_op jit(solution)/shard_map/ppermute | solution.py:403
  34.8 17.1 %collective-permute-start.16 = (bf16[48,8,128]{2,1,0:T(8,128)(2,1)}, bf16[48,8,128]{2,1,0:T(8,128)(2,1)S(1)}, u32[]{:S(2)}, u32[]{:S(2)}) collective-permute-start(bf16[48,8,128]{2,1,0:T(8,128)(2,1)} %get-tuple-element.54), channel_id=1, source_target_pairs={{0,15},{1,14},{2,13},{3,12},{4,11},{5,10},{6,9},{7,8},{8,7},{9,6},... | collective-permute-start | bytes 294920 | tf_op jit(solution)/shard_map/ppermute | solution.py:403
  37.1 0.9 %copy-start = (bf16[53,8,128]{2,1,0:T(8,128)(2,1)S(1)}, bf16[53,8,128]{2,1,0:T(8,128)(2,1)}, u32[]{:S(2)}) copy-start(bf16[53,8,128]{2,1,0:T(8,128)(2,1)} %get-tuple-element.30.own_ref) | copy-start | bytes 325636
  38.0 0.7 %copy-start.1 = (f32[384,3]{0,1:T(4,128)S(1)}, f32[384,3]{0,1:T(4,128)}, u32[]{:S(2)}) copy-start(f32[384,3]{0,1:T(4,128)} %param.12) | copy-start | bytes 13828
  38.7 0.7 %copy-start.2 = (s32[384]{0:T(512)S(1)}, s32[384]{0:T(512)}, u32[]{:S(2)}) copy-start(s32[384]{0:T(512)} %param.13) | copy-start | bytes 4612
  39.3 0.7 %copy-start.3 = (s32[64,2]{0,1:T(2,128)S(1)}, s32[64,2]{0,1:T(2,128)}, u32[]{:S(2)}) copy-start(s32[64,2]{0,1:T(2,128)} %param.10) | copy-start | bytes 1540
  40.5 5.9 %collective-permute-start.14 = (bf16[5,8,128]{2,1,0:T(8,128)(2,1)S(1)}, bf16[5,8,128]{2,1,0:T(8,128)(2,1)S(1)}, u32[]{:S(2)}, u32[]{:S(2)}) collective-permute-start(bf16[5,8,128]{2,1,0:T(8,128)(2,1)S(1)} %get-tuple-element.48), channel_id=1, source_target_pairs={{0,15},{1,14},{2,13},{3,12},{4,11},{5,10},{6,9},{7,8},{8,7},{9,6},... | collective-permute-start | bytes 30728 | tf_op jit(solution)/shard_map/ppermute | solution.py:403
  42.7 4.9 %collective-permute-start.13 = (bf16[5,8,128]{2,1,0:T(8,128)(2,1)S(1)}, bf16[5,8,128]{2,1,0:T(8,128)(2,1)S(1)}, u32[]{:S(2)}, u32[]{:S(2)}) collective-permute-start(bf16[5,8,128]{2,1,0:T(8,128)(2,1)S(1)} %get-tuple-element.48), channel_id=1, source_target_pairs={{0,13},{1,12},{2,15},{3,14},{4,9},{5,8},{6,11},{7,10},{8,5},{9,4},... | collective-permute-start | bytes 30728 | tf_op jit(solution)/shard_map/ppermute | solution.py:403

commit v12 on v11

--- a/solution.py
+++ b/solution.py
@@ -97,6 +97,7 @@
     at = chunks * capacity
     if near > 1:
         pairs = [(meta_ref, outs[x].at[pl.ds(at, depth)]) for x in schedule(near)[0]]
+        pairs += [(meta_ref, outs[devices])]
     else:
         pairs = [(meta_ref, outs[1])]
     sends = start_all(pairs, sems.at[pl.ds(1, len(pairs))])
@@ -135,17 +136,6 @@
     for j in range(8):
         high_ref[j] = jnp.where(part == j, high, 0.0).astype(jnp.bfloat16)
         low_ref[j] = jnp.where(part == j, low, 0.0).astype(jnp.bfloat16)
-
-
-def ready_kernel(at, pairs_ref, weights_ref, offset_ref, own_ref, _, *rest):
-    meta_ref, own_out_ref, pairs_out_ref, high_ref, low_ref, sems = rest
-    moves = start_all(
-        [(own_ref.at[pl.ds(at, meta_ref.shape[0])], meta_ref), (own_ref, own_out_ref)], sems
-    )
-    pairs_out_ref[...] = pairs_ref[...]
-    interpolation(weights_ref[...], offset_ref[...], high_ref, low_ref)
-    for move in moves:
-        move.wait()
 
 
 def list_rows(owner, slot, target, capacity):
@@ -365,6 +355,7 @@
             shape((rows_at + (0 if x in late else depth), parts, LANES), bf16)
             for x in range(devices)
         ]
+        outs += [shape((depth, SUB, LANES), bf16)]
     else:
         outs = [shape((devices,) + block, bf16), shape((depth, SUB, LANES), bf16)]
     sent = pl.pallas_call(
@@ -382,7 +373,7 @@
             pltpu.VMEM((LANES, LANES), f32),
             pltpu.VMEM((depth, SUB, LANES), bf16),
             pltpu.VMEM((devices,) + block, bf16),
-            dma((5 + 2 * devices,)),
+            dma((6 + 2 * devices,)),
         ],
         compiler_params=most,
         name="pack_rows",
@@ -403,37 +394,22 @@
         return lax.ppermute(array, "bl", [(d, d ^ x) for d in range(devices)])
 
     if halves:
-        arrived = {x: swap(sent[x], x) for x in range(1, devices)}
-        meta, arrived[0], pairs, high, low = pl.pallas_call(
-            functools.partial(ready_kernel, rows_at),
-            out_shape=[
-                shape((depth, parts, LANES), bf16),
-                shape(sent[0].shape, bf16),
-                shape((2, owned), i32),
-            ]
-            + [shape((parts, LANES, channels), bf16)] * 2,
-            in_specs=[vmem] * 3 + [anywhere] * 2,
-            out_specs=[vmem] * 5,
-            scratch_shapes=[dma((2,))],
-            compiler_params=some,
-            name="interpolation",
-        )(pairs, weights, offset, sent[0], arrived[near])
-        passed = [swap(meta, x) for x in late]
+        passed = [swap(sent[devices], x) for x in late]
+        arrived = {x: swap(sent[x], x) if x else sent[x] for x in range(devices)}
     else:
         arrived = {
             0: lax.all_gather(sent[1], "bl", axis=0),
             1: lax.all_to_all(sent[0], "bl", split_axis=0, concat_axis=0, tiled=True),
         }
         order, late, passed = [0], [1], []
-        high, low = pl.pallas_call(
-            lambda w, o, h, l: interpolation(w[...], o[...], h, l),
-            out_shape=[shape((parts, LANES, channels), bf16)] * 2,
-            in_specs=[vmem] * 2,
-            out_specs=[vmem] * 2,
-            compiler_params=some,
-            name="interpolation",
-        )(weights, offset)
-
+    high, low = pl.pallas_call(
+        lambda w, o, h, l: interpolation(w[...], o[...], h, l),
+        out_shape=[shape((parts, LANES, channels), bf16)] * 2,
+        in_specs=[vmem] * 2,
+        out_specs=[vmem] * 2,
+        compiler_params=some,
+        name="interpolation",
+    )(weights, offset)
     gains, recip, slots, sums = pl.pallas_call(
         functools.partial(prepare_kernel, capacity, near, stations, order, late),
         out_shape=(

time: 54.6 us -> 58.1 us (1.064)
  starting transfers between devices: 28.2 us -> 32.6 us
  Pallas kernels: 10.2 us -> 9.03 us
    ppermute x17, starting transfers between devices: 28.2 us -> 32.6 us  [swap(): return lax.ppermute(array, 'bl', [(d, d ^ x) for d in range(devices)])]
    pallas_call x1, Pallas kernels: 4.3 us -> 3.47 us  [on_device(): pl.pallas_call(functools.partial(prepare_kernel, capacity, near, stations...]
  transfers between devices with their start and end apart: 17 -> 17, of which waited for: 6 -> 4; matrix products, arithmetic and copies ran while one was open for 0% -> 0% of each run, Pallas kernels for 9% -> 7%
where the time goes in v12:
time: 58.1 us; the launch traced here: 57.1 us
  starting transfers between devices  32.6 us (56%)
  waiting for transfers between devices  12.4 us (21%)
  Pallas kernels  9.03 us (16%)
  local copies, waits for them, and re-layouts  2.95 us (5%)
    ppermute x17, starting transfers between devices, swap(): return lax.ppermute(array, 'bl', [(d, d ^ x) for d in range(devices)])  32.6 us
    ppermute x17, waiting for transfers between devices, swap(): return lax.ppermute(array, 'bl', [(d, d ^ x) for d in range(devices)])  12.4 us
    pallas_call x1, Pallas kernels, on_device(): pl.pallas_call(functools.partial(prepare_kernel, capacity, near, stations...  3.47 us
    pallas_call x1, Pallas kernels, on_device(): pl.pallas_call(functools.partial(pack_kernel, capacity, near), out_shape=...  3.24 us
    unnamed x8, local copies, waits for them, and re-layouts  2.95 us
    pallas_call x1, Pallas kernels, on_device(): pl.pallas_call(functools.partial(finish_kernel, capacity, late), out_shap...  2.03 us
  transfers between devices with their start and end apart: 17, of which 4 were waited for; matrix products, arithmetic and copies ran while one was open for 0% of the time, Pallas kernels for 7%

profile of v12, /device:TPU:0, one launch (start us, length us, event | category | flops | bytes accessed | tf_op | source)
XLA Modules:
  0.0 57.1 jit_solution(7598506244933660669)
XLA Ops:
  0.0 3.2 %pack_rows.1 = (bf16[53,8,128]{2,1,0:T(8,128)(2,1)}, bf16[53,8,128]{2,1,0:T(8,128)(2,1)}, bf16[53,8,128]{2,1,0:T(8,128)(2,1)}, bf16[53,8,128]{2,1,0:T(8,128)(2,1...) custom-call(s32[1]{0:T(128)} %bitcast.me_s.turn_s, ...), custom_call_target="tpu_custom_call" | custom-call | tf_op jit(solution)/shard_map/pack_rows/pallas_call | solution.py:361
  3.2 4.1 %collective-permute-start = (bf16[53,8,128]{2,1,0:T(8,128)(2,1)}, bf16[53,8,128]{2,1,0:T(8,128)(2,1)S(1)}, u32[]{:S(2)}, u32[]{:S(2)}) collective-permute-start(bf16[53,8,128]{2,1,0:T(8,128)(2,1)} %get-tuple-element.31), channel_id=1, source_target_pairs={{0,8},{1,9},{2,10},{3,11},{4,12},{5,13},{6,14},{7,15},{8,0},{9,1},... | collective-permute-start | bytes 325640 | tf_op jit(solution)/shard_map/ppermute | solution.py:394
  7.3 1.3 %collective-permute-start.1 = (bf16[53,8,128]{2,1,0:T(8,128)(2,1)}, bf16[53,8,128]{2,1,0:T(8,128)(2,1)S(1)}, u32[]{:S(2)}, u32[]{:S(2)}) collective-permute-start(bf16[53,8,128]{2,1,0:T(8,128)(2,1)} %get-tuple-element.32), channel_id=1, source_target_pairs={{0,10},{1,11},{2,8},{3,9},{4,14},{5,15},{6,12},{7,13},{8,2},{9,3},... | collective-permute-start | bytes 325640 | tf_op jit(solution)/shard_map/ppermute | solution.py:394
  8.6 3.7 %collective-permute-start.14 = (bf16[5,8,128]{2,1,0:T(8,128)(2,1)}, bf16[5,8,128]{2,1,0:T(8,128)(2,1)S(1)}, u32[]{:S(2)}, u32[]{:S(2)}) collective-permute-start(bf16[5,8,128]{2,1,0:T(8,128)(2,1)} %get-tuple-element.44), channel_id=1, source_target_pairs={{0,15},{1,14},{2,13},{3,12},{4,11},{5,10},{6,9},{7,8},{8,7},{9,6},... | collective-permute-start | bytes 30728 | tf_op jit(solution)/shard_map/ppermute | solution.py:394
  12.4 2.3 %collective-permute-done.14.rest_15_ = bf16[5,8,128]{2,1,0:T(8,128)(2,1)S(1)} collective-permute-done((bf16[5,8,128]{2,1,0:T(8,128)(2,1)}, bf16[5,8,128]{2,1,0:T(8,128)(2,1)S(1)}, u32[]{:S(2)}, u32[]{:S(2)}) %collective-permute-start.14) | collective-permute-done | bytes 10272 | tf_op jit(solution)/shard_map/ppermute | solution.py:394
  14.7 0.7 %collective-permute-start.3 = (bf16[53,8,128]{2,1,0:T(8,128)(2,1)}, bf16[53,8,128]{2,1,0:T(8,128)(2,1)S(1)}, u32[]{:S(2)}, u32[]{:S(2)}) collective-permute-start(bf16[53,8,128]{2,1,0:T(8,128)(2,1)} %get-tuple-element.34), channel_id=1, source_target_pairs={{0,2},{1,3},{2,0},{3,1},{4,6},{5,7},{6,4},{7,5},{8,10},{9,11},{10,... | collective-permute-start | bytes 325640 | tf_op jit(solution)/shard_map/ppermute | solution.py:394
  15.4 2.1 %collective-permute-done.13.rest_14_ = bf16[5,8,128]{2,1,0:T(8,128)(2,1)S(1)} collective-permute-done((bf16[5,8,128]{2,1,0:T(8,128)(2,1)}, bf16[5,8,128]{2,1,0:T(8,128)(2,1)S(1)}, u32[]{:S(2)}, u32[]{:S(2)}) %collective-permute-start.13) | collective-permute-done | bytes 10272 | tf_op jit(solution)/shard_map/ppermute | solution.py:394
  17.5 1.3 %collective-permute-start.4 = (bf16[53,8,128]{2,1,0:T(8,128)(2,1)}, bf16[53,8,128]{2,1,0:T(8,128)(2,1)S(1)}, u32[]{:S(2)}, u32[]{:S(2)}) collective-permute-start(bf16[53,8,128]{2,1,0:T(8,128)(2,1)} %get-tuple-element.35), channel_id=1, source_target_pairs={{0,3},{1,2},{2,1},{3,0},{4,7},{5,6},{6,5},{7,4},{8,11},{9,10},{10,... | collective-permute-start | bytes 325640 | tf_op jit(solution)/shard_map/ppermute | solution.py:394
  18.8 1.3 %collective-permute-start.5 = (bf16[53,8,128]{2,1,0:T(8,128)(2,1)}, bf16[53,8,128]{2,1,0:T(8,128)(2,1)S(1)}, u32[]{:S(2)}, u32[]{:S(2)}) collective-permute-start(bf16[53,8,128]{2,1,0:T(8,128)(2,1)} %get-tuple-element.36), channel_id=1, source_target_pairs={{0,12},{1,13},{2,14},{3,15},{4,8},{5,9},{6,10},{7,11},{8,4},{9,5},... | collective-permute-start | bytes 325640 | tf_op jit(solution)/shard_map/ppermute | solution.py:394
  20.2 2.4 %collective-permute-start.6 = (bf16[53,8,128]{2,1,0:T(8,128)(2,1)}, bf16[53,8,128]{2,1,0:T(8,128)(2,1)S(1)}, u32[]{:S(2)}, u32[]{:S(2)}) collective-permute-start(bf16[53,8,128]{2,1,0:T(8,128)(2,1)} %get-tuple-element.37), channel_id=1, source_target_pairs={{0,14},{1,15},{2,12},{3,13},{4,10},{5,11},{6,8},{7,9},{8,6},{9,7},... | collective-permute-start | bytes 325640 | tf_op jit(solution)/shard_map/ppermute | solution.py:394
  22.6 1.3 %collective-permute-start.7 = (bf16[53,8,128]{2,1,0:T(8,128)(2,1)}, bf16[53,8,128]{2,1,0:T(8,128)(2,1)S(1)}, u32[]{:S(2)}, u32[]{:S(2)}) collective-permute-start(bf16[53,8,128]{2,1,0:T(8,128)(2,1)} %get-tuple-element.38), channel_id=1, source_target_pairs={{0,4},{1,5},{2,6},{3,7},{4,0},{5,1},{6,2},{7,3},{8,12},{9,13},{10,... | collective-permute-start | bytes 325640 | tf_op jit(solution)/shard_map/ppermute | solution.py:394
  23.9 1.9 %collective-permute-start.8 = (bf16[53,8,128]{2,1,0:T(8,128)(2,1)}, bf16[53,8,128]{2,1,0:T(8,128)(2,1)S(1)}, u32[]{:S(2)}, u32[]{:S(2)}) collective-permute-start(bf16[53,8,128]{2,1,0:T(8,128)(2,1)} %get-tuple-element.39), channel_id=1, source_target_pairs={{0,9},{1,8},{2,11},{3,10},{4,13},{5,12},{6,15},{7,14},{8,1},{9,0},... | collective-permute-start | bytes 325640 | tf_op jit(solution)/shard_map/ppermute | solution.py:394
  25.8 1.2 %collective-permute-start.9 = (bf16[53,8,128]{2,1,0:T(8,128)(2,1)}, bf16[53,8,128]{2,1,0:T(8,128)(2,1)S(1)}, u32[]{:S(2)}, u32[]{:S(2)}) collective-permute-start(bf16[53,8,128]{2,1,0:T(8,128)(2,1)} %get-tuple-element.40), channel_id=1, source_target_pairs={{0,5},{1,4},{2,7},{3,6},{4,1},{5,0},{6,3},{7,2},{8,13},{9,12},{10,... | collective-permute-start | bytes 325640 | tf_op jit(solution)/shard_map/ppermute | solution.py:394
  27.0 3.6 %collective-permute-start.10 = (bf16[53,8,128]{2,1,0:T(8,128)(2,1)}, bf16[53,8,128]{2,1,0:T(8,128)(2,1)S(1)}, u32[]{:S(2)}, u32[]{:S(2)}) collective-permute-start(bf16[53,8,128]{2,1,0:T(8,128)(2,1)} %get-tuple-element.41), channel_id=1, source_target_pairs={{0,11},{1,10},{2,9},{3,8},{4,15},{5,14},{6,13},{7,12},{8,3},{9,2},... | collective-permute-start | bytes 325640 | tf_op jit(solution)/shard_map/ppermute | solution.py:394
  30.6 6.2 %collective-permute-start.11 = (bf16[53,8,128]{2,1,0:T(8,128)(2,1)}, bf16[53,8,128]{2,1,0:T(8,128)(2,1)S(1)}, u32[]{:S(2)}, u32[]{:S(2)}) collective-permute-start(bf16[53,8,128]{2,1,0:T(8,128)(2,1)} %get-tuple-element.42), channel_id=1, source_target_pairs={{0,6},{1,7},{2,4},{3,5},{4,2},{5,3},{6,0},{7,1},{8,14},{9,15},{10,... | collective-permute-start | bytes 325640 | tf_op jit(solution)/shard_map/ppermute | solution.py:394
  36.8 3.3 %collective-permute-done.8.rest_9_ = bf16[53,8,128]{2,1,0:T(8,128)(2,1)S(1)} collective-permute-done((bf16[53,8,128]{2,1,0:T(8,128)(2,1)}, bf16[53,8,128]{2,1,0:T(8,128)(2,1)S(1)}, u32[]{:S(2)}, u32[]{:S(2)}) %collective-permute-start.8) | collective-permute-done | bytes 108576 | tf_op jit(solution)/shard_map/ppermute | solution.py:394
  40.1 1.0 %collective-permute-start.15 = (bf16[48,8,128]{2,1,0:T(8,128)(2,1)}, bf16[48,8,128]{2,1,0:T(8,128)(2,1)S(1)}, u32[]{:S(2)}, u32[]{:S(2)}) collective-permute-start(bf16[48,8,128]{2,1,0:T(8,128)(2,1)} %get-tuple-element.49), channel_id=1, source_target_pairs={{0,13},{1,12},{2,15},{3,14},{4,9},{5,8},{6,11},{7,10},{8,5},{9,4},... | collective-permute-start | bytes 294920 | tf_op jit(solution)/shard_map/ppermute | solution.py:394
  41.2 2.5 %collective-permute-start.16 = (bf16[48,8,128]{2,1,0:T(8,128)(2,1)}, bf16[48,8,128]{2,1,0:T(8,128)(2,1)S(1)}, u32[]{:S(2)}, u32[]{:S(2)}) collective-permute-start(bf16[48,8,128]{2,1,0:T(8,128)(2,1)} %get-tuple-element.50), channel_id=1, source_target_pairs={{0,15},{1,14},{2,13},{3,12},{4,11},{5,10},{6,9},{7,8},{8,7},{9,6},... | collective-permute-start | bytes 294920 | tf_op jit(solution)/shard_map/ppermute | solution.py:394
  43.6 0.7 %copy-done.1 = f32[384,3]{0,1:T(4,128)S(1)} copy-done((f32[384,3]{0,1:T(4,128)S(1)}, f32[384,3]{0,1:T(4,128)}, u32[]{:S(2)}) %copy-start.1) | copy-done | bytes 4632
  44.3 0.7 %copy-done.2 = s32[384]{0:T(512)S(1)} copy-done((s32[384]{0:T(512)S(1)}, s32[384]{0:T(512)}, u32[]{:S(2)}) %copy-start.2) | copy-done | bytes 1560
  45.3 4.6 %collective-permute-done.12.rest_13_ = bf16[53,8,128]{2,1,0:T(8,128)(2,1)S(1)} collective-permute-done((bf16[53,8,128]{2,1,0:T(8,128)(2,1)}, bf16[53,8,128]{2,1,0:T(8,128)(2,1)S(1)}, u32[]{:S(2)}, u32[]{:S(2)}) %collective-permute-start.12) | collective-permute-done | bytes 108576 | tf_op jit(solution)/shard_map/ppermute | solution.py:394
  50.0 0.9 %copy-done = bf16[53,8,128]{2,1,0:T(8,128)(2,1)S(1)} copy-done((bf16[53,8,128]{2,1,0:T(8,128)(2,1)S(1)}, bf16[53,8,128]{2,1,0:T(8,128)(2,1)}, u32[]{:S(2)}) %copy-start) | copy-done | bytes 108568
  51.5 3.5 %gains_and_sums.1 = (f32[8,128,384]{2,1,0:T(8,128)S(1)}, f32[64,128]{1,0:T(8,128)S(1)}, s32[16,128]{1,0:T(8,128)S(1)}, f32[3,64,8,128]{3,2,1,0:T(8,128)S(1)}) custom-call(s32[1]{0:T(128)} %bitcast.me_s.turn_s, s32[1]{0:T(128)} %bitcast.me_s.turn_s, s32[2,64]{1,0:T(2,128)S(1)} %bitcast.12, bf16[8,128,384]{2,1,0:T(8,128)(2,1)S(1)} %get-tuple-element.28.high_ref, ...), custom_call_target="tpu_custom_call" | custom-call | tf_op jit(solution)/shard_map/gains_and_sums/pallas_call | solution.py:413
  55.0 2.0 %sum_and_apply.1 = bf16[64,8,384]{2,1,0:T(8,128)(2,1)} custom-call(s32[16,128]{1,0:T(8,128)S(1)} %get-tuple-element.45.slots_s, f32[3,64,8,128]{3,2,1,0:T(8,128)S(1)} %get-tuple-element.46.sums_ref, f32[8,128,384]{2,1,0:T(8,128)S(1)} %get-tuple-element.47.gains_ref, f32[64,128]{1,0:T(8,128)S(1)} %get-tuple-element.48.recip_ref, ...), custom_call_target="tpu_custom_call" | custom-call | tf_op jit(solution)/shard_map/sum_and_apply/pallas_call | solution.py:442
  (22 shorter events, 1.1 us)
Async XLA Ops:
  3.2 15.6 %collective-permute-start = (bf16[53,8,128]{2,1,0:T(8,128)(2,1)}, bf16[53,8,128]{2,1,0:T(8,128)(2,1)S(1)}, u32[]{:S(2)}, u32[]{:S(2)}) collective-permute-start(bf16[53,8,128]{2,1,0:T(8,128)(2,1)} %get-tuple-element.31), channel_id=1, source_target_pairs={{0,8},{1,9},{2,10},{3,11},{4,12},{5,13},{6,14},{7,15},{8,0},{9,1},... | collective-permute-start | bytes 325640 | tf_op jit(solution)/shard_map/ppermute | solution.py:394
  7.3 12.8 %collective-permute-start.1 = (bf16[53,8,128]{2,1,0:T(8,128)(2,1)}, bf16[53,8,128]{2,1,0:T(8,128)(2,1)S(1)}, u32[]{:S(2)}, u32[]{:S(2)}) collective-permute-start(bf16[53,8,128]{2,1,0:T(8,128)(2,1)} %get-tuple-element.32), channel_id=1, source_target_pairs={{0,10},{1,11},{2,8},{3,9},{4,14},{5,15},{6,12},{7,13},{8,2},{9,3},... | collective-permute-start | bytes 325640 | tf_op jit(solution)/shard_map/ppermute | solution.py:394
  8.6 14.0 %collective-permute-start.2 = (bf16[53,8,128]{2,1,0:T(8,128)(2,1)}, bf16[53,8,128]{2,1,0:T(8,128)(2,1)S(1)}, u32[]{:S(2)}, u32[]{:S(2)}) collective-permute-start(bf16[53,8,128]{2,1,0:T(8,128)(2,1)} %get-tuple-element.33), channel_id=1, source_target_pairs={{0,1},{1,0},{2,3},{3,2},{4,5},{5,4},{6,7},{7,6},{8,9},{9,8},{10,11... | collective-permute-start | bytes 325640 | tf_op jit(solution)/shard_map/ppermute | solution.py:394
  8.6 6.1 %collective-permute-start.14 = (bf16[5,8,128]{2,1,0:T(8,128)(2,1)}, bf16[5,8,128]{2,1,0:T(8,128)(2,1)S(1)}, u32[]{:S(2)}, u32[]{:S(2)}) collective-permute-start(bf16[5,8,128]{2,1,0:T(8,128)(2,1)} %get-tuple-element.44), channel_id=1, source_target_pairs={{0,15},{1,14},{2,13},{3,12},{4,11},{5,10},{6,9},{7,8},{8,7},{9,6},... | collective-permute-start | bytes 30728 | tf_op jit(solution)/shard_map/ppermute | solution.py:394
  12.3 5.2 %collective-permute-start.13 = (bf16[5,8,128]{2,1,0:T(8,128)(2,1)}, bf16[5,8,128]{2,1,0:T(8,128)(2,1)S(1)}, u32[]{:S(2)}, u32[]{:S(2)}) collective-permute-start(bf16[5,8,128]{2,1,0:T(8,128)(2,1)} %get-tuple-element.44), channel_id=1, source_target_pairs={{0,13},{1,12},{2,15},{3,14},{4,9},{5,8},{6,11},{7,10},{8,5},{9,4},... | collective-permute-start | bytes 30728 | tf_op jit(solution)/shard_map/ppermute | solution.py:394
  14.7 9.2 %collective-permute-start.3 = (bf16[53,8,128]{2,1,0:T(8,128)(2,1)}, bf16[53,8,128]{2,1,0:T(8,128)(2,1)S(1)}, u32[]{:S(2)}, u32[]{:S(2)}) collective-permute-start(bf16[53,8,128]{2,1,0:T(8,128)(2,1)} %get-tuple-element.34), channel_id=1, source_target_pairs={{0,2},{1,3},{2,0},{3,1},{4,6},{5,7},{6,4},{7,5},{8,10},{9,11},{10,... | collective-permute-start | bytes 325640 | tf_op jit(solution)/shard_map/ppermute | solution.py:394
  17.5 8.3 %collective-permute-start.4 = (bf16[53,8,128]{2,1,0:T(8,128)(2,1)}, bf16[53,8,128]{2,1,0:T(8,128)(2,1)S(1)}, u32[]{:S(2)}, u32[]{:S(2)}) collective-permute-start(bf16[53,8,128]{2,1,0:T(8,128)(2,1)} %get-tuple-element.35), channel_id=1, source_target_pairs={{0,3},{1,2},{2,1},{3,0},{4,7},{5,6},{6,5},{7,4},{8,11},{9,10},{10,... | collective-permute-start | bytes 325640 | tf_op jit(solution)/shard_map/ppermute | solution.py:394
  18.8 8.2 %collective-permute-start.5 = (bf16[53,8,128]{2,1,0:T(8,128)(2,1)}, bf16[53,8,128]{2,1,0:T(8,128)(2,1)S(1)}, u32[]{:S(2)}, u32[]{:S(2)}) collective-permute-start(bf16[53,8,128]{2,1,0:T(8,128)(2,1)} %get-tuple-element.36), channel_id=1, source_target_pairs={{0,12},{1,13},{2,14},{3,15},{4,8},{5,9},{6,10},{7,11},{8,4},{9,5},... | collective-permute-start | bytes 325640 | tf_op jit(solution)/shard_map/ppermute | solution.py:394
  20.2 10.5 %collective-permute-start.6 = (bf16[53,8,128]{2,1,0:T(8,128)(2,1)}, bf16[53,8,128]{2,1,0:T(8,128)(2,1)S(1)}, u32[]{:S(2)}, u32[]{:S(2)}) collective-permute-start(bf16[53,8,128]{2,1,0:T(8,128)(2,1)} %get-tuple-element.37), channel_id=1, source_target_pairs={{0,14},{1,15},{2,12},{3,13},{4,10},{5,11},{6,8},{7,9},{8,6},{9,7},... | collective-permute-start | bytes 325640 | tf_op jit(solution)/shard_map/ppermute | solution.py:394
  22.6 14.2 %collective-permute-start.7 = (bf16[53,8,128]{2,1,0:T(8,128)(2,1)}, bf16[53,8,128]{2,1,0:T(8,128)(2,1)S(1)}, u32[]{:S(2)}, u32[]{:S(2)}) collective-permute-start(bf16[53,8,128]{2,1,0:T(8,128)(2,1)} %get-tuple-element.38), channel_id=1, source_target_pairs={{0,4},{1,5},{2,6},{3,7},{4,0},{5,1},{6,2},{7,3},{8,12},{9,13},{10,... | collective-permute-start | bytes 325640 | tf_op jit(solution)/shard_map/ppermute | solution.py:394
  23.9 16.2 %collective-permute-start.8 = (bf16[53,8,128]{2,1,0:T(8,128)(2,1)}, bf16[53,8,128]{2,1,0:T(8,128)(2,1)S(1)}, u32[]{:S(2)}, u32[]{:S(2)}) collective-permute-start(bf16[53,8,128]{2,1,0:T(8,128)(2,1)} %get-tuple-element.39), channel_id=1, source_target_pairs={{0,9},{1,8},{2,11},{3,10},{4,13},{5,12},{6,15},{7,14},{8,1},{9,0},... | collective-permute-start | bytes 325640 | tf_op jit(solution)/shard_map/ppermute | solution.py:394
  25.8 15.3 %collective-permute-start.9 = (bf16[53,8,128]{2,1,0:T(8,128)(2,1)}, bf16[53,8,128]{2,1,0:T(8,128)(2,1)S(1)}, u32[]{:S(2)}, u32[]{:S(2)}) collective-permute-start(bf16[53,8,128]{2,1,0:T(8,128)(2,1)} %get-tuple-element.40), channel_id=1, source_target_pairs={{0,5},{1,4},{2,7},{3,6},{4,1},{5,0},{6,3},{7,2},{8,13},{9,12},{10,... | collective-permute-start | bytes 325640 | tf_op jit(solution)/shard_map/ppermute | solution.py:394
  27.0 18.3 %collective-permute-start.10 = (bf16[53,8,128]{2,1,0:T(8,128)(2,1)}, bf16[53,8,128]{2,1,0:T(8,128)(2,1)S(1)}, u32[]{:S(2)}, u32[]{:S(2)}) collective-permute-start(bf16[53,8,128]{2,1,0:T(8,128)(2,1)} %get-tuple-element.41), channel_id=1, source_target_pairs={{0,11},{1,10},{2,9},{3,8},{4,15},{5,14},{6,13},{7,12},{8,3},{9,2},... | collective-permute-start | bytes 325640 | tf_op jit(solution)/shard_map/ppermute | solution.py:394
  30.6 14.7 %collective-permute-start.11 = (bf16[53,8,128]{2,1,0:T(8,128)(2,1)}, bf16[53,8,128]{2,1,0:T(8,128)(2,1)S(1)}, u32[]{:S(2)}, u32[]{:S(2)}) collective-permute-start(bf16[53,8,128]{2,1,0:T(8,128)(2,1)} %get-tuple-element.42), channel_id=1, source_target_pairs={{0,6},{1,7},{2,4},{3,5},{4,2},{5,3},{6,0},{7,1},{8,14},{9,15},{10,... | collective-permute-start | bytes 325640 | tf_op jit(solution)/shard_map/ppermute | solution.py:394
  36.8 13.1 %collective-permute-start.12 = (bf16[53,8,128]{2,1,0:T(8,128)(2,1)}, bf16[53,8,128]{2,1,0:T(8,128)(2,1)S(1)}, u32[]{:S(2)}, u32[]{:S(2)}) collective-permute-start(bf16[53,8,128]{2,1,0:T(8,128)(2,1)} %get-tuple-element.43), channel_id=1, source_target_pairs={{0,7},{1,6},{2,5},{3,4},{4,3},{5,2},{6,1},{7,0},{8,15},{9,14},{10,... | collective-permute-start | bytes 325640 | tf_op jit(solution)/shard_map/ppermute | solution.py:394
  40.1 14.9 %collective-permute-start.15 = (bf16[48,8,128]{2,1,0:T(8,128)(2,1)}, bf16[48,8,128]{2,1,0:T(8,128)(2,1)S(1)}, u32[]{:S(2)}, u32[]{:S(2)}) collective-permute-start(bf16[48,8,128]{2,1,0:T(8,128)(2,1)} %get-tuple-element.49), channel_id=1, source_target_pairs={{0,13},{1,12},{2,15},{3,14},{4,9},{5,8},{6,11},{7,10},{8,5},{9,4},... | collective-permute-start | bytes 294920 | tf_op jit(solution)/shard_map/ppermute | solution.py:394
  41.2 13.9 %collective-permute-start.16 = (bf16[48,8,128]{2,1,0:T(8,128)(2,1)}, bf16[48,8,128]{2,1,0:T(8,128)(2,1)S(1)}, u32[]{:S(2)}, u32[]{:S(2)}) collective-permute-start(bf16[48,8,128]{2,1,0:T(8,128)(2,1)} %get-tuple-element.50), channel_id=1, source_target_pairs={{0,15},{1,14},{2,13},{3,12},{4,11},{5,10},{6,9},{7,8},{8,7},{9,6},... | collective-permute-start | bytes 294920 | tf_op jit(solution)/shard_map/ppermute | solution.py:394
  43.6 0.7 %copy-start.1 = (f32[384,3]{0,1:T(4,128)S(1)}, f32[384,3]{0,1:T(4,128)}, u32[]{:S(2)}) copy-start(f32[384,3]{0,1:T(4,128)} %param.12) | copy-start | bytes 13828
  44.3 0.7 %copy-start.2 = (s32[384]{0:T(512)S(1)}, s32[384]{0:T(512)}, u32[]{:S(2)}) copy-start(s32[384]{0:T(512)} %param.13) | copy-start | bytes 4612
  50.0 0.9 %copy-start = (bf16[53,8,128]{2,1,0:T(8,128)(2,1)S(1)}, bf16[53,8,128]{2,1,0:T(8,128)(2,1)}, u32[]{:S(2)}) copy-start(bf16[53,8,128]{2,1,0:T(8,128)(2,1)} %get-tuple-element.30.rest_0_) | copy-start | bytes 325636
  50.9 0.7 %copy-start.3 = (s32[64,2]{0,1:T(2,128)S(1)}, s32[64,2]{0,1:T(2,128)}, u32[]{:S(2)}) copy-start(s32[64,2]{0,1:T(2,128)} %param.10) | copy-start | bytes 1540
